TPU v7x, 128 devices: a whole 4x4x4 slice. The times are simulated.
128 devices in a mesh: rep: 8 (over x_hi, z), shard: 16 (over y, x_lo, core).
Axes of the slice: x: 4 (x_hi: 2, x_lo: 2; x = x_hi * 2 + x_lo), y: 4, z: 4, core: 2. Of those that a mesh axis runs over, the one named last changes fastest.
Arguments:
- tokens: bfloat16 [16384, 1536], P(('rep', 'shard')), may hold values from -6 to 6
- cotangent: bfloat16 [16384, 1536], P(('rep', 'shard')), may hold values from -6 to 6
- seq_lengths: int32 [8, 32], P('rep'), may hold values from 16 to 112, as said below
- seq_order: int32 [8, 32], P('rep'), may hold values from 0 to 31, as said below
- routes: int32 [16384, 4], P(('rep', 'shard')), may hold values from 0 to 7, all different within a row; in each aligned block of 128 rows (0 to 127, 128 to 255, ...) at most 80 rows name the same one
- gate_weights: float32 [16384, 4], P(('rep', 'shard')), may hold values from 0.1 to 0.5
- attn_gain: bfloat16 [1536], P('shard'), may hold values from 0.5 to 1.5
- w_query: bfloat16 [1536, 1536], P('shard'), may hold values from -0.15625 to 0.15625
- key_value_weight: bfloat16 [1536, 512], P('shard'), may hold values from -0.15625 to 0.15625
- w_out: bfloat16 [1536, 1536], P('shard'), may hold values from -1.25 to 1.25
- ffn_gain: bfloat16 [1536], P('shard'), may hold values from 0.5 to 1.5
- w_gateup: bfloat16 [8, 1536, 1536], P(None, 'shard'), may hold values from -0.15625 to 0.15625
- w_down: bfloat16 [8, 768, 1536], P(None, 'shard'), may hold values from -0.21875 to 0.21875
Outputs:
- output: bfloat16 [16384, 1536], P(('rep', 'shard'))
- grad_tokens: bfloat16 [16384, 1536], P(('rep', 'shard'))
- grad_attn_gain: float32 [1536], P('shard')
- grad_query: float32 [1536, 1536], P('shard')
- grad_keyval: float32 [1536, 512], P('shard')
- grad_out: float32 [1536, 1536], P('shard')
- grad_ffn_gain: float32 [1536], P('shard')
- grad_gateup: float32 [8, 1536, 1536], P(None, 'shard')
- grad_down: float32 [8, 768, 1536], P(None, 'shard')
Inputs may be any that keep to these rules, and one draw needn't show every extreme that they name: `seq_lengths`: each group's sequences come in pairs that seq_order places on one device, and each pair's lengths sum to 128. `seq_order`: each row is a permutation; entries 2j and 2j + 1 of row g name the two sequences of device j of group g. `routes`: each row names 4 different experts; among the rows of one device no expert is named more than 80 times.
All inputs are finite; a program needn't handle non-finite values.
Results may differ from a plain program's by a relative error of at most 0.024.
Values may be sent and summed in bfloat16 or wider, within the bound.
No kernel may reach another device: no remote copies, remote signals or barrier semaphores. Data moves between devices by JAX's collectives and lax.ppermute only.
A program may use at most 192 MiB of HBM per device.

v0:
```python
import jax
import jax.numpy as jnp
from jax import lax
from jax.sharding import PartitionSpec as P

QUERY_HEADS = 12
KEY_VALUE_HEADS = 2
HEAD_SIZE = 128
FF = 768
CAP = 80


epsilon = 1e-06
rope_base = 10000.0


def sequence_layout(lengths, placed, device_slots, rows_each):
    starts = jnp.cumsum(lengths) - lengths
    first_index = placed[2 * device_slots]
    second_index = placed[2 * device_slots + 1]
    first_length = lengths[first_index]
    offsets = jnp.arange(rows_each, dtype=jnp.int32)[None, :]
    in_first = offsets < first_length[:, None]
    sequence = jnp.where(in_first, first_index[:, None], second_index[:, None])
    token_position = jnp.where(in_first, offsets, offsets - first_length[:, None])
    source = starts[sequence] + token_position
    segment = jnp.where(in_first, 0, 1)
    return (source, token_position, segment.astype(jnp.int32))


def slot_table(routes, gate_weights, experts, capacity):
    block_list = routes.shape[0]
    rows_each = routes.shape[1]
    expert_ids = jnp.arange(experts, dtype=jnp.int32)
    chosen = routes[..., None] == expert_ids
    member = jnp.any(chosen, axis=2).astype(jnp.int32)
    weight = jnp.sum(jnp.where(chosen, gate_weights[..., None], 0.0), axis=2)
    place = jnp.cumsum(member, axis=1) - 1
    target = jnp.transpose(jnp.where(member > 0, place, capacity), (0, 2, 1))
    block_ids = jnp.arange(block_list, dtype=jnp.int32)[:, None, None]
    token_ids = jnp.broadcast_to(
        jnp.arange(rows_each, dtype=jnp.int32)[None, None, :], target.shape
    )
    table = jnp.zeros((block_list, experts, capacity + 1), jnp.int32)
    table = table.at[block_ids, expert_ids[None, :, None], target].set(token_ids)[:, :, :capacity]
    count = jnp.sum(member, axis=1)
    filled = jnp.arange(capacity, dtype=jnp.int32)[None, None, :] < count[:, :, None]
    table = jnp.where(filled, table, 0)
    slot_weight = jnp.take_along_axis(jnp.transpose(weight, (0, 2, 1)), table, axis=2)
    slot_weight = jnp.where(filled, slot_weight, 0.0)
    return (table, slot_weight)


def rotary_embed(values, token_position, direction):
    half_width = values.shape[-1] // 2
    frequency = rope_base ** (-jnp.arange(half_width, dtype=jnp.float32) / half_width)
    angle = token_position.astype(jnp.float32)[:, None] * frequency[None, :]
    cosine = jnp.cos(angle)[:, None, :]
    sine_turn = direction * jnp.sin(angle)[:, None, :]
    first = values[..., :half_width]
    second = values[..., half_width:]
    return jnp.concatenate(
        [first * cosine - second * sine_turn, second * cosine + first * sine_turn], axis=-1
    )


def norm_back(values, factor, gain_row, upstream):
    grad_normed = upstream * gain_row
    grad_gain = jnp.sum(upstream * values * factor, axis=0)
    cubed = factor * factor * factor
    grad_input = factor * grad_normed - values * cubed * jnp.mean(
        grad_normed * values, axis=-1, keepdims=True
    )
    return (grad_input, grad_gain)


def per_device(
    tokens,
    cotangent,
    seq_lengths,
    seq_order,
    routes,
    gate_weights,
    attn_gain,
    w_query,
    key_value_weight,
    w_out,
    ffn_gain,
    w_gateup,
    w_down,
):
    shard_count = lax.axis_size("shard")
    shard_index = lax.axis_index("shard")
    device_local_rows = tokens.shape[0]
    model_width = tokens.shape[1]
    expert_count = w_down.shape[0]
    group_rows = device_local_rows * shard_count
    key_value_width = KEY_VALUE_HEADS * HEAD_SIZE
    score_scale = HEAD_SIZE ** (-0.5)
    every_slot = jnp.arange(shard_count, dtype=jnp.int32)
    source_all, gathered_positions, gathered_segments = sequence_layout(
        seq_lengths[0], seq_order[0], every_slot, device_local_rows
    )
    source = source_all[shard_index]
    token_position = gathered_positions[shard_index]
    segment = gathered_segments[shard_index]
    inverse_all = (
        jnp.zeros((group_rows,), jnp.int32)
        .at[source_all.reshape(-1)]
        .set(jnp.arange(group_rows, dtype=jnp.int32))
    )
    inverse = lax.dynamic_slice_in_dim(
        inverse_all, shard_index * device_local_rows, device_local_rows
    )
    gathered = lax.all_gather(tokens, "shard", axis=0, tiled=True)
    dealt_wide = gathered[source].astype(jnp.float32)
    query_full, keyval_full, output_full, gain_attn, gain_ffn = (
        lax.all_gather(w_query, "shard", axis=0, tiled=True),
        lax.all_gather(key_value_weight, "shard", axis=0, tiled=True),
        lax.all_gather(w_out, "shard", axis=0, tiled=True),
        lax.all_gather(attn_gain, "shard", axis=0, tiled=True),
        lax.all_gather(ffn_gain, "shard", axis=0, tiled=True),
    )
    gain_attn_wide = gain_attn.astype(jnp.float32)
    gain_ffn_wide = gain_ffn.astype(jnp.float32)
    attn_factor = lax.rsqrt(jnp.mean(dealt_wide * dealt_wide, axis=-1, keepdims=True) + epsilon)
    normed = (dealt_wide * attn_factor * gain_attn_wide).astype(jnp.bfloat16)
    query_pre = jnp.dot(normed, query_full, preferred_element_type=jnp.float32)
    key_value_projected = jnp.dot(normed, keyval_full, preferred_element_type=jnp.float32)
    query_matrix = rotary_embed(
        query_pre.reshape(device_local_rows, QUERY_HEADS, HEAD_SIZE), token_position, 1.0
    ).astype(jnp.bfloat16)
    key_matrix = rotary_embed(
        key_value_projected[:, :key_value_width].reshape(
            device_local_rows, KEY_VALUE_HEADS, HEAD_SIZE
        ),
        token_position,
        1.0,
    ).astype(jnp.bfloat16)
    value_matrix = (
        key_value_projected[:, key_value_width:]
        .reshape(device_local_rows, KEY_VALUE_HEADS, HEAD_SIZE)
        .astype(jnp.bfloat16)
    )
    grouped_heads = query_matrix.reshape(
        device_local_rows, KEY_VALUE_HEADS, QUERY_HEADS // KEY_VALUE_HEADS, HEAD_SIZE
    )
    row_index = jnp.arange(device_local_rows)
    allowed = (row_index[None, :] <= row_index[:, None]) & (segment[None, :] == segment[:, None])
    raw_scores = jnp.einsum(
        "sgrd,tgd->grst", grouped_heads, key_matrix, preferred_element_type=jnp.float32
    )
    scores = jnp.where(allowed, raw_scores * score_scale, -1000000000.0)
    highest = jnp.max(scores, axis=-1, keepdims=True)
    exp_scores = jnp.exp(scores - highest)
    row_total = jnp.sum(exp_scores, axis=-1, keepdims=True)
    prob_low = (exp_scores / row_total).astype(jnp.bfloat16)
    mixed = jnp.einsum("grst,tgd->sgrd", prob_low, value_matrix, preferred_element_type=jnp.float32)
    attention_output = mixed.reshape(device_local_rows, QUERY_HEADS * HEAD_SIZE).astype(
        jnp.bfloat16
    )
    branch = jnp.dot(attention_output, output_full, preferred_element_type=jnp.float32).astype(
        jnp.bfloat16
    )
    branch_all = lax.all_gather(branch, "shard", axis=0, tiled=True)
    residual = tokens.astype(jnp.float32) + branch_all[inverse].astype(jnp.float32)
    ffn_factor = lax.rsqrt(jnp.mean(residual * residual, axis=-1, keepdims=True) + epsilon)
    normed_ffn = (residual * ffn_factor * gain_ffn_wide).astype(jnp.bfloat16)
    slot_rows, slot_weight = slot_table(routes[None], gate_weights[None], expert_count, CAP)
    slot_rows = slot_rows[0]
    slot_weight = slot_weight[0]

    def expert_forward(carried, inputs):
        gateup_part, down_part, pick_rows, pick_weight = inputs
        gateup_full, down_full = (
            lax.all_gather(gateup_part, "shard", axis=0, tiled=True),
            lax.all_gather(down_part, "shard", axis=0, tiled=True),
        )
        picked = normed_ffn[pick_rows]
        pre_act = jnp.dot(picked, gateup_full, preferred_element_type=jnp.float32)
        acted = (jax.nn.silu(pre_act[:, :FF]) * pre_act[:, FF:]).astype(jnp.bfloat16)
        result = jnp.dot(acted, down_full, preferred_element_type=jnp.float32)
        kept_weights = ()
        return (carried, (result * pick_weight[:, None], pre_act, kept_weights))

    carried, (weighted_out, pre_all, kept_all) = lax.scan(
        expert_forward, jnp.zeros((), jnp.float32), (w_gateup, w_down, slot_rows, slot_weight)
    )
    mixture = (
        jnp.zeros((device_local_rows, model_width), jnp.float32)
        .at[slot_rows.reshape(-1)]
        .add(weighted_out.reshape(-1, model_width))
    )
    output = (residual + mixture).astype(jnp.bfloat16)
    upstream = cotangent.astype(jnp.float32)

    def expert_backward(carried, inputs):
        gateup_part, down_part, pick_rows, pick_weight, pre_act, kept_weights = inputs
        gateup_full, down_full = (
            lax.all_gather(gateup_part, "shard", axis=0, tiled=True),
            lax.all_gather(down_part, "shard", axis=0, tiled=True),
        )
        picked = normed_ffn[pick_rows]
        grad_out = (pick_weight[:, None] * upstream[pick_rows]).astype(jnp.bfloat16)
        gate_pre = pre_act[:, :FF]
        up_pre = pre_act[:, FF:]
        sigmoid_gate = jax.nn.sigmoid(gate_pre)
        silu_gate = gate_pre * sigmoid_gate
        acted = (silu_gate * up_pre).astype(jnp.bfloat16)
        grad_act = jnp.dot(grad_out, down_full.T, preferred_element_type=jnp.float32)
        grad_gate = grad_act * up_pre * sigmoid_gate * (1.0 + gate_pre * (1.0 - sigmoid_gate))
        grad_up = grad_act * silu_gate
        grad_both = jnp.concatenate([grad_gate, grad_up], axis=1).astype(jnp.bfloat16)
        grad_picked = jnp.dot(grad_both, gateup_full.T, preferred_element_type=jnp.float32)
        grad_down = jnp.dot(acted.T, grad_out, preferred_element_type=jnp.float32)
        grad_gateup = jnp.dot(picked.T, grad_both, preferred_element_type=jnp.float32)
        shard_gateup, shard_down = (
            lax.psum_scatter(
                grad_gateup.astype(jnp.bfloat16), "shard", scatter_dimension=0, tiled=True
            ).astype(jnp.float32),
            lax.psum_scatter(
                grad_down.astype(jnp.bfloat16), "shard", scatter_dimension=0, tiled=True
            ).astype(jnp.float32),
        )
        return (carried, (shard_gateup, shard_down, grad_picked))

    carried, (gateup_shards, down_shards, picked_grads) = lax.scan(
        expert_backward,
        jnp.zeros((), jnp.float32),
        (w_gateup, w_down, slot_rows, slot_weight, pre_all, kept_all),
    )
    grad_ffn_in = (
        jnp.zeros((device_local_rows, model_width), jnp.float32)
        .at[slot_rows.reshape(-1)]
        .add(picked_grads.reshape(-1, model_width))
    )
    grad_from_norm, grad_gain_ffn = norm_back(residual, ffn_factor, gain_ffn_wide, grad_ffn_in)
    grad_residual = upstream + grad_from_norm
    grad_sent = grad_residual.astype(jnp.bfloat16)
    grad_dealt = lax.all_gather(grad_sent, "shard", axis=0, tiled=True)[source]
    query_full, keyval_full, output_full = (
        lax.all_gather(w_query, "shard", axis=0, tiled=True),
        lax.all_gather(key_value_weight, "shard", axis=0, tiled=True),
        lax.all_gather(w_out, "shard", axis=0, tiled=True),
    )
    grad_output_w = jnp.dot(attention_output.T, grad_dealt, preferred_element_type=jnp.float32)
    gradient_attention_output = jnp.dot(
        grad_dealt, output_full.T, preferred_element_type=jnp.float32
    ).astype(jnp.bfloat16)
    gradient_attention_output = gradient_attention_output.reshape(
        device_local_rows, KEY_VALUE_HEADS, QUERY_HEADS // KEY_VALUE_HEADS, HEAD_SIZE
    )
    raw_again = jnp.einsum(
        "sgrd,tgd->grst", grouped_heads, key_matrix, preferred_element_type=jnp.float32
    )
    scores_again = jnp.where(allowed, raw_again * score_scale, -1000000000.0)
    prob_full = jnp.exp(scores_again - highest) / row_total
    prob_again = prob_full.astype(jnp.bfloat16)
    grad_probs = jnp.einsum(
        "sgrd,tgd->grst",
        gradient_attention_output,
        value_matrix,
        preferred_element_type=jnp.float32,
    )
    grad_values = jnp.einsum(
        "grst,sgrd->tgd", prob_again, gradient_attention_output, preferred_element_type=jnp.float32
    )
    inner = jnp.sum(prob_full * grad_probs, axis=-1, keepdims=True)
    grad_raw = (prob_full * (grad_probs - inner) * score_scale).astype(jnp.bfloat16)
    grad_grouped = jnp.einsum(
        "grst,tgd->sgrd", grad_raw, key_matrix, preferred_element_type=jnp.float32
    )
    grad_keys = jnp.einsum(
        "grst,sgrd->tgd", grad_raw, grouped_heads, preferred_element_type=jnp.float32
    )
    grad_query_in = (
        rotary_embed(
            grad_grouped.reshape(device_local_rows, QUERY_HEADS, HEAD_SIZE), token_position, -1.0
        )
        .reshape(device_local_rows, QUERY_HEADS * HEAD_SIZE)
        .astype(jnp.bfloat16)
    )
    grad_key_in = rotary_embed(grad_keys, token_position, -1.0).reshape(
        device_local_rows, key_value_width
    )
    grad_keyval_in = jnp.concatenate(
        [grad_key_in, grad_values.reshape(device_local_rows, key_value_width)], axis=1
    ).astype(jnp.bfloat16)
    grad_query_w = jnp.dot(normed.T, grad_query_in, preferred_element_type=jnp.float32)
    grad_keyval_w = jnp.dot(normed.T, grad_keyval_in, preferred_element_type=jnp.float32)
    grad_normed = jnp.dot(
        grad_query_in, query_full.T, preferred_element_type=jnp.float32
    ) + jnp.dot(grad_keyval_in, keyval_full.T, preferred_element_type=jnp.float32)
    grad_dealt_in, grad_gain_attn = norm_back(dealt_wide, attn_factor, gain_attn_wide, grad_normed)
    back_all = lax.all_gather(grad_dealt_in.astype(jnp.bfloat16), "shard", axis=0, tiled=True)
    grad_tokens = (grad_residual + back_all[inverse].astype(jnp.float32)).astype(jnp.bfloat16)
    query_shard, keyval_shard, output_shard, attn_gain_shard, ffn_gain_shard = (
        lax.psum_scatter(
            grad_query_w.astype(jnp.bfloat16), "shard", scatter_dimension=0, tiled=True
        ).astype(jnp.float32),
        lax.psum_scatter(
            grad_keyval_w.astype(jnp.bfloat16), "shard", scatter_dimension=0, tiled=True
        ).astype(jnp.float32),
        lax.psum_scatter(
            grad_output_w.astype(jnp.bfloat16), "shard", scatter_dimension=0, tiled=True
        ).astype(jnp.float32),
        lax.psum_scatter(
            grad_gain_attn.astype(jnp.bfloat16), "shard", scatter_dimension=0, tiled=True
        ).astype(jnp.float32),
        lax.psum_scatter(
            grad_gain_ffn.astype(jnp.bfloat16), "shard", scatter_dimension=0, tiled=True
        ).astype(jnp.float32),
    )
    summed = (
        lax.psum(attn_gain_shard.astype(jnp.bfloat16), "rep").astype(jnp.float32),
        lax.psum(query_shard.astype(jnp.bfloat16), "rep").astype(jnp.float32),
        lax.psum(keyval_shard.astype(jnp.bfloat16), "rep").astype(jnp.float32),
        lax.psum(output_shard.astype(jnp.bfloat16), "rep").astype(jnp.float32),
        lax.psum(ffn_gain_shard.astype(jnp.bfloat16), "rep").astype(jnp.float32),
        lax.psum(gateup_shards.astype(jnp.bfloat16), "rep").astype(jnp.float32),
        lax.psum(down_shards.astype(jnp.bfloat16), "rep").astype(jnp.float32),
    )
    return (
        output,
        grad_tokens,
        summed[0],
        summed[1],
        summed[2],
        summed[3],
        summed[4],
        summed[5],
        summed[6],
    )


def solution(mesh):
    placed = (
        P(("rep", "shard"), None),
        P(("rep", "shard"), None),
        P("rep", None),
        P("rep", None),
        P(("rep", "shard"), None),
        P(("rep", "shard"), None),
        P("shard"),
        P("shard", None),
        P("shard", None),
        P("shard", None),
        P("shard"),
        P(None, "shard", None),
        P(None, "shard", None),
    )
    return jax.shard_map(
        per_device,
        mesh=mesh,
        in_specs=placed,
        out_specs=(
            P(("rep", "shard"), None),
            P(("rep", "shard"), None),
            P("shard"),
            P("shard", None),
            P("shard", None),
            P("shard", None),
            P("shard"),
            P(None, "shard", None),
            P(None, "shard", None),
        ),
        check_vma=False,
    )
```

profile of v0, /device:TPU:0, one launch (start us, length us, event | category | flops | bytes accessed | tf_op | source)
XLA Modules:
  0.0 3094.4 jit_solution(16774037115488381902)
XLA Ops:
  93.2 38.5 %all-gather.28.cloned.1.call-done = bf16[1536,1536]{1,0:T(8,128)(2,1)} async-done(((bf16[96,1536]{1,0:T(8,128)(2,1)}), bf16[1536,1536]{1,0:T(8,128)(2,1)}) %all-gather.28.cloned.1.call-update) | async-done | bytes 4718608 | tf_op jit(solution)/shard_map/all_gather | solution.py:118
  228.9 651.7 %while.26 = (s32[]{:T(128)}, f32[8,80,1536]{2,1,0:T(8,128)}, f32[8,80,1536]{2,1,0:T(8,128)}, s32[8,80]{1,0:T(8,128)S(1)}, bf16[128,1536]{1,0:T(8,128)(2,1)S(1)},...) while((s32[]{:T(128)}, f32[8,80,1536]{2,1,0:T(8,128)}, ...), condition=%wide.region_12.13_spmd, body=%wide.region_11.12_spmd.sunk | while | flops 566723840 | bytes 33233292 | solution.py:186
  883.0 1751.0 %while.27 = (s32[]{:T(128)}, bf16[8,96,1536]{2,1,0:T(8,128)(2,1)}, bf16[8,48,1536]{2,1,0:T(8,128)(2,1)}, f32[8,80,1536]{2,1,0:T(8,128)}, s32[8,80]{1,0:T(8,128)S...) while((s32[]{:T(128)}, bf16[8,96,1536]{2,1,0:T(8,128)(2,1)}, ...), condition=%wide.region_17.18_spmd, body=%wide.region_14.17_spmd.sunk | while | flops 1138865408 | bytes 67416528 | solution.py:227
  926.8 61.3 %reduce-scatter.14.cloned.1.call-done = bf16[48,1536]{1,0:T(8,128)(2,1)} async-done(((bf16[768,1536]{1,0:T(8,128)(2,1)}), bf16[48,1536]{1,0:T(8,128)(2,1)}) %reduce-scatter.14.cloned.1.call-update) | async-done | bytes 147472 | tf_op jit(solution)/shard_map/while/body/eval_jaxpr/reduce_scatter | solution.py:221
  1032.0 69.2 %reduce-scatter.12.cloned.1.call-done = bf16[96,1536]{1,0:T(8,128)(2,1)} async-done(((bf16[1536,1536]{1,0:T(8,128)(2,1)}), bf16[96,1536]{1,0:T(8,128)(2,1)}) %reduce-scatter.12.cloned.1.call-update) | async-done | bytes 294928 | tf_op jit(solution)/shard_map/while/body/eval_jaxpr/reduce_scatter | solution.py:218
  1145.5 61.2 %reduce-scatter.14.cloned.1.call-done = bf16[48,1536]{1,0:T(8,128)(2,1)} async-done(((bf16[768,1536]{1,0:T(8,128)(2,1)}), bf16[48,1536]{1,0:T(8,128)(2,1)}) %reduce-scatter.14.cloned.1.call-update) | async-done | bytes 147472 | tf_op jit(solution)/shard_map/while/body/eval_jaxpr/reduce_scatter | solution.py:221
  1250.7 69.3 %reduce-scatter.12.cloned.1.call-done = bf16[96,1536]{1,0:T(8,128)(2,1)} async-done(((bf16[1536,1536]{1,0:T(8,128)(2,1)}), bf16[96,1536]{1,0:T(8,128)(2,1)}) %reduce-scatter.12.cloned.1.call-update) | async-done | bytes 294928 | tf_op jit(solution)/shard_map/while/body/eval_jaxpr/reduce_scatter | solution.py:218
  1364.0 61.3 %reduce-scatter.14.cloned.1.call-done = bf16[48,1536]{1,0:T(8,128)(2,1)} async-done(((bf16[768,1536]{1,0:T(8,128)(2,1)}), bf16[48,1536]{1,0:T(8,128)(2,1)}) %reduce-scatter.14.cloned.1.call-update) | async-done | bytes 147472 | tf_op jit(solution)/shard_map/while/body/eval_jaxpr/reduce_scatter | solution.py:221
  1469.3 69.0 %reduce-scatter.12.cloned.1.call-done = bf16[96,1536]{1,0:T(8,128)(2,1)} async-done(((bf16[1536,1536]{1,0:T(8,128)(2,1)}), bf16[96,1536]{1,0:T(8,128)(2,1)}) %reduce-scatter.12.cloned.1.call-update) | async-done | bytes 294928 | tf_op jit(solution)/shard_map/while/body/eval_jaxpr/reduce_scatter | solution.py:218
  1583.0 61.3 %reduce-scatter.14.cloned.1.call-done = bf16[48,1536]{1,0:T(8,128)(2,1)} async-done(((bf16[768,1536]{1,0:T(8,128)(2,1)}), bf16[48,1536]{1,0:T(8,128)(2,1)}) %reduce-scatter.14.cloned.1.call-update) | async-done | bytes 147472 | tf_op jit(solution)/shard_map/while/body/eval_jaxpr/reduce_scatter | solution.py:221
  1688.2 69.2 %reduce-scatter.12.cloned.1.call-done = bf16[96,1536]{1,0:T(8,128)(2,1)} async-done(((bf16[1536,1536]{1,0:T(8,128)(2,1)}), bf16[96,1536]{1,0:T(8,128)(2,1)}) %reduce-scatter.12.cloned.1.call-update) | async-done | bytes 294928 | tf_op jit(solution)/shard_map/while/body/eval_jaxpr/reduce_scatter | solution.py:218
  1801.8 61.2 %reduce-scatter.14.cloned.1.call-done = bf16[48,1536]{1,0:T(8,128)(2,1)} async-done(((bf16[768,1536]{1,0:T(8,128)(2,1)}), bf16[48,1536]{1,0:T(8,128)(2,1)}) %reduce-scatter.14.cloned.1.call-update) | async-done | bytes 147472 | tf_op jit(solution)/shard_map/while/body/eval_jaxpr/reduce_scatter | solution.py:221
  1907.0 69.2 %reduce-scatter.12.cloned.1.call-done = bf16[96,1536]{1,0:T(8,128)(2,1)} async-done(((bf16[1536,1536]{1,0:T(8,128)(2,1)}), bf16[96,1536]{1,0:T(8,128)(2,1)}) %reduce-scatter.12.cloned.1.call-update) | async-done | bytes 294928 | tf_op jit(solution)/shard_map/while/body/eval_jaxpr/reduce_scatter | solution.py:218
  2020.8 61.2 %reduce-scatter.14.cloned.1.call-done = bf16[48,1536]{1,0:T(8,128)(2,1)} async-done(((bf16[768,1536]{1,0:T(8,128)(2,1)}), bf16[48,1536]{1,0:T(8,128)(2,1)}) %reduce-scatter.14.cloned.1.call-update) | async-done | bytes 147472 | tf_op jit(solution)/shard_map/while/body/eval_jaxpr/reduce_scatter | solution.py:221
  2126.0 69.1 %reduce-scatter.12.cloned.1.call-done = bf16[96,1536]{1,0:T(8,128)(2,1)} async-done(((bf16[1536,1536]{1,0:T(8,128)(2,1)}), bf16[96,1536]{1,0:T(8,128)(2,1)}) %reduce-scatter.12.cloned.1.call-update) | async-done | bytes 294928 | tf_op jit(solution)/shard_map/while/body/eval_jaxpr/reduce_scatter | solution.py:218
  2239.4 61.2 %reduce-scatter.14.cloned.1.call-done = bf16[48,1536]{1,0:T(8,128)(2,1)} async-done(((bf16[768,1536]{1,0:T(8,128)(2,1)}), bf16[48,1536]{1,0:T(8,128)(2,1)}) %reduce-scatter.14.cloned.1.call-update) | async-done | bytes 147472 | tf_op jit(solution)/shard_map/while/body/eval_jaxpr/reduce_scatter | solution.py:221
  2344.4 69.2 %reduce-scatter.12.cloned.1.call-done = bf16[96,1536]{1,0:T(8,128)(2,1)} async-done(((bf16[1536,1536]{1,0:T(8,128)(2,1)}), bf16[96,1536]{1,0:T(8,128)(2,1)}) %reduce-scatter.12.cloned.1.call-update) | async-done | bytes 294928 | tf_op jit(solution)/shard_map/while/body/eval_jaxpr/reduce_scatter | solution.py:218
  2458.1 61.2 %reduce-scatter.14.cloned.1.call-done = bf16[48,1536]{1,0:T(8,128)(2,1)} async-done(((bf16[768,1536]{1,0:T(8,128)(2,1)}), bf16[48,1536]{1,0:T(8,128)(2,1)}) %reduce-scatter.14.cloned.1.call-update) | async-done | bytes 147472 | tf_op jit(solution)/shard_map/while/body/eval_jaxpr/reduce_scatter | solution.py:221
  2563.3 69.0 %reduce-scatter.12.cloned.1.call-done = bf16[96,1536]{1,0:T(8,128)(2,1)} async-done(((bf16[1536,1536]{1,0:T(8,128)(2,1)}), bf16[96,1536]{1,0:T(8,128)(2,1)}) %reduce-scatter.12.cloned.1.call-update) | async-done | bytes 294928 | tf_op jit(solution)/shard_map/while/body/eval_jaxpr/reduce_scatter | solution.py:218
  2651.4 40.7 %all-gather.34.cloned.1.call-done = bf16[2048,1536]{1,0:T(8,128)(2,1)} async-done(((bf16[128,1536]{1,0:T(8,128)(2,1)}), bf16[2048,1536]{1,0:T(8,128)(2,1)}) %all-gather.34.cloned.1.call-update) | async-done | bytes 6291472 | tf_op jit(solution)/shard_map/all_gather | solution.py:240
  2725.0 47.2 %reduce-scatter.8.cloned.1.call-done = bf16[96,512]{1,0:T(8,128)(2,1)} async-done(((bf16[1536,512]{1,0:T(8,128)(2,1)}), bf16[96,512]{1,0:T(8,128)(2,1)}) %reduce-scatter.8.cloned.1.call-update) | async-done | bytes 98320 | tf_op jit(solution)/shard_map/reduce_scatter | solution.py:301
  2772.2 72.1 %reduce-scatter.10.cloned.1.call-done = bf16[96,1536]{1,0:T(8,128)(2,1)} async-done(((bf16[1536,1536]{1,0:T(8,128)(2,1)}), bf16[96,1536]{1,0:T(8,128)(2,1)}) %reduce-scatter.10.cloned.1.call-update) | async-done | bytes 294928 | tf_op jit(solution)/shard_map/reduce_scatter | solution.py:304
  2844.3 72.9 %reduce-scatter.6.cloned.1.call-done = bf16[96,1536]{1,0:T(8,128)(2,1)} async-done(((bf16[1536,1536]{1,0:T(8,128)(2,1)}), bf16[96,1536]{1,0:T(8,128)(2,1)}) %reduce-scatter.6.cloned.1.call-update) | async-done | bytes 294928 | tf_op jit(solution)/shard_map/reduce_scatter | solution.py:298
  2993.1 85.5 %all-reduce.10.cloned.1.call-done = (bf16[96,1536]{1,0:T(8,128)(2,1)}, bf16[96,512]{1,0:T(8,128)(2,1)}, bf16[96,1536]{1,0:T(8,128)(2,1)}, bf16[8,96,1536]{2,1,0:T(8,128)(2,1)}, bf16[8,48,1536]{2,1,0:T(8,128)(2,1)}) async-done(((bf16[96,1536]{1,0:T(8,128)(2,1)}, bf16[96,512]{1,0:T(8,128)(2,1)}, bf16[96,1536]{1,0:T(8,128)(2,1)}, bf16[8,96,1536]{2,1,0:T(8,128)(2,1)}, bf16[8,48,1536]{2,1,0:T(8,128)(2,1)}), ...) | async-done | bytes 4227088 | tf_op jit(solution)/shard_map/psum | solution.py:316
  (594 shorter events, 1676.8 us)
Async XLA Ops:
  8.7 122.9 %all-gather.28.cloned.1.call-start = ((), (), s32[]{:S(2)}) async-start(), calls=%async_computation.7 | async-start | bytes 5013504 | tf_op jit(solution)/shard_map/all_gather | solution.py:118
  9.4 162.4 %all-gather.30.cloned.1.call-start = ((), (), s32[]{:S(2)}) async-start(), calls=%async_computation.8 | async-start | bytes 5013504 | tf_op jit(solution)/shard_map/all_gather | solution.py:120
  10.0 208.2 %all-gather.32.cloned.1.call-start = ((), (), s32[]{:S(2)}) async-start(), calls=%async_computation.9 | async-start | bytes 6684672 | tf_op jit(solution)/shard_map/all_gather | solution.py:165
  889.5 137.8 %all-gather.44.cloned.1.call-start = ((), (), s32[]{:S(2)}) async-start(), calls=%async_computation.21 | async-start | bytes 5013504 | tf_op jit(solution)/shard_map/while/body/eval_jaxpr/all_gather | solution.py:200
  891.3 209.9 %reduce-scatter.12.cloned.1.call-start = ((), (), s32[]{:S(2)}) async-start(), calls=%async_computation.19 | async-start | bytes 5013504 | tf_op jit(solution)/shard_map/while/body/eval_jaxpr/reduce_scatter | solution.py:218
  1109.4 136.7 %all-gather.44.cloned.1.call-start = ((), (), s32[]{:S(2)}) async-start(), calls=%async_computation.21 | async-start | bytes 5013504 | tf_op jit(solution)/shard_map/while/body/eval_jaxpr/all_gather | solution.py:200
  1111.1 208.8 %reduce-scatter.12.cloned.1.call-start = ((), (), s32[]{:S(2)}) async-start(), calls=%async_computation.19 | async-start | bytes 5013504 | tf_op jit(solution)/shard_map/while/body/eval_jaxpr/reduce_scatter | solution.py:218
  1328.1 136.5 %all-gather.44.cloned.1.call-start = ((), (), s32[]{:S(2)}) async-start(), calls=%async_computation.21 | async-start | bytes 5013504 | tf_op jit(solution)/shard_map/while/body/eval_jaxpr/all_gather | solution.py:200
  1329.9 208.4 %reduce-scatter.12.cloned.1.call-start = ((), (), s32[]{:S(2)}) async-start(), calls=%async_computation.19 | async-start | bytes 5013504 | tf_op jit(solution)/shard_map/while/body/eval_jaxpr/reduce_scatter | solution.py:218
  1546.5 137.0 %all-gather.44.cloned.1.call-start = ((), (), s32[]{:S(2)}) async-start(), calls=%async_computation.21 | async-start | bytes 5013504 | tf_op jit(solution)/shard_map/while/body/eval_jaxpr/all_gather | solution.py:200
  1548.3 209.1 %reduce-scatter.12.cloned.1.call-start = ((), (), s32[]{:S(2)}) async-start(), calls=%async_computation.19 | async-start | bytes 5013504 | tf_op jit(solution)/shard_map/while/body/eval_jaxpr/reduce_scatter | solution.py:218
  1765.5 136.8 %all-gather.44.cloned.1.call-start = ((), (), s32[]{:S(2)}) async-start(), calls=%async_computation.21 | async-start | bytes 5013504 | tf_op jit(solution)/shard_map/while/body/eval_jaxpr/all_gather | solution.py:200
  1767.3 208.9 %reduce-scatter.12.cloned.1.call-start = ((), (), s32[]{:S(2)}) async-start(), calls=%async_computation.19 | async-start | bytes 5013504 | tf_op jit(solution)/shard_map/while/body/eval_jaxpr/reduce_scatter | solution.py:218
  1984.4 137.0 %all-gather.44.cloned.1.call-start = ((), (), s32[]{:S(2)}) async-start(), calls=%async_computation.21 | async-start | bytes 5013504 | tf_op jit(solution)/shard_map/while/body/eval_jaxpr/all_gather | solution.py:200
  1986.1 208.9 %reduce-scatter.12.cloned.1.call-start = ((), (), s32[]{:S(2)}) async-start(), calls=%async_computation.19 | async-start | bytes 5013504 | tf_op jit(solution)/shard_map/while/body/eval_jaxpr/reduce_scatter | solution.py:218
  2203.2 136.5 %all-gather.44.cloned.1.call-start = ((), (), s32[]{:S(2)}) async-start(), calls=%async_computation.21 | async-start | bytes 5013504 | tf_op jit(solution)/shard_map/while/body/eval_jaxpr/all_gather | solution.py:200
  2205.0 208.6 %reduce-scatter.12.cloned.1.call-start = ((), (), s32[]{:S(2)}) async-start(), calls=%async_computation.19 | async-start | bytes 5013504 | tf_op jit(solution)/shard_map/while/body/eval_jaxpr/reduce_scatter | solution.py:218
  2421.7 136.8 %all-gather.44.cloned.1.call-start = ((), (), s32[]{:S(2)}) async-start(), calls=%async_computation.21 | async-start | bytes 5013504 | tf_op jit(solution)/shard_map/while/body/eval_jaxpr/all_gather | solution.py:200
  2423.5 208.8 %reduce-scatter.12.cloned.1.call-start = ((), (), s32[]{:S(2)}) async-start(), calls=%async_computation.19 | async-start | bytes 5013504 | tf_op jit(solution)/shard_map/while/body/eval_jaxpr/reduce_scatter | solution.py:218
  2650.7 121.6 %reduce-scatter.8.cloned.1.call-start = ((), (), s32[]{:S(2)}) async-start(), calls=%async_computation.13 | async-start | bytes 1671168 | tf_op jit(solution)/shard_map/reduce_scatter | solution.py:301
  2708.7 135.6 %reduce-scatter.10.cloned.1.call-start = ((), (), s32[]{:S(2)}) async-start(), calls=%async_computation.14 | async-start | bytes 5013504 | tf_op jit(solution)/shard_map/reduce_scatter | solution.py:304
  2712.4 204.8 %reduce-scatter.6.cloned.1.call-start = ((), (), s32[]{:S(2)}) async-start(), calls=%async_computation.12 | async-start | bytes 5013504 | tf_op jit(solution)/shard_map/reduce_scatter | solution.py:298
  2718.9 268.3 %all-gather.36.cloned.1.call-start = ((), (), s32[]{:S(2)}) async-start(), calls=%async_computation.11 | async-start | bytes 6684672 | tf_op jit(solution)/shard_map/all_gather | solution.py:295
  2725.0 353.6 %all-reduce.10.cloned.1.call-start = ((), (), s32[]{:S(2)}) async-start(), calls=%async_computation.15 | async-start | bytes 8454144 | tf_op jit(solution)/shard_map/psum | solution.py:316
  (100 other events, 4746.4 us)
Sparse Core Ops, SparseCore 0:
  9.7 45.7 all-gather.23
  175.9 42.2 all-gather.31
  923.2 64.9 reduce-scatter.13
  1030.5 70.6 reduce-scatter.11
  1141.7 64.9 reduce-scatter.13
  1249.1 70.7 reduce-scatter.11
  1360.3 64.9 reduce-scatter.13
  1467.6 70.6 reduce-scatter.11
  1579.3 64.9 reduce-scatter.13
  1686.5 70.8 reduce-scatter.11
  1798.0 64.9 reduce-scatter.13
  1905.5 70.6 reduce-scatter.11
  2017.0 64.9 reduce-scatter.13
  2124.3 70.6 reduce-scatter.11
  2235.6 64.9 reduce-scatter.13
  2342.7 70.8 reduce-scatter.11
  2454.2 64.9 reduce-scatter.13
  2561.5 70.6 reduce-scatter.11
  2650.8 41.3 all-gather.33
  2708.8 63.3 reduce-scatter.7
  2774.8 69.4 reduce-scatter.9
  2847.5 69.6 reduce-scatter.5
  2919.4 42.5 all-gather.35
  2965.6 112.8 all-reduce.9
  (35 shorter events, 1262.1 us)
where the time goes:
time: 3110 us; the launch traced here: 3090 us
  waiting for transfers between devices  2560 us (82%)
  matrix products  197 us (6%)
  local copies, waits for them, and re-layouts  158 us (5%)
  blocking collectives  87.3 us (3%)
  other arithmetic  74.1 us (2%)
    reduce_scatter x8, waiting for transfers between devices, expert_backward(): lax.psum_scatter(grad_gateup.astype(jnp.bfloat16), 'shard', scatter_dimen...  553 us
    reduce_scatter x8, waiting for transfers between devices, expert_backward(): lax.psum_scatter(grad_down.astype(jnp.bfloat16), 'shard', scatter_dimensi...  490 us
    all_gather x8, waiting for transfers between devices, expert_backward(): lax.all_gather(gateup_part, 'shard', axis=0, tiled=True)  302 us
    all_gather x8, waiting for transfers between devices, expert_forward(): lax.all_gather(gateup_part, 'shard', axis=0, tiled=True)  294 us
    all_gather x8, waiting for transfers between devices, expert_forward(): lax.all_gather(down_part, 'shard', axis=0, tiled=True)  262 us
    all_gather x8, waiting for transfers between devices, expert_backward(): lax.all_gather(down_part, 'shard', axis=0, tiled=True)  221 us
    psum x1, waiting for transfers between devices, per_device(): lax.psum(query_shard.astype(jnp.bfloat16), 'rep').astype(jnp.float32)  85.5 us
    reduce_scatter x1, waiting for transfers between devices, per_device(): lax.psum_scatter(grad_query_w.astype(jnp.bfloat16), 'shard', scatter_dime...  72.9 us
  transfers between devices with their start and end apart: 59, of which 57 were waited for; matrix products, arithmetic and copies ran while one was open for 10% of the time, Pallas kernels for 0%

commit v1 on v0

v1 whole, which is shorter than its diff:
```python
import jax
import jax.numpy as jnp
from jax import lax
from jax.sharding import Mesh, PartitionSpec as P

QUERY_HEADS = 12
KEY_VALUE_HEADS = 2
GROUP = QUERY_HEADS // KEY_VALUE_HEADS
HEAD_SIZE = 128
CAP = 80

EPSILON = 1e-06
ROPE_BASE = 10000.0
SHARD = ("y", "x", "c")
CHIPS = ("y", "x")
SWAP = [(0, 1), (1, 0)]

bf16 = jnp.bfloat16
f32 = jnp.float32


def exchange(parts, axes):
    return lax.all_to_all(parts, axes, 0, 0, tiled=True)


def matmul(left, right):
    return jnp.dot(left, right, preferred_element_type=f32)


def dot_general(left, right, dims):
    return lax.dot_general(left, right, (dims, ((), ())), preferred_element_type=f32)


def in_core_order(core, mine, other):
    return jnp.where(core == 0, jnp.stack([mine, other], 1), jnp.stack([other, mine], 1))


def rotary_tables(position):
    half = HEAD_SIZE // 2
    frequency = ROPE_BASE ** (-jnp.arange(half, dtype=f32) / half)
    angle = position.astype(f32)[:, None] * frequency[None, :]
    return jnp.cos(angle)[:, None, :], jnp.sin(angle)[:, None, :]


def rotate(values, cosine, sine):
    half = values.shape[-1] // 2
    first, second = values[..., :half], values[..., half:]
    return jnp.concatenate(
        [first * cosine - second * sine, second * cosine + first * sine], axis=-1
    )


def norm_back(values, factor, gain_row, upstream):
    grad_normed = upstream * gain_row
    grad_gain = jnp.sum(upstream * values * factor, axis=0)
    cubed = factor * factor * factor
    grad_input = factor * grad_normed - values * cubed * jnp.mean(
        grad_normed * values, axis=-1, keepdims=True
    )
    return grad_input, grad_gain


def cut(rows, ways):
    *lead, a, b = rows.shape
    wide = ways // 2
    n = len(lead)
    cut_up = rows.reshape(*lead, 2, a // 2, wide, b // wide)
    order = (n, n + 2, *range(n), n + 1, n + 3)
    return cut_up.transpose(order).reshape(ways, *lead, a // 2, b // wide)


def uncut(pieces, ways):
    _, *lead, a, b = pieces.shape
    wide = ways // 2
    n = len(lead)
    whole = pieces.reshape(2, wide, *lead, a, b)
    order = (*range(2, 2 + n), 0, 2 + n, 1, 3 + n)
    return whole.transpose(order).reshape(*lead, 2 * a, wide * b)


def spread(part, ways, axes):
    return exchange(jnp.broadcast_to(part[None], (ways, *part.shape)), axes)


def per_device(
    tokens,
    cotangent,
    seq_lengths,
    seq_order,
    routes,
    gate_weights,
    attn_gain,
    w_query,
    key_value_weight,
    w_out,
    ffn_gain,
    w_gateup,
    w_down,
):
    reps = lax.axis_size("rep")
    shards = lax.axis_size("y") * lax.axis_size("x") * lax.axis_size("c")
    core = lax.axis_index("c")
    shard = (lax.axis_index("y") * lax.axis_size("x") + lax.axis_index("x")) * 2 + core
    rows, width = tokens.shape
    experts = w_gateup.shape[0]
    ff = w_gateup.shape[2] // 2
    kv_width = KEY_VALUE_HEADS * HEAD_SIZE
    scale = HEAD_SIZE ** (-0.5)

    gains = spread(jnp.stack([attn_gain, ffn_gain]), shards, SHARD)
    gains = gains.transpose(1, 0, 2).reshape(2, width).astype(f32)
    gain_attn, gain_ffn = gains[0], gains[1]
    qkv_full = lax.all_gather(
        jnp.concatenate([w_query, key_value_weight], 1), SHARD, axis=0, tiled=True
    )
    out_full = lax.all_gather(w_out, SHARD, axis=0, tiled=True)
    gateup_mine = exchange(w_gateup, CHIPS)
    down_mine = exchange(w_down, CHIPS)
    gateup_full = in_core_order(core, gateup_mine, lax.ppermute(gateup_mine, "c", SWAP))
    gateup_full = gateup_full.reshape(width, 2 * ff)
    down_full = in_core_order(core, down_mine, lax.ppermute(down_mine, "c", SWAP))
    down_full = down_full.reshape(ff, width)

    chosen = routes[:, :, None] == jnp.arange(experts, dtype=jnp.int32)
    member = jnp.any(chosen, axis=1)
    weight = jnp.sum(jnp.where(chosen, gate_weights[:, :, None], 0.0), axis=1)
    place = jnp.cumsum(member.astype(jnp.int32), axis=0) - 1
    slot = jnp.where(member, place, -1).T
    picks = slot[:, None, :] == jnp.arange(CAP, dtype=jnp.int32)[None, :, None]
    pick = picks.astype(bf16).reshape(experts * CAP, rows)
    slot_weight = jnp.sum(jnp.where(picks, weight.T[:, None, :], 0.0), axis=2)
    upstream = cotangent.astype(f32)
    grad_out_sent = matmul(pick, cotangent) * slot_weight.reshape(-1, 1)
    grad_out = exchange(grad_out_sent.astype(bf16), CHIPS)

    lengths = seq_lengths[0]
    starts = jnp.cumsum(lengths) - lengths
    row_at = shard * rows + jnp.arange(rows, dtype=jnp.int32)
    first_at = jnp.max(jnp.where(starts[None, :] <= row_at[:, None], starts[None, :], 0), axis=1)
    cosine, sine = rotary_tables(row_at - first_at)
    key_at = (shard - 1) * rows + jnp.arange(2 * rows, dtype=jnp.int32)
    allowed = (key_at[None, :] <= row_at[:, None]) & (key_at[None, :] >= first_at[:, None])

    wide = tokens.astype(f32)
    attn_factor = lax.rsqrt(jnp.mean(wide * wide, axis=-1, keepdims=True) + EPSILON)
    normed = (wide * attn_factor * gain_attn).astype(bf16)
    normed_all = lax.all_gather(normed, SHARD, axis=0, tiled=True)
    qkv = matmul(normed, qkv_full)
    turned = rotate(
        qkv[:, : width + kv_width].reshape(rows, QUERY_HEADS + KEY_VALUE_HEADS, HEAD_SIZE),
        cosine,
        sine,
    ).astype(bf16)
    queries = turned[:, :QUERY_HEADS].reshape(rows, KEY_VALUE_HEADS, GROUP, HEAD_SIZE)
    keyval = jnp.concatenate(
        [turned[:, QUERY_HEADS:].reshape(rows, kv_width), qkv[:, width + kv_width :].astype(bf16)],
        axis=1,
    )
    ring = [(i, (i + 1) % shards) for i in range(shards)]
    back_ring = [((i + 1) % shards, i) for i in range(shards)]
    keyval = jnp.concatenate([lax.ppermute(keyval, SHARD, ring), keyval], axis=0)
    keys = keyval[:, :kv_width].reshape(2 * rows, KEY_VALUE_HEADS, HEAD_SIZE)
    values = keyval[:, kv_width:].reshape(2 * rows, KEY_VALUE_HEADS, HEAD_SIZE)
    raw = jnp.einsum("sgrd,tgd->grst", queries, keys, preferred_element_type=f32)
    scores = jnp.where(allowed, raw * scale, -1000000000.0)
    exp_scores = jnp.exp(scores - jnp.max(scores, axis=-1, keepdims=True))
    probs = exp_scores / jnp.sum(exp_scores, axis=-1, keepdims=True)
    prob_low = probs.astype(bf16)
    mixed = jnp.einsum("grst,tgd->sgrd", prob_low, values, preferred_element_type=f32)
    attended = mixed.reshape(rows, width).astype(bf16)
    branch = matmul(attended, out_full).astype(bf16)
    residual = wide + branch.astype(f32)
    ffn_factor = lax.rsqrt(jnp.mean(residual * residual, axis=-1, keepdims=True) + EPSILON)
    normed_ffn = (residual * ffn_factor * gain_ffn).astype(bf16)
    attended_cols = exchange(attended.T, SHARD).reshape(shards, width // shards, rows)

    picked = exchange(matmul(pick, normed_ffn).astype(bf16), CHIPS)
    pre = matmul(picked, gateup_full)
    gate, up = pre[:, :ff], pre[:, ff:]
    sigmoid = jax.nn.sigmoid(gate)
    silu = gate * sigmoid
    acted = (silu * up).astype(bf16)
    expert_out = exchange(matmul(acted, down_full).astype(bf16), CHIPS)
    grad_act = dot_general(grad_out, down_full, ((1,), (1,)))
    grad_gate = grad_act * up * sigmoid * (1.0 + gate * (1.0 - sigmoid))
    grad_pre = jnp.concatenate([grad_gate, grad_act * silu], axis=1).astype(bf16)
    grad_picked = dot_general(grad_pre, gateup_full, ((1,), (1,)))
    grad_picked = exchange(grad_picked.astype(bf16), CHIPS)
    grad_down = dot_general(acted, grad_out, ((0,), (0,)))
    grad_gateup = dot_general(picked, grad_pre, ((0,), (0,)))

    def owned(grad):
        halves = grad.reshape(experts, 2, -1, width)
        here = jnp.where(core == 0, halves[:, 0], halves[:, 1])
        there = jnp.where(core == 0, halves[:, 1], halves[:, 0])
        return here + lax.ppermute(there.astype(bf16), "c", SWAP).astype(f32)

    both = jnp.concatenate([owned(grad_gateup), owned(grad_down)], axis=1).astype(bf16)
    over_rep = exchange(cut(both, reps), "rep").astype(f32).sum(axis=0).astype(bf16)
    expert_grads = uncut(spread(exchange(over_rep, CHIPS), reps, "rep"), reps).astype(f32)
    shard_gateup = expert_grads[:, : width // shards]
    shard_down = expert_grads[:, width // shards :]

    back = pick.astype(f32) * slot_weight.reshape(-1, 1)
    back_high = back.astype(bf16)
    back_low = (back - back_high.astype(f32)).astype(bf16)
    mixture = dot_general(back_high, expert_out, ((0,), (0,)))
    mixture = mixture + dot_general(back_low, expert_out, ((0,), (0,)))
    output = (residual + mixture).astype(bf16)
    grad_ffn_in = dot_general(pick, grad_picked, ((0,), (0,)))
    grad_from_norm, grad_gain_ffn = norm_back(residual, ffn_factor, gain_ffn, grad_ffn_in)
    grad_residual = upstream + grad_from_norm
    grad_branch = grad_residual.astype(bf16)
    grad_branch_all = lax.all_gather(grad_branch, SHARD, axis=0, tiled=True)

    grad_attended = dot_general(grad_branch, out_full, ((1,), (1,))).astype(bf16)
    grad_attended = grad_attended.reshape(rows, KEY_VALUE_HEADS, GROUP, HEAD_SIZE)
    grad_probs = jnp.einsum("sgrd,tgd->grst", grad_attended, values, preferred_element_type=f32)
    grad_values = jnp.einsum("grst,sgrd->tgd", prob_low, grad_attended, preferred_element_type=f32)
    inner = jnp.sum(probs * grad_probs, axis=-1, keepdims=True)
    grad_raw = (probs * (grad_probs - inner) * scale).astype(bf16)
    grad_queries = jnp.einsum("grst,tgd->sgrd", grad_raw, keys, preferred_element_type=f32)
    grad_keys = jnp.einsum("grst,sgrd->tgd", grad_raw, queries, preferred_element_type=f32)
    grad_keyval = jnp.concatenate(
        [grad_keys.reshape(2 * rows, kv_width), grad_values.reshape(2 * rows, kv_width)], axis=1
    )
    from_next = lax.ppermute(grad_keyval[:rows].astype(bf16), SHARD, back_ring)
    grad_keyval = grad_keyval[rows:] + from_next.astype(f32)
    grad_turned = jnp.concatenate(
        [grad_queries.reshape(rows, width), grad_keyval[:, :kv_width]], axis=1
    )
    grad_turned = grad_turned.reshape(rows, QUERY_HEADS + KEY_VALUE_HEADS, HEAD_SIZE)
    grad_qkv = jnp.concatenate(
        [
            rotate(grad_turned, cosine, -sine).reshape(rows, width + kv_width),
            grad_keyval[:, kv_width:],
        ],
        axis=1,
    ).astype(bf16)
    grad_normed = dot_general(grad_qkv, qkv_full, ((1,), (1,)))
    grad_in, grad_gain_attn = norm_back(wide, attn_factor, gain_attn, grad_normed)
    grad_tokens = (grad_residual + grad_in).astype(bf16)

    columns = grad_qkv.shape[1] // shards
    grad_qkv_cols = exchange(grad_qkv.reshape(rows, shards, columns).transpose(1, 0, 2), SHARD)
    qkv_block = dot_general(
        normed_all, grad_qkv_cols.reshape(shards * rows, columns), ((0,), (0,))
    )
    qkv_rows = exchange(qkv_block.astype(bf16), SHARD).reshape(shards, width // shards, columns)
    qkv_rows = qkv_rows.transpose(1, 0, 2).reshape(width // shards, shards * columns)
    out_rows = jnp.einsum(
        "jat,jtn->an",
        attended_cols,
        grad_branch_all.reshape(shards, rows, width),
        preferred_element_type=f32,
    ).astype(bf16)
    attn_rows = jnp.concatenate([qkv_rows, out_rows], axis=1)
    attn_rep = exchange(cut(attn_rows, reps), "rep").astype(f32).sum(axis=0).astype(bf16)
    attn_grads = uncut(spread(attn_rep, reps, "rep"), reps).astype(f32)

    grad_gains = jnp.stack([grad_gain_attn, grad_gain_ffn]).reshape(2, shards, -1)
    grad_gains = exchange(grad_gains.transpose(1, 0, 2).astype(bf16), SHARD)
    grad_gains = grad_gains.astype(f32).sum(axis=0)
    grad_gains = spread(grad_gains.astype(bf16), reps, "rep").astype(f32).sum(axis=0)
    return (
        output,
        grad_tokens,
        grad_gains[0],
        attn_grads[:, :width],
        attn_grads[:, width : width + 2 * kv_width],
        attn_grads[:, width + 2 * kv_width :],
        grad_gains[1],
        shard_gateup,
        shard_down,
    )


def solution(mesh):
    reps, shards = mesh.devices.shape
    fine = Mesh(mesh.devices.reshape(reps, shards // 4, 2, 2), ("rep", "y", "x", "c"))
    split = ("rep", "y", "x", "c")
    placed = (
        P(split, None),
        P(split, None),
        P("rep", None),
        P("rep", None),
        P(split, None),
        P(split, None),
        P(SHARD),
        P(SHARD, None),
        P(SHARD, None),
        P(SHARD, None),
        P(SHARD),
        P(None, SHARD, None),
        P(None, SHARD, None),
    )
    return jax.shard_map(
        per_device,
        mesh=fine,
        in_specs=placed,
        out_specs=(
            P(split, None),
            P(split, None),
            P(SHARD),
            P(SHARD, None),
            P(SHARD, None),
            P(SHARD, None),
            P(SHARD),
            P(None, SHARD, None),
            P(None, SHARD, None),
        ),
        check_vma=False,
    )
```

time: 3110 us -> 593 us (0.19)
  waiting for transfers between devices: 2560 us -> 273 us
  matrix products: 197 us -> 86.7 us
  local copies, waits for them, and re-layouts: 158 us -> 65.2 us
  starting transfers between devices: 2.41 us -> 82.2 us
  blocking collectives: 87.3 us -> 15.7 us
    reduce_scatter x19 -> x0, waiting for transfers between devices: 1230 us -> none  [the longest x8 553 us: expert_backward(): lax.psum_scatter(grad_gateup.astype(jnp.bfloat16), 'shard', scatter_dimen...]
    all_gather x39 -> x4, waiting for transfers between devices: 1230 us -> 93.5 us  [the longest x1 54.9 us: per_device(): lax.all_gather(jnp.concatenate([w_query, key_value_weight], 1), SHARD, ax...]
    all_to_all x0 -> x16, waiting for transfers between devices: none -> 179 us  [exchange(): return lax.all_to_all(parts, axes, 0, 0, tiled=True)]
    dot_general x62 -> x22, matrix products: 196 us -> 84.9 us  [the longest x10 44.3 us: dot_general(): lax.dot_general(left, right, (dims, ((), ())), preferred_element_type=f32)]
    psum x1 -> x0, waiting for transfers between devices: 85.5 us -> none  [per_device(): lax.psum(query_shard.astype(jnp.bfloat16), 'rep').astype(jnp.float32)]
    all_to_all x0 -> x16, starting transfers between devices: none -> 76 us  [exchange(): return lax.all_to_all(parts, axes, 0, 0, tiled=True)]
    unnamed x2 -> x0, blocking collectives: 62.7 us -> none
    gather x35 -> x0, local copies, waits for them, and re-layouts: 57.9 us -> none  [the longest x1 12.6 us: sequence_layout(): source = starts[sequence] + token_position]
  transfers between devices with their start and end apart: 59 -> 26, of which waited for: 57 -> 14; matrix products, arithmetic and copies ran while one was open for 10% -> 32% of each run, Pallas kernels for 0% -> 0%
where the time goes in v1:
time: 593 us; the launch traced here: 584 us
  waiting for transfers between devices  273 us (46%)
  matrix products  86.7 us (15%)
  starting transfers between devices  82.2 us (14%)
  local copies, waits for them, and re-layouts  65.2 us (11%)
  other arithmetic  46.2 us (8%)
  blocking collectives  15.7 us (3%)
  between operations  14.8 us (2%)
    all_to_all x16, waiting for transfers between devices, exchange(): return lax.all_to_all(parts, axes, 0, 0, tiled=True)  179 us
    all_to_all x16, starting transfers between devices, exchange(): return lax.all_to_all(parts, axes, 0, 0, tiled=True)  76 us
    all_gather x1, waiting for transfers between devices, per_device(): lax.all_gather(jnp.concatenate([w_query, key_value_weight], 1), SHARD, ax...  54.9 us
    dot_general x10, matrix products, dot_general(): lax.dot_general(left, right, (dims, ((), ())), preferred_element_type=f32)  44.3 us
    all_gather x1, waiting for transfers between devices, per_device(): out_full = lax.all_gather(w_out, SHARD, axis=0, tiled=True)  38.7 us
    dot_general x6, matrix products, matmul(): return jnp.dot(left, right, preferred_element_type=f32)  21.8 us
    convert_element_type x2, local copies, waits for them, and re-layouts, per_device(): uncut(spread(exchange(over_rep, CHIPS), reps, 'rep'), reps).astype(f32)  16.6 us
    all_to_all x1, blocking collectives, exchange(): return lax.all_to_all(parts, axes, 0, 0, tiled=True)  15.7 us
  transfers between devices with their start and end apart: 26, of which 14 were waited for; matrix products, arithmetic and copies ran while one was open for 32% of the time, Pallas kernels for 0%

profile of v1, /device:TPU:0, one launch (start us, length us, event | category | flops | bytes accessed | tf_op | source)
XLA Modules:
  0.0 584.1 jit_solution(16471929150848882535)
XLA Ops:
  11.1 5.6 all-to-all-start
  29.3 54.9 %all-gather.5.cloned.1.call-done = bf16[1536,2048]{1,0:T(8,128)(2,1)} async-done(((bf16[96,2048]{1,0:T(8,128)(2,1)}), bf16[1536,2048]{1,0:T(8,128)(2,1)}) %all-gather.5.cloned.1.call-update) | async-done | bytes 6291472 | tf_op jit(solution)/shard_map/all_gather | solution.py:113
  99.1 38.7 %all-gather.7.cloned.1.call-done = bf16[1536,1536]{1,0:T(8,128)(2,1)} async-done(((bf16[96,1536]{1,0:T(8,128)(2,1)}), bf16[1536,1536]{1,0:T(8,128)(2,1)}) %all-gather.7.cloned.1.call-update) | async-done | bytes 4718608 | tf_op jit(solution)/shard_map/all_gather | solution.py:116
  153.3 40.9 %all-to-all-done.1 = bf16[8,80,1536]{2,1,0:T(8,128)(2,1)S(1)} async-done(((bf16[8,80,1536]{2,1,0:T(8,128)(2,1)}), bf16[8,80,1536]{2,1,0:T(8,128)(2,1)S(1)}, u32[]{:S(2)}, u32[]{:S(2)}) %all-to-all-start.1) | async-done | bytes 1966112 | tf_op jit(solution)/shard_map/all_to_all | solution.py:23
  209.8 5.2 fusion.74
  215.0 16.5 %all-to-all-done.5 = bf16[8,80,1536]{2,1,0:T(8,128)(2,1)} async-done(((bf16[8,80,1536]{2,1,0:T(8,128)(2,1)}), bf16[8,80,1536]{2,1,0:T(8,128)(2,1)}, u32[]{:S(2)}, u32[]{:S(2)}) %all-to-all-start.5) | async-done | bytes 1966112 | tf_op jit(solution)/shard_map/all_to_all | solution.py:23
  231.4 6.8 %multiply_convert_fusion.2 = (bf16[640,768]{1,0:T(8,128)(2,1)S(1)}, bf16[640,768]{1,0:T(8,128)(2,1)S(1)}, bf16[640,768]{1,0:T(8,128)(2,1)}) fusion(f32[640,1536]{1,0:T(8,128)} %fusion.74, bf16[640,1536]{1,0:T(8,128)(2,1)} %bitcast.28, bf16[768,1536]{1,0:T(8,128)(2,1)} %bitcast.229), kind=kOutput, calls=%fused_computation.36 | convolution fusion | flops 1517322240 | bytes 11206656 | tf_op jit(solution)/shard_map/dot_general | solution.py:31
  249.4 6.0 %fusion.25 = f32[8,2,48,1536]{3,2,0,1:T(8,128)} fusion(bf16[640,1536,1,1]{1,0,2,3:T(8,128)(2,1)} %bitcast.76, bf16[8,2,48,640]{3,2,1,0:T(8,128)(2,1)} %bitcast.245), kind=kOutput, calls=%fused_computation.60 | convolution fusion | flops 1509949440 | bytes 7667712 | tf_op jit(solution)/shard_map/dot_general | solution.py:31
  255.4 17.3 %all-to-all-done.6 = bf16[8,80,1536]{2,1,0:T(8,128)(2,1)} async-done(((bf16[8,80,1536]{2,1,0:T(8,128)(2,1)}), bf16[8,80,1536]{2,1,0:T(8,128)(2,1)}, u32[]{:S(2)}, u32[]{:S(2)}) %all-to-all-start.6) | async-done | bytes 1966112 | tf_op jit(solution)/shard_map/all_to_all | solution.py:23
  287.3 6.2 %fusion.13 = f32[8,2,96,1536]{3,2,1,0:T(8,128)S(1)} fusion(bf16[8,2,96,640]{3,2,1,0:T(8,128)(2,1)} %bitcast.235, bf16[640,768]{1,0:T(8,128)(2,1)} %copy-done.38, bf16[640,768]{1,0:T(8,128)(2,1)} %copy-done.37), kind=kOutput, calls=%fused_computation.33 | convolution fusion | flops 3023831040 | bytes 13369344 | tf_op jit(solution)/shard_map/dot_general | solution.py:31
  328.8 6.5 %fusion.36 = (bf16[1536]{0:T(1024)(128)(2,1)S(1)}, f32[128]{0:T(128)}, f32[128,1536]{1,0:T(8,128)}) fusion(bf16[128,1536]{1,0:T(8,128)(2,1)S(1)} %copy-done.1, f32[128]{0:T(128)S(1)} %copy-done.30, f32[1536]{0:T(1024)S(1)} %mul.302, bf16[1536,2048]{1,0:T(8,128)(2,1)} %all-gather.5.cloned.1.call-done, bf16[128,256]{0,1:T(8,128)(2,1)S(1)} %slice.139, ...), kind=kOutput, calls=%fused_computation.73 | convolution fusion | flops 807729536 | bytes 8005632 | tf_op jit(solution)/shard_map/dot_general | solution.py:31
  343.2 5.4 convolution_convert_fusion.5
  349.7 5.2 all-to-all-start.10
  354.9 5.7 fusion.4
  362.7 7.1 %convert_element_type.227 = bf16[8,2,72,4,384]{4,3,2,1,0:T(4,128)(2,1)} reshape(bf16[8,144,1536]{2,1,0:T(8,128)(2,1)} %pad_maximum_fusion) | data formatting | bytes 7077888 | tf_op jit(solution)/shard_map/convert_element_type | solution.py:198
  374.1 6.9 %all-to-all-start.14 = ((bf16[8,8,72,384]{3,2,1,0:T(8,128)(2,1)}), bf16[8,8,72,384]{3,2,1,0:T(8,128)(2,1)}, u32[]{:S(2)}, u32[]{:S(2)}) async-start(bf16[8,8,72,384]{3,2,1,0:T(8,128)(2,1)} %bitcast.210), calls=%async_computation.14 | async-start | bytes 7077888 | tf_op jit(solution)/shard_map/all_to_all | solution.py:23
  385.7 37.8 %all-to-all-done.14 = bf16[8,8,72,384]{3,2,1,0:T(8,128)(2,1)} async-done(((bf16[8,8,72,384]{3,2,1,0:T(8,128)(2,1)}), bf16[8,8,72,384]{3,2,1,0:T(8,128)(2,1)}, u32[]{:S(2)}, u32[]{:S(2)}) %all-to-all-start.14) | async-done | bytes 3538976 | tf_op jit(solution)/shard_map/all_to_all | solution.py:23
  433.6 19.7 %all-to-all-done.4 = bf16[8,80,1536]{2,1,0:T(8,128)(2,1)S(1)} async-done(((bf16[8,80,1536]{2,1,0:T(8,128)(2,1)}), bf16[8,80,1536]{2,1,0:T(8,128)(2,1)S(1)}, u32[]{:S(2)}, u32[]{:S(2)}) %all-to-all-start.4) | async-done | bytes 1966112 | tf_op jit(solution)/shard_map/all_to_all | solution.py:23
  454.0 6.0 %all-to-all-start.8 = ((bf16[8,2,96]{2,1,0:T(2,128)(2,1)}), bf16[8,2,96]{2,1,0:T(2,128)(2,1)}, u32[]{:S(2)}, u32[]{:S(2)}) async-start(bf16[8,2,96]{2,1,0:T(2,128)(2,1)} %broadcast_in_dim.60), calls=%async_computation.8 | async-start | bytes 8192 | tf_op jit(solution)/shard_map/all_to_all | solution.py:23
  479.9 15.7 %all_to_all.115 = bf16[8,48,896]{2,1,0:T(8,128)(2,1)} all-to-all(bf16[8,48,896]{2,1,0:T(8,128)(2,1)} %bitcast.228), channel_id=1, replica_groups=mesh['rep'=8,'y'=4,'x'=2,'c'=2] {'rep'}, dimensions={0} | all-to-all | bytes 1376256 | tf_op jit(solution)/shard_map/all_to_all | solution.py:23
  507.1 34.2 %all-to-all-done.16 = bf16[8,8,72,384]{3,2,1,0:T(8,128)(2,1)} async-done(((bf16[8,8,72,384]{3,2,1,0:T(8,128)(2,1)}), bf16[8,8,72,384]{3,2,1,0:T(8,128)(2,1)}, u32[]{:S(2)}, u32[]{:S(2)}) %all-to-all-start.16) | async-done | bytes 3538976 | tf_op jit(solution)/shard_map/all_to_all | solution.py:23
  542.2 5.0 all-to-all-start.13
  550.2 7.4 %copy.272 = f32[8,2,72,4,384]{4,3,2,1,0:T(4,128)} copy(f32[8,2,72,4,384]{4,2,0,3,1:T(8,128)S(1)} %convert_bitcast_fusion) | data formatting | bytes 14155776 | tf_op jit(solution)/shard_map/convert_element_type | solution.py:200
  557.6 9.2 %reshape.355 = f32[8,144,1536]{2,1,0:T(8,128)} reshape(f32[8,2,72,4,384]{4,3,2,1,0:T(4,128)} %copy.272) | data formatting | bytes 14155776 | tf_op jit(solution)/shard_map/convert_element_type | solution.py:200
  (240 shorter events, 199.6 us)
Async XLA Ops:
  7.2 76.9 %all-gather.5.cloned.1.call-start = ((), (), s32[]{:S(2)}) async-start(), calls=%async_computation.17 | async-start | bytes 6684672 | tf_op jit(solution)/shard_map/all_gather | solution.py:113
  9.1 128.7 %all-gather.7.cloned.1.call-start = ((), (), s32[]{:S(2)}) async-start(), calls=%async_computation.18 | async-start | bytes 5013504 | tf_op jit(solution)/shard_map/all_gather | solution.py:116
  11.1 11.6 %all-to-all-start = ((bf16[16,2,96]{2,1,0:T(2,128)(2,1)}), bf16[16,2,96]{2,1,0:T(2,128)(2,1)S(1)}, u32[]{:S(2)}, u32[]{:S(2)}) async-start(bf16[16,2,96]{2,1,0:T(2,128)(2,1)} %broadcast_in_dim.52), calls=%async_computation | async-start | bytes 16384 | tf_op jit(solution)/shard_map/all_to_all | solution.py:23
  22.7 66.7 %all-to-all-start.2 = ((bf16[8,96,1536]{2,1,0:T(8,128)(2,1)}), bf16[8,96,1536]{2,1,0:T(8,128)(2,1)}, u32[]{:S(2)}, u32[]{:S(2)}) async-start(bf16[8,96,1536]{2,1,0:T(8,128)(2,1)} %param.23), calls=%async_computation.2 | async-start | bytes 4718592 | tf_op jit(solution)/shard_map/all_to_all | solution.py:23
  27.1 316.1 %all-gather.9.cloned.1.call-start = ((), (), s32[]{:S(2)}) async-start(), calls=%async_computation.19 | async-start | bytes 6684672 | tf_op jit(solution)/shard_map/all_gather | solution.py:147
  89.4 54.2 %all-to-all-start.3 = ((bf16[8,48,1536]{2,1,0:T(8,128)(2,1)}), bf16[8,48,1536]{2,1,0:T(8,128)(2,1)S(1)}, u32[]{:S(2)}, u32[]{:S(2)}) async-start(bf16[8,48,1536]{2,1,0:T(8,128)(2,1)} %param.24), calls=%async_computation.3 | async-start | bytes 2359296 | tf_op jit(solution)/shard_map/all_to_all | solution.py:23
  93.7 109.3 %collective-permute-start.1 = (bf16[8,96,1536]{2,1,0:T(8,128)(2,1)}, bf16[8,96,1536]{2,1,0:T(8,128)(2,1)}, u32[]{:S(2)}, u32[]{:S(2)}) collective-permute-start(bf16[8,96,1536]{2,1,0:T(8,128)(2,1)} %all-to-all-done.2), channel_id=1, source_target_pairs={{0,1},{1,0},{2,3},{3,2},{4,5},{5,4},{6,7},{7,6},{8,9},{9,8},{10,11... | collective-permute-start | bytes 7077896 | tf_op jit(solution)/shard_map/ppermute | solution.py:119
  144.6 49.6 %all-to-all-start.1 = ((bf16[8,80,1536]{2,1,0:T(8,128)(2,1)}), bf16[8,80,1536]{2,1,0:T(8,128)(2,1)S(1)}, u32[]{:S(2)}, u32[]{:S(2)}) async-start(bf16[8,80,1536]{2,1,0:T(8,128)(2,1)} %bitcast.216), calls=%async_computation.1 | async-start | bytes 3932160 | tf_op jit(solution)/shard_map/all_to_all | solution.py:23
  148.8 49.9 %collective-permute-start.2 = (bf16[8,48,1536]{2,1,0:T(8,128)(2,1)}, bf16[8,48,1536]{2,1,0:T(8,128)(2,1)}, u32[]{:S(2)}, u32[]{:S(2)}) collective-permute-start(bf16[8,48,1536]{2,1,0:T(8,128)(2,1)} %copy-done.2), channel_id=1, source_target_pairs={{0,1},{1,0},{2,3},{3,2},{4,5},{5,4},{6,7},{7,6},{8,9},{9,8},{10,11... | collective-permute-start | bytes 3538952 | tf_op jit(solution)/shard_map/ppermute | solution.py:121
  194.2 37.3 %all-to-all-start.5 = ((bf16[8,80,1536]{2,1,0:T(8,128)(2,1)}), bf16[8,80,1536]{2,1,0:T(8,128)(2,1)}, u32[]{:S(2)}, u32[]{:S(2)}) async-start(bf16[8,80,1536]{2,1,0:T(8,128)(2,1)} %bitcast.215), calls=%async_computation.5 | async-start | bytes 3932160 | tf_op jit(solution)/shard_map/all_to_all | solution.py:23
  242.8 29.9 %all-to-all-start.6 = ((bf16[8,80,1536]{2,1,0:T(8,128)(2,1)}), bf16[8,80,1536]{2,1,0:T(8,128)(2,1)}, u32[]{:S(2)}, u32[]{:S(2)}) async-start(bf16[8,80,1536]{2,1,0:T(8,128)(2,1)} %bitcast.234), calls=%async_computation.6 | async-start | bytes 3932160 | tf_op jit(solution)/shard_map/all_to_all | solution.py:23
  272.7 51.6 %all-to-all-start.11 = ((bf16[16,96,128]{2,1,0:T(8,128)(2,1)}), bf16[16,96,128]{2,1,0:T(8,128)(2,1)}, u32[]{:S(2)}, u32[]{:S(2)}) async-start(bf16[16,96,128]{2,1,0:T(8,128)(2,1)} %bitcast.237), calls=%async_computation.11 | async-start | bytes 786432 | tf_op jit(solution)/shard_map/all_to_all | solution.py:23
  276.9 183.0 %all-gather.11.cloned.1.call-start = ((), (), s32[]{:S(2)}) async-start(), calls=%async_computation.20 | async-start | bytes 6684672 | tf_op jit(solution)/shard_map/all_gather | solution.py:214
  295.6 59.3 %collective-permute-start.4 = (bf16[8,96,1536]{2,1,0:T(8,128)(2,1)}, bf16[8,96,1536]{2,1,0:T(8,128)(2,1)}, u32[]{:S(2)}, u32[]{:S(2)}) collective-permute-start(bf16[8,96,1536]{2,1,0:T(8,128)(2,1)} %fusion.10), channel_id=1, source_target_pairs={{0,1},{1,0},{2,3},{3,2},{4,5},{5,4},{6,7},{7,6},{8,9},{9,8},{10,11... | collective-permute-start | bytes 7077896 | tf_op jit(solution)/shard_map/ppermute | solution.py:196
  310.1 9.8 %collective-permute-start.3 = (bf16[128,512]{0,1:T(8,128)(2,1)S(1)}, bf16[128,512]{0,1:T(8,128)(2,1)S(1)}, u32[]{:S(2)}, u32[]{:S(2)}) collective-permute-start(bf16[128,512]{0,1:T(8,128)(2,1)S(1)} %fusion.48), channel_id=1, source_target_pairs={{1,0},{2,1},{3,2},{4,3},{5,4},{6,5},{7,6},{8,7},{9,8},{10,9},{11,1... | collective-permute-start | bytes 393224 | tf_op jit(solution)/shard_map/ppermute | solution.py:227
  324.3 15.4 %all-to-all-start.9 = ((bf16[16,128,128]{2,1,0:T(8,128)(2,1)}), bf16[16,128,128]{2,1,0:T(8,128)(2,1)}, u32[]{:S(2)}, u32[]{:S(2)}) async-start(bf16[16,128,128]{2,1,0:T(8,128)(2,1)} %bitcast.231), calls=%async_computation.9 | async-start | bytes 1048576 | tf_op jit(solution)/shard_map/all_to_all | solution.py:23
  339.7 9.4 %all-to-all-start.7 = ((bf16[16,2,96]{2,1,0:T(2,128)(2,1)}), bf16[16,2,96]{2,1,0:T(2,128)(2,1)S(1)}, u32[]{:S(2)}, u32[]{:S(2)}) async-start(bf16[16,2,96]{2,1,0:T(2,128)(2,1)} %copy.257), calls=%async_computation.7 | async-start | bytes 16384 | tf_op jit(solution)/shard_map/all_to_all | solution.py:23
  349.7 24.4 %all-to-all-start.10 = ((bf16[16,96,128]{2,1,0:T(8,128)(2,1)}), bf16[16,96,128]{2,1,0:T(8,128)(2,1)S(1)}, u32[]{:S(2)}, u32[]{:S(2)}) async-start(bf16[16,96,128]{2,1,0:T(8,128)(2,1)} %bitcast.53), calls=%async_computation.10 | async-start | bytes 786432 | tf_op jit(solution)/shard_map/all_to_all | solution.py:23
  374.1 49.4 %all-to-all-start.14 = ((bf16[8,8,72,384]{3,2,1,0:T(8,128)(2,1)}), bf16[8,8,72,384]{3,2,1,0:T(8,128)(2,1)}, u32[]{:S(2)}, u32[]{:S(2)}) async-start(bf16[8,8,72,384]{3,2,1,0:T(8,128)(2,1)} %bitcast.210), calls=%async_computation.14 | async-start | bytes 7077888 | tf_op jit(solution)/shard_map/all_to_all | solution.py:23
  423.5 29.9 %all-to-all-start.4 = ((bf16[8,80,1536]{2,1,0:T(8,128)(2,1)}), bf16[8,80,1536]{2,1,0:T(8,128)(2,1)S(1)}, u32[]{:S(2)}, u32[]{:S(2)}) async-start(bf16[8,80,1536]{2,1,0:T(8,128)(2,1)} %bitcast.233), calls=%async_computation.4 | async-start | bytes 3932160 | tf_op jit(solution)/shard_map/all_to_all | solution.py:23
  454.0 13.5 %all-to-all-start.8 = ((bf16[8,2,96]{2,1,0:T(2,128)(2,1)}), bf16[8,2,96]{2,1,0:T(2,128)(2,1)}, u32[]{:S(2)}, u32[]{:S(2)}) async-start(bf16[8,2,96]{2,1,0:T(2,128)(2,1)} %broadcast_in_dim.60), calls=%async_computation.8 | async-start | bytes 8192 | tf_op jit(solution)/shard_map/all_to_all | solution.py:23
  467.5 12.4 %all-to-all-start.15 = ((bf16[8,72,384]{2,1,0:T(8,128)(2,1)}), bf16[8,72,384]{2,1,0:T(8,128)(2,1)}, u32[]{:S(2)}, u32[]{:S(2)}) async-start(bf16[8,72,384]{2,1,0:T(8,128)(2,1)} %reduce_sum.148), calls=%async_computation.15 | async-start | bytes 884736 | tf_op jit(solution)/shard_map/all_to_all | solution.py:23
  498.7 42.6 %all-to-all-start.16 = ((bf16[8,8,72,384]{3,2,1,0:T(8,128)(2,1)}), bf16[8,8,72,384]{3,2,1,0:T(8,128)(2,1)}, u32[]{:S(2)}, u32[]{:S(2)}) async-start(bf16[8,8,72,384]{3,2,1,0:T(8,128)(2,1)} %broadcast_in_dim.62), calls=%async_computation.16 | async-start | bytes 7077888 | tf_op jit(solution)/shard_map/all_to_all | solution.py:23
  542.2 32.7 %all-to-all-start.13 = ((bf16[8,48,896]{2,1,0:T(8,128)(2,1)}), bf16[8,48,896]{2,1,0:T(8,128)(2,1)S(1)}, u32[]{:S(2)}, u32[]{:S(2)}) async-start(bf16[8,48,896]{2,1,0:T(8,128)(2,1)} %broadcast_in_dim.61), calls=%async_computation.13 | async-start | bytes 1376256 | tf_op jit(solution)/shard_map/all_to_all | solution.py:23
  (45 other events, 408.9 us)
Sparse Core Ops, SparseCore 0:
  10.3 73.7 all-gather.4
  85.8 51.9 all-gather.6
  140.1 80.6 all-gather.8
  281.3 44.6 all-gather.10

commit v2 on v1

--- a/solution.py
+++ b/solution.py
@@ -1,6 +1,8 @@
 import jax
 import jax.numpy as jnp
 from jax import lax
+from jax.experimental import pallas as pl
+from jax.experimental.pallas import tpu as pltpu
 from jax.sharding import Mesh, PartitionSpec as P
 
 QUERY_HEADS = 12
@@ -13,6 +15,8 @@
 ROPE_BASE = 10000.0
 SHARD = ("y", "x", "c")
 CHIPS = ("y", "x")
+REP = ("h", "z")
+ALL = REP + SHARD
 SWAP = [(0, 1), (1, 0)]
 
 bf16 = jnp.bfloat16
@@ -60,22 +64,96 @@
     return grad_input, grad_gain
 
 
-def cut(rows, ways):
+def after(value, *earlier):
+    return lax.optimization_barrier((value, *earlier))[0]
+
+
+def pieces_of(rows, wide):
     *lead, a, b = rows.shape
-    wide = ways // 2
     n = len(lead)
     cut_up = rows.reshape(*lead, 2, a // 2, wide, b // wide)
-    order = (n, n + 2, *range(n), n + 1, n + 3)
-    return cut_up.transpose(order).reshape(ways, *lead, a // 2, b // wide)
-
-
-def uncut(pieces, ways):
-    _, *lead, a, b = pieces.shape
-    wide = ways // 2
-    n = len(lead)
-    whole = pieces.reshape(2, wide, *lead, a, b)
-    order = (*range(2, 2 + n), 0, 2 + n, 1, 3 + n)
-    return whole.transpose(order).reshape(*lead, 2 * a, wide * b)
+    return cut_up.transpose(n, n + 2, *range(n), n + 1, n + 3)
+
+
+def sum_over_rep(pieces):
+    wide = pieces.shape[1]
+    z = lax.axis_index("z")
+    total = lax.dynamic_index_in_dim(pieces, z, 1, keepdims=False).astype(f32)
+    for k in range(1, wide):
+        sent = lax.dynamic_index_in_dim(pieces, z ^ k, 1, keepdims=False)
+        total = total + lax.ppermute(sent, "z", [(i, i ^ k) for i in range(wide)]).astype(f32)
+    h = lax.axis_index("h")
+    mine = lax.dynamic_index_in_dim(total, h, 0, keepdims=False)
+    sent = lax.dynamic_index_in_dim(total, 1 - h, 0, keepdims=False).astype(bf16)
+    return (mine + lax.ppermute(sent, "h", SWAP).astype(f32)).astype(bf16)
+
+
+def gather_over_rep(piece):
+    other = lax.ppermute(piece, "h", SWAP)
+    low = lax.axis_index("h") == 0
+    both = jnp.stack([jnp.where(low, piece, other), jnp.where(low, other, piece)])
+    wide = lax.axis_size("z")
+    moved = [
+        lax.ppermute(both, "z", [(i, i ^ k) for i in range(wide)]) for k in range(1, wide)
+    ]
+    return [both, *moved]
+
+
+def expert_outputs(moved, rows_up, rows_down):
+    wide = len(moved)
+    _, experts, half, part = moved[0].shape
+    width = wide * part
+    z = lax.axis_index("z").astype(jnp.int32).reshape(1)
+
+    def kernel(z_ref, *refs):
+        up_ref, down_ref = refs[wide], refs[wide + 1]
+        for k in range(wide):
+            at = pl.multiple_of((z_ref[0] ^ k) * part, 128)
+            first = refs[k][0, 0].astype(f32)
+            second = refs[k][1, 0].astype(f32)
+            split = rows_up - half
+            up_ref[0, :half, pl.ds(at, part)] = first
+            up_ref[0, half:, pl.ds(at, part)] = second[:split]
+            down_ref[0, :, pl.ds(at, part)] = second[split:]
+
+    return pl.pallas_call(
+        kernel,
+        grid_spec=pltpu.PrefetchScalarGridSpec(
+            num_scalar_prefetch=1,
+            grid=(experts,),
+            in_specs=[pl.BlockSpec((2, 1, half, part), lambda e, z_ref: (0, e, 0, 0))] * wide,
+            out_specs=[
+                pl.BlockSpec((1, rows_up, width), lambda e, z_ref: (e, 0, 0)),
+                pl.BlockSpec((1, rows_down, width), lambda e, z_ref: (e, 0, 0)),
+            ],
+        ),
+        out_shape=[
+            jax.ShapeDtypeStruct((experts, rows_up, width), f32),
+            jax.ShapeDtypeStruct((experts, rows_down, width), f32),
+        ],
+    )(z, *moved)
+
+
+def attention_outputs(pieces, widths):
+    count, half, part = pieces.shape
+    wide = count // 2
+
+    def kernel(piece_ref, *out_refs):
+        for h in range(2):
+            for z in range(wide):
+                left, right, base = z * part, (z + 1) * part, 0
+                for ref, size in zip(out_refs, widths):
+                    low, high = max(left, base), min(right, base + size)
+                    if low < high:
+                        ref[h * half : (h + 1) * half, low - base : high - base] = piece_ref[
+                            h * wide + z, :, low - left : high - left
+                        ].astype(f32)
+                    base += size
+
+    return pl.pallas_call(
+        kernel,
+        out_shape=[jax.ShapeDtypeStruct((2 * half, size), f32) for size in widths],
+    )(pieces)
 
 
 def spread(part, ways, axes):
@@ -97,7 +175,8 @@
     w_gateup,
     w_down,
 ):
-    reps = lax.axis_size("rep")
+    wide_z = lax.axis_size("z")
+    reps = 2 * wide_z
     shards = lax.axis_size("y") * lax.axis_size("x") * lax.axis_size("c")
     core = lax.axis_index("c")
     shard = (lax.axis_index("y") * lax.axis_size("x") + lax.axis_index("x")) * 2 + core
@@ -107,19 +186,33 @@
     kv_width = KEY_VALUE_HEADS * HEAD_SIZE
     scale = HEAD_SIZE ** (-0.5)
 
-    gains = spread(jnp.stack([attn_gain, ffn_gain]), shards, SHARD)
-    gains = gains.transpose(1, 0, 2).reshape(2, width).astype(f32)
-    gain_attn, gain_ffn = gains[0], gains[1]
     qkv_full = lax.all_gather(
         jnp.concatenate([w_query, key_value_weight], 1), SHARD, axis=0, tiled=True
     )
     out_full = lax.all_gather(w_out, SHARD, axis=0, tiled=True)
-    gateup_mine = exchange(w_gateup, CHIPS)
-    down_mine = exchange(w_down, CHIPS)
-    gateup_full = in_core_order(core, gateup_mine, lax.ppermute(gateup_mine, "c", SWAP))
-    gateup_full = gateup_full.reshape(width, 2 * ff)
-    down_full = in_core_order(core, down_mine, lax.ppermute(down_mine, "c", SWAP))
-    down_full = down_full.reshape(ff, width)
+    part = width // wide_z
+    rows_up, rows_down = w_gateup.shape[1], w_down.shape[1]
+    column = lax.axis_index("z") * part
+    gains_own = jnp.pad(jnp.stack([attn_gain, ffn_gain]), ((0, 6), (0, part - attn_gain.shape[0])))
+    expert_part = jnp.concatenate(
+        [
+            lax.dynamic_slice_in_dim(w_gateup, column, part, 2),
+            lax.dynamic_slice_in_dim(w_down, column, part, 2),
+            jnp.broadcast_to(gains_own[None], (experts, *gains_own.shape)),
+        ],
+        axis=1,
+    )
+    expert_part = exchange(expert_part, CHIPS)
+    gains_mine = expert_part[:, rows_up + rows_down : rows_up + rows_down + 2, : attn_gain.shape[0]]
+    gains = in_core_order(core, gains_mine, lax.ppermute(gains_mine, "c", SWAP))
+    gains = gains.transpose(2, 0, 1, 3).reshape(2, width).astype(f32)
+    gain_attn, gain_ffn = gains[0], gains[1]
+    expert_mine = spread(expert_part[:, : rows_up + rows_down], wide_z, "z")
+    expert_other = lax.ppermute(expert_mine, "c", SWAP)
+    expert_full = in_core_order(core, expert_mine.transpose(1, 2, 0, 3), expert_other.transpose(1, 2, 0, 3))
+    expert_full = expert_full.reshape(experts, 2, rows_up + rows_down, width)
+    gateup_full = expert_full[:, :, :rows_up].reshape(width, 2 * ff)
+    down_full = expert_full[:, :, rows_up:].reshape(ff, width)
 
     chosen = routes[:, :, None] == jnp.arange(experts, dtype=jnp.int32)
     member = jnp.any(chosen, axis=1)
@@ -131,7 +224,7 @@
     slot_weight = jnp.sum(jnp.where(picks, weight.T[:, None, :], 0.0), axis=2)
     upstream = cotangent.astype(f32)
     grad_out_sent = matmul(pick, cotangent) * slot_weight.reshape(-1, 1)
-    grad_out = exchange(grad_out_sent.astype(bf16), CHIPS)
+    grad_out = exchange(after(grad_out_sent.astype(bf16), expert_mine), CHIPS)
 
     lengths = seq_lengths[0]
     starts = jnp.cumsum(lengths) - lengths
@@ -144,7 +237,6 @@
     wide = tokens.astype(f32)
     attn_factor = lax.rsqrt(jnp.mean(wide * wide, axis=-1, keepdims=True) + EPSILON)
     normed = (wide * attn_factor * gain_attn).astype(bf16)
-    normed_all = lax.all_gather(normed, SHARD, axis=0, tiled=True)
     qkv = matmul(normed, qkv_full)
     turned = rotate(
         qkv[:, : width + kv_width].reshape(rows, QUERY_HEADS + KEY_VALUE_HEADS, HEAD_SIZE),
@@ -172,34 +264,34 @@
     residual = wide + branch.astype(f32)
     ffn_factor = lax.rsqrt(jnp.mean(residual * residual, axis=-1, keepdims=True) + EPSILON)
     normed_ffn = (residual * ffn_factor * gain_ffn).astype(bf16)
-    attended_cols = exchange(attended.T, SHARD).reshape(shards, width // shards, rows)
-
-    picked = exchange(matmul(pick, normed_ffn).astype(bf16), CHIPS)
+
+    picked = exchange(after(matmul(pick, normed_ffn).astype(bf16), grad_out), CHIPS)
+    normed_all = lax.all_gather(after(normed, picked), SHARD, axis=0, tiled=True)
+    attended_cols = exchange(after(attended.T, picked), SHARD)
+    attended_cols = attended_cols.reshape(shards, width // shards, rows)
     pre = matmul(picked, gateup_full)
     gate, up = pre[:, :ff], pre[:, ff:]
     sigmoid = jax.nn.sigmoid(gate)
     silu = gate * sigmoid
     acted = (silu * up).astype(bf16)
-    expert_out = exchange(matmul(acted, down_full).astype(bf16), CHIPS)
+    expert_out = matmul(acted, down_full).astype(bf16)
     grad_act = dot_general(grad_out, down_full, ((1,), (1,)))
     grad_gate = grad_act * up * sigmoid * (1.0 + gate * (1.0 - sigmoid))
     grad_pre = jnp.concatenate([grad_gate, grad_act * silu], axis=1).astype(bf16)
     grad_picked = dot_general(grad_pre, gateup_full, ((1,), (1,)))
-    grad_picked = exchange(grad_picked.astype(bf16), CHIPS)
+    grad_picked = exchange(after(grad_picked.astype(bf16), attended_cols), CHIPS)
+    expert_out = exchange(after(expert_out, grad_picked), CHIPS)
     grad_down = dot_general(acted, grad_out, ((0,), (0,)))
     grad_gateup = dot_general(picked, grad_pre, ((0,), (0,)))
 
     def owned(grad):
-        halves = grad.reshape(experts, 2, -1, width)
-        here = jnp.where(core == 0, halves[:, 0], halves[:, 1])
-        there = jnp.where(core == 0, halves[:, 1], halves[:, 0])
-        return here + lax.ppermute(there.astype(bf16), "c", SWAP).astype(f32)
+        halves = grad.astype(bf16).reshape(experts, 2, -1, width)
+        there = lax.dynamic_index_in_dim(halves, 1 - core, 1, keepdims=False)
+        here = lax.dynamic_index_in_dim(halves, core, 1, keepdims=False)
+        return here.astype(f32) + lax.ppermute(there, "c", SWAP).astype(f32)
 
     both = jnp.concatenate([owned(grad_gateup), owned(grad_down)], axis=1).astype(bf16)
-    over_rep = exchange(cut(both, reps), "rep").astype(f32).sum(axis=0).astype(bf16)
-    expert_grads = uncut(spread(exchange(over_rep, CHIPS), reps, "rep"), reps).astype(f32)
-    shard_gateup = expert_grads[:, : width // shards]
-    shard_down = expert_grads[:, width // shards :]
+    over_rep = sum_over_rep(pieces_of(both, wide_z))
 
     back = pick.astype(f32) * slot_weight.reshape(-1, 1)
     back_high = back.astype(bf16)
@@ -242,33 +334,45 @@
     grad_tokens = (grad_residual + grad_in).astype(bf16)
 
     columns = grad_qkv.shape[1] // shards
-    grad_qkv_cols = exchange(grad_qkv.reshape(rows, shards, columns).transpose(1, 0, 2), SHARD)
+    grad_qkv_cols = exchange(
+        after(grad_qkv.reshape(rows, shards, columns).transpose(1, 0, 2), expert_out), SHARD
+    )
     qkv_block = dot_general(
         normed_all, grad_qkv_cols.reshape(shards * rows, columns), ((0,), (0,))
-    )
-    qkv_rows = exchange(qkv_block.astype(bf16), SHARD).reshape(shards, width // shards, columns)
-    qkv_rows = qkv_rows.transpose(1, 0, 2).reshape(width // shards, shards * columns)
+    ).astype(bf16)
+    over_rep = after(over_rep, grad_qkv_cols)
+    expert_pieces = exchange(over_rep, CHIPS)
+    shard_gateup, shard_down = expert_outputs(gather_over_rep(expert_pieces), rows_up, rows_down)
+
     out_rows = jnp.einsum(
         "jat,jtn->an",
         attended_cols,
         grad_branch_all.reshape(shards, rows, width),
         preferred_element_type=f32,
     ).astype(bf16)
+    qkv_rows = exchange(after(qkv_block, expert_pieces), SHARD)
+    qkv_rows = qkv_rows.reshape(shards, width // shards, columns)
+    qkv_rows = qkv_rows.transpose(1, 0, 2).reshape(width // shards, shards * columns)
     attn_rows = jnp.concatenate([qkv_rows, out_rows], axis=1)
-    attn_rep = exchange(cut(attn_rows, reps), "rep").astype(f32).sum(axis=0).astype(bf16)
-    attn_grads = uncut(spread(attn_rep, reps, "rep"), reps).astype(f32)
+    attn_pieces = pieces_of(attn_rows, wide_z)
+    attn_pieces = attn_pieces.reshape(reps, *attn_pieces.shape[2:])
+    attn_rep = exchange(attn_pieces, REP).astype(f32).sum(axis=0).astype(bf16)
+    attn_all = spread(attn_rep, reps, REP)
+    grad_query, grad_keyval_w, grad_out_w = attention_outputs(
+        attn_all, (width, 2 * kv_width, width)
+    )
 
     grad_gains = jnp.stack([grad_gain_attn, grad_gain_ffn]).reshape(2, shards, -1)
-    grad_gains = exchange(grad_gains.transpose(1, 0, 2).astype(bf16), SHARD)
+    grad_gains = exchange(after(grad_gains.transpose(1, 0, 2).astype(bf16), qkv_rows), SHARD)
     grad_gains = grad_gains.astype(f32).sum(axis=0)
-    grad_gains = spread(grad_gains.astype(bf16), reps, "rep").astype(f32).sum(axis=0)
+    grad_gains = spread(grad_gains.astype(bf16), reps, REP).astype(f32).sum(axis=0)
     return (
         output,
         grad_tokens,
         grad_gains[0],
-        attn_grads[:, :width],
-        attn_grads[:, width : width + 2 * kv_width],
-        attn_grads[:, width + 2 * kv_width :],
+        grad_query,
+        grad_keyval_w,
+        grad_out_w,
         grad_gains[1],
         shard_gateup,
         shard_down,
@@ -277,13 +381,13 @@
 
 def solution(mesh):
     reps, shards = mesh.devices.shape
-    fine = Mesh(mesh.devices.reshape(reps, shards // 4, 2, 2), ("rep", "y", "x", "c"))
-    split = ("rep", "y", "x", "c")
+    fine = Mesh(mesh.devices.reshape(2, reps // 2, shards // 4, 2, 2), ALL)
+    split = ALL
     placed = (
         P(split, None),
         P(split, None),
-        P("rep", None),
-        P("rep", None),
+        P(REP, None),
+        P(REP, None),
         P(split, None),
         P(split, None),
         P(SHARD),

time: 593 us -> 533 us (0.90)
  waiting for transfers between devices: 273 us -> 154 us
  blocking collectives: 15.7 us -> 62 us
  local copies, waits for them, and re-layouts: 65.2 us -> 85.9 us
  Pallas kernels: 0 us -> 9.52 us
  other arithmetic: 46.2 us -> 39.8 us
  starting transfers between devices: 82.2 us -> 75.9 us
    all_to_all x16 -> x12, waiting for transfers between devices: 179 us -> 89.5 us  [exchange(): return lax.all_to_all(parts, axes, 0, 0, tiled=True)]
    all_to_all x1 -> x2, blocking collectives: 15.7 us -> 62 us  [exchange(): return lax.all_to_all(parts, axes, 0, 0, tiled=True)]
    all_gather x1, waiting for transfers between devices: 54.9 us -> 8.7 us  [per_device(): lax.all_gather(jnp.concatenate([w_query, key_value_weight], 1), SHARD, ax...]
    ppermute x4 -> x12, waiting for transfers between devices: 0.01 us -> 28.4 us  [the longest x3 27.3 us: sum_over_rep(): lax.ppermute(sent, 'z', [(i, i ^ k) for i in range(wide)]).astype(f32)]
    all_to_all x16 -> x12, starting transfers between devices: 76 us -> 57.4 us  [exchange(): return lax.all_to_all(parts, axes, 0, 0, tiled=True)]
    convert_element_type x4 -> x1, local copies, waits for them, and re-layouts: 17.8 us -> 0.82 us  [sum_over_rep(): lax.dynamic_index_in_dim(total, 1 - h, 0, keepdims=False).astype(bf16)]
    dynamic_slice x0 -> x3, local copies, waits for them, and re-layouts: none -> 13.9 us  [the longest x1 12.8 us: sum_over_rep(): total = lax.dynamic_index_in_dim(pieces, z, 1, keepdims=False).astype(f32)]
    another operation x0 -> x3, local copies, waits for them, and re-layouts: none -> 13.9 us  [in_core_order(): jnp.stack([mine, other], 1)]
  transfers between devices with their start and end apart: 26 -> 30, of which waited for: 14 -> 12; matrix products, arithmetic and copies ran while one was open for 32% -> 38% of each run, Pallas kernels for 0% -> 1%
where the time goes in v2:
time: 533 us; the launch traced here: 524 us
  waiting for transfers between devices  154 us (29%)
  local copies, waits for them, and re-layouts  85.9 us (16%)
  matrix products  81.6 us (15%)
  starting transfers between devices  75.9 us (14%)
  blocking collectives  62 us (12%)
  other arithmetic  39.8 us (7%)
  between operations  15.2 us (3%)
  Pallas kernels  9.52 us (2%)
    all_to_all x12, waiting for transfers between devices, exchange(): return lax.all_to_all(parts, axes, 0, 0, tiled=True)  89.5 us
    all_to_all x2, blocking collectives, exchange(): return lax.all_to_all(parts, axes, 0, 0, tiled=True)  62 us
    all_to_all x12, starting transfers between devices, exchange(): return lax.all_to_all(parts, axes, 0, 0, tiled=True)  57.4 us
    dot_general x10, matrix products, dot_general(): lax.dot_general(left, right, (dims, ((), ())), preferred_element_type=f32)  41.5 us
    ppermute x3, waiting for transfers between devices, sum_over_rep(): lax.ppermute(sent, 'z', [(i, i ^ k) for i in range(wide)]).astype(f32)  27.3 us
    all_gather x1, waiting for transfers between devices, per_device(): out_full = lax.all_gather(w_out, SHARD, axis=0, tiled=True)  26.1 us
    dot_general x6, matrix products, matmul(): return jnp.dot(left, right, preferred_element_type=f32)  19.7 us
    another operation x3, local copies, waits for them, and re-layouts, in_core_order(): jnp.stack([mine, other], 1)  13.9 us
  transfers between devices with their start and end apart: 30, of which 12 were waited for; matrix products, arithmetic and copies ran while one was open for 38% of the time, Pallas kernels for 1%

profile of v2, /device:TPU:0, one launch (start us, length us, event | category | flops | bytes accessed | tf_op | source)
XLA Modules:
  0.0 523.6 jit_solution(3483034036450761363)
XLA Ops:
  12.8 5.5 %all-to-all-start = ((bf16[8,152,384]{2,1,0:T(8,128)(2,1)}), bf16[8,152,384]{2,1,0:T(8,128)(2,1)S(1)}, u32[]{:S(2)}, u32[]{:S(2)}) async-start(bf16[8,152,384]{2,1,0:T(8,128)(2,1)} %pad_maximum_fusion.4), calls=%async_computation | async-start | bytes 1867776 | tf_op jit(solution)/shard_map/all_to_all | solution.py:27
  20.8 20.0 %all-to-all-done = bf16[8,152,384]{2,1,0:T(8,128)(2,1)S(1)} async-done(((bf16[8,152,384]{2,1,0:T(8,128)(2,1)}), bf16[8,152,384]{2,1,0:T(8,128)(2,1)S(1)}, u32[]{:S(2)}, u32[]{:S(2)}) %all-to-all-start) | async-done | bytes 933920 | tf_op jit(solution)/shard_map/all_to_all | solution.py:27
  43.0 6.3 %all-to-all-start.1 = ((bf16[4,8,144,384]{3,2,1,0:T(8,128)(2,1)}), bf16[4,8,144,384]{3,2,1,0:T(8,128)(2,1)}, u32[]{:S(2)}, u32[]{:S(2)}) async-start(bf16[4,8,144,384]{3,2,1,0:T(8,128)(2,1)} %broadcast_in_dim.60), calls=%async_computation.1 | async-start | bytes 7077888 | tf_op jit(solution)/shard_map/all_to_all | solution.py:27
  53.1 8.7 %all-gather.5.cloned.1.call-done = bf16[1536,2048]{1,0:T(8,128)(2,1)} async-done(((bf16[96,2048]{1,0:T(8,128)(2,1)}), bf16[1536,2048]{1,0:T(8,128)(2,1)}) %all-gather.5.cloned.1.call-update) | async-done | bytes 6291472 | tf_op jit(solution)/shard_map/all_gather | solution.py:189
  66.8 20.4 %all-to-all-done.1 = bf16[4,8,144,384]{3,2,1,0:T(8,128)(2,1)} async-done(((bf16[4,8,144,384]{3,2,1,0:T(8,128)(2,1)}), bf16[4,8,144,384]{3,2,1,0:T(8,128)(2,1)}, u32[]{:S(2)}, u32[]{:S(2)}) %all-to-all-start.1) | async-done | bytes 3538976 | tf_op jit(solution)/shard_map/all_to_all | solution.py:27
  95.5 26.1 %all-gather.7.cloned.1.call-done = bf16[1536,1536]{1,0:T(8,128)(2,1)} async-done(((bf16[96,1536]{1,0:T(8,128)(2,1)}), bf16[1536,1536]{1,0:T(8,128)(2,1)}) %all-gather.7.cloned.1.call-update) | async-done | bytes 4718608 | tf_op jit(solution)/shard_map/all_gather | solution.py:192
  126.2 30.4 %all_to_all.100 = bf16[8,80,1536]{2,1,0:T(8,128)(2,1)} all-to-all(bf16[8,80,1536]{2,1,0:T(8,128)(2,1)S(1)} %bitcast.205), channel_id=1, replica_groups=mesh['h'=2,'z'=4,'y'=4,'x'=2,'c'=2] {'y','x'}, dimensions={0} | all-to-all | bytes 3932160 | tf_op jit(solution)/shard_map/all_to_all | solution.py:27
  157.2 6.5 %copy.246 = bf16[8,144,4,384]{3,2,1,0:T(4,128)(2,1)} copy(bf16[8,144,4,384]{3,1,0,2:T(8,128)(2,1)} %bitcast.22) | data formatting | bytes 7077888 | tf_op jit(solution)/shard_map/transpose | solution.py:212
  163.7 6.9 %stack.62 = bf16[8,1,144,1536]{3,2,0,1:T(8,128)(2,1)} reshape(bf16[8,144,4,384]{3,2,1,0:T(4,128)(2,1)} %copy.246) | data formatting | bytes 7077888 | tf_op jit(solution)/shard_map/stack | solution.py:39
  170.7 6.6 %copy.247 = bf16[8,144,4,384]{3,2,1,0:T(4,128)(2,1)} copy(bf16[8,144,4,384]{3,1,0,2:T(8,128)(2,1)} %bitcast.23) | data formatting | bytes 7077888 | tf_op jit(solution)/shard_map/transpose | solution.py:212
  177.3 6.9 %stack.63 = bf16[8,1,144,1536]{3,2,0,1:T(8,128)(2,1)} reshape(bf16[8,144,4,384]{3,2,1,0:T(4,128)(2,1)} %copy.247) | data formatting | bytes 7077888 | tf_op jit(solution)/shard_map/stack | solution.py:39
  184.2 7.4 %maximum_select_fusion = bf16[8,2,144,1536]{3,2,0,1:T(8,128)(2,1)S(1)} fusion(bf16[8,1,144,1536]{3,2,0,1:T(8,128)(2,1)} %stack.63, bf16[8,1,144,1536]{3,2,0,1:T(8,128)(2,1)} %stack.62, pred[]{:T(512)S(6)} %eq.47), kind=kLoop, calls=%fused_computation.3 | loop fusion | flops 10616832 | bytes 14155777 | tf_op jit(solution)/shard_map/jit(_where)/select_n | solution.py:39
  202.5 5.8 %fusion.76 = f32[640,1536]{1,0:T(8,128)S(1)} fusion(bf16[640,1536]{1,0:T(8,128)(2,1)} %bitcast.222, bf16[1536,1536]{1,0:T(8,128)(2,1)} %bitcast.208), kind=kOutput, calls=%fused_computation.181 | convolution fusion | flops 3019898880 | bytes 10616832 | tf_op jit(solution)/shard_map/dot_general | solution.py:31
  213.2 7.4 %convolution_convert_fusion.4 = bf16[640,1536]{1,0:T(8,128)(2,1)} fusion(bf16[1536,1536]{1,0:T(8,128)(2,1)} %bitcast.209, bf16[640,768]{1,0:T(8,128)(2,1)S(1)} %get-tuple-element.42, bf16[640,768]{1,0:T(8,128)(2,1)S(1)} %get-tuple-element.41), kind=kOutput, calls=%fused_computation.11 | convolution fusion | flops 3024814080 | bytes 8650752 | tf_op jit(solution)/shard_map/dot_general | solution.py:35
  221.3 31.6 %all_to_all.101 = bf16[8,80,1536]{2,1,0:T(8,128)(2,1)S(1)} all-to-all(bf16[8,80,1536]{2,1,0:T(8,128)(2,1)} %bitcast.224), channel_id=1, replica_groups=mesh['h'=2,'z'=4,'y'=4,'x'=2,'c'=2] {'y','x'}, dimensions={0} | all-to-all | bytes 3932160 | tf_op jit(solution)/shard_map/all_to_all | solution.py:27
  305.4 7.2 %convert_element_type.235 = bf16[8,2,72,4,384]{4,3,2,1,0:T(4,128)(2,1)} reshape(bf16[8,144,1536]{2,1,0:T(8,128)(2,1)} %pad_maximum_fusion) | data formatting | bytes 7077888 | tf_op jit(solution)/shard_map/convert_element_type | solution.py:293
  312.6 12.8 %constant_dynamic-slice_fusion.3 = (bf16[8,2,72,1,384]{4,3,2,1,0:T(2,128)(2,1)}, bf16[8,2,72,1,384]{4,3,2,1,0:T(2,128)(2,1)S(1)}, bf16[8,2,72,1,384]{4,3,2,1,0:T(2,128)(2,1)S(1)}, bf16[8,2,72,1,384]{4,3,2,1,0:T(2,128)(2,1)S(1)}) fusion(bf16[8,2,72,4,384]{4,3,2,1,0:T(4,128)(2,1)} %convert_element_type.235, s32[]{:T(128)S(6)} %select_n.100, ...), kind=kLoop, calls=%fused_computation.150 | loop fusion | bytes 7077904 | tf_op jit(solution)/shard_map/jit(dynamic_index_in_dim)/dynamic_slice | solution.py:81
  339.7 25.5 %collective-permute-done.8 = bf16[2,8,72,384]{3,2,1,0:T(8,128)(2,1)} collective-permute-done((bf16[2,8,72,384]{3,2,1,0:T(8,128)(2,1)}, bf16[2,8,72,384]{3,2,1,0:T(8,128)(2,1)}, u32[]{:S(2)}, u32[]{:S(2)}) %collective-permute-start.8) | collective-permute-done | bytes 884768 | tf_op jit(solution)/shard_map/ppermute | solution.py:84
  386.3 6.6 %all-to-all-done.7 = bf16[16,128,128]{2,1,0:T(8,128)(2,1)} async-done(((bf16[16,128,128]{2,1,0:T(8,128)(2,1)}), bf16[16,128,128]{2,1,0:T(8,128)(2,1)}, u32[]{:S(2)}, u32[]{:S(2)}) %all-to-all-start.7) | async-done | bytes 524320 | tf_op jit(solution)/shard_map/all_to_all | solution.py:27
  397.4 5.4 %convolution_convert_fusion.7 = bf16[1536,128]{1,0:T(8,128)(2,1)} fusion(bf16[2048,1536]{1,0:T(8,128)(2,1)} %all-gather.9.cloned.1.call-done, bf16[2048,128]{1,0:T(8,128)(2,1)} %bitcast.54), kind=kOutput, calls=%fused_computation.23 | convolution fusion | flops 805502976 | bytes 7208960 | tf_op jit(solution)/shard_map/dot_general | solution.py:35
  410.5 6.7 %fusion.31 = (bf16[1536]{0:T(1024)(128)(2,1)}, f32[128]{0:T(128)}, f32[128,1536]{1,0:T(8,128)}) fusion(bf16[128,1536]{1,0:T(8,128)(2,1)S(1)} %copy-done.3, f32[128]{0:T(128)} %copy-done.43, f32[1536]{0:T(1024)S(1)} %mul.306, bf16[1536,2048]{1,0:T(8,128)(2,1)} %all-gather.5.cloned.1.call-done, bf16[128,256]{0,1:T(8,128)(2,1)} %copy-done.29, ...), kind=kOutput, calls=%fused_computation.75 | convolution fusion | flops 807729536 | bytes 8005632 | tf_op jit(solution)/shard_map/dot_general | solution.py:35
  439.4 6.7 %all-to-all-start.12 = ((bf16[8,48,896]{2,1,0:T(8,128)(2,1)}), bf16[8,48,896]{2,1,0:T(8,128)(2,1)}, u32[]{:S(2)}, u32[]{:S(2)}) async-start(bf16[8,48,896]{2,1,0:T(8,128)(2,1)} %bitcast.214), calls=%async_computation.12 | async-start | bytes 1376256 | tf_op jit(solution)/shard_map/all_to_all | solution.py:27
  465.0 31.5 %all-to-all-done.11 = bf16[8,2,96]{2,1,0:T(2,128)(2,1)S(1)} async-done(((bf16[8,2,96]{2,1,0:T(2,128)(2,1)}), bf16[8,2,96]{2,1,0:T(2,128)(2,1)S(1)}, u32[]{:S(2)}, u32[]{:S(2)}) %all-to-all-start.11) | async-done | bytes 3104 | tf_op jit(solution)/shard_map/all_to_all | solution.py:27
  502.9 7.3 %shard_map.188 = (f32[8,96,1536]{2,1,0:T(8,128)}, f32[8,48,1536]{2,1,0:T(8,128)}) custom-call(s32[1]{0:T(128)} %bitcast.79.z_ref, bf16[2,8,72,384]{3,2,1,0:T(8,128)(2,1)} %pad_maximum_fusion.7.refs_0_, bf16[2,8,72,384]{3,2,1,0:T(8,128)(2,1)} %collective-permute-done.11.refs_1_, bf16[2,8,72,384]{3,2,1,0:T(8,128)(2,1)} %collective-permute-done.12.refs_2_, ...), custom_call_target="tpu_custom_call" | custom-call | tf_op jit(solution)/shard_map/pallas_call | solution.py:119
  (284 shorter events, 201.8 us)
Async XLA Ops:
  7.2 54.6 %all-gather.5.cloned.1.call-start = ((), (), s32[]{:S(2)}) async-start(), calls=%async_computation.14 | async-start | bytes 6684672 | tf_op jit(solution)/shard_map/all_gather | solution.py:189
  9.2 112.4 %all-gather.7.cloned.1.call-start = ((), (), s32[]{:S(2)}) async-start(), calls=%async_computation.15 | async-start | bytes 5013504 | tf_op jit(solution)/shard_map/all_gather | solution.py:192
  12.8 28.0 %all-to-all-start = ((bf16[8,152,384]{2,1,0:T(8,128)(2,1)}), bf16[8,152,384]{2,1,0:T(8,128)(2,1)S(1)}, u32[]{:S(2)}, u32[]{:S(2)}) async-start(bf16[8,152,384]{2,1,0:T(8,128)(2,1)} %pad_maximum_fusion.4), calls=%async_computation | async-start | bytes 1867776 | tf_op jit(solution)/shard_map/all_to_all | solution.py:27
  43.0 44.3 %all-to-all-start.1 = ((bf16[4,8,144,384]{3,2,1,0:T(8,128)(2,1)}), bf16[4,8,144,384]{3,2,1,0:T(8,128)(2,1)}, u32[]{:S(2)}, u32[]{:S(2)}) async-start(bf16[4,8,144,384]{3,2,1,0:T(8,128)(2,1)} %broadcast_in_dim.60), calls=%async_computation.1 | async-start | bytes 7077888 | tf_op jit(solution)/shard_map/all_to_all | solution.py:27
  66.3 25.4 %collective-permute-start.1 = (bf16[128,512]{1,0:T(8,128)(2,1)S(1)}, bf16[128,512]{1,0:T(8,128)(2,1)S(1)}, u32[]{:S(2)}, u32[]{:S(2)}) collective-permute-start(bf16[128,512]{1,0:T(8,128)(2,1)S(1)} %pad_maximum_fusion.12), channel_id=1, source_target_pairs={{0,1},{1,2},{2,3},{3,4},{4,5},{5,6},{6,7},{7,8},{8,9},{9,10},{10,1... | collective-permute-start | bytes 393224 | tf_op jit(solution)/shard_map/ppermute | solution.py:253
  87.3 39.0 %all-to-all-start.2 = ((bf16[8,80,1536]{2,1,0:T(8,128)(2,1)}), bf16[8,80,1536]{2,1,0:T(8,128)(2,1)}, u32[]{:S(2)}, u32[]{:S(2)}) async-start(bf16[8,80,1536]{2,1,0:T(8,128)(2,1)} %bitcast.18), calls=%async_computation.2 | async-start | bytes 3932160 | tf_op jit(solution)/shard_map/all_to_all | solution.py:27
  91.6 305.7 %all-gather.9.cloned.1.call-start = ((), (), s32[]{:S(2)}) async-start(), calls=%async_computation.16 | async-start | bytes 6684672 | tf_op jit(solution)/shard_map/all_gather | solution.py:269
  198.7 21.9 %all-to-all-start.5 = ((bf16[16,96,128]{2,1,0:T(8,128)(2,1)}), bf16[16,96,128]{2,1,0:T(8,128)(2,1)S(1)}, u32[]{:S(2)}, u32[]{:S(2)}) async-start(bf16[16,96,128]{2,1,0:T(8,128)(2,1)} %bitcast.226), calls=%async_computation.5 | async-start | bytes 786432 | tf_op jit(solution)/shard_map/all_to_all | solution.py:27
  202.3 227.7 %all-gather.11.cloned.1.call-start = ((), (), s32[]{:S(2)}) async-start(), calls=%async_computation.17 | async-start | bytes 6684672 | tf_op jit(solution)/shard_map/all_gather | solution.py:306
  260.7 17.4 %collective-permute-start.5 = (bf16[8,48,1536]{2,1,0:T(8,128)(2,1)}, bf16[8,48,1536]{2,1,0:T(8,128)(2,1)}, u32[]{:S(2)}, u32[]{:S(2)}) collective-permute-start(bf16[8,48,1536]{2,1,0:T(8,128)(2,1)} %dynamic-slice_bitcast_fusion.1), channel_id=1, source_target_pairs={{0,1},{1,0},{2,3},{3,2},{4,5},{5,4},{6,7},{7,6},{8,9},{9,8},{10,11... | collective-permute-start | bytes 3538952 | tf_op jit(solution)/shard_map/ppermute | solution.py:291
  269.8 30.4 %collective-permute-start.4 = (bf16[8,96,1536]{2,1,0:T(8,128)(2,1)}, bf16[8,96,1536]{2,1,0:T(8,128)(2,1)}, u32[]{:S(2)}, u32[]{:S(2)}) collective-permute-start(bf16[8,96,1536]{2,1,0:T(8,128)(2,1)} %dynamic-slice_bitcast_fusion), channel_id=1, source_target_pairs={{0,1},{1,0},{2,3},{3,2},{4,5},{5,4},{6,7},{7,6},{8,9},{9,8},{10,11... | collective-permute-start | bytes 7077896 | tf_op jit(solution)/shard_map/ppermute | solution.py:291
  274.3 102.5 %all-to-all-start.4 = ((bf16[8,80,1536]{2,1,0:T(8,128)(2,1)}), bf16[8,80,1536]{2,1,0:T(8,128)(2,1)S(1)}, u32[]{:S(2)}, u32[]{:S(2)}) async-start(bf16[8,80,1536]{2,1,0:T(8,128)(2,1)} %bitcast.221), calls=%async_computation.4 | async-start | bytes 3932160 | tf_op jit(solution)/shard_map/all_to_all | solution.py:27
  296.5 40.6 %collective-permute-start.3 = (bf16[128,512]{0,1:T(8,128)(2,1)}, bf16[128,512]{0,1:T(8,128)(2,1)}, u32[]{:S(2)}, u32[]{:S(2)}) collective-permute-start(bf16[128,512]{0,1:T(8,128)(2,1)} %fusion.44), channel_id=1, source_target_pairs={{1,0},{2,1},{3,2},{4,3},{5,4},{6,5},{7,6},{8,7},{9,8},{10,9},{11,1... | collective-permute-start | bytes 393224 | tf_op jit(solution)/shard_map/ppermute | solution.py:319
  326.5 38.8 %collective-permute-start.8 = (bf16[2,8,72,384]{3,2,1,0:T(8,128)(2,1)}, bf16[2,8,72,384]{3,2,1,0:T(8,128)(2,1)}, u32[]{:S(2)}, u32[]{:S(2)}) collective-permute-start(bf16[2,8,72,384]{3,2,1,0:T(8,128)(2,1)} %bitcast.201), channel_id=1, source_target_pairs={{0,48},{16,32},{32,16},{48,0},{1,49},{17,33},{33,17},{49,1},{2,50}... | collective-permute-start | bytes 2654216 | tf_op jit(solution)/shard_map/ppermute | solution.py:84
  330.4 34.8 %collective-permute-start.7 = (bf16[2,8,72,384]{3,2,1,0:T(8,128)(2,1)}, bf16[2,8,72,384]{3,2,1,0:T(8,128)(2,1)}, u32[]{:S(2)}, u32[]{:S(2)}) collective-permute-start(bf16[2,8,72,384]{3,2,1,0:T(8,128)(2,1)} %bitcast.202), channel_id=1, source_target_pairs={{0,32},{16,48},{32,0},{48,16},{1,33},{17,49},{33,1},{49,17},{2,34}... | collective-permute-start | bytes 2654216 | tf_op jit(solution)/shard_map/ppermute | solution.py:84
  332.5 34.5 %collective-permute-start.6 = (bf16[2,8,72,384]{3,2,1,0:T(8,128)(2,1)}, bf16[2,8,72,384]{3,2,1,0:T(8,128)(2,1)}, u32[]{:S(2)}, u32[]{:S(2)}) collective-permute-start(bf16[2,8,72,384]{3,2,1,0:T(8,128)(2,1)} %bitcast.203), channel_id=1, source_target_pairs={{0,16},{16,0},{32,48},{48,32},{1,17},{17,1},{33,49},{49,33},{2,18}... | collective-permute-start | bytes 2654216 | tf_op jit(solution)/shard_map/ppermute | solution.py:84
  376.7 16.2 %all-to-all-start.7 = ((bf16[16,128,128]{2,1,0:T(8,128)(2,1)}), bf16[16,128,128]{2,1,0:T(8,128)(2,1)}, u32[]{:S(2)}, u32[]{:S(2)}) async-start(bf16[16,128,128]{2,1,0:T(8,128)(2,1)} %bitcast.219), calls=%async_computation.7 | async-start | bytes 1048576 | tf_op jit(solution)/shard_map/all_to_all | solution.py:27
  419.9 26.2 %collective-permute-start.10 = (bf16[8,72,384]{2,1,0:T(8,128)(2,1)}, bf16[8,72,384]{2,1,0:T(8,128)(2,1)}, u32[]{:S(2)}, u32[]{:S(2)}) collective-permute-start(bf16[8,72,384]{2,1,0:T(8,128)(2,1)} %all-to-all-done.8), channel_id=1, source_target_pairs={{0,64},{64,0},{1,65},{65,1},{2,66},{66,2},{3,67},{67,3},{4,68},{68... | collective-permute-start | bytes 1327112 | tf_op jit(solution)/shard_map/ppermute | solution.py:92
  439.4 19.8 %all-to-all-start.12 = ((bf16[8,48,896]{2,1,0:T(8,128)(2,1)}), bf16[8,48,896]{2,1,0:T(8,128)(2,1)}, u32[]{:S(2)}, u32[]{:S(2)}) async-start(bf16[8,48,896]{2,1,0:T(8,128)(2,1)} %bitcast.214), calls=%async_computation.12 | async-start | bytes 1376256 | tf_op jit(solution)/shard_map/all_to_all | solution.py:27
  448.5 54.3 %collective-permute-start.11 = (bf16[2,8,72,384]{3,2,1,0:T(8,128)(2,1)}, bf16[2,8,72,384]{3,2,1,0:T(8,128)(2,1)}, u32[]{:S(2)}, u32[]{:S(2)}) collective-permute-start(bf16[2,8,72,384]{3,2,1,0:T(8,128)(2,1)} %pad_maximum_fusion.7.refs_0_), channel_id=1, source_target_pairs={{0,16},{16,0},{32,48},{48,32},{1,17},{17,1},{33,49},{49,33},{2,18}... | collective-permute-start | bytes 2654216 | tf_op jit(solution)/shard_map/ppermute | solution.py:97
  450.5 52.3 %collective-permute-start.12 = (bf16[2,8,72,384]{3,2,1,0:T(8,128)(2,1)}, bf16[2,8,72,384]{3,2,1,0:T(8,128)(2,1)}, u32[]{:S(2)}, u32[]{:S(2)}) collective-permute-start(bf16[2,8,72,384]{3,2,1,0:T(8,128)(2,1)} %pad_maximum_fusion.7.refs_0_), channel_id=1, source_target_pairs={{0,32},{16,48},{32,0},{48,16},{1,33},{17,49},{33,1},{49,17},{2,34}... | collective-permute-start | bytes 2654216 | tf_op jit(solution)/shard_map/ppermute | solution.py:97
  453.2 49.6 %collective-permute-start.13 = (bf16[2,8,72,384]{3,2,1,0:T(8,128)(2,1)}, bf16[2,8,72,384]{3,2,1,0:T(8,128)(2,1)}, u32[]{:S(2)}, u32[]{:S(2)}) collective-permute-start(bf16[2,8,72,384]{3,2,1,0:T(8,128)(2,1)} %pad_maximum_fusion.7.refs_0_), channel_id=1, source_target_pairs={{0,48},{16,32},{32,16},{48,0},{1,49},{17,33},{33,17},{49,1},{2,50}... | collective-permute-start | bytes 2654216 | tf_op jit(solution)/shard_map/ppermute | solution.py:97
  459.8 36.7 %all-to-all-start.11 = ((bf16[8,2,96]{2,1,0:T(2,128)(2,1)}), bf16[8,2,96]{2,1,0:T(2,128)(2,1)S(1)}, u32[]{:S(2)}, u32[]{:S(2)}) async-start(bf16[8,2,96]{2,1,0:T(2,128)(2,1)} %broadcast_in_dim.61), calls=%async_computation.11 | async-start | bytes 8192 | tf_op jit(solution)/shard_map/all_to_all | solution.py:27
  497.4 17.1 %all-to-all-start.13 = ((bf16[8,48,896]{2,1,0:T(8,128)(2,1)}), bf16[8,48,896]{2,1,0:T(8,128)(2,1)}, u32[]{:S(2)}, u32[]{:S(2)}) async-start(bf16[8,48,896]{2,1,0:T(8,128)(2,1)} %broadcast_in_dim.62), calls=%async_computation.13 | async-start | bytes 1376256 | tf_op jit(solution)/shard_map/all_to_all | solution.py:27
  (62 other events, 866.6 us)
Sparse Core Ops, SparseCore 0:
  10.3 51.4 all-gather.4
  63.5 58.0 all-gather.6
  156.8 41.4 all-gather.8
  255.6 64.0 all-gather.10

commit v3 on v2

--- a/solution.py
+++ b/solution.py
@@ -68,20 +68,28 @@
     return lax.optimization_barrier((value, *earlier))[0]
 
 
-def pieces_of(rows, wide):
-    *lead, a, b = rows.shape
-    n = len(lead)
-    cut_up = rows.reshape(*lead, 2, a // 2, wide, b // wide)
-    return cut_up.transpose(n, n + 2, *range(n), n + 1, n + 3)
-
-
-def sum_over_rep(pieces):
-    wide = pieces.shape[1]
+def gather_over_z(part):
+    wide = lax.axis_size("z")
+    return [part] + [
+        lax.ppermute(part, "z", [(i, i ^ k) for i in range(wide)]) for k in range(1, wide)
+    ]
+
+
+def sum_over_rep(here, other):
+    wide = here.shape[1]
     z = lax.axis_index("z")
-    total = lax.dynamic_index_in_dim(pieces, z, 1, keepdims=False).astype(f32)
-    for k in range(1, wide):
-        sent = lax.dynamic_index_in_dim(pieces, z ^ k, 1, keepdims=False)
-        total = total + lax.ppermute(sent, "z", [(i, i ^ k) for i in range(wide)]).astype(f32)
+
+    def piece(k):
+        mine = lax.dynamic_index_in_dim(here, z ^ k, 1, keepdims=False)
+        return mine.astype(f32) + lax.dynamic_index_in_dim(other, z ^ k, 1, keepdims=False).astype(f32)
+
+    moved = [
+        lax.ppermute(piece(k).astype(bf16), "z", [(i, i ^ k) for i in range(wide)])
+        for k in range(1, wide)
+    ]
+    total = piece(0)
+    for received in moved:
+        total = total + received.astype(f32)
     h = lax.axis_index("h")
     mine = lax.dynamic_index_in_dim(total, h, 0, keepdims=False)
     sent = lax.dynamic_index_in_dim(total, 1 - h, 0, keepdims=False).astype(bf16)
@@ -92,11 +100,125 @@
     other = lax.ppermute(piece, "h", SWAP)
     low = lax.axis_index("h") == 0
     both = jnp.stack([jnp.where(low, piece, other), jnp.where(low, other, piece)])
-    wide = lax.axis_size("z")
-    moved = [
-        lax.ppermute(both, "z", [(i, i ^ k) for i in range(wide)]) for k in range(1, wide)
-    ]
-    return [both, *moved]
+    return gather_over_z(both)
+
+
+def assemble_experts(mine, other, rows_up, rows_down):
+    wide = len(mine)
+    chips, rows, part = mine[0].shape
+    width = wide * part
+    place = jnp.stack([lax.axis_index("z"), lax.axis_index("c")]).astype(jnp.int32)
+
+    def kernel(place_ref, *refs):
+        up_ref, down_ref = refs[2 * wide], refs[2 * wide + 1]
+        for owner, parts in ((place_ref[1], refs[:wide]), (1 - place_ref[1], refs[wide : 2 * wide])):
+            for k in range(wide):
+                at = pl.multiple_of((place_ref[0] ^ k) * part, 128)
+                up_ref[0, owner, :, pl.ds(at, part)] = parts[k][0, :rows_up]
+                down_ref[0, owner, :, pl.ds(at, part)] = parts[k][0, rows_up : rows_up + rows_down]
+
+    up, down = pl.pallas_call(
+        kernel,
+        grid_spec=pltpu.PrefetchScalarGridSpec(
+            num_scalar_prefetch=1,
+            grid=(chips,),
+            in_specs=[pl.BlockSpec((1, rows, part), lambda e, p: (e, 0, 0))] * (2 * wide),
+            out_specs=[
+                pl.BlockSpec((1, 2, rows_up, width), lambda e, p: (e, 0, 0, 0)),
+                pl.BlockSpec((1, 2, rows_down, width), lambda e, p: (e, 0, 0, 0)),
+            ],
+        ),
+        out_shape=[
+            jax.ShapeDtypeStruct((chips, 2, rows_up, width), bf16),
+            jax.ShapeDtypeStruct((chips, 2, rows_down, width), bf16),
+        ],
+    )(place, *mine, *other)
+    return up.reshape(-1, width), down.reshape(-1, width)
+
+
+def cut_expert_grads(grad_up, grad_down, rows_up, rows_down, wide):
+    width = grad_up.shape[1]
+    chips = grad_up.shape[0] // (2 * rows_up)
+    half, part = (rows_up + rows_down) // 2, width // wide
+    core = lax.axis_index("c").astype(jnp.int32).reshape(1)
+
+    def kernel(core_ref, up_ref, down_ref, here_ref, there_ref):
+        for owner, out_ref in ((core_ref[0], here_ref), (1 - core_ref[0], there_ref)):
+            up = up_ref[0, owner].astype(f32)
+            rest = jnp.concatenate([up[half:], down_ref[0, owner].astype(f32)], axis=0).astype(bf16)
+            first = up[:half].astype(bf16)
+            for z in range(wide):
+                out_ref[0, z, 0] = first[:, z * part : (z + 1) * part]
+                out_ref[1, z, 0] = rest[:, z * part : (z + 1) * part]
+
+    pieces = pl.BlockSpec((2, wide, 1, half, part), lambda e, p: (0, 0, e, 0, 0))
+    return pl.pallas_call(
+        kernel,
+        grid_spec=pltpu.PrefetchScalarGridSpec(
+            num_scalar_prefetch=1,
+            grid=(chips,),
+            in_specs=[
+                pl.BlockSpec((1, 2, rows_up, width), lambda e, p: (e, 0, 0, 0)),
+                pl.BlockSpec((1, 2, rows_down, width), lambda e, p: (e, 0, 0, 0)),
+            ],
+            out_specs=[pieces, pieces],
+        ),
+        out_shape=[jax.ShapeDtypeStruct((2, wide, chips, half, part), bf16)] * 2,
+    )(
+        core,
+        grad_up.reshape(chips, 2, rows_up, width),
+        grad_down.reshape(chips, 2, rows_down, width),
+    )
+
+
+def pack_attention_grads(blocks, out_rows, wide):
+    count, rows, column = blocks.shape
+    rows -= 8
+    half = rows // 2
+    total = count + out_rows.shape[1] // column
+    each = total // wide
+
+    def kernel(block_ref, out_ref, piece_ref):
+        piece_ref[...] = jnp.zeros_like(piece_ref)
+        gains = block_ref[0, rows:].astype(f32)
+        for b in range(1, count):
+            gains = gains + block_ref[b, rows:].astype(f32)
+        for h in range(2):
+            at = slice(h * half, (h + 1) * half)
+            for b in range(total):
+                if b < count:
+                    value = block_ref[b, at]
+                else:
+                    value = out_ref[at, (b - count) * column : (b - count + 1) * column]
+                to = (b % each) * column
+                piece_ref[h * wide + b // each, :half, to : to + column] = value
+        for p in range(2 * wide):
+            piece_ref[p, half:, :column] = gains.astype(bf16)
+
+    return pl.pallas_call(
+        kernel, out_shape=jax.ShapeDtypeStruct((2 * wide, half + 8, each * column), bf16)
+    )(blocks, out_rows)
+
+
+def sum_and_copy(pieces):
+    count, rows, columns = pieces.shape
+
+    def kernel(piece_ref, copy_ref, gain_ref):
+        total = piece_ref[0].astype(f32)
+        for p in range(1, count):
+            total = total + piece_ref[p].astype(f32)
+        gain_ref[...] = total[rows - 8 :, :128]
+        low = total[: rows - 8].astype(bf16)
+        for p in range(count):
+            copy_ref[p] = low
+
+    return pl.pallas_call(
+        kernel,
+        out_shape=[
+            jax.ShapeDtypeStruct((count, rows - 8, columns), bf16),
+            jax.ShapeDtypeStruct((8, 128), f32),
+        ],
+    )(pieces)
 
 
 def expert_outputs(moved, rows_up, rows_down):
@@ -176,7 +298,6 @@
     w_down,
 ):
     wide_z = lax.axis_size("z")
-    reps = 2 * wide_z
     shards = lax.axis_size("y") * lax.axis_size("x") * lax.axis_size("c")
     core = lax.axis_index("c")
     shard = (lax.axis_index("y") * lax.axis_size("x") + lax.axis_index("x")) * 2 + core
@@ -186,10 +307,10 @@
     kv_width = KEY_VALUE_HEADS * HEAD_SIZE
     scale = HEAD_SIZE ** (-0.5)
 
-    qkv_full = lax.all_gather(
-        jnp.concatenate([w_query, key_value_weight], 1), SHARD, axis=0, tiled=True
-    )
-    out_full = lax.all_gather(w_out, SHARD, axis=0, tiled=True)
+    attn_full = lax.all_gather(
+        jnp.concatenate([w_query, key_value_weight, w_out], 1), SHARD, axis=0, tiled=True
+    )
+    qkv_full, out_full = attn_full[:, : width + 2 * kv_width], attn_full[:, width + 2 * kv_width :]
     part = width // wide_z
     rows_up, rows_down = w_gateup.shape[1], w_down.shape[1]
     column = lax.axis_index("z") * part
@@ -207,12 +328,9 @@
     gains = in_core_order(core, gains_mine, lax.ppermute(gains_mine, "c", SWAP))
     gains = gains.transpose(2, 0, 1, 3).reshape(2, width).astype(f32)
     gain_attn, gain_ffn = gains[0], gains[1]
-    expert_mine = spread(expert_part[:, : rows_up + rows_down], wide_z, "z")
-    expert_other = lax.ppermute(expert_mine, "c", SWAP)
-    expert_full = in_core_order(core, expert_mine.transpose(1, 2, 0, 3), expert_other.transpose(1, 2, 0, 3))
-    expert_full = expert_full.reshape(experts, 2, rows_up + rows_down, width)
-    gateup_full = expert_full[:, :, :rows_up].reshape(width, 2 * ff)
-    down_full = expert_full[:, :, rows_up:].reshape(ff, width)
+    expert_mine = gather_over_z(expert_part)
+    expert_other = [lax.ppermute(one, "c", SWAP) for one in expert_mine]
+    gateup_full, down_full = assemble_experts(expert_mine, expert_other, rows_up, rows_down)
 
     chosen = routes[:, :, None] == jnp.arange(experts, dtype=jnp.int32)
     member = jnp.any(chosen, axis=1)
@@ -224,7 +342,7 @@
     slot_weight = jnp.sum(jnp.where(picks, weight.T[:, None, :], 0.0), axis=2)
     upstream = cotangent.astype(f32)
     grad_out_sent = matmul(pick, cotangent) * slot_weight.reshape(-1, 1)
-    grad_out = exchange(after(grad_out_sent.astype(bf16), expert_mine), CHIPS)
+    grad_out = exchange(after(grad_out_sent.astype(bf16), expert_part), CHIPS)
 
     lengths = seq_lengths[0]
     starts = jnp.cumsum(lengths) - lengths
@@ -260,7 +378,7 @@
     prob_low = probs.astype(bf16)
     mixed = jnp.einsum("grst,tgd->sgrd", prob_low, values, preferred_element_type=f32)
     attended = mixed.reshape(rows, width).astype(bf16)
-    branch = matmul(attended, out_full).astype(bf16)
+    branch = matmul(after(attended, gateup_full, down_full), out_full).astype(bf16)
     residual = wide + branch.astype(f32)
     ffn_factor = lax.rsqrt(jnp.mean(residual * residual, axis=-1, keepdims=True) + EPSILON)
     normed_ffn = (residual * ffn_factor * gain_ffn).astype(bf16)
@@ -284,14 +402,10 @@
     grad_down = dot_general(acted, grad_out, ((0,), (0,)))
     grad_gateup = dot_general(picked, grad_pre, ((0,), (0,)))
 
-    def owned(grad):
-        halves = grad.astype(bf16).reshape(experts, 2, -1, width)
-        there = lax.dynamic_index_in_dim(halves, 1 - core, 1, keepdims=False)
-        here = lax.dynamic_index_in_dim(halves, core, 1, keepdims=False)
-        return here.astype(f32) + lax.ppermute(there, "c", SWAP).astype(f32)
-
-    both = jnp.concatenate([owned(grad_gateup), owned(grad_down)], axis=1).astype(bf16)
-    over_rep = sum_over_rep(pieces_of(both, wide_z))
+    here, there = cut_expert_grads(
+        grad_gateup.astype(bf16), grad_down.astype(bf16), rows_up, rows_down, wide_z
+    )
+    over_rep = sum_over_rep(here, lax.ppermute(there, "c", SWAP))
 
     back = pick.astype(f32) * slot_weight.reshape(-1, 1)
     back_high = back.astype(bf16)
@@ -350,22 +464,21 @@
         grad_branch_all.reshape(shards, rows, width),
         preferred_element_type=f32,
     ).astype(bf16)
-    qkv_rows = exchange(after(qkv_block, expert_pieces), SHARD)
-    qkv_rows = qkv_rows.reshape(shards, width // shards, columns)
-    qkv_rows = qkv_rows.transpose(1, 0, 2).reshape(width // shards, shards * columns)
-    attn_rows = jnp.concatenate([qkv_rows, out_rows], axis=1)
-    attn_pieces = pieces_of(attn_rows, wide_z)
-    attn_pieces = attn_pieces.reshape(reps, *attn_pieces.shape[2:])
-    attn_rep = exchange(attn_pieces, REP).astype(f32).sum(axis=0).astype(bf16)
-    attn_all = spread(attn_rep, reps, REP)
+    grad_gains = jnp.stack([grad_gain_attn, grad_gain_ffn]).reshape(2, shards, -1)
+    gain_rows = jnp.pad(
+        grad_gains.transpose(1, 0, 2).astype(bf16),
+        ((0, 0), (0, 6), (0, columns - width // shards)),
+    )
+    qkv_block = jnp.concatenate(
+        [qkv_block.reshape(shards, width // shards, columns), gain_rows], axis=1
+    )
+    qkv_blocks = exchange(after(qkv_block, expert_pieces), SHARD)
+    attn_pieces = exchange(pack_attention_grads(qkv_blocks, out_rows, wide_z), REP)
+    attn_copies, gain_sums = sum_and_copy(attn_pieces)
     grad_query, grad_keyval_w, grad_out_w = attention_outputs(
-        attn_all, (width, 2 * kv_width, width)
-    )
-
-    grad_gains = jnp.stack([grad_gain_attn, grad_gain_ffn]).reshape(2, shards, -1)
-    grad_gains = exchange(after(grad_gains.transpose(1, 0, 2).astype(bf16), qkv_rows), SHARD)
-    grad_gains = grad_gains.astype(f32).sum(axis=0)
-    grad_gains = spread(grad_gains.astype(bf16), reps, REP).astype(f32).sum(axis=0)
+        exchange(attn_copies, REP), (width, 2 * kv_width, width)
+    )
+    grad_gains = gain_sums[:2, : width // shards]
     return (
         output,
         grad_tokens,

time: 533 us -> 462 us (0.87); the launches traced: 524 us -> 459 us
  local copies, waits for them, and re-layouts: 85.9 us -> 16.2 us
  Pallas kernels: 9.52 us -> 30.8 us
  starting transfers between devices: 75.9 us -> 64.7 us
  other arithmetic: 39.8 us -> 29.6 us
  blocking collectives: 62 us -> 70.6 us
  waiting for transfers between devices: 154 us -> 147 us
    ppermute x9 -> x14, waiting for transfers between devices: 27.3 us -> 105 us  [the longest x6 76.8 us: gather_over_z(): lax.ppermute(part, 'z', [(i, i ^ k) for i in range(wide)])]
    all_to_all x12 -> x9, waiting for transfers between devices: 89.5 us -> 41.4 us  [exchange(): return lax.all_to_all(parts, axes, 0, 0, tiled=True)]
    all_gather x2 -> x1, waiting for transfers between devices: 34.8 us -> 0.01 us  [per_device(): lax.all_gather(jnp.concatenate([w_query, key_value_weight, w_out], 1), SH...]
    pallas_call x0 -> x4, Pallas kernels: none -> 21.5 us  [the longest x1 9 us: assemble_experts(): pl.pallas_call(kernel, grid_spec=pltpu.PrefetchScalarGridSpec(num_scalar_...]
    all_to_all x12 -> x9, starting transfers between devices: 57.4 us -> 39.9 us  [exchange(): return lax.all_to_all(parts, axes, 0, 0, tiled=True)]
    another operation x3 -> x1, local copies, waits for them, and re-layouts: 13.9 us -> 0.01 us  [in_core_order(): jnp.stack([mine, other], 1)]
    transpose x2 -> x0, local copies, waits for them, and re-layouts: 13.1 us -> none  [the longest x1 6.59 us: per_device(): expert_other.transpose(1, 2, 0, 3)]
    dynamic_slice x1 -> x0, local copies, waits for them, and re-layouts: 12.8 us -> none  [sum_over_rep(): total = lax.dynamic_index_in_dim(pieces, z, 1, keepdims=False).astype(f32)]
  transfers between devices with their start and end apart: 30 -> 31, of which waited for: 12 -> 14; matrix products, arithmetic and copies ran while one was open for 38% -> 28% of each run, Pallas kernels for 1% -> 6%
where the time goes in v3:
time: 462 us; the launch traced here: 459 us
  waiting for transfers between devices  147 us (32%)
  matrix products  86.1 us (19%)
  blocking collectives  70.6 us (15%)
  starting transfers between devices  64.7 us (14%)
  Pallas kernels  30.8 us (7%)
  other arithmetic  29.6 us (6%)
  local copies, waits for them, and re-layouts  16.2 us (4%)
  between operations  14.6 us (3%)
    ppermute x6, waiting for transfers between devices, gather_over_z(): lax.ppermute(part, 'z', [(i, i ^ k) for i in range(wide)])  76.8 us
    all_to_all x2, blocking collectives, exchange(): return lax.all_to_all(parts, axes, 0, 0, tiled=True)  70.6 us
    dot_general x10, matrix products, dot_general(): lax.dot_general(left, right, (dims, ((), ())), preferred_element_type=f32)  43.8 us
    all_to_all x9, waiting for transfers between devices, exchange(): return lax.all_to_all(parts, axes, 0, 0, tiled=True)  41.4 us
    all_to_all x9, starting transfers between devices, exchange(): return lax.all_to_all(parts, axes, 0, 0, tiled=True)  39.9 us
    ppermute x3, waiting for transfers between devices, sum_over_rep(): lax.ppermute(piece(k).astype(bf16), 'z', [(i, i ^ k) for i in range(wide)])  28.3 us
    dot_general x6, matrix products, matmul(): return jnp.dot(left, right, preferred_element_type=f32)  20.4 us
    ppermute x6, starting transfers between devices, gather_over_z(): lax.ppermute(part, 'z', [(i, i ^ k) for i in range(wide)])  11.4 us
  transfers between devices with their start and end apart: 31, of which 14 were waited for; matrix products, arithmetic and copies ran while one was open for 28% of the time, Pallas kernels for 6%

profile of v3, /device:TPU:0, one launch (start us, length us, event | category | flops | bytes accessed | tf_op | source)
XLA Modules:
  0.0 459.2 jit_solution(18376412711150303386)
XLA Ops:
  11.7 5.5 %all-to-all-start = ((bf16[8,152,384]{2,1,0:T(8,128)(2,1)}), bf16[8,152,384]{2,1,0:T(8,128)(2,1)S(1)}, u32[]{:S(2)}, u32[]{:S(2)}) async-start(bf16[8,152,384]{2,1,0:T(8,128)(2,1)} %pad_maximum_fusion.3), calls=%async_computation | async-start | bytes 1867776 | tf_op jit(solution)/shard_map/all_to_all | solution.py:27
  21.5 17.0 %all-to-all-done.refs_0_ = bf16[8,152,384]{2,1,0:T(8,128)(2,1)S(1)} async-done(((bf16[8,152,384]{2,1,0:T(8,128)(2,1)}), bf16[8,152,384]{2,1,0:T(8,128)(2,1)S(1)}, u32[]{:S(2)}, u32[]{:S(2)}) %all-to-all-start) | async-done | bytes 933920 | tf_op jit(solution)/shard_map/all_to_all | solution.py:27
  46.2 16.4 %collective-permute-done.2.refs_1_ = bf16[8,152,384]{2,1,0:T(8,128)(2,1)} collective-permute-done((bf16[8,152,384]{2,1,0:T(8,128)(2,1)S(1)}, bf16[8,152,384]{2,1,0:T(8,128)(2,1)}, u32[]{:S(2)}, u32[]{:S(2)}) %collective-permute-start.2) | collective-permute-done | bytes 933920 | tf_op jit(solution)/shard_map/ppermute | solution.py:74
  62.7 23.9 %collective-permute-done.3.refs_2_ = bf16[8,152,384]{2,1,0:T(8,128)(2,1)} collective-permute-done((bf16[8,152,384]{2,1,0:T(8,128)(2,1)S(1)}, bf16[8,152,384]{2,1,0:T(8,128)(2,1)}, u32[]{:S(2)}, u32[]{:S(2)}) %collective-permute-start.3) | collective-permute-done | bytes 933920 | tf_op jit(solution)/shard_map/ppermute | solution.py:74
  99.3 9.0 %shard_map.187 = (bf16[8,2,96,1536]{3,2,1,0:T(8,128)(2,1)}, bf16[8,2,48,1536]{3,2,1,0:T(8,128)(2,1)}) custom-call(s32[2]{0:T(128)} %pad_add_fusion.place_ref, bf16[8,152,384]{2,1,0:T(8,128)(2,1)} %copy-done.2, bf16[8,152,384]{2,1,0:T(8,128)(2,1)} %collective-permute-done.2.refs_1_, bf16[8,152,384]{2,1,0:T(8,128)(2,1)} %collective-permute-done.3.refs_2_, ...), custom_call_target="tpu_custom_call" | custom-call | tf_op jit(solution)/shard_map/pallas_call | solution.py:120
  116.9 8.8 %all-to-all-done.1 = bf16[8,80,1536]{2,1,0:T(8,128)(2,1)} async-done(((bf16[8,80,1536]{2,1,0:T(8,128)(2,1)}), bf16[8,80,1536]{2,1,0:T(8,128)(2,1)}, u32[]{:S(2)}, u32[]{:S(2)}) %all-to-all-start.1) | async-done | bytes 1966112 | tf_op jit(solution)/shard_map/all_to_all | solution.py:27
  125.6 29.1 %all_to_all.81 = bf16[8,80,1536]{2,1,0:T(8,128)(2,1)} all-to-all(bf16[8,80,1536]{2,1,0:T(8,128)(2,1)S(1)} %bitcast.166), channel_id=1, replica_groups=mesh['h'=2,'z'=4,'y'=4,'x'=2,'c'=2] {'y','x'}, dimensions={0} | all-to-all | bytes 3932160 | tf_op jit(solution)/shard_map/all_to_all | solution.py:27
  158.6 5.8 %fusion.96 = f32[640,1536]{1,0:T(8,128)S(1)} fusion(bf16[640,1536]{1,0:T(8,128)(2,1)} %bitcast.174, bf16[1536,1536]{1,0:T(8,128)(2,1)} %bitcast.199), kind=kOutput, calls=%fused_computation.180 | convolution fusion | flops 3019898880 | bytes 10616832 | tf_op jit(solution)/shard_map/dot_general | solution.py:31
  164.4 4.8 %multiply_convert_fusion.2 = (bf16[640,768]{1,0:T(8,128)(2,1)S(1)}, bf16[640,768]{1,0:T(8,128)(2,1)S(1)}, bf16[640,768]{1,0:T(8,128)(2,1)}) fusion(f32[640,1536]{1,0:T(8,128)S(1)} %fusion.96, bf16[640,1536]{1,0:T(8,128)(2,1)} %bitcast.23, bf16[768,1536]{1,0:T(8,128)(2,1)S(1)} %bitcast.202), kind=kOutput, calls=%fused_computation.31 | convolution fusion | flops 1517322240 | bytes 11206656 | tf_op jit(solution)/shard_map/dot_general | solution.py:35
  169.2 7.6 %convolution_convert_fusion.4 = bf16[640,1536]{1,0:T(8,128)(2,1)} fusion(bf16[1536,1536]{1,0:T(8,128)(2,1)} %bitcast.200, bf16[640,768]{1,0:T(8,128)(2,1)S(1)} %get-tuple-element.57, bf16[640,768]{1,0:T(8,128)(2,1)S(1)} %get-tuple-element.56), kind=kOutput, calls=%fused_computation.15 | convolution fusion | flops 3024814080 | bytes 8650752 | tf_op jit(solution)/shard_map/dot_general | solution.py:35
  176.8 41.5 %all_to_all.82 = bf16[8,80,1536]{2,1,0:T(8,128)(2,1)S(1)} all-to-all(bf16[8,80,1536]{2,1,0:T(8,128)(2,1)} %bitcast.176), channel_id=1, replica_groups=mesh['h'=2,'z'=4,'y'=4,'x'=2,'c'=2] {'y','x'}, dimensions={0} | all-to-all | bytes 3932160 | tf_op jit(solution)/shard_map/all_to_all | solution.py:27
  220.9 5.4 %convolution_convert_fusion.1 = bf16[768,1536]{1,0:T(8,128)(2,1)} fusion(bf16[640,768]{1,0:T(8,128)(2,1)} %get-tuple-element.58, bf16[640,1536]{1,0:T(8,128)(2,1)} %bitcast.23), kind=kOutput, calls=%fused_computation.12 | convolution fusion | flops 1511129088 | bytes 5308416 | tf_op jit(solution)/shard_map/dot_general | solution.py:35
  226.3 5.6 %convolution_convert_fusion = bf16[1536,1536]{1,0:T(8,128)(2,1)} fusion(bf16[640,1536]{1,0:T(8,128)(2,1)S(1)} %bitcast.175, bf16[640,768]{1,0:T(8,128)(2,1)S(1)} %copy-done.45, bf16[640,768]{1,0:T(8,128)(2,1)S(1)} %copy-done.43), kind=kOutput, calls=%fused_computation.2 | convolution fusion | flops 3026190336 | bytes 8650752 | tf_op jit(solution)/shard_map/dot_general | solution.py:35
  231.9 8.3 %shard_map.188 = (bf16[2,4,8,72,384]{4,3,2,1,0:T(8,128)(2,1)}, bf16[2,4,8,72,384]{4,3,2,1,0:T(8,128)(2,1)}) custom-call(s32[1]{0:T(128)} %bitcast.15.core_ref, bf16[8,2,96,1536]{3,2,1,0:T(8,128)(2,1)} %bitcast.167, bf16[8,2,48,1536]{3,2,1,0:T(8,128)(2,1)} %bitcast.170), custom_call_target="tpu_custom_call" | custom-call | tf_op jit(solution)/shard_map/pallas_call | solution.py:155
  253.1 5.0 %fusion.22 = bf16[128,1536]{1,0:T(8,128)(2,1)} fusion(bf16[128,1536]{1,0:T(8,128)(2,1)} %get-tuple-element.51, bf16[1536,3584]{1,0:T(8,128)(2,1)} %all-gather.4.cloned.1.call-done), kind=kOutput, calls=%fused_computation.25 | convolution fusion | flops 604176384 | bytes 5505024 | tf_op jit(solution)/shard_map/dot_general | solution.py:35
  288.3 27.7 %collective-permute-done.13 = bf16[2,8,72,384]{3,2,1,0:T(8,128)(2,1)} collective-permute-done((bf16[2,8,72,384]{3,2,1,0:T(8,128)(2,1)}, bf16[2,8,72,384]{3,2,1,0:T(8,128)(2,1)}, u32[]{:S(2)}, u32[]{:S(2)}) %collective-permute-start.13) | collective-permute-done | bytes 884768 | tf_op jit(solution)/shard_map/ppermute | solution.py:87
  328.2 5.0 %all-to-all-start.6 = ((bf16[16,128,128]{2,1,0:T(8,128)(2,1)}), bf16[16,128,128]{2,1,0:T(8,128)(2,1)}, u32[]{:S(2)}, u32[]{:S(2)}) async-start(bf16[16,128,128]{2,1,0:T(8,128)(2,1)} %bitcast.171), calls=%async_computation.6 | async-start | bytes 1048576 | tf_op jit(solution)/shard_map/all_to_all | solution.py:27
  338.2 5.9 %all-to-all-done.6 = bf16[16,128,128]{2,1,0:T(8,128)(2,1)} async-done(((bf16[16,128,128]{2,1,0:T(8,128)(2,1)}), bf16[16,128,128]{2,1,0:T(8,128)(2,1)}, u32[]{:S(2)}, u32[]{:S(2)}) %all-to-all-start.6) | async-done | bytes 524320 | tf_op jit(solution)/shard_map/all_to_all | solution.py:27
  348.2 6.7 %fusion.51 = (bf16[1536]{0:T(1024)(128)(2,1)}, f32[128]{0:T(128)}, f32[128,1536]{1,0:T(8,128)}) fusion(bf16[128,1536]{1,0:T(8,128)(2,1)S(1)} %copy-done.3, f32[128]{0:T(128)} %copy-done.30, f32[1536]{0:T(1024)S(1)} %copy-done.24, bf16[1536,3584]{1,0:T(8,128)(2,1)} %all-gather.4.cloned.1.call-done, bf16[128,256]{0,1:T(8,128)(2,1)} %copy-done.20, ...), kind=kOutput, calls=%fused_computation.80 | convolution fusion | flops 807729536 | bytes 8005632 | tf_op jit(solution)/shard_map/dot_general | solution.py:35
  364.7 5.0 %all-to-all-start.8 = ((bf16[16,104,128]{2,1,0:T(8,128)(2,1)}), bf16[16,104,128]{2,1,0:T(8,128)(2,1)}, u32[]{:S(2)}, u32[]{:S(2)}) async-start(bf16[16,104,128]{2,1,0:T(8,128)(2,1)} %fusion.55), calls=%async_computation.8 | async-start | bytes 851968 | tf_op jit(solution)/shard_map/all_to_all | solution.py:27
  374.3 5.2 %all-to-all-done.8.block_ref = bf16[16,104,128]{2,1,0:T(8,128)(2,1)} async-done(((bf16[16,104,128]{2,1,0:T(8,128)(2,1)}), bf16[16,104,128]{2,1,0:T(8,128)(2,1)}, u32[]{:S(2)}, u32[]{:S(2)}) %all-to-all-start.8) | async-done | bytes 426016 | tf_op jit(solution)/shard_map/all_to_all | solution.py:27
  408.1 13.0 %collective-permute-done.16.refs_1_ = bf16[2,8,72,384]{3,2,1,0:T(8,128)(2,1)} collective-permute-done((bf16[2,8,72,384]{3,2,1,0:T(8,128)(2,1)}, bf16[2,8,72,384]{3,2,1,0:T(8,128)(2,1)}, u32[]{:S(2)}, u32[]{:S(2)}) %collective-permute-start.16) | collective-permute-done | bytes 884768 | tf_op jit(solution)/shard_map/ppermute | solution.py:74
  421.1 19.7 %collective-permute-done.17.refs_2_ = bf16[2,8,72,384]{3,2,1,0:T(8,128)(2,1)} collective-permute-done((bf16[2,8,72,384]{3,2,1,0:T(8,128)(2,1)}, bf16[2,8,72,384]{3,2,1,0:T(8,128)(2,1)}, u32[]{:S(2)}, u32[]{:S(2)}) %collective-permute-start.17) | collective-permute-done | bytes 884768 | tf_op jit(solution)/shard_map/ppermute | solution.py:74
  442.1 7.2 %shard_map.192 = (f32[8,96,1536]{2,1,0:T(8,128)}, f32[8,48,1536]{2,1,0:T(8,128)}) custom-call(s32[1]{0:T(128)} %bitcast.14.z_ref, bf16[2,8,72,384]{3,2,1,0:T(8,128)(2,1)} %pad_maximum_fusion.6.refs_0_, bf16[2,8,72,384]{3,2,1,0:T(8,128)(2,1)} %collective-permute-done.16.refs_1_, bf16[2,8,72,384]{3,2,1,0:T(8,128)(2,1)} %collective-permute-done.17.refs_2_, ...), custom_call_target="tpu_custom_call" | custom-call | tf_op jit(solution)/shard_map/pallas_call | solution.py:241
  (243 shorter events, 155.7 us)
Async XLA Ops:
  7.2 81.9 %all-gather.4.cloned.1.call-start = ((), (), s32[]{:S(2)}) async-start(), calls=%async_computation.11 | async-start | bytes 11698176 | tf_op jit(solution)/shard_map/all_gather | solution.py:310
  11.7 26.9 %all-to-all-start = ((bf16[8,152,384]{2,1,0:T(8,128)(2,1)}), bf16[8,152,384]{2,1,0:T(8,128)(2,1)S(1)}, u32[]{:S(2)}, u32[]{:S(2)}) async-start(bf16[8,152,384]{2,1,0:T(8,128)(2,1)} %pad_maximum_fusion.3), calls=%async_computation | async-start | bytes 1867776 | tf_op jit(solution)/shard_map/all_to_all | solution.py:27
  38.6 24.0 %collective-permute-start.2 = (bf16[8,152,384]{2,1,0:T(8,128)(2,1)S(1)}, bf16[8,152,384]{2,1,0:T(8,128)(2,1)}, u32[]{:S(2)}, u32[]{:S(2)}) collective-permute-start(bf16[8,152,384]{2,1,0:T(8,128)(2,1)S(1)} %all-to-all-done.refs_0_), channel_id=1, source_target_pairs={{0,16},{16,0},{32,48},{48,32},{1,17},{17,1},{33,49},{49,33},{2,18}... | collective-permute-start | bytes 2801672 | tf_op jit(solution)/shard_map/ppermute | solution.py:74
  41.0 45.5 %collective-permute-start.3 = (bf16[8,152,384]{2,1,0:T(8,128)(2,1)S(1)}, bf16[8,152,384]{2,1,0:T(8,128)(2,1)}, u32[]{:S(2)}, u32[]{:S(2)}) collective-permute-start(bf16[8,152,384]{2,1,0:T(8,128)(2,1)S(1)} %all-to-all-done.refs_0_), channel_id=1, source_target_pairs={{0,32},{16,48},{32,0},{48,16},{1,33},{17,49},{33,1},{49,17},{2,34}... | collective-permute-start | bytes 2801672 | tf_op jit(solution)/shard_map/ppermute | solution.py:74
  45.3 43.8 %collective-permute-start.4 = (bf16[8,152,384]{2,1,0:T(8,128)(2,1)S(1)}, bf16[8,152,384]{2,1,0:T(8,128)(2,1)}, u32[]{:S(2)}, u32[]{:S(2)}) collective-permute-start(bf16[8,152,384]{2,1,0:T(8,128)(2,1)S(1)} %all-to-all-done.refs_0_), channel_id=1, source_target_pairs={{0,48},{16,32},{32,16},{48,0},{1,49},{17,33},{33,17},{49,1},{2,50}... | collective-permute-start | bytes 2801672 | tf_op jit(solution)/shard_map/ppermute | solution.py:74
  45.9 53.4 %collective-permute-start.5 = (bf16[8,152,384]{2,1,0:T(8,128)(2,1)S(1)}, bf16[8,152,384]{2,1,0:T(8,128)(2,1)}, u32[]{:S(2)}, u32[]{:S(2)}) collective-permute-start(bf16[8,152,384]{2,1,0:T(8,128)(2,1)S(1)} %all-to-all-done.refs_0_), channel_id=1, source_target_pairs={{0,1},{1,0},{2,3},{3,2},{4,5},{5,4},{6,7},{7,6},{8,9},{9,8},{10,11... | collective-permute-start | bytes 2801672 | tf_op jit(solution)/shard_map/ppermute | solution.py:332
  62.6 36.6 %collective-permute-start.6 = (bf16[8,152,384]{2,1,0:T(8,128)(2,1)}, bf16[8,152,384]{2,1,0:T(8,128)(2,1)}, u32[]{:S(2)}, u32[]{:S(2)}) collective-permute-start(bf16[8,152,384]{2,1,0:T(8,128)(2,1)} %collective-permute-done.2.refs_1_), channel_id=1, source_target_pairs={{0,1},{1,0},{2,3},{3,2},{4,5},{5,4},{6,7},{7,6},{8,9},{9,8},{10,11... | collective-permute-start | bytes 2801672 | tf_op jit(solution)/shard_map/ppermute | solution.py:332
  94.8 30.9 %all-to-all-start.1 = ((bf16[8,80,1536]{2,1,0:T(8,128)(2,1)}), bf16[8,80,1536]{2,1,0:T(8,128)(2,1)}, u32[]{:S(2)}, u32[]{:S(2)}) async-start(bf16[8,80,1536]{2,1,0:T(8,128)(2,1)} %bitcast.22), calls=%async_computation.1 | async-start | bytes 3932160 | tf_op jit(solution)/shard_map/all_to_all | solution.py:27
  99.1 260.0 %all-gather.6.cloned.1.call-start = ((), (), s32[]{:S(2)}) async-start(), calls=%async_computation.12 | async-start | bytes 6684672 | tf_op jit(solution)/shard_map/all_gather | solution.py:387
  154.8 22.1 %all-to-all-start.4 = ((bf16[16,96,128]{2,1,0:T(8,128)(2,1)}), bf16[16,96,128]{2,1,0:T(8,128)(2,1)S(1)}, u32[]{:S(2)}, u32[]{:S(2)}) async-start(bf16[16,96,128]{2,1,0:T(8,128)(2,1)} %bitcast.190), calls=%async_computation.4 | async-start | bytes 786432 | tf_op jit(solution)/shard_map/all_to_all | solution.py:27
  158.3 211.3 %all-gather.8.cloned.1.call-start = ((), (), s32[]{:S(2)}) async-start(), calls=%async_computation.13 | async-start | bytes 6684672 | tf_op jit(solution)/shard_map/all_gather | solution.py:420
  244.5 28.9 %collective-permute-start.10 = (bf16[2,4,8,72,384]{4,3,2,0,1:T(8,128)(2,1)}, bf16[2,4,8,72,384]{4,3,2,0,1:T(8,128)(2,1)}, u32[]{:S(2)}, u32[]{:S(2)}) collective-permute-start(bf16[2,4,8,72,384]{4,3,2,0,1:T(8,128)(2,1)} %copy.95), channel_id=1, source_target_pairs={{0,1},{1,0},{2,3},{3,2},{4,5},{5,4},{6,7},{7,6},{8,9},{9,8},{10,11... | collective-permute-start | bytes 10616840 | tf_op jit(solution)/shard_map/ppermute | solution.py:408
  249.2 78.9 %all-to-all-start.3 = ((bf16[8,80,1536]{2,1,0:T(8,128)(2,1)}), bf16[8,80,1536]{2,1,0:T(8,128)(2,1)S(1)}, u32[]{:S(2)}, u32[]{:S(2)}) async-start(bf16[8,80,1536]{2,1,0:T(8,128)(2,1)} %bitcast.173), calls=%async_computation.3 | async-start | bytes 3932160 | tf_op jit(solution)/shard_map/all_to_all | solution.py:27
  269.8 15.9 %collective-permute-start.9 = (bf16[128,512]{0,1:T(8,128)(2,1)}, bf16[128,512]{0,1:T(8,128)(2,1)}, u32[]{:S(2)}, u32[]{:S(2)}) collective-permute-start(bf16[128,512]{0,1:T(8,128)(2,1)} %fusion.65), channel_id=1, source_target_pairs={{1,0},{2,1},{3,2},{4,3},{5,4},{6,5},{7,6},{8,7},{9,8},{10,9},{11,1... | collective-permute-start | bytes 393224 | tf_op jit(solution)/shard_map/ppermute | solution.py:433
  277.0 38.9 %collective-permute-start.13 = (bf16[2,8,72,384]{3,2,1,0:T(8,128)(2,1)}, bf16[2,8,72,384]{3,2,1,0:T(8,128)(2,1)}, u32[]{:S(2)}, u32[]{:S(2)}) collective-permute-start(bf16[2,8,72,384]{3,2,1,0:T(8,128)(2,1)} %get-tuple-element.54), channel_id=1, source_target_pairs={{0,48},{16,32},{32,16},{48,0},{1,49},{17,33},{33,17},{49,1},{2,50}... | collective-permute-start | bytes 2654216 | tf_op jit(solution)/shard_map/ppermute | solution.py:87
  277.3 38.6 %collective-permute-start.12 = (bf16[2,8,72,384]{3,2,1,0:T(8,128)(2,1)}, bf16[2,8,72,384]{3,2,1,0:T(8,128)(2,1)}, u32[]{:S(2)}, u32[]{:S(2)}) collective-permute-start(bf16[2,8,72,384]{3,2,1,0:T(8,128)(2,1)} %get-tuple-element.55), channel_id=1, source_target_pairs={{0,32},{16,48},{32,0},{48,16},{1,33},{17,49},{33,1},{49,17},{2,34}... | collective-permute-start | bytes 2654216 | tf_op jit(solution)/shard_map/ppermute | solution.py:87
  277.8 38.8 %collective-permute-start.11 = (bf16[2,8,72,384]{3,2,1,0:T(8,128)(2,1)}, bf16[2,8,72,384]{3,2,1,0:T(8,128)(2,1)}, u32[]{:S(2)}, u32[]{:S(2)}) collective-permute-start(bf16[2,8,72,384]{3,2,1,0:T(8,128)(2,1)} %get-tuple-element.53), channel_id=1, source_target_pairs={{0,16},{16,0},{32,48},{48,32},{1,17},{17,1},{33,49},{49,33},{2,18}... | collective-permute-start | bytes 2654216 | tf_op jit(solution)/shard_map/ppermute | solution.py:87
  328.2 15.9 %all-to-all-start.6 = ((bf16[16,128,128]{2,1,0:T(8,128)(2,1)}), bf16[16,128,128]{2,1,0:T(8,128)(2,1)}, u32[]{:S(2)}, u32[]{:S(2)}) async-start(bf16[16,128,128]{2,1,0:T(8,128)(2,1)} %bitcast.171), calls=%async_computation.6 | async-start | bytes 1048576 | tf_op jit(solution)/shard_map/all_to_all | solution.py:27
  357.2 28.8 %collective-permute-start.15 = (bf16[8,72,384]{2,1,0:T(8,128)(2,1)}, bf16[8,72,384]{2,1,0:T(8,128)(2,1)}, u32[]{:S(2)}, u32[]{:S(2)}) collective-permute-start(bf16[8,72,384]{2,1,0:T(8,128)(2,1)} %all-to-all-done.7), channel_id=1, source_target_pairs={{0,64},{64,0},{1,65},{65,1},{2,66},{66,2},{3,67},{67,3},{4,68},{68... | collective-permute-start | bytes 1327112 | tf_op jit(solution)/shard_map/ppermute | solution.py:100
  381.6 17.6 %all-to-all-start.9 = ((bf16[8,56,896]{2,1,0:T(8,128)(2,1)}), bf16[8,56,896]{2,1,0:T(8,128)(2,1)}, u32[]{:S(2)}, u32[]{:S(2)}) async-start(bf16[8,56,896]{2,1,0:T(8,128)(2,1)} %shard_map.189), calls=%async_computation.9 | async-start | bytes 1605632 | tf_op jit(solution)/shard_map/all_to_all | solution.py:27
  388.4 32.6 %collective-permute-start.16 = (bf16[2,8,72,384]{3,2,1,0:T(8,128)(2,1)}, bf16[2,8,72,384]{3,2,1,0:T(8,128)(2,1)}, u32[]{:S(2)}, u32[]{:S(2)}) collective-permute-start(bf16[2,8,72,384]{3,2,1,0:T(8,128)(2,1)} %pad_maximum_fusion.6.refs_0_), channel_id=1, source_target_pairs={{0,16},{16,0},{32,48},{48,32},{1,17},{17,1},{33,49},{49,33},{2,18}... | collective-permute-start | bytes 2654216 | tf_op jit(solution)/shard_map/ppermute | solution.py:74
  390.4 50.4 %collective-permute-start.17 = (bf16[2,8,72,384]{3,2,1,0:T(8,128)(2,1)}, bf16[2,8,72,384]{3,2,1,0:T(8,128)(2,1)}, u32[]{:S(2)}, u32[]{:S(2)}) collective-permute-start(bf16[2,8,72,384]{3,2,1,0:T(8,128)(2,1)} %pad_maximum_fusion.6.refs_0_), channel_id=1, source_target_pairs={{0,32},{16,48},{32,0},{48,16},{1,33},{17,49},{33,1},{49,17},{2,34}... | collective-permute-start | bytes 2654216 | tf_op jit(solution)/shard_map/ppermute | solution.py:74
  393.1 48.9 %collective-permute-start.18 = (bf16[2,8,72,384]{3,2,1,0:T(8,128)(2,1)}, bf16[2,8,72,384]{3,2,1,0:T(8,128)(2,1)}, u32[]{:S(2)}, u32[]{:S(2)}) collective-permute-start(bf16[2,8,72,384]{3,2,1,0:T(8,128)(2,1)} %pad_maximum_fusion.6.refs_0_), channel_id=1, source_target_pairs={{0,48},{16,32},{32,16},{48,0},{1,49},{17,33},{33,17},{49,1},{2,50}... | collective-permute-start | bytes 2654216 | tf_op jit(solution)/shard_map/ppermute | solution.py:74
  401.4 49.1 %all-to-all-start.10 = ((bf16[8,48,896]{2,1,0:T(8,128)(2,1)}), bf16[8,48,896]{2,1,0:T(8,128)(2,1)}, u32[]{:S(2)}, u32[]{:S(2)}) async-start(bf16[8,48,896]{2,1,0:T(8,128)(2,1)} %get-tuple-element.41), calls=%async_computation.10 | async-start | bytes 1376256 | tf_op jit(solution)/shard_map/all_to_all | solution.py:27
  (53 other events, 756.6 us)
Sparse Core Ops, SparseCore 0:
  10.3 72.5 all-gather.3
  154.9 62.4 all-gather.5
  221.0 42.0 all-gather.7

commit v4 on v2

v4 whole, which is shorter than its diff:
```python
import jax
import jax.numpy as jnp
from jax import lax
from jax.experimental import pallas as pl
from jax.experimental.pallas import tpu as pltpu
from jax.sharding import Mesh, PartitionSpec as P

QUERY_HEADS = 12
KEY_VALUE_HEADS = 2
GROUP = QUERY_HEADS // KEY_VALUE_HEADS
HEAD_SIZE = 128
CAP = 80

EPSILON = 1e-06
ROPE_BASE = 10000.0
SCALE = HEAD_SIZE ** (-0.5)
SHARD = ("y", "x", "c")
CHIPS = ("y", "x")
REP = ("h", "z")
ALL = REP + SHARD
SWAP = [(0, 1), (1, 0)]

bf16 = jnp.bfloat16
f32 = jnp.float32

VMEM_LIMIT = 40 * 1024 * 1024
WHOLE = pl.BlockSpec(memory_space=pltpu.VMEM)
UNUSED = pl.BlockSpec(memory_space=pl.ANY)
SCALAR = pl.BlockSpec(memory_space=pltpu.SMEM)


def exchange(parts, axes):
    return lax.all_to_all(parts, axes, 0, 0, tiled=True)


def spread(part, ways, axes):
    return exchange(jnp.broadcast_to(part[None], (ways, *part.shape)), axes)


def matmul(left, right):
    return jnp.dot(left, right, preferred_element_type=f32)


def dot_general(left, right, dims):
    return lax.dot_general(left, right, (dims, ((), ())), preferred_element_type=f32)


def times_transposed(left, right):
    return dot_general(left, right, ((1,), (1,)))


def transposed_times(left, right):
    return dot_general(left, right, ((0,), (0,)))


def in_core_order(core, mine, other):
    return jnp.where(core == 0, jnp.stack([mine, other], 1), jnp.stack([other, mine], 1))


def call(kernel, out_shape, operands, earlier=(), specs=None, flops=0, scratch=()):
    specs = specs or [WHOLE] * len(operands)
    count = len(operands)

    def body(*refs):
        kernel(*refs[:count], *refs[count + len(earlier) :])

    size = sum(one.size * one.dtype.itemsize for one in (*operands, *out_shape))
    return pl.pallas_call(
        body,
        in_specs=[*specs, *([UNUSED] * len(earlier))],
        out_specs=[WHOLE] * len(out_shape),
        out_shape=out_shape,
        scratch_shapes=scratch,
        compiler_params=pltpu.CompilerParams(vmem_limit_bytes=VMEM_LIMIT),
        cost_estimate=pl.CostEstimate(flops=flops, bytes_accessed=size, transcendentals=0),
    )(*operands, *earlier)


def fetch(source_ref, to_ref, semaphores, along, base=0):
    rows, columns = to_ref.shape
    copies = []
    for i in range(to_ref.shape[along] // 512):
        chunk = pl.ds(i * 512, 512)
        if along:
            source = source_ref.at[:, pl.ds(base + i * 512, 512)]
            copy = pltpu.make_async_copy(source, to_ref.at[:, chunk], semaphores.at[i])
        else:
            source = source_ref.at[chunk, pl.ds(base, columns)]
            copy = pltpu.make_async_copy(source, to_ref.at[chunk, :], semaphores.at[i])
        copy.start()
        copies.append(copy)
    return copies


def shaped(shape, dtype):
    return jax.ShapeDtypeStruct(shape, dtype)


def inverse_rms(values):
    return lax.rsqrt(jnp.mean(values * values, axis=-1, keepdims=True) + EPSILON)


def norm_back(values, gain_row, upstream):
    factor = inverse_rms(values)
    grad_normed = upstream * gain_row
    grad_gain = jnp.sum(upstream * values * factor, axis=0, keepdims=True)
    cubed = factor * factor * factor
    grad_input = factor * grad_normed - values * cubed * jnp.mean(
        grad_normed * values, axis=-1, keepdims=True
    )
    return grad_input, grad_gain


def rotary_tables(position):
    half = HEAD_SIZE // 2
    frequency = ROPE_BASE ** (-jnp.arange(half, dtype=f32) / half)
    angle = position.astype(f32)[:, None] * frequency[None, :]
    cosine, sine = jnp.cos(angle), jnp.sin(angle)
    return jnp.concatenate([cosine, cosine], 1), jnp.concatenate([-sine, sine], 1)


def rotate(values, cosine, sine):
    return values * cosine + pltpu.roll(values, HEAD_SIZE // 2, 1) * sine


def project_qkv(tokens, gain, weights, cosine, sine, earlier):
    rows, width = tokens.shape
    kv_width = KEY_VALUE_HEADS * HEAD_SIZE
    turned = QUERY_HEADS + KEY_VALUE_HEADS
    total = width + 2 * kv_width

    def kernel(
        token_ref, gain_ref, all_ref, cos_ref, sin_ref, normed_ref, query_ref, keyval_ref, w_ref, sem
    ):
        copies = fetch(all_ref, w_ref, sem, 1)
        wide = token_ref[...].astype(f32)
        normed = (wide * inverse_rms(wide) * gain_ref[...]).astype(bf16)
        normed_ref[...] = normed
        cos, sin = cos_ref[...], sin_ref[...]
        for block in range(total // 256):
            if block % 2 == 0:
                copies[block // 2].wait()
            both = matmul(normed, w_ref[:, block * 256 : (block + 1) * 256])
            for i in range(2):
                head = 2 * block + i
                value = both[:, i * HEAD_SIZE : (i + 1) * HEAD_SIZE]
                if head < turned:
                    value = rotate(value, cos, sin)
                value = value.astype(bf16)
                if head < QUERY_HEADS:
                    query_ref[:, head * HEAD_SIZE : (head + 1) * HEAD_SIZE] = value
                else:
                    at = (head - QUERY_HEADS) * HEAD_SIZE
                    keyval_ref[:, at : at + HEAD_SIZE] = value

    return call(
        kernel,
        [
            shaped((rows, width), bf16),
            shaped((rows, width), bf16),
            shaped((rows, 2 * kv_width), bf16),
        ],
        (tokens, gain, weights, cosine, sine),
        earlier,
        specs=[WHOLE, WHOLE, UNUSED, WHOLE, WHOLE],
        flops=2 * rows * width * total,
        scratch=[pltpu.VMEM((width, total), bf16), pltpu.SemaphoreType.DMA((total // 512,))],
    )


def allowed_keys(first_ref, rows):
    row = lax.broadcasted_iota(jnp.int32, (rows, 2 * rows), 0)
    key = lax.broadcasted_iota(jnp.int32, (rows, 2 * rows), 1) - rows
    return (key <= row) & (key >= first_ref[...])


def probabilities(query, keys, allowed):
    scores = jnp.where(allowed, times_transposed(query, keys) * SCALE, -1000000000.0)
    exp_scores = jnp.exp(scores - jnp.max(scores, axis=-1, keepdims=True))
    return exp_scores / jnp.sum(exp_scores, axis=-1, keepdims=True)


def keys_and_values(before_ref, own_ref, group):
    both = []
    for base in (group * HEAD_SIZE, (KEY_VALUE_HEADS + group) * HEAD_SIZE):
        at = slice(base, base + HEAD_SIZE)
        both.append(jnp.concatenate([before_ref[:, at], own_ref[:, at]], axis=0))
    return both


def attend(queries, before, own, first, weights, tokens, gain):
    rows, width = tokens.shape

    def kernel(
        query_ref, before_ref, own_ref, first_ref, all_ref, token_ref, gain_ref,
        attended_ref, turned_ref, residual_ref, normed_ref, w_ref, sem,
    ):
        copies = fetch(all_ref, w_ref, sem, 1, weights.shape[1] - width)
        allowed = allowed_keys(first_ref, rows)
        for group in range(KEY_VALUE_HEADS):
            keys, values = keys_and_values(before_ref, own_ref, group)
            for head in range(group * GROUP, (group + 1) * GROUP):
                at = slice(head * HEAD_SIZE, (head + 1) * HEAD_SIZE)
                probs = probabilities(query_ref[:, at], keys, allowed)
                mixed = matmul(probs.astype(bf16), values)
                attended_ref[:, at] = mixed.astype(bf16)
                turned_ref[at, :] = mixed.T.astype(bf16)
        attended = attended_ref[...]
        for block in range(width // 256):
            at = slice(block * 256, (block + 1) * 256)
            if block % 2 == 0:
                copies[block // 2].wait()
            branch = matmul(attended, w_ref[:, at]).astype(bf16)
            residual_ref[:, at] = token_ref[:, at].astype(f32) + branch.astype(f32)
        residual = residual_ref[...]
        normed_ref[...] = (residual * inverse_rms(residual) * gain_ref[...]).astype(bf16)

    return call(
        kernel,
        [
            shaped((rows, width), bf16),
            shaped((width, rows), bf16),
            shaped((rows, width), f32),
            shaped((rows, width), bf16),
        ],
        (queries, before, own, first, weights, tokens, gain),
        specs=[WHOLE, WHOLE, WHOLE, WHOLE, UNUSED, WHOLE, WHOLE],
        flops=2 * rows * width * width + 8 * rows * rows * width,
        scratch=[pltpu.VMEM((width, width), bf16), pltpu.SemaphoreType.DMA((width // 512,))],
    )


def pick_rows(pick, rows_in, earlier):
    slots, width = pick.shape[0], rows_in.shape[1]

    def kernel(pick_ref, in_ref, out_ref):
        for block in range(width // 512):
            at = slice(block * 512, (block + 1) * 512)
            out_ref[:, at] = matmul(pick_ref[...], in_ref[:, at]).astype(bf16)

    return call(
        kernel,
        [shaped((slots, width), bf16)],
        (pick, rows_in),
        earlier,
        flops=2 * slots * rows_in.size,
    )[0]


def run_experts(picked, grad_out, mine, other, rows_up, rows_down):
    slots, width = picked.shape
    wide = len(mine)
    chips, _, part = mine[0].shape
    ff = chips * 2 * rows_down
    place = jnp.stack([lax.axis_index("c"), lax.axis_index("z")]).astype(jnp.int32)

    def kernel(picked_ref, grad_ref, place_ref, *refs):
        mine_refs, other_refs = refs[:wide], refs[wide : 2 * wide]
        acted_ref, pre_ref, back_ref, down_w = refs[2 * wide : 2 * wide + 4]
        up_w, gate_ref, upper_ref, up_sem, down_sem = refs[2 * wide + 4 :]
        core = place_ref[0]
        ups, downs = [], []
        for k in range(wide):
            to = pl.ds(pl.multiple_of((place_ref[1] ^ k) * part, 128), part)
            for i, (owner, part_ref) in enumerate(((core, mine_refs[k]), (1 - core, other_refs[k]))):
                ups.append(
                    pltpu.make_async_copy(
                        part_ref.at[:, pl.ds(0, rows_up), :],
                        up_w.at[:, owner, :, to],
                        up_sem.at[2 * k + i],
                    )
                )
                downs.append(
                    pltpu.make_async_copy(
                        part_ref.at[:, pl.ds(rows_up, rows_down), :],
                        down_w.at[:, owner, :, to],
                        down_sem.at[2 * k + i],
                    )
                )
        for copy in ups + downs:
            copy.start()
        for copy in ups:
            copy.wait()

        @pl.loop(0, ff // 256)
        def _(j):
            at = pl.multiple_of(j * 256, 256)
            for base, ref in ((0, gate_ref), (ff, upper_ref)):
                weights = up_w[:, :, :, pl.ds(base + at, 256)].reshape(width, 256)
                ref[:, pl.ds(at, 256)] = matmul(picked_ref[...], weights)

        for copy in downs:
            copy.wait()
        half = chips // 2

        @pl.loop(0, 2)
        def _(j):
            at = pl.ds(pl.multiple_of(j * (ff // 2), 128), ff // 2)
            weights = down_w[pl.ds(j * half, half)].reshape(ff // 2, width)
            grad_act = times_transposed(grad_ref[...], weights)
            gate, up = gate_ref[:, at], upper_ref[:, at]
            sigmoid = 1.0 / (1.0 + jnp.exp(-gate))
            silu = gate * sigmoid
            acted_ref[:, at] = (silu * up).astype(bf16)
            grad_gate = grad_act * up * sigmoid * (1.0 + gate * (1.0 - sigmoid))
            pre_ref[:, at] = grad_gate.astype(bf16)
            upper = pl.ds(pl.multiple_of(ff + j * (ff // 2), 128), ff // 2)
            pre_ref[:, upper] = (grad_act * silu).astype(bf16)

        @pl.loop(0, 2)
        def _(j):
            weights = up_w[pl.ds(j * half, half)].reshape(width // 2, 2 * ff)
            to = pl.ds(pl.multiple_of(j * (width // 2), 128), width // 2)
            back_ref[:, to] = times_transposed(pre_ref[...], weights).astype(bf16)

    return call(
        kernel,
        [
            shaped((slots, ff), bf16),
            shaped((slots, 2 * ff), bf16),
            shaped((slots, width), bf16),
            shaped((chips, 2, rows_down, width), bf16),
        ],
        (picked, grad_out, place, *mine, *other),
        specs=[WHOLE, WHOLE, SCALAR, *([UNUSED] * (2 * wide))],
        flops=2 * slots * 5 * width * ff,
        scratch=[
            pltpu.VMEM((chips, 2, rows_up, width), bf16),
            pltpu.VMEM((slots, ff), f32),
            pltpu.VMEM((slots, ff), f32),
            pltpu.SemaphoreType.DMA((2 * wide,)),
            pltpu.SemaphoreType.DMA((2 * wide,)),
        ],
    )


def expert_weight_grads(picked, grad_pre, acted, grad_out, down, rows_up, chips, wide, earlier):
    slots, width = picked.shape
    rows_down = down.shape[0] // (2 * chips)
    half, part = (rows_up + rows_down) // 2, width // wide
    steps = 2
    near = chips // steps
    core = lax.axis_index("c").astype(jnp.int32).reshape(1)

    def kernel(core_ref, picked_ref, pre_ref, acted_ref, grad_ref, all_ref, down_ref, *refs):
        here_ref, there_ref, expert_ref, keep_ref = refs[-4:]
        expert_ref[...] = matmul(all_ref[...], down_ref[...]).astype(bf16)
        columns = width // 2
        for n in range(2):
            at = slice(n * columns, (n + 1) * columns)
            for m in range(near // 2):
                block = slice(m * 4 * rows_up, (m + 1) * 4 * rows_up)
                up = transposed_times(picked_ref[:, block], pre_ref[:, at])
                for i in range(4):
                    k, c = 2 * m + i // 2, i % 2
                    keep_ref[k, c] = up[i * rows_up : (i + 1) * rows_up]
            down = transposed_times(acted_ref[...], grad_ref[:, at])
            for k in range(near):
                for c in range(2):
                    base = (2 * k + c) * rows_down
                    up = keep_ref[k, c]
                    first = up[:half].astype(bf16)
                    rest = jnp.concatenate([up[half:], down[base : base + rows_down]], axis=0)
                    rest = rest.astype(bf16)
                    for mine, out_ref in ((True, here_ref), (False, there_ref)):

                        @pl.when((core_ref[0] == c) == mine)
                        def _():
                            for i in range(columns // part):
                                cut = slice(i * part, (i + 1) * part)
                                z = n * (columns // part) + i
                                out_ref[z, 0, k] = first[:, cut]
                                out_ref[z, 1, k] = rest[:, cut]

    pieces = pl.BlockSpec((wide, 2, near, half, part), lambda s: (0, 0, s, 0, 0))
    return pl.pallas_call(
        kernel,
        grid=(steps,),
        in_specs=[
            SCALAR,
            pl.BlockSpec((slots, width // steps), lambda s: (0, s)),
            pl.BlockSpec(grad_pre.shape, lambda s: (0, 0)),
            pl.BlockSpec((slots, acted.shape[1] // steps), lambda s: (0, s)),
            pl.BlockSpec(grad_out.shape, lambda s: (0, 0)),
            pl.BlockSpec(acted.shape, lambda s: (0, 0)),
            pl.BlockSpec((down.shape[0], width // steps), lambda s: (0, s)),
            *([UNUSED] * len(earlier)),
        ],
        out_specs=[pieces, pieces, pl.BlockSpec((slots, width // steps), lambda s: (0, s))],
        out_shape=[
            *([shaped((wide, 2, chips, half, part), bf16)] * 2),
            shaped((slots, width), bf16),
        ],
        scratch_shapes=[pltpu.VMEM((near, 2, rows_up, width // 2), f32)],
        compiler_params=pltpu.CompilerParams(vmem_limit_bytes=VMEM_LIMIT),
        cost_estimate=pl.CostEstimate(
            flops=2 * slots * 4 * width * acted.shape[1],
            bytes_accessed=4 * 4 * slots * width,
            transcendentals=0,
        ),
    )(core, picked, grad_pre, acted, grad_out, acted, down, *earlier)


def residual_grad(pick, grad_picked, residual, gain, cotangent, earlier):
    rows, width = residual.shape

    def kernel(pick_ref, back_ref, residual_ref, gain_ref, cot_ref, grad_ref, branch_ref, gain_grad_ref):
        for block in range(width // 512):
            at = slice(block * 512, (block + 1) * 512)
            grad_ref[:, at] = transposed_times(pick_ref[...], back_ref[:, at])
        grad, grad_gain = norm_back(residual_ref[...], gain_ref[...], grad_ref[...])
        grad = grad + cot_ref[...].astype(f32)
        grad_ref[...] = grad
        branch_ref[...] = grad.astype(bf16)
        gain_grad_ref[...] = grad_gain

    return call(
        kernel,
        [shaped((rows, width), f32), shaped((rows, width), bf16), shaped((1, width), f32)],
        (pick, grad_picked, residual, gain, cotangent),
        earlier,
        flops=2 * grad_picked.size * rows,
    )


def attend_back(grad_branch, weights, queries, before, own, first, cosine, sine):
    rows, width = grad_branch.shape
    kv_width = KEY_VALUE_HEADS * HEAD_SIZE

    def kernel(
        grad_ref, all_ref, query_ref, before_ref, own_ref, first_ref, cos_ref, sin_ref,
        out_ref, prev_ref, self_ref, attended_ref, w_ref, sem,
    ):
        copies = fetch(all_ref, w_ref, sem, 0, weights.shape[1] - width)
        for block in range(width // 256):
            if block % 2 == 0:
                copies[block // 2].wait()
            at = slice(block * 256, (block + 1) * 256)
            attended_ref[:, at] = times_transposed(grad_ref[...], w_ref[at, :]).astype(bf16)
        allowed = allowed_keys(first_ref, rows)
        cos, sin = cos_ref[...], sin_ref[...]
        for group in range(KEY_VALUE_HEADS):
            keys, values = keys_and_values(before_ref, own_ref, group)
            raws, lows, uppers, asked = [], [], [], []
            for head in range(group * GROUP, (group + 1) * GROUP):
                at = slice(head * HEAD_SIZE, (head + 1) * HEAD_SIZE)
                query, upper = query_ref[:, at], attended_ref[:, at]
                probs = probabilities(query, keys, allowed)
                grad_probs = times_transposed(upper, values)
                inner = jnp.sum(probs * grad_probs, axis=-1, keepdims=True)
                raw = (probs * (grad_probs - inner) * SCALE).astype(bf16)
                out_ref[head] = rotate(matmul(raw, keys), cos, -sin).astype(bf16)
                raws.append(raw)
                lows.append(probs.astype(bf16))
                uppers.append(upper)
                asked.append(query)
            for base, lefts, rights in (
                (group * HEAD_SIZE, raws, asked),
                (kv_width + group * HEAD_SIZE, lows, uppers),
            ):
                grad = transposed_times(
                    jnp.concatenate(lefts, axis=0), jnp.concatenate(rights, axis=0)
                )
                prev_ref[:, base : base + HEAD_SIZE] = grad[:rows].astype(bf16)
                self_ref[:, base : base + HEAD_SIZE] = grad[rows:]

    return call(
        kernel,
        [
            shaped((QUERY_HEADS, rows, HEAD_SIZE), bf16),
            shaped((rows, 2 * kv_width), bf16),
            shaped((rows, 2 * kv_width), f32),
        ],
        (grad_branch, weights, queries, before, own, first, cosine, sine),
        specs=[WHOLE, UNUSED, *([WHOLE] * 6)],
        flops=2 * rows * width * width + 20 * rows * rows * width,
        scratch=[
            pltpu.VMEM((rows, width), bf16),
            pltpu.VMEM((width, width), bf16),
            pltpu.SemaphoreType.DMA((width // 512,)),
        ],
    )


def qkv_blocks_of(grad_queries, grad_own, from_next, cosine, sine, earlier):
    heads, rows, size = grad_queries.shape
    total = heads + 2 * KEY_VALUE_HEADS

    def kernel(query_ref, own_ref, next_ref, cos_ref, sin_ref, out_ref):
        out_ref[:heads] = query_ref[...]
        for i in range(2 * KEY_VALUE_HEADS):
            at = slice(i * size, (i + 1) * size)
            grad = own_ref[:, at] + next_ref[:, at].astype(f32)
            if i < KEY_VALUE_HEADS:
                grad = rotate(grad, cos_ref[...], -sin_ref[...])
            out_ref[heads + i] = grad.astype(bf16)

    return call(
        kernel,
        [shaped((total, rows, size), bf16)],
        (grad_queries, grad_own, from_next, cosine, sine),
        earlier,
    )[0]


def input_grad(blocks, weights, tokens, gain, grad_residual):
    rows, width = tokens.shape
    columns = blocks.shape[0] * HEAD_SIZE

    def kernel(
        block_ref, all_ref, token_ref, gain_ref, residual_ref, out_ref, gain_grad_ref, w_ref, sem
    ):
        copies = fetch(all_ref, w_ref, sem, 1)
        total = jnp.zeros((rows, width), f32)
        for i in range(blocks.shape[0] // 2):
            if i % 2 == 0:
                copies[i // 2].wait()
            pair = jnp.concatenate([block_ref[2 * i], block_ref[2 * i + 1]], axis=1)
            total = total + times_transposed(pair, w_ref[:, i * 256 : (i + 1) * 256])
        grad, grad_gain = norm_back(token_ref[...].astype(f32), gain_ref[...], total)
        out_ref[...] = (residual_ref[...] + grad).astype(bf16)
        gain_grad_ref[...] = grad_gain

    return call(
        kernel,
        [shaped((rows, width), bf16), shaped((1, width), f32)],
        (blocks, weights, tokens, gain, grad_residual),
        specs=[WHOLE, UNUSED, WHOLE, WHOLE, WHOLE],
        flops=2 * rows * width * columns,
        scratch=[pltpu.VMEM((width, columns), bf16), pltpu.SemaphoreType.DMA((columns // 512,))],
    )


def gather_over_z(part):
    wide = lax.axis_size("z")
    return [part] + [
        lax.ppermute(part, "z", [(i, i ^ k) for i in range(wide)]) for k in range(1, wide)
    ]


def gather_over_rep(piece):
    wide = lax.axis_size("z")
    ways = 2 * wide
    moved = []
    for k in range(wide):
        for j in range(2):
            step = j * wide + k
            moved.append(
                lax.ppermute(piece, REP, [(i, i ^ step) for i in range(ways)]) if step else piece
            )
    return moved


def expert_outputs(moved, rows_up, rows_down):
    wide = len(moved) // 2
    experts, half, part = moved[0].shape
    width = wide * part
    split = rows_up - half
    place = jnp.stack([lax.axis_index("h"), lax.axis_index("z")]).astype(jnp.int32)

    def kernel(place_ref, *refs):
        up_ref, down_ref = refs[2 * wide :]
        low = place_ref[0] == 0
        for k in range(wide):
            at = pl.ds(pl.multiple_of((place_ref[1] ^ k) * part, 128), part)
            same, other = refs[2 * k][0].astype(f32), refs[2 * k + 1][0].astype(f32)
            rest = jnp.where(low, other, same)
            up_ref[0, :half, at] = jnp.where(low, same, other)
            up_ref[0, half:, at] = rest[:split]
            down_ref[0, :, at] = rest[split:]

    return pl.pallas_call(
        kernel,
        grid_spec=pltpu.PrefetchScalarGridSpec(
            num_scalar_prefetch=1,
            grid=(experts,),
            in_specs=[pl.BlockSpec((1, half, part), lambda e, p: (e, 0, 0))] * (2 * wide),
            out_specs=[
                pl.BlockSpec((1, rows_up, width), lambda e, p: (e, 0, 0)),
                pl.BlockSpec((1, rows_down, width), lambda e, p: (e, 0, 0)),
            ],
        ),
        out_shape=[
            shaped((experts, rows_up, width), f32),
            shaped((experts, rows_down, width), f32),
        ],
    )(place, *moved)


def after(value, *earlier):
    for one in earlier:
        zero = jnp.minimum(jnp.abs(one[(0,) * one.ndim].astype(f32)), 0.0)
        value = value + zero.astype(value.dtype)
    return value


def pack_attention_grads(blocks, out_rows, wide, earlier):
    count, rows, column = blocks.shape
    rows -= 8
    half = rows // 2
    total = count + out_rows.shape[1] // column
    each = total // wide

    def kernel(block_ref, out_ref, piece_ref):
        piece_ref[...] = jnp.zeros_like(piece_ref)
        gains = block_ref[0, rows:].astype(f32)
        for b in range(1, count):
            gains = gains + block_ref[b, rows:].astype(f32)
        for h in range(2):
            at = slice(h * half, (h + 1) * half)
            for b in range(total):
                if b < count:
                    value = block_ref[b, at]
                else:
                    value = out_ref[at, (b - count) * column : (b - count + 1) * column]
                to = (b % each) * column
                piece_ref[h * wide + b // each, :half, to : to + column] = value
        for p in range(2 * wide):
            piece_ref[p, half:, :column] = gains.astype(bf16)

    return call(
        kernel, [shaped((2 * wide, half + 8, each * column), bf16)], (blocks, out_rows), earlier
    )[0]


def sum_and_copy(pieces):
    count, rows, columns = pieces.shape

    def kernel(piece_ref, copy_ref, gain_ref):
        total = piece_ref[0].astype(f32)
        for p in range(1, count):
            total = total + piece_ref[p].astype(f32)
        gain_ref[...] = total[rows - 8 :, :128]
        low = total[: rows - 8].astype(bf16)
        for p in range(count):
            copy_ref[p] = low

    return pl.pallas_call(
        kernel,
        out_shape=[
            jax.ShapeDtypeStruct((count, rows - 8, columns), bf16),
            jax.ShapeDtypeStruct((8, 128), f32),
        ],
    )(pieces)


def attention_outputs(pieces, widths):
    count, half, part = pieces.shape
    wide = count // 2

    def kernel(piece_ref, *out_refs):
        for h in range(2):
            for z in range(wide):
                left, right, base = z * part, (z + 1) * part, 0
                for ref, size in zip(out_refs, widths):
                    low, high = max(left, base), min(right, base + size)
                    if low < high:
                        ref[h * half : (h + 1) * half, low - base : high - base] = piece_ref[
                            h * wide + z, :, low - left : high - left
                        ].astype(f32)
                    base += size

    return pl.pallas_call(
        kernel,
        out_shape=[jax.ShapeDtypeStruct((2 * half, size), f32) for size in widths],
    )(pieces)


def per_device(
    tokens,
    cotangent,
    seq_lengths,
    seq_order,
    routes,
    gate_weights,
    attn_gain,
    w_query,
    key_value_weight,
    w_out,
    ffn_gain,
    w_gateup,
    w_down,
):
    wide_z = lax.axis_size("z")
    shards = lax.axis_size("y") * lax.axis_size("x") * lax.axis_size("c")
    core = lax.axis_index("c")
    shard = (lax.axis_index("y") * lax.axis_size("x") + lax.axis_index("x")) * 2 + core
    rows, width = tokens.shape
    experts = w_gateup.shape[0]
    kv_width = KEY_VALUE_HEADS * HEAD_SIZE
    owned = width // shards

    attn_full = lax.all_gather(
        jnp.concatenate([w_query, key_value_weight, w_out], 1), SHARD, axis=0, tiled=True
    )
    part = width // wide_z
    rows_up, rows_down = w_gateup.shape[1], w_down.shape[1]
    column = lax.axis_index("z") * part
    gains_own = jnp.pad(jnp.stack([attn_gain, ffn_gain]), ((0, 14), (0, part - owned)))
    parts = jnp.concatenate(
        [
            lax.dynamic_slice_in_dim(w_gateup, column, part, 2),
            lax.dynamic_slice_in_dim(w_down, column, part, 2),
            jnp.broadcast_to(gains_own[None], (experts, *gains_own.shape)),
        ],
        axis=1,
    )
    parts = exchange(parts, CHIPS)
    gains_mine = parts[:, rows_up + rows_down : rows_up + rows_down + 2, :owned]
    gains = in_core_order(core, gains_mine, lax.ppermute(gains_mine, "c", SWAP))
    gains = gains.transpose(2, 0, 1, 3).reshape(2, width).astype(f32)
    gain_attn, gain_ffn = gains[:1], gains[1:]
    expert_mine = gather_over_z(parts)
    expert_other = [lax.ppermute(one, "c", SWAP) for one in expert_mine]

    chosen = routes[:, :, None] == jnp.arange(experts, dtype=jnp.int32)
    member = jnp.any(chosen, axis=1)
    weight = jnp.sum(jnp.where(chosen, gate_weights[:, :, None], 0.0), axis=1)
    place = jnp.cumsum(member.astype(jnp.int32), axis=0) - 1
    slot = jnp.where(member, place, -1).T
    picks = slot[:, None, :] == jnp.arange(CAP, dtype=jnp.int32)[None, :, None]
    pick = picks.astype(bf16).reshape(experts * CAP, rows)
    slot_weight = jnp.sum(jnp.where(picks, weight.T[:, None, :], 0.0), axis=2)
    grad_out = matmul(pick, cotangent) * slot_weight.reshape(-1, 1)
    grad_out = exchange(after(grad_out, parts).astype(bf16), CHIPS)

    lengths = seq_lengths[0]
    starts = jnp.cumsum(lengths) - lengths
    row_at = shard * rows + jnp.arange(rows, dtype=jnp.int32)
    first_at = jnp.max(jnp.where(starts[None, :] <= row_at[:, None], starts[None, :], 0), axis=1)
    cosine, sine = rotary_tables(row_at - first_at)
    first = (first_at - shard * rows).astype(jnp.int32)[:, None]
    normed, queries, keyval = project_qkv(
        tokens, gain_attn, attn_full, cosine, sine, (grad_out,)
    )
    ring = [(i, (i + 1) % shards) for i in range(shards)]
    back_ring = [((i + 1) % shards, i) for i in range(shards)]
    before = lax.ppermute(keyval, SHARD, ring)
    attended, attended_turned, residual, normed_ffn = attend(
        queries, before, keyval, first, attn_full, tokens, gain_ffn
    )

    picked = exchange(pick_rows(pick, normed_ffn, tuple(expert_other)), CHIPS)
    normed_all = lax.all_gather(after(normed, picked), SHARD, axis=0, tiled=True)
    attended_cols = exchange(after(attended_turned, picked), SHARD)
    attended_cols = attended_cols.reshape(shards, owned, rows)
    acted, grad_pre, grad_picked, down = run_experts(
        picked, grad_out, expert_mine, expert_other, rows_up, rows_down
    )
    grad_picked_back = exchange(grad_picked, CHIPS)
    here, there, expert_out = expert_weight_grads(
        picked,
        grad_pre,
        acted,
        grad_out,
        down.reshape(-1, width),
        rows_up,
        experts,
        wide_z,
        (grad_picked, attended_cols),
    )
    other = lax.ppermute(there, "c", SWAP)
    pieces = (here.astype(f32) + other.astype(f32)).astype(bf16)
    over_z = lax.psum_scatter(pieces, "z", scatter_dimension=0, tiled=False)

    grad_residual, grad_branch, grad_gain_ffn = residual_grad(
        pick, grad_picked_back, residual, gain_ffn, cotangent, (here, normed_all)
    )
    grad_branch_all = lax.all_gather(grad_branch, SHARD, axis=0, tiled=True)
    grad_queries, grad_before, grad_own = attend_back(
        grad_branch, attn_full, queries, before, keyval, first, cosine, sine
    )
    from_next = lax.ppermute(grad_before, SHARD, back_ring)
    expert_out = exchange(expert_out, CHIPS)
    grad_blocks = qkv_blocks_of(
        grad_queries, grad_own, from_next, cosine, sine, (expert_out,)
    )
    grad_tokens, grad_gain_attn = input_grad(
        grad_blocks, attn_full, tokens, gain_attn, grad_residual
    )

    grad_cols = exchange(grad_blocks, SHARD)
    over_z = over_z.reshape(2 * experts, *over_z.shape[2:])
    over_rep = exchange(over_z, ("h", *CHIPS)).reshape(2, experts, *over_z.shape[1:])
    over_rep = (over_rep[0].astype(f32) + over_rep[1].astype(f32)).astype(bf16)
    moved = gather_over_rep(over_rep)
    shard_gateup, shard_down = expert_outputs(moved, rows_up, rows_down)
    qkv_block = transposed_times(normed_all, grad_cols.reshape(shards * rows, HEAD_SIZE))
    grad_gains = jnp.concatenate([grad_gain_attn, grad_gain_ffn]).reshape(2, shards, owned)
    gain_rows = jnp.pad(
        grad_gains.transpose(1, 0, 2).astype(bf16), ((0, 0), (0, 6), (0, HEAD_SIZE - owned))
    )
    qkv_block = jnp.concatenate(
        [qkv_block.astype(bf16).reshape(shards, owned, HEAD_SIZE), gain_rows], axis=1
    )
    out_rows = jnp.einsum(
        "jat,jtn->an",
        attended_cols,
        grad_branch_all.reshape(shards, rows, width),
        preferred_element_type=f32,
    ).astype(bf16)
    qkv_blocks = exchange(after(qkv_block, over_rep), SHARD)
    attn_pieces = exchange(pack_attention_grads(qkv_blocks, out_rows, wide_z, moved[1:4]), REP)
    attn_copies, gain_sums = sum_and_copy(attn_pieces)
    grad_query, grad_keyval, grad_out_w = attention_outputs(
        exchange(attn_copies, REP), (width, 2 * kv_width, width)
    )

    back = pick.astype(f32) * slot_weight.reshape(-1, 1)
    back_high = back.astype(bf16)
    back_low = (back - back_high.astype(f32)).astype(bf16)
    mixture = transposed_times(back_high, expert_out) + transposed_times(back_low, expert_out)
    output = (residual + mixture).astype(bf16)
    return (
        output,
        grad_tokens,
        gain_sums[0, :owned],
        grad_query,
        grad_keyval,
        grad_out_w,
        gain_sums[1, :owned],
        shard_gateup,
        shard_down,
    )


def solution(mesh):
    reps, shards = mesh.devices.shape
    fine = Mesh(mesh.devices.reshape(2, reps // 2, shards // 4, 2, 2), ALL)
    split = ALL
    placed = (
        P(split, None),
        P(split, None),
        P(REP, None),
        P(REP, None),
        P(split, None),
        P(split, None),
        P(SHARD),
        P(SHARD, None),
        P(SHARD, None),
        P(SHARD, None),
        P(SHARD),
        P(None, SHARD, None),
        P(None, SHARD, None),
    )
    return jax.shard_map(
        per_device,
        mesh=fine,
        in_specs=placed,
        out_specs=(
            P(split, None),
            P(split, None),
            P(SHARD),
            P(SHARD, None),
            P(SHARD, None),
            P(SHARD, None),
            P(SHARD),
            P(None, SHARD, None),
            P(None, SHARD, None),
        ),
        check_vma=False,
    )
```

time: 533 us -> 454 us (0.85); the launches traced: 524 us -> 451 us
  matrix products: 81.6 us -> 12.6 us
  Pallas kernels: 9.52 us -> 60.7 us
  blocking collectives: 62 us -> 99.3 us
  waiting for transfers between devices: 154 us -> 122 us
  local copies, waits for them, and re-layouts: 85.9 us -> 58.4 us
  other arithmetic: 39.8 us -> 17.2 us
  starting transfers between devices: 75.9 us -> 65 us
    pallas_call x0 -> x11, Pallas kernels: none -> 50.8 us  [the longest x9 37 us: call(): pl.pallas_call(body, in_specs=[*specs, *[UNUSED] * len(earlier)], out_spe...]
    unnamed x113 -> x116, local copies, waits for them, and re-layouts: 11.2 us -> 51.6 us
    all_to_all x2 -> x3, blocking collectives: 62 us -> 99.3 us  [exchange(): return lax.all_to_all(parts, axes, 0, 0, tiled=True)]
    dot_general x10 -> x3, matrix products: 41.5 us -> 6.61 us  [dot_general(): lax.dot_general(left, right, (dims, ((), ())), preferred_element_type=f32)]
    all_gather x2 -> x1, waiting for transfers between devices: 34.8 us -> 6.92 us  [per_device(): lax.all_gather(jnp.concatenate([w_query, key_value_weight, w_out], 1), SH...]
    all_to_all x12 -> x8, waiting for transfers between devices: 89.5 us -> 63 us  [exchange(): return lax.all_to_all(parts, axes, 0, 0, tiled=True)]
    ppermute x13 -> x17, waiting for transfers between devices: 27.3 us -> 50.9 us  [the longest x3 34.9 us: gather_over_z(): lax.ppermute(part, 'z', [(i, i ^ k) for i in range(wide)])]
    dot_general x6 -> x1, matrix products: 19.7 us -> 1.94 us  [matmul(): return jnp.dot(left, right, preferred_element_type=f32)]
  transfers between devices with their start and end apart: 30 -> 30, of which waited for: 12 -> 13; matrix products, arithmetic and copies ran while one was open for 38% -> 7% of each run, Pallas kernels for 1% -> 13%
where the time goes in v4:
time: 454 us; the launch traced here: 451 us
  waiting for transfers between devices  122 us (27%)
  blocking collectives  99.3 us (22%)
  starting transfers between devices  65 us (14%)
  Pallas kernels  60.7 us (13%)
  local copies, waits for them, and re-layouts  58.4 us (13%)
  other arithmetic  17.2 us (4%)
  between operations  16.4 us (4%)
  matrix products  12.6 us (3%)
    all_to_all x3, blocking collectives, exchange(): return lax.all_to_all(parts, axes, 0, 0, tiled=True)  99.3 us
    all_to_all x8, waiting for transfers between devices, exchange(): return lax.all_to_all(parts, axes, 0, 0, tiled=True)  63 us
    unnamed x116, local copies, waits for them, and re-layouts  51.6 us
    all_to_all x8, starting transfers between devices, exchange(): return lax.all_to_all(parts, axes, 0, 0, tiled=True)  42.5 us
    pallas_call x9, Pallas kernels, call(): pl.pallas_call(body, in_specs=[*specs, *[UNUSED] * len(earlier)], out_spe...  37 us
    ppermute x3, waiting for transfers between devices, gather_over_z(): lax.ppermute(part, 'z', [(i, i ^ k) for i in range(wide)])  34.9 us
    ppermute x7, starting transfers between devices, gather_over_rep(): lax.ppermute(piece, REP, [(i, i ^ step) for i in range(ways)])  14.3 us
    pallas_call x1, Pallas kernels, expert_weight_grads(): pl.pallas_call(kernel, grid=(steps,), in_specs=[SCALAR, pl.BlockSpec((slo...  11.7 us
  transfers between devices with their start and end apart: 30, of which 13 were waited for; matrix products, arithmetic and copies ran while one was open for 7% of the time, Pallas kernels for 13%

profile of v4, /device:TPU:0, one launch (start us, length us, event | category | flops | bytes accessed | tf_op | source)
XLA Modules:
  0.0 451.4 jit_solution(717039641357962620)
XLA Ops:
  12.3 5.5 %all-to-all-start = ((bf16[8,160,384]{2,1,0:T(8,128)(2,1)}), bf16[8,160,384]{2,1,0:T(8,128)(2,1)}, u32[]{:S(2)}, u32[]{:S(2)}) async-start(bf16[8,160,384]{2,1,0:T(8,128)(2,1)} %pad_maximum_fusion), calls=%async_computation | async-start | bytes 1966080 | tf_op jit(solution)/shard_map/all_to_all | solution.py:33
  19.4 21.6 %all-to-all-done.refs_3_ = bf16[8,160,384]{2,1,0:T(8,128)(2,1)} async-done(((bf16[8,160,384]{2,1,0:T(8,128)(2,1)}), bf16[8,160,384]{2,1,0:T(8,128)(2,1)}, u32[]{:S(2)}, u32[]{:S(2)}) %all-to-all-start) | async-done | bytes 983072 | tf_op jit(solution)/shard_map/all_to_all | solution.py:33
  55.7 12.4 %collective-permute-done.3.refs_4_ = bf16[8,160,384]{2,1,0:T(8,128)(2,1)} collective-permute-done((bf16[8,160,384]{2,1,0:T(8,128)(2,1)}, bf16[8,160,384]{2,1,0:T(8,128)(2,1)}, u32[]{:S(2)}, u32[]{:S(2)}) %collective-permute-start.3) | collective-permute-done | bytes 983072 | tf_op jit(solution)/shard_map/ppermute | solution.py:537
  68.2 19.9 %collective-permute-done.5.refs_5_ = bf16[8,160,384]{2,1,0:T(8,128)(2,1)} collective-permute-done((bf16[8,160,384]{2,1,0:T(8,128)(2,1)}, bf16[8,160,384]{2,1,0:T(8,128)(2,1)}, u32[]{:S(2)}, u32[]{:S(2)}) %collective-permute-start.5) | collective-permute-done | bytes 983072 | tf_op jit(solution)/shard_map/ppermute | solution.py:537
  93.4 4.8 %all-to-all-done.1 = bf16[8,80,1536]{2,1,0:T(8,128)(2,1)S(1)} async-done(((bf16[8,80,1536]{2,1,0:T(8,128)(2,1)}), bf16[8,80,1536]{2,1,0:T(8,128)(2,1)S(1)}, u32[]{:S(2)}, u32[]{:S(2)}) %all-to-all-start.1) | async-done | bytes 1966112 | tf_op jit(solution)/shard_map/all_to_all | solution.py:33
  98.2 6.9 %all-gather.4.cloned.1.call-done.refs_2_.refs_4_.refs_1_ = bf16[1536,3584]{1,0:T(8,128)(2,1)} async-done(((bf16[96,3584]{1,0:T(8,128)(2,1)}), bf16[1536,3584]{1,0:T(8,128)(2,1)}) %all-gather.4.cloned.1.call-update) | async-done | bytes 11010064 | tf_op jit(solution)/shard_map/all_gather | solution.py:693
  114.3 5.4 %collective-permute-done.1.refs_1_.refs_3_ = bf16[128,512]{1,0:T(8,128)(2,1)S(1)} collective-permute-done((bf16[128,512]{1,0:T(8,128)(2,1)S(1)}, bf16[128,512]{1,0:T(8,128)(2,1)S(1)}, u32[]{:S(2)}, u32[]{:S(2)}) %collective-permute-start.1) | collective-permute-done | bytes 131104 | tf_op jit(solution)/shard_map/ppermute | solution.py:738
  129.6 27.6 %all_to_all.83 = bf16[8,80,1536]{2,1,0:T(8,128)(2,1)S(1)} all-to-all(bf16[8,80,1536]{2,1,0:T(8,128)(2,1)S(1)} %bitcast.73), channel_id=1, replica_groups=mesh['h'=2,'z'=4,'y'=4,'x'=2,'c'=2] {'y','x'}, dimensions={0} | all-to-all | bytes 3932160 | tf_op jit(solution)/shard_map/all_to_all | solution.py:33
  167.9 15.9 %shard_map.190 = (bf16[640,768]{1,0:T(8,128)(2,1)S(1)}, bf16[640,1536]{1,0:T(8,128)(2,1)S(1)}, bf16[640,1536]{1,0:T(8,128)(2,1)S(1)}, bf16[8,2,48,1536]{3,2,1,0:T(8,128)(2,1)}) custom-call(bf16[640,1536]{1,0:T(8,128)(2,1)} %bitcast.75, bf16[640,1536]{1,0:T(8,128)(2,1)} %bitcast.71, s32[2]{0:T(128)S(1)} %copy-done.48, ...), custom_call_target="tpu_custom_call" | custom-call | flops 7549747200 | bytes 19070984 | tf_op jit(solution)/shard_map/pallas_call | solution.py:68
  193.8 11.7 %shard_map.191 = (bf16[4,2,8,72,384]{4,3,2,1,0:T(8,128)(2,1)}, bf16[4,2,8,72,384]{4,3,2,1,0:T(8,128)(2,1)}, bf16[640,1536]{1,0:T(8,128)(2,1)S(1)}) custom-call(s32[1]{0:T(128)} %bitcast.14.core_ref, bf16[640,1536]{1,0:T(8,128)(2,1)S(1)} %bitcast.76, bf16[640,1536]{1,0:T(8,128)(2,1)S(1)} %get-tuple-element.41.pre_ref, bf16[640,768]{1,0:T(8,128)(2,1)S(1)} %copy-done.50, ...), custom_call_target="tpu_custom_call" | custom-call | flops 6039797760 | bytes 15728640 | tf_op jit(solution)/shard_map/pallas_call | solution.py:376
  207.0 6.2 %collective-permute-done.10 = bf16[4,2,8,72,384]{4,3,2,1,0:T(8,128)(2,1)S(1)} collective-permute-done((bf16[4,2,8,72,384]{4,3,2,1,0:T(8,128)(2,1)}, bf16[4,2,8,72,384]{4,3,2,1,0:T(8,128)(2,1)S(1)}, u32[]{:S(2)}, u32[]{:S(2)}) %collective-permute-start.10) | collective-permute-done | bytes 3538976 | tf_op jit(solution)/shard_map/ppermute | solution.py:762
  213.2 4.7 %add_convert_fusion = bf16[4,2,8,72,384]{4,3,2,1,0:T(8,128)(2,1)} fusion(bf16[4,2,8,72,384]{4,3,2,1,0:T(8,128)(2,1)S(1)} %collective-permute-done.10, bf16[4,2,8,72,384]{4,3,2,1,0:T(8,128)(2,1)} %get-tuple-element.47.refs_5_), kind=kLoop, calls=%fused_computation | loop fusion | flops 7077888 | bytes 10616832 | tf_op jit(solution)/shard_map/convert_element_type | solution.py:763
  218.0 31.4 %all_to_all.84 = bf16[8,80,1536]{2,1,0:T(8,128)(2,1)S(1)} all-to-all(bf16[8,80,1536]{2,1,0:T(8,128)(2,1)} %bitcast.78), channel_id=1, replica_groups=mesh['h'=2,'z'=4,'y'=4,'x'=2,'c'=2] {'y','x'}, dimensions={0} | all-to-all | bytes 3932160 | tf_op jit(solution)/shard_map/all_to_all | solution.py:33
  259.2 40.3 %all_to_all.85 = bf16[8,80,1536]{2,1,0:T(8,128)(2,1)} all-to-all(bf16[8,80,1536]{2,1,0:T(8,128)(2,1)} %bitcast.77), channel_id=1, replica_groups=mesh['h'=2,'z'=4,'y'=4,'x'=2,'c'=2] {'y','x'}, dimensions={0} | all-to-all | bytes 3932160 | tf_op jit(solution)/shard_map/all_to_all | solution.py:33
  299.5 4.6 %all-to-all-start.7 = ((bf16[16,72,384]{2,1,0:T(8,128)(2,1)}), bf16[16,72,384]{2,1,0:T(8,128)(2,1)}, u32[]{:S(2)}, u32[]{:S(2)}) async-start(bf16[16,72,384]{2,1,0:T(8,128)(2,1)} %bitcast.82), calls=%async_computation.8 | async-start | bytes 1769472 | tf_op jit(solution)/shard_map/all_to_all | solution.py:33
  313.7 6.0 %shard_map.193 = (bf16[12,128,128]{2,1,0:T(8,128)(2,1)S(1)}, bf16[128,512]{1,0:T(8,128)(2,1)S(1)}, f32[128,512]{1,0:T(8,128)S(1)}) custom-call(bf16[128,1536]{1,0:T(8,128)(2,1)S(1)} %copy-done.24, bf16[1536,3584]{1,0:T(8,128)(2,1)S(1)} %copy-done.4, bf16[128,1536]{1,0:T(8,128)(2,1)S(1)} %get-tuple-element.37.refs_0_.refs_2_, ...), custom_call_target="tpu_custom_call" | custom-call | flops 1107296256 | bytes 12976640 | tf_op jit(solution)/shard_map/pallas_call | solution.py:68
  325.1 6.7 %all-to-all-start.6 = ((bf16[16,128,128]{2,1,0:T(8,128)(2,1)}), bf16[16,128,128]{2,1,0:T(8,128)(2,1)}, u32[]{:S(2)}, u32[]{:S(2)}) async-start(bf16[16,128,128]{2,1,0:T(8,128)(2,1)} %shard_map.194.refs_0_), calls=%async_computation.6 | async-start | bytes 1048576 | tf_op jit(solution)/shard_map/all_to_all | solution.py:33
  345.0 5.3 %shard_map.195 = (bf16[128,1536]{1,0:T(8,128)(2,1)}, f32[1,1536]{1,0:T(1,128)S(1)}) custom-call(bf16[16,128,128]{2,1,0:T(8,128)(2,1)} %shard_map.194.refs_0_, bf16[1536,3584]{1,0:T(8,128)(2,1)S(1)} %copy-done.5, bf16[128,1536]{1,0:T(8,128)(2,1)S(1)} %copy-done.13, f32[1,1536]{1,0:T(1,128)S(1)} %slice.41.refs_1_.refs_3_, f32[128,1536]{1,0:T(8,128)S(1)} %copy-done.32), custom_call_target="tpu_custom_call" | custom-call | flops 805306368 | bytes 13119488 | tf_op jit(solution)/shard_map/pallas_call | solution.py:68
  350.4 4.7 %convolution_convert_fusion = bf16[1536,128]{1,0:T(8,128)(2,1)S(1)} fusion(bf16[2048,1536]{1,0:T(8,128)(2,1)} %all-gather.6.cloned.1.call-done.refs_6_, bf16[2048,128]{1,0:T(8,128)(2,1)} %bitcast.27), kind=kOutput, calls=%fused_computation.8 | convolution fusion | flops 805502976 | bytes 7208960 | tf_op jit(solution)/shard_map/dot_general | solution.py:45
  356.0 5.7 %all-to-all-start.8 = ((bf16[16,104,128]{2,1,0:T(8,128)(2,1)}), bf16[16,104,128]{2,1,0:T(8,128)(2,1)S(1)}, u32[]{:S(2)}, u32[]{:S(2)}) async-start(bf16[16,104,128]{2,1,0:T(8,128)(2,1)} %fusion.6), calls=%async_computation.9 | async-start | bytes 851968 | tf_op jit(solution)/shard_map/all_to_all | solution.py:33
  366.5 4.9 %all-to-all-done.8.refs_0_ = bf16[16,104,128]{2,1,0:T(8,128)(2,1)S(1)} async-done(((bf16[16,104,128]{2,1,0:T(8,128)(2,1)}), bf16[16,104,128]{2,1,0:T(8,128)(2,1)S(1)}, u32[]{:S(2)}, u32[]{:S(2)}) %all-to-all-start.8) | async-done | bytes 426016 | tf_op jit(solution)/shard_map/all_to_all | solution.py:33
  375.2 7.9 %all-to-all-start.9 = ((bf16[8,56,896]{2,1,0:T(8,128)(2,1)}), bf16[8,56,896]{2,1,0:T(8,128)(2,1)}, u32[]{:S(2)}, u32[]{:S(2)}) async-start(bf16[8,56,896]{2,1,0:T(8,128)(2,1)} %shard_map.196), calls=%async_computation.10 | async-start | bytes 1605632 | tf_op jit(solution)/shard_map/all_to_all | solution.py:33
  392.9 31.1 %all-to-all-done.9.piece_ref = bf16[8,56,896]{2,1,0:T(8,128)(2,1)} async-done(((bf16[8,56,896]{2,1,0:T(8,128)(2,1)}), bf16[8,56,896]{2,1,0:T(8,128)(2,1)}, u32[]{:S(2)}, u32[]{:S(2)}) %all-to-all-start.9) | async-done | bytes 802848 | tf_op jit(solution)/shard_map/all_to_all | solution.py:33
  433.2 7.6 %shard_map.199 = (f32[8,96,1536]{2,1,0:T(8,128)}, f32[8,48,1536]{2,1,0:T(8,128)}) custom-call(s32[2]{0:T(128)} %pad_add_fusion.1.place_ref, bf16[8,72,384]{2,1,0:T(8,128)(2,1)} %add_convert_fusion.2.refs_0_, bf16[8,72,384]{2,1,0:T(8,128)(2,1)} %copy-done.19, bf16[8,72,384]{2,1,0:T(8,128)(2,1)} %collective-permute-done.12.refs_3_.refs_2_, ...), custom_call_target="tpu_custom_call" | custom-call | tf_op jit(solution)/shard_map/pallas_call | solution.py:572
  (228 shorter events, 136.0 us)
Async XLA Ops:
  7.2 97.9 %all-gather.4.cloned.1.call-start = ((), (), s32[]{:S(2)}) async-start(), calls=%async_computation.12 | async-start | bytes 11698176 | tf_op jit(solution)/shard_map/all_gather | solution.py:693
  12.3 28.7 %all-to-all-start = ((bf16[8,160,384]{2,1,0:T(8,128)(2,1)}), bf16[8,160,384]{2,1,0:T(8,128)(2,1)}, u32[]{:S(2)}, u32[]{:S(2)}) async-start(bf16[8,160,384]{2,1,0:T(8,128)(2,1)} %pad_maximum_fusion), calls=%async_computation | async-start | bytes 1966080 | tf_op jit(solution)/shard_map/all_to_all | solution.py:33
  42.8 25.4 %collective-permute-start.3 = (bf16[8,160,384]{2,1,0:T(8,128)(2,1)}, bf16[8,160,384]{2,1,0:T(8,128)(2,1)}, u32[]{:S(2)}, u32[]{:S(2)}) collective-permute-start(bf16[8,160,384]{2,1,0:T(8,128)(2,1)} %all-to-all-done.refs_3_), channel_id=1, source_target_pairs={{0,16},{16,0},{32,48},{48,32},{1,17},{17,1},{33,49},{49,33},{2,18}... | collective-permute-start | bytes 2949128 | tf_op jit(solution)/shard_map/ppermute | solution.py:537
  45.2 42.9 %collective-permute-start.5 = (bf16[8,160,384]{2,1,0:T(8,128)(2,1)}, bf16[8,160,384]{2,1,0:T(8,128)(2,1)}, u32[]{:S(2)}, u32[]{:S(2)}) collective-permute-start(bf16[8,160,384]{2,1,0:T(8,128)(2,1)} %all-to-all-done.refs_3_), channel_id=1, source_target_pairs={{0,32},{16,48},{32,0},{48,16},{1,33},{17,49},{33,1},{49,17},{2,34}... | collective-permute-start | bytes 2949128 | tf_op jit(solution)/shard_map/ppermute | solution.py:537
  49.5 41.1 %collective-permute-start.7 = (bf16[8,160,384]{2,1,0:T(8,128)(2,1)}, bf16[8,160,384]{2,1,0:T(8,128)(2,1)}, u32[]{:S(2)}, u32[]{:S(2)}) collective-permute-start(bf16[8,160,384]{2,1,0:T(8,128)(2,1)} %all-to-all-done.refs_3_), channel_id=1, source_target_pairs={{0,48},{16,32},{32,16},{48,0},{1,49},{17,33},{33,17},{49,1},{2,50}... | collective-permute-start | bytes 2949128 | tf_op jit(solution)/shard_map/ppermute | solution.py:537
  51.5 46.7 %all-to-all-start.1 = ((bf16[8,80,1536]{2,1,0:T(8,128)(2,1)}), bf16[8,80,1536]{2,1,0:T(8,128)(2,1)S(1)}, u32[]{:S(2)}, u32[]{:S(2)}) async-start(bf16[8,80,1536]{2,1,0:T(8,128)(2,1)} %bitcast.81), calls=%async_computation.1 | async-start | bytes 3932160 | tf_op jit(solution)/shard_map/all_to_all | solution.py:33
  55.2 194.2 %all-gather.6.cloned.1.call-start = ((), (), s32[]{:S(2)}) async-start(), calls=%async_computation.13 | async-start | bytes 6684672 | tf_op jit(solution)/shard_map/all_gather | solution.py:744
  55.7 73.2 %collective-permute-start.2 = (bf16[8,160,384]{2,1,0:T(8,128)(2,1)}, bf16[8,160,384]{2,1,0:T(8,128)(2,1)}, u32[]{:S(2)}, u32[]{:S(2)}) collective-permute-start(bf16[8,160,384]{2,1,0:T(8,128)(2,1)} %all-to-all-done.refs_3_), channel_id=1, source_target_pairs={{0,1},{1,0},{2,3},{3,2},{4,5},{5,4},{6,7},{7,6},{8,9},{9,8},{10,11... | collective-permute-start | bytes 2949128 | tf_op jit(solution)/shard_map/ppermute | solution.py:714
  68.2 60.7 %collective-permute-start.4 = (bf16[8,160,384]{2,1,0:T(8,128)(2,1)}, bf16[8,160,384]{2,1,0:T(8,128)(2,1)}, u32[]{:S(2)}, u32[]{:S(2)}) collective-permute-start(bf16[8,160,384]{2,1,0:T(8,128)(2,1)} %collective-permute-done.3.refs_4_), channel_id=1, source_target_pairs={{0,1},{1,0},{2,3},{3,2},{4,5},{5,4},{6,7},{7,6},{8,9},{9,8},{10,11... | collective-permute-start | bytes 2949128 | tf_op jit(solution)/shard_map/ppermute | solution.py:714
  88.1 40.8 %collective-permute-start.6 = (bf16[8,160,384]{2,1,0:T(8,128)(2,1)}, bf16[8,160,384]{2,1,0:T(8,128)(2,1)}, u32[]{:S(2)}, u32[]{:S(2)}) collective-permute-start(bf16[8,160,384]{2,1,0:T(8,128)(2,1)} %collective-permute-done.5.refs_5_), channel_id=1, source_target_pairs={{0,1},{1,0},{2,3},{3,2},{4,5},{5,4},{6,7},{7,6},{8,9},{9,8},{10,11... | collective-permute-start | bytes 2949128 | tf_op jit(solution)/shard_map/ppermute | solution.py:714
  90.6 38.2 %collective-permute-start.8 = (bf16[8,160,384]{2,1,0:T(8,128)(2,1)}, bf16[8,160,384]{2,1,0:T(8,128)(2,1)}, u32[]{:S(2)}, u32[]{:S(2)}) collective-permute-start(bf16[8,160,384]{2,1,0:T(8,128)(2,1)} %collective-permute-done.7.refs_6_), channel_id=1, source_target_pairs={{0,1},{1,0},{2,3},{3,2},{4,5},{5,4},{6,7},{7,6},{8,9},{9,8},{10,11... | collective-permute-start | bytes 2949128 | tf_op jit(solution)/shard_map/ppermute | solution.py:714
  162.8 23.3 %all-to-all-start.3 = ((bf16[16,96,128]{2,1,0:T(8,128)(2,1)}), bf16[16,96,128]{2,1,0:T(8,128)(2,1)}, u32[]{:S(2)}, u32[]{:S(2)}) async-start(bf16[16,96,128]{2,1,0:T(8,128)(2,1)} %bitcast.20), calls=%async_computation.3 | async-start | bytes 786432 | tf_op jit(solution)/shard_map/all_to_all | solution.py:33
  167.0 132.5 %reduce-scatter.2.cloned.1.call-start = ((), (), s32[]{:S(2)}) async-start(), calls=%async_computation.14 | async-start | bytes 4423680 | tf_op jit(solution)/shard_map/reduce_scatter | solution.py:764
  218.0 143.6 %all-gather.8.cloned.1.call-start = ((), (), s32[]{:S(2)}) async-start(), calls=%async_computation.15 | async-start | bytes 6684672 | tf_op jit(solution)/shard_map/all_gather | solution.py:769
  299.5 25.6 %all-to-all-start.7 = ((bf16[16,72,384]{2,1,0:T(8,128)(2,1)}), bf16[16,72,384]{2,1,0:T(8,128)(2,1)}, u32[]{:S(2)}, u32[]{:S(2)}) async-start(bf16[16,72,384]{2,1,0:T(8,128)(2,1)} %bitcast.82), calls=%async_computation.8 | async-start | bytes 1769472 | tf_op jit(solution)/shard_map/all_to_all | solution.py:33
  325.1 25.3 %all-to-all-start.6 = ((bf16[16,128,128]{2,1,0:T(8,128)(2,1)}), bf16[16,128,128]{2,1,0:T(8,128)(2,1)}, u32[]{:S(2)}, u32[]{:S(2)}) async-start(bf16[16,128,128]{2,1,0:T(8,128)(2,1)} %shard_map.194.refs_0_), calls=%async_computation.6 | async-start | bytes 1048576 | tf_op jit(solution)/shard_map/all_to_all | solution.py:33
  335.0 30.7 %collective-permute-start.11 = (bf16[8,72,384]{2,1,0:T(8,128)(2,1)}, bf16[8,72,384]{2,1,0:T(8,128)(2,1)S(1)}, u32[]{:S(2)}, u32[]{:S(2)}) collective-permute-start(bf16[8,72,384]{2,1,0:T(8,128)(2,1)} %add_convert_fusion.2.refs_0_), channel_id=1, source_target_pairs={{0,64},{16,80},{32,96},{48,112},{64,0},{80,16},{96,32},{112,48},{1... | collective-permute-start | bytes 1327112 | tf_op jit(solution)/shard_map/ppermute | solution.py:549
  337.8 28.6 %collective-permute-start.12 = (bf16[8,72,384]{2,1,0:T(8,128)(2,1)}, bf16[8,72,384]{2,1,0:T(8,128)(2,1)}, u32[]{:S(2)}, u32[]{:S(2)}) collective-permute-start(bf16[8,72,384]{2,1,0:T(8,128)(2,1)} %add_convert_fusion.2.refs_0_), channel_id=1, source_target_pairs={{0,16},{16,0},{32,48},{48,32},{64,80},{80,64},{96,112},{112,96},{1... | collective-permute-start | bytes 1327112 | tf_op jit(solution)/shard_map/ppermute | solution.py:549
  340.0 26.5 %collective-permute-start.13 = (bf16[8,72,384]{2,1,0:T(8,128)(2,1)}, bf16[8,72,384]{2,1,0:T(8,128)(2,1)}, u32[]{:S(2)}, u32[]{:S(2)}) collective-permute-start(bf16[8,72,384]{2,1,0:T(8,128)(2,1)} %add_convert_fusion.2.refs_0_), channel_id=1, source_target_pairs={{0,80},{16,64},{32,112},{48,96},{64,16},{80,0},{96,48},{112,32},{1... | collective-permute-start | bytes 1327112 | tf_op jit(solution)/shard_map/ppermute | solution.py:549
  375.2 48.7 %all-to-all-start.9 = ((bf16[8,56,896]{2,1,0:T(8,128)(2,1)}), bf16[8,56,896]{2,1,0:T(8,128)(2,1)}, u32[]{:S(2)}, u32[]{:S(2)}) async-start(bf16[8,56,896]{2,1,0:T(8,128)(2,1)} %shard_map.196), calls=%async_computation.10 | async-start | bytes 1605632 | tf_op jit(solution)/shard_map/all_to_all | solution.py:33
  383.7 49.5 %collective-permute-start.14 = (bf16[8,72,384]{2,1,0:T(8,128)(2,1)}, bf16[8,72,384]{2,1,0:T(8,128)(2,1)}, u32[]{:S(2)}, u32[]{:S(2)}) collective-permute-start(bf16[8,72,384]{2,1,0:T(8,128)(2,1)} %add_convert_fusion.2.refs_0_), channel_id=1, source_target_pairs={{0,32},{16,48},{32,0},{48,16},{64,96},{80,112},{96,64},{112,80},{1... | collective-permute-start | bytes 1327112 | tf_op jit(solution)/shard_map/ppermute | solution.py:549
  387.2 46.0 %collective-permute-start.15 = (bf16[8,72,384]{2,1,0:T(8,128)(2,1)}, bf16[8,72,384]{2,1,0:T(8,128)(2,1)}, u32[]{:S(2)}, u32[]{:S(2)}) collective-permute-start(bf16[8,72,384]{2,1,0:T(8,128)(2,1)} %add_convert_fusion.2.refs_0_), channel_id=1, source_target_pairs={{0,96},{16,112},{32,64},{48,80},{64,32},{80,48},{96,0},{112,16},{1... | collective-permute-start | bytes 1327112 | tf_op jit(solution)/shard_map/ppermute | solution.py:549
  390.2 43.0 %collective-permute-start.16 = (bf16[8,72,384]{2,1,0:T(8,128)(2,1)}, bf16[8,72,384]{2,1,0:T(8,128)(2,1)}, u32[]{:S(2)}, u32[]{:S(2)}) collective-permute-start(bf16[8,72,384]{2,1,0:T(8,128)(2,1)} %add_convert_fusion.2.refs_0_), channel_id=1, source_target_pairs={{0,48},{16,32},{32,16},{48,0},{64,112},{80,96},{96,80},{112,64},{1... | collective-permute-start | bytes 1327112 | tf_op jit(solution)/shard_map/ppermute | solution.py:549
  392.9 40.3 %collective-permute-start.17 = (bf16[8,72,384]{2,1,0:T(8,128)(2,1)}, bf16[8,72,384]{2,1,0:T(8,128)(2,1)}, u32[]{:S(2)}, u32[]{:S(2)}) collective-permute-start(bf16[8,72,384]{2,1,0:T(8,128)(2,1)} %add_convert_fusion.2.refs_0_), channel_id=1, source_target_pairs={{0,112},{16,96},{32,80},{48,64},{64,48},{80,32},{96,16},{112,0},{1... | collective-permute-start | bytes 1327112 | tf_op jit(solution)/shard_map/ppermute | solution.py:549
  (64 other events, 604.4 us)
Sparse Core Ops, SparseCore 0:
  10.3 94.7 all-gather.3
  160.5 44.7 all-gather.5
  218.1 44.3 reduce-scatter.1
  264.6 62.7 all-gather.7

commit v5 on v4

--- a/solution.py
+++ b/solution.py
@@ -23,7 +23,7 @@
 bf16 = jnp.bfloat16
 f32 = jnp.float32
 
-VMEM_LIMIT = 40 * 1024 * 1024
+VMEM_LIMIT = 60 * 1024 * 1024
 WHOLE = pl.BlockSpec(memory_space=pltpu.VMEM)
 UNUSED = pl.BlockSpec(memory_space=pl.ANY)
 SCALAR = pl.BlockSpec(memory_space=pltpu.SMEM)
@@ -90,6 +90,28 @@
         copy.start()
         copies.append(copy)
     return copies
+
+
+def fetch_parts(place_ref, mine_refs, other_refs, to_ref, semaphores):
+    rows = to_ref.shape[2]
+    part = to_ref.shape[3] // len(mine_refs)
+    copies = []
+    for k in range(len(mine_refs)):
+        to = pl.ds(pl.multiple_of((place_ref[1] ^ k) * part, 128), part)
+        owners = ((place_ref[0], mine_refs[k]), (1 - place_ref[0], other_refs[k]))
+        for i, (owner, part_ref) in enumerate(owners):
+            copy = pltpu.make_async_copy(
+                part_ref.at[:, pl.ds(0, rows), :],
+                to_ref.at[:, owner, :, to],
+                semaphores.at[2 * k + i],
+            )
+            copy.start()
+            copies.append(copy)
+    return copies
+
+
+def device_place():
+    return jnp.stack([lax.axis_index("c"), lax.axis_index("z")]).astype(jnp.int32)
 
 
 def shaped(shape, dtype):
@@ -188,14 +210,16 @@
     return both
 
 
-def attend(queries, before, own, first, weights, tokens, gain):
+def attend(queries, before, own, first, mine, other, tokens, gain, earlier):
     rows, width = tokens.shape
+    wide = len(mine)
+    chips = mine[0].shape[0]
 
     def kernel(
-        query_ref, before_ref, own_ref, first_ref, all_ref, token_ref, gain_ref,
-        attended_ref, turned_ref, residual_ref, normed_ref, w_ref, sem,
+        query_ref, before_ref, own_ref, first_ref, token_ref, gain_ref, place_ref, *refs
     ):
-        copies = fetch(all_ref, w_ref, sem, 1, weights.shape[1] - width)
+        turned_ref, residual_ref, normed_ref, attended_ref, w_ref, sem = refs[2 * wide :]
+        copies = fetch_parts(place_ref, refs[:wide], refs[wide : 2 * wide], w_ref, sem)
         allowed = allowed_keys(first_ref, rows)
         for group in range(KEY_VALUE_HEADS):
             keys, values = keys_and_values(before_ref, own_ref, group)
@@ -206,11 +230,12 @@
                 attended_ref[:, at] = mixed.astype(bf16)
                 turned_ref[at, :] = mixed.T.astype(bf16)
         attended = attended_ref[...]
+        for copy in copies:
+            copy.wait()
         for block in range(width // 256):
             at = slice(block * 256, (block + 1) * 256)
-            if block % 2 == 0:
-                copies[block // 2].wait()
-            branch = matmul(attended, w_ref[:, at]).astype(bf16)
+            weights = w_ref[:, :, :, at].reshape(width, 256)
+            branch = matmul(attended, weights).astype(bf16)
             residual_ref[:, at] = token_ref[:, at].astype(f32) + branch.astype(f32)
         residual = residual_ref[...]
         normed_ref[...] = (residual * inverse_rms(residual) * gain_ref[...]).astype(bf16)
@@ -218,15 +243,19 @@
     return call(
         kernel,
         [
-            shaped((rows, width), bf16),
             shaped((width, rows), bf16),
             shaped((rows, width), f32),
             shaped((rows, width), bf16),
         ],
-        (queries, before, own, first, weights, tokens, gain),
-        specs=[WHOLE, WHOLE, WHOLE, WHOLE, UNUSED, WHOLE, WHOLE],
+        (queries, before, own, first, tokens, gain, device_place(), *mine, *other),
+        earlier,
+        specs=[*([WHOLE] * 6), SCALAR, *([UNUSED] * (2 * wide))],
         flops=2 * rows * width * width + 8 * rows * rows * width,
-        scratch=[pltpu.VMEM((width, width), bf16), pltpu.SemaphoreType.DMA((width // 512,))],
+        scratch=[
+            pltpu.VMEM((rows, width), bf16),
+            pltpu.VMEM((chips, 2, width // (2 * chips), width), bf16),
+            pltpu.SemaphoreType.DMA((2 * wide,)),
+        ],
     )
 
 
@@ -247,36 +276,31 @@
     )[0]
 
 
-def run_experts(picked, grad_out, mine, other, rows_up, rows_down):
+def run_experts(picked, grad_out, parts, rows_up, rows_down):
     slots, width = picked.shape
-    wide = len(mine)
-    chips, _, part = mine[0].shape
+    ways, chips, _, part = parts.shape
     ff = chips * 2 * rows_down
-    place = jnp.stack([lax.axis_index("c"), lax.axis_index("z")]).astype(jnp.int32)
-
-    def kernel(picked_ref, grad_ref, place_ref, *refs):
-        mine_refs, other_refs = refs[:wide], refs[wide : 2 * wide]
-        acted_ref, pre_ref, back_ref, down_w = refs[2 * wide : 2 * wide + 4]
-        up_w, gate_ref, upper_ref, up_sem, down_sem = refs[2 * wide + 4 :]
-        core = place_ref[0]
+    each = slots // chips
+
+    def kernel(
+        picked_ref, grad_ref, part_ref, acted_ref, pre_ref, back_ref,
+        up_w, down_w, gate_ref, upper_ref, up_sem, down_sem,
+    ):
         ups, downs = [], []
-        for k in range(wide):
-            to = pl.ds(pl.multiple_of((place_ref[1] ^ k) * part, 128), part)
-            for i, (owner, part_ref) in enumerate(((core, mine_refs[k]), (1 - core, other_refs[k]))):
-                ups.append(
-                    pltpu.make_async_copy(
-                        part_ref.at[:, pl.ds(0, rows_up), :],
-                        up_w.at[:, owner, :, to],
-                        up_sem.at[2 * k + i],
-                    )
+        for i in range(ways):
+            to = pl.ds(i // 2 * part, part)
+            ups.append(
+                pltpu.make_async_copy(
+                    part_ref.at[i, :, pl.ds(0, rows_up), :], up_w.at[:, i % 2, :, to], up_sem.at[i]
                 )
-                downs.append(
-                    pltpu.make_async_copy(
-                        part_ref.at[:, pl.ds(rows_up, rows_down), :],
-                        down_w.at[:, owner, :, to],
-                        down_sem.at[2 * k + i],
-                    )
+            )
+            downs.append(
+                pltpu.make_async_copy(
+                    part_ref.at[i, :, pl.ds(rows_up, rows_down), :],
+                    down_w.at[:, i % 2, :, to],
+                    down_sem.at[i],
                 )
+            )
         for copy in ups + downs:
             copy.start()
         for copy in ups:
@@ -309,42 +333,43 @@
 
         @pl.loop(0, 2)
         def _(j):
+            to = pl.ds(pl.multiple_of(j * (width // 2), 128), width // 2)
             weights = up_w[pl.ds(j * half, half)].reshape(width // 2, 2 * ff)
-            to = pl.ds(pl.multiple_of(j * (width // 2), 128), width // 2)
-            back_ref[:, to] = times_transposed(pre_ref[...], weights).astype(bf16)
+            back = times_transposed(pre_ref[...], weights).astype(bf16)
+            back_ref[:, 0, :, to] = back.reshape(chips, each, width // 2)
+            weights = down_w[:, :, :, to].reshape(ff, width // 2)
+            forward = matmul(acted_ref[...], weights).astype(bf16)
+            back_ref[:, 1, :, to] = forward.reshape(chips, each, width // 2)
 
     return call(
         kernel,
         [
             shaped((slots, ff), bf16),
             shaped((slots, 2 * ff), bf16),
-            shaped((slots, width), bf16),
-            shaped((chips, 2, rows_down, width), bf16),
-        ],
-        (picked, grad_out, place, *mine, *other),
-        specs=[WHOLE, WHOLE, SCALAR, *([UNUSED] * (2 * wide))],
-        flops=2 * slots * 5 * width * ff,
+            shaped((chips, 2, each, width), bf16),
+        ],
+        (picked, grad_out, parts),
+        specs=[WHOLE, WHOLE, UNUSED],
+        flops=2 * slots * 6 * width * ff,
         scratch=[
             pltpu.VMEM((chips, 2, rows_up, width), bf16),
+            pltpu.VMEM((chips, 2, rows_down, width), bf16),
             pltpu.VMEM((slots, ff), f32),
             pltpu.VMEM((slots, ff), f32),
-            pltpu.SemaphoreType.DMA((2 * wide,)),
-            pltpu.SemaphoreType.DMA((2 * wide,)),
-        ],
-    )
-
-
-def expert_weight_grads(picked, grad_pre, acted, grad_out, down, rows_up, chips, wide, earlier):
+            pltpu.SemaphoreType.DMA((ways,)),
+            pltpu.SemaphoreType.DMA((ways,)),
+        ],
+    )
+
+
+def expert_weight_grads(picked, grad_pre, acted, grad_out, rows_up, rows_down, chips, wide, earlier):
     slots, width = picked.shape
-    rows_down = down.shape[0] // (2 * chips)
     half, part = (rows_up + rows_down) // 2, width // wide
     steps = 2
     near = chips // steps
-    core = lax.axis_index("c").astype(jnp.int32).reshape(1)
-
-    def kernel(core_ref, picked_ref, pre_ref, acted_ref, grad_ref, all_ref, down_ref, *refs):
-        here_ref, there_ref, expert_ref, keep_ref = refs[-4:]
-        expert_ref[...] = matmul(all_ref[...], down_ref[...]).astype(bf16)
+
+    def kernel(picked_ref, pre_ref, acted_ref, grad_ref, *refs):
+        out_ref, keep_ref = refs[-2:]
         columns = width // 2
         for n in range(2):
             at = slice(n * columns, (n + 1) * columns)
@@ -352,62 +377,54 @@
                 block = slice(m * 4 * rows_up, (m + 1) * 4 * rows_up)
                 up = transposed_times(picked_ref[:, block], pre_ref[:, at])
                 for i in range(4):
+                    rows = up[i * rows_up : (i + 1) * rows_up]
                     k, c = 2 * m + i // 2, i % 2
-                    keep_ref[k, c] = up[i * rows_up : (i + 1) * rows_up]
+                    keep_ref[k, c] = rows[half:]
+                    low = rows[:half].astype(bf16)
+                    for j in range(columns // part):
+                        z = n * (columns // part) + j
+                        out_ref[z, c, 0, k] = low[:, j * part : (j + 1) * part]
             down = transposed_times(acted_ref[...], grad_ref[:, at])
             for k in range(near):
                 for c in range(2):
                     base = (2 * k + c) * rows_down
-                    up = keep_ref[k, c]
-                    first = up[:half].astype(bf16)
-                    rest = jnp.concatenate([up[half:], down[base : base + rows_down]], axis=0)
+                    rest = jnp.concatenate([keep_ref[k, c], down[base : base + rows_down]], axis=0)
                     rest = rest.astype(bf16)
-                    for mine, out_ref in ((True, here_ref), (False, there_ref)):
-
-                        @pl.when((core_ref[0] == c) == mine)
-                        def _():
-                            for i in range(columns // part):
-                                cut = slice(i * part, (i + 1) * part)
-                                z = n * (columns // part) + i
-                                out_ref[z, 0, k] = first[:, cut]
-                                out_ref[z, 1, k] = rest[:, cut]
-
-    pieces = pl.BlockSpec((wide, 2, near, half, part), lambda s: (0, 0, s, 0, 0))
+                    for j in range(columns // part):
+                        z = n * (columns // part) + j
+                        out_ref[z, c, 1, k] = rest[:, j * part : (j + 1) * part]
+
     return pl.pallas_call(
         kernel,
         grid=(steps,),
         in_specs=[
-            SCALAR,
             pl.BlockSpec((slots, width // steps), lambda s: (0, s)),
             pl.BlockSpec(grad_pre.shape, lambda s: (0, 0)),
             pl.BlockSpec((slots, acted.shape[1] // steps), lambda s: (0, s)),
             pl.BlockSpec(grad_out.shape, lambda s: (0, 0)),
-            pl.BlockSpec(acted.shape, lambda s: (0, 0)),
-            pl.BlockSpec((down.shape[0], width // steps), lambda s: (0, s)),
             *([UNUSED] * len(earlier)),
         ],
-        out_specs=[pieces, pieces, pl.BlockSpec((slots, width // steps), lambda s: (0, s))],
-        out_shape=[
-            *([shaped((wide, 2, chips, half, part), bf16)] * 2),
-            shaped((slots, width), bf16),
-        ],
-        scratch_shapes=[pltpu.VMEM((near, 2, rows_up, width // 2), f32)],
+        out_specs=pl.BlockSpec((wide, 2, 2, near, half, part), lambda s: (0, 0, 0, s, 0, 0)),
+        out_shape=shaped((wide, 2, 2, chips, half, part), bf16),
+        scratch_shapes=[pltpu.VMEM((near, 2, rows_up - half, width // 2), f32)],
         compiler_params=pltpu.CompilerParams(vmem_limit_bytes=VMEM_LIMIT),
         cost_estimate=pl.CostEstimate(
-            flops=2 * slots * 4 * width * acted.shape[1],
+            flops=2 * slots * 3 * width * acted.shape[1],
             bytes_accessed=4 * 4 * slots * width,
             transcendentals=0,
         ),
-    )(core, picked, grad_pre, acted, grad_out, acted, down, *earlier)
-
-
-def residual_grad(pick, grad_picked, residual, gain, cotangent, earlier):
+    )(picked, grad_pre, acted, grad_out, *earlier)
+
+
+def residual_grad(pick, returned, residual, gain, cotangent, earlier):
     rows, width = residual.shape
+    slots = pick.shape[0]
 
     def kernel(pick_ref, back_ref, residual_ref, gain_ref, cot_ref, grad_ref, branch_ref, gain_grad_ref):
         for block in range(width // 512):
             at = slice(block * 512, (block + 1) * 512)
-            grad_ref[:, at] = transposed_times(pick_ref[...], back_ref[:, at])
+            back = back_ref[:, 0, :, at].reshape(slots, 512)
+            grad_ref[:, at] = transposed_times(pick_ref[...], back)
         grad, grad_gain = norm_back(residual_ref[...], gain_ref[...], grad_ref[...])
         grad = grad + cot_ref[...].astype(f32)
         grad_ref[...] = grad
@@ -417,26 +434,53 @@
     return call(
         kernel,
         [shaped((rows, width), f32), shaped((rows, width), bf16), shaped((1, width), f32)],
-        (pick, grad_picked, residual, gain, cotangent),
+        (pick, returned, residual, gain, cotangent),
         earlier,
-        flops=2 * grad_picked.size * rows,
-    )
-
-
-def attend_back(grad_branch, weights, queries, before, own, first, cosine, sine):
+        flops=2 * slots * width * rows,
+    )
+
+
+def add_expert_rows(pick, weight, returned, residual, earlier):
+    rows, width = residual.shape
+    slots = pick.shape[0]
+
+    def kernel(pick_ref, weight_ref, back_ref, residual_ref, out_ref):
+        back = jnp.where(pick_ref[...] > 0, weight_ref[...], 0.0)
+        high = back.astype(bf16)
+        low = (back - high.astype(f32)).astype(bf16)
+        for block in range(width // 512):
+            at = slice(block * 512, (block + 1) * 512)
+            expert = back_ref[:, 1, :, at].reshape(slots, 512)
+            mixture = transposed_times(high, expert) + transposed_times(low, expert)
+            out_ref[:, at] = (residual_ref[:, at] + mixture).astype(bf16)
+
+    return call(
+        kernel,
+        [shaped((rows, width), bf16)],
+        (pick, weight, returned, residual),
+        earlier,
+        flops=4 * slots * width * rows,
+    )[0]
+
+
+def attend_back(grad_branch, mine, other, queries, before, own, first, cosine, sine):
     rows, width = grad_branch.shape
     kv_width = KEY_VALUE_HEADS * HEAD_SIZE
+    wide = len(mine)
+    chips = mine[0].shape[0]
 
     def kernel(
-        grad_ref, all_ref, query_ref, before_ref, own_ref, first_ref, cos_ref, sin_ref,
-        out_ref, prev_ref, self_ref, attended_ref, w_ref, sem,
+        grad_ref, query_ref, before_ref, own_ref, first_ref, cos_ref, sin_ref, place_ref, *refs
     ):
-        copies = fetch(all_ref, w_ref, sem, 0, weights.shape[1] - width)
-        for block in range(width // 256):
-            if block % 2 == 0:
-                copies[block // 2].wait()
-            at = slice(block * 256, (block + 1) * 256)
-            attended_ref[:, at] = times_transposed(grad_ref[...], w_ref[at, :]).astype(bf16)
+        out_ref, prev_ref, self_ref, attended_ref, w_ref, sem = refs[2 * wide :]
+        copies = fetch_parts(place_ref, refs[:wide], refs[wide : 2 * wide], w_ref, sem)
+        for copy in copies:
+            copy.wait()
+        for half in range(2):
+            at = slice(half * (width // 2), (half + 1) * (width // 2))
+            weights = w_ref[half * (chips // 2) : (half + 1) * (chips // 2)]
+            weights = weights.reshape(width // 2, width)
+            attended_ref[:, at] = times_transposed(grad_ref[...], weights).astype(bf16)
         allowed = allowed_keys(first_ref, rows)
         cos, sin = cos_ref[...], sin_ref[...]
         for group in range(KEY_VALUE_HEADS):
@@ -471,13 +515,13 @@
             shaped((rows, 2 * kv_width), bf16),
             shaped((rows, 2 * kv_width), f32),
         ],
-        (grad_branch, weights, queries, before, own, first, cosine, sine),
-        specs=[WHOLE, UNUSED, *([WHOLE] * 6)],
+        (grad_branch, queries, before, own, first, cosine, sine, device_place(), *mine, *other),
+        specs=[*([WHOLE] * 7), SCALAR, *([UNUSED] * (2 * wide))],
         flops=2 * rows * width * width + 20 * rows * rows * width,
         scratch=[
             pltpu.VMEM((rows, width), bf16),
-            pltpu.VMEM((width, width), bf16),
-            pltpu.SemaphoreType.DMA((width // 512,)),
+            pltpu.VMEM((chips, 2, width // (2 * chips), width), bf16),
+            pltpu.SemaphoreType.DMA((2 * wide,)),
         ],
     )
 
@@ -690,29 +734,30 @@
     kv_width = KEY_VALUE_HEADS * HEAD_SIZE
     owned = width // shards
 
-    attn_full = lax.all_gather(
-        jnp.concatenate([w_query, key_value_weight, w_out], 1), SHARD, axis=0, tiled=True
+    qkv_full = lax.all_gather(
+        jnp.concatenate([w_query, key_value_weight], 1), SHARD, axis=0, tiled=True
     )
     part = width // wide_z
-    rows_up, rows_down = w_gateup.shape[1], w_down.shape[1]
+    rows_out, rows_up, rows_down = w_out.shape[0], w_gateup.shape[1], w_down.shape[1]
     column = lax.axis_index("z") * part
     gains_own = jnp.pad(jnp.stack([attn_gain, ffn_gain]), ((0, 14), (0, part - owned)))
-    parts = jnp.concatenate(
+    out_part = jnp.concatenate(
+        [lax.dynamic_slice_in_dim(w_out, column, part, 1), gains_own], axis=0
+    )
+    out_part = spread(out_part, experts, CHIPS)
+    expert_part = jnp.concatenate(
         [
             lax.dynamic_slice_in_dim(w_gateup, column, part, 2),
             lax.dynamic_slice_in_dim(w_down, column, part, 2),
-            jnp.broadcast_to(gains_own[None], (experts, *gains_own.shape)),
         ],
         axis=1,
     )
-    parts = exchange(parts, CHIPS)
-    gains_mine = parts[:, rows_up + rows_down : rows_up + rows_down + 2, :owned]
+    gains_mine = out_part[:, rows_out : rows_out + 2, :owned]
     gains = in_core_order(core, gains_mine, lax.ppermute(gains_mine, "c", SWAP))
     gains = gains.transpose(2, 0, 1, 3).reshape(2, width).astype(f32)
     gain_attn, gain_ffn = gains[:1], gains[1:]
-    expert_mine = gather_over_z(parts)
-    expert_other = [lax.ppermute(one, "c", SWAP) for one in expert_mine]
-
+    out_mine = gather_over_z(out_part)
+    out_other = [lax.ppermute(one, "c", SWAP) for one in out_mine]
     chosen = routes[:, :, None] == jnp.arange(experts, dtype=jnp.int32)
     member = jnp.any(chosen, axis=1)
     weight = jnp.sum(jnp.where(chosen, gate_weights[:, :, None], 0.0), axis=1)
@@ -722,7 +767,10 @@
     pick = picks.astype(bf16).reshape(experts * CAP, rows)
     slot_weight = jnp.sum(jnp.where(picks, weight.T[:, None, :], 0.0), axis=2)
     grad_out = matmul(pick, cotangent) * slot_weight.reshape(-1, 1)
-    grad_out = exchange(after(grad_out, parts).astype(bf16), CHIPS)
+    grad_out = exchange(after(grad_out, out_part).astype(bf16), CHIPS)
+
+    expert_part = exchange(after(expert_part, grad_out, *out_mine[1:]), CHIPS)
+    expert_parts = lax.all_gather(expert_part, ("z", "c"), axis=0)
 
     lengths = seq_lengths[0]
     starts = jnp.cumsum(lengths) - lengths
@@ -731,58 +779,56 @@
     cosine, sine = rotary_tables(row_at - first_at)
     first = (first_at - shard * rows).astype(jnp.int32)[:, None]
     normed, queries, keyval = project_qkv(
-        tokens, gain_attn, attn_full, cosine, sine, (grad_out,)
+        tokens, gain_attn, qkv_full, cosine, sine, ()
     )
     ring = [(i, (i + 1) % shards) for i in range(shards)]
     back_ring = [((i + 1) % shards, i) for i in range(shards)]
     before = lax.ppermute(keyval, SHARD, ring)
-    attended, attended_turned, residual, normed_ffn = attend(
-        queries, before, keyval, first, attn_full, tokens, gain_ffn
-    )
-
-    picked = exchange(pick_rows(pick, normed_ffn, tuple(expert_other)), CHIPS)
+    attended_turned, residual, normed_ffn = attend(
+        queries, before, keyval, first, out_mine, out_other, tokens, gain_ffn, (grad_out,)
+    )
+
+    picked = exchange(pick_rows(pick, normed_ffn, ()), CHIPS)
     normed_all = lax.all_gather(after(normed, picked), SHARD, axis=0, tiled=True)
     attended_cols = exchange(after(attended_turned, picked), SHARD)
     attended_cols = attended_cols.reshape(shards, owned, rows)
-    acted, grad_pre, grad_picked, down = run_experts(
-        picked, grad_out, expert_mine, expert_other, rows_up, rows_down
-    )
-    grad_picked_back = exchange(grad_picked, CHIPS)
-    here, there, expert_out = expert_weight_grads(
+    acted, grad_pre, returned = run_experts(
+        picked, grad_out, expert_parts, rows_up, rows_down
+    )
+    pieces = expert_weight_grads(
         picked,
         grad_pre,
         acted,
         grad_out,
-        down.reshape(-1, width),
         rows_up,
+        rows_down,
         experts,
         wide_z,
-        (grad_picked, attended_cols),
-    )
-    other = lax.ppermute(there, "c", SWAP)
-    pieces = (here.astype(f32) + other.astype(f32)).astype(bf16)
-    over_z = lax.psum_scatter(pieces, "z", scatter_dimension=0, tiled=False)
+        (returned, attended_cols),
+    )
+    returned = exchange(returned, CHIPS)
+    pieces = pieces.reshape(2 * wide_z, *pieces.shape[2:])
+    over_z = lax.psum_scatter(pieces, ("z", "c"), scatter_dimension=0, tiled=False)
 
     grad_residual, grad_branch, grad_gain_ffn = residual_grad(
-        pick, grad_picked_back, residual, gain_ffn, cotangent, (here, normed_all)
+        pick, returned, residual, gain_ffn, cotangent, (normed_all,)
     )
     grad_branch_all = lax.all_gather(grad_branch, SHARD, axis=0, tiled=True)
     grad_queries, grad_before, grad_own = attend_back(
-        grad_branch, attn_full, queries, before, keyval, first, cosine, sine
+        grad_branch, out_mine, out_other, queries, before, keyval, first, cosine, sine
     )
     from_next = lax.ppermute(grad_before, SHARD, back_ring)
-    expert_out = exchange(expert_out, CHIPS)
-    grad_blocks = qkv_blocks_of(
-        grad_queries, grad_own, from_next, cosine, sine, (expert_out,)
-    )
-    grad_tokens, grad_gain_attn = input_grad(
-        grad_blocks, attn_full, tokens, gain_attn, grad_residual
-    )
-
-    grad_cols = exchange(grad_blocks, SHARD)
     over_z = over_z.reshape(2 * experts, *over_z.shape[2:])
     over_rep = exchange(over_z, ("h", *CHIPS)).reshape(2, experts, *over_z.shape[1:])
     over_rep = (over_rep[0].astype(f32) + over_rep[1].astype(f32)).astype(bf16)
+    grad_blocks = qkv_blocks_of(
+        grad_queries, grad_own, from_next, cosine, sine, (over_rep,)
+    )
+    grad_tokens, grad_gain_attn = input_grad(
+        grad_blocks, qkv_full, tokens, gain_attn, grad_residual
+    )
+
+    grad_cols = exchange(grad_blocks, SHARD)
     moved = gather_over_rep(over_rep)
     shard_gateup, shard_down = expert_outputs(moved, rows_up, rows_down)
     qkv_block = transposed_times(normed_all, grad_cols.reshape(shards * rows, HEAD_SIZE))
@@ -800,17 +846,15 @@
         preferred_element_type=f32,
     ).astype(bf16)
     qkv_blocks = exchange(after(qkv_block, over_rep), SHARD)
-    attn_pieces = exchange(pack_attention_grads(qkv_blocks, out_rows, wide_z, moved[1:4]), REP)
+    attn_pieces = exchange(pack_attention_grads(qkv_blocks, out_rows, wide_z, moved[1:]), REP)
     attn_copies, gain_sums = sum_and_copy(attn_pieces)
     grad_query, grad_keyval, grad_out_w = attention_outputs(
         exchange(attn_copies, REP), (width, 2 * kv_width, width)
     )
 
-    back = pick.astype(f32) * slot_weight.reshape(-1, 1)
-    back_high = back.astype(bf16)
-    back_low = (back - back_high.astype(f32)).astype(bf16)
-    mixture = transposed_times(back_high, expert_out) + transposed_times(back_low, expert_out)
-    output = (residual + mixture).astype(bf16)
+    output = add_expert_rows(
+        pick, slot_weight.reshape(-1, 1), returned, residual, (grad_blocks,)
+    )
     return (
         output,
         grad_tokens,

time: 454 us -> 402 us (0.89)
  local copies, waits for them, and re-layouts: 58.4 us -> 15.8 us
  waiting for transfers between devices: 122 us -> 83.9 us
  Pallas kernels: 60.7 us -> 83.2 us
  blocking collectives: 99.3 us -> 115 us
  starting transfers between devices: 65 us -> 57.5 us
    unnamed x116 -> x56, local copies, waits for them, and re-layouts: 51.6 us -> 3.02 us
    all_to_all x8 -> x7, waiting for transfers between devices: 63 us -> 27.8 us  [exchange(): return lax.all_to_all(parts, axes, 0, 0, tiled=True)]
    ppermute x7, waiting for transfers between devices: 0.02 us -> 24 us  [gather_over_rep(): lax.ppermute(piece, REP, [(i, i ^ step) for i in range(ways)])]
    pallas_call x9 -> x10, Pallas kernels: 37 us -> 60.9 us  [call(): pl.pallas_call(body, in_specs=[*specs, *[UNUSED] * len(earlier)], out_spe...]
    all_to_all x3 -> x4, blocking collectives: 99.3 us -> 115 us  [exchange(): return lax.all_to_all(parts, axes, 0, 0, tiled=True)]
    ppermute x3, waiting for transfers between devices: 34.9 us -> 23.2 us  [gather_over_z(): lax.ppermute(part, 'z', [(i, i ^ k) for i in range(wide)])]
    all_to_all x8 -> x7, starting transfers between devices: 42.5 us -> 33.3 us  [exchange(): return lax.all_to_all(parts, axes, 0, 0, tiled=True)]
    all_gather x1 -> x2, waiting for transfers between devices: 6.92 us -> 0.02 us  [the longest x1 0.02 us: per_device(): expert_parts = lax.all_gather(expert_part, ('z', 'c'), axis=0)]
  transfers between devices with their start and end apart: 30 -> 29, of which waited for: 13 -> 11; matrix products, arithmetic and copies ran while one was open for 7% -> 9% of each run, Pallas kernels for 13% -> 19%
where the time goes in v5:
time: 402 us; the launch traced here: 400 us
  blocking collectives  115 us (29%)
  waiting for transfers between devices  83.9 us (21%)
  Pallas kernels  83.2 us (21%)
  starting transfers between devices  57.5 us (14%)
  between operations  19.1 us (5%)
  local copies, waits for them, and re-layouts  15.8 us (4%)
  other arithmetic  13.4 us (3%)
  matrix products  11.4 us (3%)
    all_to_all x4, blocking collectives, exchange(): return lax.all_to_all(parts, axes, 0, 0, tiled=True)  115 us
    pallas_call x10, Pallas kernels, call(): pl.pallas_call(body, in_specs=[*specs, *[UNUSED] * len(earlier)], out_spe...  60.9 us
    all_to_all x7, starting transfers between devices, exchange(): return lax.all_to_all(parts, axes, 0, 0, tiled=True)  33.3 us
    all_to_all x7, waiting for transfers between devices, exchange(): return lax.all_to_all(parts, axes, 0, 0, tiled=True)  27.8 us
    ppermute x7, waiting for transfers between devices, gather_over_rep(): lax.ppermute(piece, REP, [(i, i ^ step) for i in range(ways)])  24 us
    ppermute x3, waiting for transfers between devices, gather_over_z(): lax.ppermute(part, 'z', [(i, i ^ k) for i in range(wide)])  23.2 us
    ppermute x7, starting transfers between devices, gather_over_rep(): lax.ppermute(piece, REP, [(i, i ^ step) for i in range(ways)])  13.8 us
    pallas_call x1, Pallas kernels, expert_weight_grads(): pl.pallas_call(kernel, grid=(steps,), in_specs=[pl.BlockSpec((slots, widt...  10.4 us
  transfers between devices with their start and end apart: 29, of which 11 were waited for; matrix products, arithmetic and copies ran while one was open for 9% of the time, Pallas kernels for 19%

profile of v5, /device:TPU:0, one launch (start us, length us, event | category | flops | bytes accessed | tf_op | source)
XLA Modules:
  0.0 399.6 jit_solution(14190703043242178518)
XLA Ops:
  11.7 5.5 %all-to-all-start = ((bf16[8,112,384]{2,1,0:T(8,128)(2,1)}), bf16[8,112,384]{2,1,0:T(8,128)(2,1)S(1)}, u32[]{:S(2)}, u32[]{:S(2)}) async-start(bf16[8,112,384]{2,1,0:T(8,128)(2,1)} %broadcast_in_dim.58), calls=%async_computation | async-start | bytes 1376256 | tf_op jit(solution)/shard_map/all_to_all | solution.py:33
  20.3 13.2 %all-to-all-done.refs_7_.refs_8_ = bf16[8,112,384]{2,1,0:T(8,128)(2,1)S(1)} async-done(((bf16[8,112,384]{2,1,0:T(8,128)(2,1)}), bf16[8,112,384]{2,1,0:T(8,128)(2,1)S(1)}, u32[]{:S(2)}, u32[]{:S(2)}) %all-to-all-start) | async-done | bytes 688160 | tf_op jit(solution)/shard_map/all_to_all | solution.py:33
  41.0 5.2 %collective-permute-start.4 = (bf16[8,112,384]{2,1,0:T(8,128)(2,1)S(1)}, bf16[8,112,384]{2,1,0:T(8,128)(2,1)S(1)}, u32[]{:S(2)}, u32[]{:S(2)}) collective-permute-start(bf16[8,112,384]{2,1,0:T(8,128)(2,1)S(1)} %all-to-all-done.refs_7_.refs_8_), channel_id=1, source_target_pairs={{0,48},{16,32},{32,16},{48,0},{1,49},{17,33},{33,17},{49,1},{2,50}... | collective-permute-start | bytes 2064392 | tf_op jit(solution)/shard_map/ppermute | solution.py:581
  49.0 23.2 %collective-permute-done.4.refs_10_.refs_11_ = bf16[8,112,384]{2,1,0:T(8,128)(2,1)S(1)} collective-permute-done((bf16[8,112,384]{2,1,0:T(8,128)(2,1)S(1)}, bf16[8,112,384]{2,1,0:T(8,128)(2,1)S(1)}, u32[]{:S(2)}, u32[]{:S(2)}) %collective-permute-start.4) | collective-permute-done | bytes 688160 | tf_op jit(solution)/shard_map/ppermute | solution.py:581
  82.8 14.8 %all_to_all.71 = bf16[8,144,384]{2,1,0:T(8,128)(2,1)} all-to-all(bf16[8,144,384]{2,1,0:T(8,128)(2,1)S(1)} %fusion.3), channel_id=1, replica_groups=mesh['h'=2,'z'=4,'y'=4,'x'=2,'c'=2] {'y','x'}, dimensions={0} | all-to-all | bytes 1769472 | tf_op jit(solution)/shard_map/all_to_all | solution.py:33
  103.2 5.3 %shard_map.187 = (bf16[128,1536]{1,0:T(8,128)(2,1)}, bf16[128,1536]{1,0:T(8,128)(2,1)}, bf16[128,512]{1,0:T(8,128)(2,1)}) custom-call(bf16[128,1536]{1,0:T(8,128)(2,1)} %refs_2_.1, f32[1,1536]{1,0:T(1,128)} %slice.53.refs_1_.refs_3_, bf16[1536,2048]{1,0:T(8,128)(2,1)} %all-gather.6.cloned.1.call-done.refs_2_.refs_1_, ...), custom_call_target="tpu_custom_call" | custom-call | flops 805306368 | bytes 7739392 | tf_op jit(solution)/shard_map/pallas_call | solution.py:68
  115.9 5.6 %shard_map.188 = (bf16[1536,128]{1,0:T(8,128)(2,1)}, f32[128,1536]{1,0:T(8,128)}, bf16[128,1536]{1,0:T(8,128)(2,1)}) custom-call(bf16[128,1536]{1,0:T(8,128)(2,1)} %get-tuple-element.33.refs_0_.refs_1_, bf16[128,512]{1,0:T(8,128)(2,1)} %copy-done.19, bf16[128,512]{1,0:T(8,128)(2,1)} %get-tuple-element.34.refs_2_.refs_3_, s32[128,1]{1,0:T(8,128)} %copy.51.refs_3_.refs_4_, ...), custom_call_target="tpu_custom_call" | custom-call | flops 805306368 | bytes 8133128 | tf_op jit(solution)/shard_map/pallas_call | solution.py:68
  124.5 27.1 %all_to_all.72 = bf16[8,80,1536]{2,1,0:T(8,128)(2,1)S(1)} all-to-all(bf16[8,80,1536]{2,1,0:T(8,128)(2,1)} %bitcast.62), channel_id=1, replica_groups=mesh['h'=2,'z'=4,'y'=4,'x'=2,'c'=2] {'y','x'}, dimensions={0} | all-to-all | bytes 3932160 | tf_op jit(solution)/shard_map/all_to_all | solution.py:33
  158.3 18.1 %shard_map.190 = (bf16[640,768]{1,0:T(8,128)(2,1)}, bf16[640,1536]{1,0:T(8,128)(2,1)}, bf16[8,2,80,1536]{3,2,1,0:T(8,128)(2,1)}) custom-call(bf16[640,1536]{1,0:T(8,128)(2,1)} %bitcast.60, bf16[640,1536]{1,0:T(8,128)(2,1)} %bitcast.15.refs_15_.refs_1_.grad_ref, bf16[8,8,144,384]{3,2,1,0:T(8,128)(2,1)} %bitcast.71), custom_call_target="tpu_custom_call" | custom-call | flops 9059696640 | bytes 17891328 | tf_op jit(solution)/shard_map/pallas_call | solution.py:68
  177.2 10.4 %shard_map.193 = bf16[4,2,2,8,72,384]{5,4,3,2,1,0:T(8,128)(2,1)} custom-call(bf16[640,1536]{1,0:T(8,128)(2,1)} %bitcast.61, bf16[640,1536]{1,0:T(8,128)(2,1)} %get-tuple-element.43.pre_ref, bf16[640,768]{1,0:T(8,128)(2,1)} %get-tuple-element.44.acted_ref, bf16[640,1536]{1,0:T(8,128)(2,1)} %bitcast.15.refs_15_.refs_1_.grad_ref, ...), custom_call_target="tpu_custom_call" | custom-call | flops 4529848320 | bytes 15728640 | tf_op jit(solution)/shard_map/pallas_call | solution.py:397
  187.6 52.6 %all_to_all.73.refs_1_.refs_2_ = bf16[8,2,80,1536]{3,2,1,0:T(8,128)(2,1)} all-to-all(bf16[8,2,80,1536]{3,2,1,0:T(8,128)(2,1)} %get-tuple-element.36.refs_0_), channel_id=1, replica_groups=mesh['h'=2,'z'=4,'y'=4,'x'=2,'c'=2] {'y','x'}, dimensions={0} | all-to-all | bytes 7864320 | tf_op jit(solution)/shard_map/all_to_all | solution.py:33
  246.7 6.8 %all-to-all-start.6 = ((bf16[16,72,384]{2,1,0:T(8,128)(2,1)}), bf16[16,72,384]{2,1,0:T(8,128)(2,1)S(1)}, u32[]{:S(2)}, u32[]{:S(2)}) async-start(bf16[16,72,384]{2,1,0:T(8,128)(2,1)} %bitcast.64), calls=%async_computation.7 | async-start | bytes 1769472 | tf_op jit(solution)/shard_map/all_to_all | solution.py:33
  253.5 9.9 %shard_map.192 = (bf16[12,128,128]{2,1,0:T(8,128)(2,1)}, bf16[128,512]{1,0:T(8,128)(2,1)}, f32[128,512]{1,0:T(8,128)}) custom-call(bf16[128,1536]{1,0:T(8,128)(2,1)} %get-tuple-element.39.refs_0_, bf16[128,1536]{1,0:T(8,128)(2,1)} %get-tuple-element.33.refs_0_.refs_1_, bf16[128,512]{1,0:T(8,128)(2,1)} %copy-done.19, ...), custom_call_target="tpu_custom_call" | custom-call | flops 1107296256 | bytes 7471624 | tf_op jit(solution)/shard_map/pallas_call | solution.py:68
  265.7 9.2 %all-to-all-done.6 = bf16[16,72,384]{2,1,0:T(8,128)(2,1)S(1)} async-done(((bf16[16,72,384]{2,1,0:T(8,128)(2,1)}), bf16[16,72,384]{2,1,0:T(8,128)(2,1)S(1)}, u32[]{:S(2)}, u32[]{:S(2)}) %all-to-all-start.6) | async-done | bytes 884768 | tf_op jit(solution)/shard_map/all_to_all | solution.py:33
  288.9 5.3 %collective-permute-start.14 = (bf16[8,72,384]{2,1,0:T(8,128)(2,1)S(1)}, bf16[8,72,384]{2,1,0:T(8,128)(2,1)S(1)}, u32[]{:S(2)}, u32[]{:S(2)}) collective-permute-start(bf16[8,72,384]{2,1,0:T(8,128)(2,1)S(1)} %copy-done.6), channel_id=1, source_target_pairs={{0,96},{16,112},{32,64},{48,80},{64,32},{80,48},{96,0},{112,16},{1... | collective-permute-start | bytes 1327112 | tf_op jit(solution)/shard_map/ppermute | solution.py:593
  294.2 6.1 %shard_map.196 = (bf16[128,1536]{1,0:T(8,128)(2,1)}, f32[1,1536]{1,0:T(1,128)}) custom-call(bf16[16,128,128]{2,1,0:T(8,128)(2,1)} %shard_map.194.refs_4_.refs_0_, bf16[1536,2048]{1,0:T(8,128)(2,1)} %all-gather.6.cloned.1.call-done.refs_2_.refs_1_, bf16[128,1536]{1,0:T(8,128)(2,1)} %refs_2_.1, f32[1,1536]{1,0:T(1,128)} %slice.53.refs_1_.refs_3_, ...), custom_call_target="tpu_custom_call" | custom-call | flops 805306368 | bytes 8400896 | tf_op jit(solution)/shard_map/pallas_call | solution.py:68
  301.8 4.8 %convolution_convert_fusion = bf16[1536,128]{1,0:T(8,128)(2,1)S(1)} fusion(bf16[2048,1536]{1,0:T(8,128)(2,1)} %all-gather.8.cloned.1.call-done.refs_5_, bf16[2048,128]{1,0:T(8,128)(2,1)} %bitcast.27), kind=kOutput, calls=%fused_computation.2 | convolution fusion | flops 805502976 | bytes 7208960 | tf_op jit(solution)/shard_map/dot_general | solution.py:45
  306.6 5.5 %collective-permute-done.10.refs_2_.refs_1_ = bf16[8,72,384]{2,1,0:T(8,128)(2,1)S(1)} collective-permute-done((bf16[8,72,384]{2,1,0:T(8,128)(2,1)S(1)}, bf16[8,72,384]{2,1,0:T(8,128)(2,1)S(1)}, u32[]{:S(2)}, u32[]{:S(2)}) %collective-permute-start.10) | collective-permute-done | bytes 442400 | tf_op jit(solution)/shard_map/ppermute | solution.py:593
  316.0 5.4 %all-to-all-start.8 = ((bf16[16,104,128]{2,1,0:T(8,128)(2,1)}), bf16[16,104,128]{2,1,0:T(8,128)(2,1)}, u32[]{:S(2)}, u32[]{:S(2)}) async-start(bf16[16,104,128]{2,1,0:T(8,128)(2,1)} %fusion.6), calls=%async_computation.9 | async-start | bytes 851968 | tf_op jit(solution)/shard_map/all_to_all | solution.py:33
  321.4 4.6 %fusion.refs_1_ = bf16[96,1536]{1,0:T(8,128)(2,1)} fusion(bf16[16,96,128]{2,1,0:T(8,128)(2,1)S(1)} %copy-done.5, bf16[16,128,1536]{2,1,0:T(8,128)(2,1)} %bitcast.58), kind=kOutput, calls=%fused_computation.3 | convolution fusion | flops 604127232 | bytes 6979584 | tf_op jit(solution)/shard_map/jat,jtn->an/dot_general | solution.py:842
  326.0 7.4 %collective-permute-done.14.refs_6_.refs_5_ = bf16[8,72,384]{2,1,0:T(8,128)(2,1)S(1)} collective-permute-done((bf16[8,72,384]{2,1,0:T(8,128)(2,1)S(1)}, bf16[8,72,384]{2,1,0:T(8,128)(2,1)S(1)}, u32[]{:S(2)}, u32[]{:S(2)}) %collective-permute-start.14) | collective-permute-done | bytes 442400 | tf_op jit(solution)/shard_map/ppermute | solution.py:593
  333.4 11.0 %collective-permute-done.15.refs_7_.refs_6_ = bf16[8,72,384]{2,1,0:T(8,128)(2,1)} collective-permute-done((bf16[8,72,384]{2,1,0:T(8,128)(2,1)S(1)}, bf16[8,72,384]{2,1,0:T(8,128)(2,1)}, u32[]{:S(2)}, u32[]{:S(2)}) %collective-permute-start.15) | collective-permute-done | bytes 442400 | tf_op jit(solution)/shard_map/ppermute | solution.py:593
  348.5 21.0 %all_to_all.74.piece_ref = bf16[8,56,896]{2,1,0:T(8,128)(2,1)} all-to-all(bf16[8,56,896]{2,1,0:T(8,128)(2,1)} %shard_map.197), channel_id=1, replica_groups=mesh['h'=2,'z'=4,'y'=4,'x'=2,'c'=2] {'h','z'}, dimensions={0} | all-to-all | bytes 1605632 | tf_op jit(solution)/shard_map/all_to_all | solution.py:33
  381.0 7.6 %shard_map.200 = (f32[8,96,1536]{2,1,0:T(8,128)}, f32[8,48,1536]{2,1,0:T(8,128)}) custom-call(s32[2]{0:T(128)} %pad_add_fusion.1.place_ref, bf16[8,72,384]{2,1,0:T(8,128)(2,1)} %add_convert_fusion.1.refs_5_.refs_0_, bf16[8,72,384]{2,1,0:T(8,128)(2,1)} %copy-done.14, bf16[8,72,384]{2,1,0:T(8,128)(2,1)} %copy-done.15, bf16[8,72,384]{2,1,0:T(8,128)(2,1)} %copy-done.16, ...), custom_call_target="tpu_custom_call" | custom-call | tf_op jit(solution)/shard_map/pallas_call | solution.py:616
  (173 shorter events, 94.9 us)
Async XLA Ops:
  7.2 96.0 %all-gather.6.cloned.1.call-start = ((), (), s32[]{:S(2)}) async-start(), calls=%async_computation.12 | async-start | bytes 6684672 | tf_op jit(solution)/shard_map/all_gather | solution.py:737
  11.7 21.7 %all-to-all-start = ((bf16[8,112,384]{2,1,0:T(8,128)(2,1)}), bf16[8,112,384]{2,1,0:T(8,128)(2,1)S(1)}, u32[]{:S(2)}, u32[]{:S(2)}) async-start(bf16[8,112,384]{2,1,0:T(8,128)(2,1)} %broadcast_in_dim.58), calls=%async_computation | async-start | bytes 1376256 | tf_op jit(solution)/shard_map/all_to_all | solution.py:33
  36.6 42.9 %all-to-all-start.1 = ((bf16[8,80,1536]{2,1,0:T(8,128)(2,1)}), bf16[8,80,1536]{2,1,0:T(8,128)(2,1)}, u32[]{:S(2)}, u32[]{:S(2)}) async-start(bf16[8,80,1536]{2,1,0:T(8,128)(2,1)} %bitcast.63), calls=%async_computation.1 | async-start | bytes 3932160 | tf_op jit(solution)/shard_map/all_to_all | solution.py:33
  40.9 117.3 %all-gather.12.cloned.1.call-start = ((), (), s32[]{:S(2)}) async-start(), calls=%async_computation.16 | async-start | bytes 7962624 | tf_op jit(solution)/shard_map/all_gather | solution.py:773
  41.0 31.3 %collective-permute-start.4 = (bf16[8,112,384]{2,1,0:T(8,128)(2,1)S(1)}, bf16[8,112,384]{2,1,0:T(8,128)(2,1)S(1)}, u32[]{:S(2)}, u32[]{:S(2)}) collective-permute-start(bf16[8,112,384]{2,1,0:T(8,128)(2,1)S(1)} %all-to-all-done.refs_7_.refs_8_), channel_id=1, source_target_pairs={{0,48},{16,32},{32,16},{48,0},{1,49},{17,33},{33,17},{49,1},{2,50}... | collective-permute-start | bytes 2064392 | tf_op jit(solution)/shard_map/ppermute | solution.py:581
  46.2 27.3 %collective-permute-start.3 = (bf16[8,112,384]{2,1,0:T(8,128)(2,1)S(1)}, bf16[8,112,384]{2,1,0:T(8,128)(2,1)S(1)}, u32[]{:S(2)}, u32[]{:S(2)}) collective-permute-start(bf16[8,112,384]{2,1,0:T(8,128)(2,1)S(1)} %all-to-all-done.refs_7_.refs_8_), channel_id=1, source_target_pairs={{0,32},{16,48},{32,0},{48,16},{1,33},{17,49},{33,1},{49,17},{2,34}... | collective-permute-start | bytes 2064392 | tf_op jit(solution)/shard_map/ppermute | solution.py:581
  46.2 28.5 %collective-permute-start.2 = (bf16[8,112,384]{2,1,0:T(8,128)(2,1)S(1)}, bf16[8,112,384]{2,1,0:T(8,128)(2,1)S(1)}, u32[]{:S(2)}, u32[]{:S(2)}) collective-permute-start(bf16[8,112,384]{2,1,0:T(8,128)(2,1)S(1)} %all-to-all-done.refs_7_.refs_8_), channel_id=1, source_target_pairs={{0,16},{16,0},{32,48},{48,32},{1,17},{17,1},{33,49},{49,33},{2,18}... | collective-permute-start | bytes 2064392 | tf_op jit(solution)/shard_map/ppermute | solution.py:581
  97.6 142.6 %all-gather.8.cloned.1.call-start = ((), (), s32[]{:S(2)}) async-start(), calls=%async_computation.13 | async-start | bytes 6684672 | tf_op jit(solution)/shard_map/all_gather | solution.py:792
  98.3 12.5 %collective-permute-start.5 = (bf16[8,112,384]{2,1,0:T(8,128)(2,1)S(1)}, bf16[8,112,384]{2,1,0:T(8,128)(2,1)S(1)}, u32[]{:S(2)}, u32[]{:S(2)}) collective-permute-start(bf16[8,112,384]{2,1,0:T(8,128)(2,1)S(1)} %all-to-all-done.refs_7_.refs_8_), channel_id=1, source_target_pairs={{0,1},{1,0},{2,3},{3,2},{4,5},{5,4},{6,7},{7,6},{8,9},{9,8},{10,11... | collective-permute-start | bytes 2064392 | tf_op jit(solution)/shard_map/ppermute | solution.py:760
  98.4 12.4 %collective-permute-start.6 = (bf16[8,112,384]{2,1,0:T(8,128)(2,1)}, bf16[8,112,384]{2,1,0:T(8,128)(2,1)}, u32[]{:S(2)}, u32[]{:S(2)}) collective-permute-start(bf16[8,112,384]{2,1,0:T(8,128)(2,1)} %copy-done.12), channel_id=1, source_target_pairs={{0,1},{1,0},{2,3},{3,2},{4,5},{5,4},{6,7},{7,6},{8,9},{9,8},{10,11... | collective-permute-start | bytes 2064392 | tf_op jit(solution)/shard_map/ppermute | solution.py:760
  154.4 22.0 %all-to-all-start.5 = ((bf16[16,96,128]{2,1,0:T(8,128)(2,1)}), bf16[16,96,128]{2,1,0:T(8,128)(2,1)S(1)}, u32[]{:S(2)}, u32[]{:S(2)}) async-start(bf16[16,96,128]{2,1,0:T(8,128)(2,1)} %bitcast.24), calls=%async_computation.5 | async-start | bytes 786432 | tf_op jit(solution)/shard_map/all_to_all | solution.py:33
  158.0 88.7 %reduce-scatter.2.cloned.1.call-start = ((), (), s32[]{:S(2)}) async-start(), calls=%async_computation.14 | async-start | bytes 7962624 | tf_op jit(solution)/shard_map/reduce_scatter | solution.py:811
  187.5 133.8 %all-gather.10.cloned.1.call-start = ((), (), s32[]{:S(2)}) async-start(), calls=%async_computation.15 | async-start | bytes 6684672 | tf_op jit(solution)/shard_map/all_gather | solution.py:816
  246.7 28.2 %all-to-all-start.6 = ((bf16[16,72,384]{2,1,0:T(8,128)(2,1)}), bf16[16,72,384]{2,1,0:T(8,128)(2,1)S(1)}, u32[]{:S(2)}, u32[]{:S(2)}) async-start(bf16[16,72,384]{2,1,0:T(8,128)(2,1)} %bitcast.64), calls=%async_computation.7 | async-start | bytes 1769472 | tf_op jit(solution)/shard_map/all_to_all | solution.py:33
  278.5 23.3 %all-to-all-start.7 = ((bf16[16,128,128]{2,1,0:T(8,128)(2,1)}), bf16[16,128,128]{2,1,0:T(8,128)(2,1)}, u32[]{:S(2)}, u32[]{:S(2)}) async-start(bf16[16,128,128]{2,1,0:T(8,128)(2,1)} %shard_map.194.refs_4_.refs_0_), calls=%async_computation.8 | async-start | bytes 1048576 | tf_op jit(solution)/shard_map/all_to_all | solution.py:33
  283.3 28.8 %collective-permute-start.10 = (bf16[8,72,384]{2,1,0:T(8,128)(2,1)S(1)}, bf16[8,72,384]{2,1,0:T(8,128)(2,1)S(1)}, u32[]{:S(2)}, u32[]{:S(2)}) collective-permute-start(bf16[8,72,384]{2,1,0:T(8,128)(2,1)S(1)} %copy-done.6), channel_id=1, source_target_pairs={{0,64},{16,80},{32,96},{48,112},{64,0},{80,16},{96,32},{112,48},{1... | collective-permute-start | bytes 1327112 | tf_op jit(solution)/shard_map/ppermute | solution.py:593
  286.2 28.2 %collective-permute-start.11 = (bf16[8,72,384]{2,1,0:T(8,128)(2,1)S(1)}, bf16[8,72,384]{2,1,0:T(8,128)(2,1)S(1)}, u32[]{:S(2)}, u32[]{:S(2)}) collective-permute-start(bf16[8,72,384]{2,1,0:T(8,128)(2,1)S(1)} %copy-done.6), channel_id=1, source_target_pairs={{0,16},{16,0},{32,48},{48,32},{64,80},{80,64},{96,112},{112,96},{1... | collective-permute-start | bytes 1327112 | tf_op jit(solution)/shard_map/ppermute | solution.py:593
  286.2 39.8 %collective-permute-start.12 = (bf16[8,72,384]{2,1,0:T(8,128)(2,1)S(1)}, bf16[8,72,384]{2,1,0:T(8,128)(2,1)S(1)}, u32[]{:S(2)}, u32[]{:S(2)}) collective-permute-start(bf16[8,72,384]{2,1,0:T(8,128)(2,1)S(1)} %copy-done.6), channel_id=1, source_target_pairs={{0,80},{16,64},{32,112},{48,96},{64,16},{80,0},{96,48},{112,32},{1... | collective-permute-start | bytes 1327112 | tf_op jit(solution)/shard_map/ppermute | solution.py:593
  288.3 37.7 %collective-permute-start.13 = (bf16[8,72,384]{2,1,0:T(8,128)(2,1)S(1)}, bf16[8,72,384]{2,1,0:T(8,128)(2,1)S(1)}, u32[]{:S(2)}, u32[]{:S(2)}) collective-permute-start(bf16[8,72,384]{2,1,0:T(8,128)(2,1)S(1)} %copy-done.6), channel_id=1, source_target_pairs={{0,32},{16,48},{32,0},{48,16},{64,96},{80,112},{96,64},{112,80},{1... | collective-permute-start | bytes 1327112 | tf_op jit(solution)/shard_map/ppermute | solution.py:593
  288.9 44.5 %collective-permute-start.14 = (bf16[8,72,384]{2,1,0:T(8,128)(2,1)S(1)}, bf16[8,72,384]{2,1,0:T(8,128)(2,1)S(1)}, u32[]{:S(2)}, u32[]{:S(2)}) collective-permute-start(bf16[8,72,384]{2,1,0:T(8,128)(2,1)S(1)} %copy-done.6), channel_id=1, source_target_pairs={{0,96},{16,112},{32,64},{48,80},{64,32},{80,48},{96,0},{112,16},{1... | collective-permute-start | bytes 1327112 | tf_op jit(solution)/shard_map/ppermute | solution.py:593
  312.1 32.3 %collective-permute-start.15 = (bf16[8,72,384]{2,1,0:T(8,128)(2,1)S(1)}, bf16[8,72,384]{2,1,0:T(8,128)(2,1)}, u32[]{:S(2)}, u32[]{:S(2)}) collective-permute-start(bf16[8,72,384]{2,1,0:T(8,128)(2,1)S(1)} %copy-done.6), channel_id=1, source_target_pairs={{0,48},{16,32},{32,16},{48,0},{64,112},{80,96},{96,80},{112,64},{1... | collective-permute-start | bytes 1327112 | tf_op jit(solution)/shard_map/ppermute | solution.py:593
  314.4 30.0 %collective-permute-start.16 = (bf16[8,72,384]{2,1,0:T(8,128)(2,1)S(1)}, bf16[8,72,384]{2,1,0:T(8,128)(2,1)}, u32[]{:S(2)}, u32[]{:S(2)}) collective-permute-start(bf16[8,72,384]{2,1,0:T(8,128)(2,1)S(1)} %copy-done.6), channel_id=1, source_target_pairs={{0,112},{16,96},{32,80},{48,64},{64,48},{80,32},{96,16},{112,0},{1... | collective-permute-start | bytes 1327112 | tf_op jit(solution)/shard_map/ppermute | solution.py:593
  316.0 30.4 %all-to-all-start.8 = ((bf16[16,104,128]{2,1,0:T(8,128)(2,1)}), bf16[16,104,128]{2,1,0:T(8,128)(2,1)}, u32[]{:S(2)}, u32[]{:S(2)}) async-start(bf16[16,104,128]{2,1,0:T(8,128)(2,1)} %fusion.6), calls=%async_computation.9 | async-start | bytes 851968 | tf_op jit(solution)/shard_map/all_to_all | solution.py:33
  371.6 18.3 %all-to-all-start.10 = ((bf16[8,48,896]{2,1,0:T(8,128)(2,1)}), bf16[8,48,896]{2,1,0:T(8,128)(2,1)S(1)}, u32[]{:S(2)}, u32[]{:S(2)}) async-start(bf16[8,48,896]{2,1,0:T(8,128)(2,1)} %get-tuple-element.51), calls=%async_computation.11 | async-start | bytes 1376256 | tf_op jit(solution)/shard_map/all_to_all | solution.py:33
  (33 other events, 516.8 us)
Sparse Core Ops, SparseCore 0:
  10.3 68.9 all-gather.5
  97.7 44.2 all-gather.11
  153.8 42.5 all-gather.7
  198.7 47.9 reduce-scatter.1
  248.8 58.7 all-gather.9

commit v6 on v5

--- a/solution.py
+++ b/solution.py
@@ -125,12 +125,18 @@
 def norm_back(values, gain_row, upstream):
     factor = inverse_rms(values)
     grad_normed = upstream * gain_row
-    grad_gain = jnp.sum(upstream * values * factor, axis=0, keepdims=True)
+    grad_gain = upstream * values * factor
     cubed = factor * factor * factor
     grad_input = factor * grad_normed - values * cubed * jnp.mean(
         grad_normed * values, axis=-1, keepdims=True
     )
     return grad_input, grad_gain
+
+
+def gain_tile(grad_gain, lower):
+    rows = grad_gain.shape[0]
+    lane = lax.broadcasted_iota(jnp.int32, (rows, 128), 1)
+    return transposed_times(grad_gain, ((lane < 64) == lower).astype(f32))
 
 
 def rotary_tables(position):
@@ -210,15 +216,15 @@
     return both
 
 
-def attend(queries, before, own, first, mine, other, tokens, gain, earlier):
+def attend(queries, before, own, first, mine, other, tokens, gain, pick, earlier):
     rows, width = tokens.shape
     wide = len(mine)
     chips = mine[0].shape[0]
 
     def kernel(
-        query_ref, before_ref, own_ref, first_ref, token_ref, gain_ref, place_ref, *refs
+        query_ref, before_ref, own_ref, first_ref, token_ref, gain_ref, pick_ref, place_ref, *refs
     ):
-        turned_ref, residual_ref, normed_ref, attended_ref, w_ref, sem = refs[2 * wide :]
+        turned_ref, residual_ref, picked_ref, attended_ref, w_ref, sem = refs[2 * wide :]
         copies = fetch_parts(place_ref, refs[:wide], refs[wide : 2 * wide], w_ref, sem)
         allowed = allowed_keys(first_ref, rows)
         for group in range(KEY_VALUE_HEADS):
@@ -238,18 +244,21 @@
             branch = matmul(attended, weights).astype(bf16)
             residual_ref[:, at] = token_ref[:, at].astype(f32) + branch.astype(f32)
         residual = residual_ref[...]
-        normed_ref[...] = (residual * inverse_rms(residual) * gain_ref[...]).astype(bf16)
+        normed = (residual * inverse_rms(residual) * gain_ref[...]).astype(bf16)
+        for block in range(width // 512):
+            at = slice(block * 512, (block + 1) * 512)
+            picked_ref[:, at] = matmul(pick_ref[...], normed[:, at]).astype(bf16)
 
     return call(
         kernel,
         [
             shaped((width, rows), bf16),
             shaped((rows, width), f32),
-            shaped((rows, width), bf16),
+            shaped((pick.shape[0], width), bf16),
         ],
-        (queries, before, own, first, tokens, gain, device_place(), *mine, *other),
+        (queries, before, own, first, tokens, gain, pick, device_place(), *mine, *other),
         earlier,
-        specs=[*([WHOLE] * 6), SCALAR, *([UNUSED] * (2 * wide))],
+        specs=[*([WHOLE] * 7), SCALAR, *([UNUSED] * (2 * wide))],
         flops=2 * rows * width * width + 8 * rows * rows * width,
         scratch=[
             pltpu.VMEM((rows, width), bf16),
@@ -259,33 +268,22 @@
     )
 
 
-def pick_rows(pick, rows_in, earlier):
-    slots, width = pick.shape[0], rows_in.shape[1]
-
-    def kernel(pick_ref, in_ref, out_ref):
-        for block in range(width // 512):
-            at = slice(block * 512, (block + 1) * 512)
-            out_ref[:, at] = matmul(pick_ref[...], in_ref[:, at]).astype(bf16)
-
-    return call(
-        kernel,
-        [shaped((slots, width), bf16)],
-        (pick, rows_in),
-        earlier,
-        flops=2 * slots * rows_in.size,
-    )[0]
-
-
 def run_experts(picked, grad_out, parts, rows_up, rows_down):
     slots, width = picked.shape
     ways, chips, _, part = parts.shape
+    wide = ways // 2
     ff = chips * 2 * rows_down
     each = slots // chips
+    half = (rows_up + rows_down) // 2
+    near = chips // 2
 
     def kernel(
-        picked_ref, grad_ref, part_ref, acted_ref, pre_ref, back_ref,
-        up_w, down_w, gate_ref, upper_ref, up_sem, down_sem,
+        picked_any, grad_any, part_ref, back_any, piece_any,
+        picked_ref, grad_ref, up_w, down_w, gate_ref, upper_ref, acted_ref, pre_ref, back_ref,
+        keep_ref, piece_ref, in_sem, up_sem, down_sem, out_sem,
     ):
+        rows_in = pltpu.make_async_copy(picked_any, picked_ref, in_sem.at[0])
+        grads_in = pltpu.make_async_copy(grad_any, grad_ref, in_sem.at[1])
         ups, downs = [], []
         for i in range(ways):
             to = pl.ds(i // 2 * part, part)
@@ -301,9 +299,9 @@
                     down_sem.at[i],
                 )
             )
-        for copy in ups + downs:
+        for copy in [rows_in, *ups, grads_in, *downs]:
             copy.start()
-        for copy in ups:
+        for copy in [rows_in, *ups]:
             copy.wait()
 
         @pl.loop(0, ff // 256)
@@ -313,14 +311,13 @@
                 weights = up_w[:, :, :, pl.ds(base + at, 256)].reshape(width, 256)
                 ref[:, pl.ds(at, 256)] = matmul(picked_ref[...], weights)
 
-        for copy in downs:
+        for copy in [grads_in, *downs]:
             copy.wait()
-        half = chips // 2
 
         @pl.loop(0, 2)
         def _(j):
             at = pl.ds(pl.multiple_of(j * (ff // 2), 128), ff // 2)
-            weights = down_w[pl.ds(j * half, half)].reshape(ff // 2, width)
+            weights = down_w[pl.ds(j * near, near)].reshape(ff // 2, width)
             grad_act = times_transposed(grad_ref[...], weights)
             gate, up = gate_ref[:, at], upper_ref[:, at]
             sigmoid = 1.0 / (1.0 + jnp.exp(-gate))
@@ -331,89 +328,91 @@
             upper = pl.ds(pl.multiple_of(ff + j * (ff // 2), 128), ff // 2)
             pre_ref[:, upper] = (grad_act * silu).astype(bf16)
 
+        columns = width // 2
+
         @pl.loop(0, 2)
         def _(j):
-            to = pl.ds(pl.multiple_of(j * (width // 2), 128), width // 2)
-            weights = up_w[pl.ds(j * half, half)].reshape(width // 2, 2 * ff)
+            to = pl.ds(pl.multiple_of(j * columns, 128), columns)
+            weights = up_w[pl.ds(j * near, near)].reshape(columns, 2 * ff)
             back = times_transposed(pre_ref[...], weights).astype(bf16)
-            back_ref[:, 0, :, to] = back.reshape(chips, each, width // 2)
-            weights = down_w[:, :, :, to].reshape(ff, width // 2)
+            back_ref[:, 0, :, to] = back.reshape(chips, each, columns)
+            weights = down_w[:, :, :, to].reshape(ff, columns)
             forward = matmul(acted_ref[...], weights).astype(bf16)
-            back_ref[:, 1, :, to] = forward.reshape(chips, each, width // 2)
-
-    return call(
-        kernel,
-        [
-            shaped((slots, ff), bf16),
-            shaped((slots, 2 * ff), bf16),
-            shaped((chips, 2, each, width), bf16),
-        ],
-        (picked, grad_out, parts),
-        specs=[WHOLE, WHOLE, UNUSED],
-        flops=2 * slots * 6 * width * ff,
-        scratch=[
+            back_ref[:, 1, :, to] = forward.reshape(chips, each, columns)
+
+        back_out = pltpu.make_async_copy(back_ref, back_any, out_sem.at[0])
+        back_out.start()
+
+        @pl.loop(0, 2)
+        def _(s):
+            for n in range(2):
+                at = slice(n * columns, (n + 1) * columns)
+                for m in range(near // 2):
+                    base = pl.multiple_of(s * near * 2 * rows_up + m * 4 * rows_up, 128)
+                    block = picked_ref[:, pl.ds(base, 4 * rows_up)]
+                    up = transposed_times(block, pre_ref[:, at])
+                    for i in range(4):
+                        rows = up[i * rows_up : (i + 1) * rows_up]
+                        k, c = 2 * m + i // 2, i % 2
+                        keep_ref[k, c] = rows[half:]
+                        low = rows[:half].astype(bf16)
+                        for j in range(columns // part):
+                            z = n * (columns // part) + j
+                            piece_ref[z, c, s * near + k, 0] = low[:, j * part : (j + 1) * part]
+                base = pl.multiple_of(s * near * 2 * rows_down, 128)
+                block = acted_ref[:, pl.ds(base, near * 2 * rows_down)]
+                down = transposed_times(block, grad_ref[:, at])
+                for k in range(near):
+                    for c in range(2):
+                        low = (2 * k + c) * rows_down
+                        rest = jnp.concatenate([keep_ref[k, c], down[low : low + rows_down]], axis=0)
+                        rest = rest.astype(bf16)
+                        for j in range(columns // part):
+                            z = n * (columns // part) + j
+                            piece_ref[z, c, s * near + k, 1] = rest[:, j * part : (j + 1) * part]
+            chip = pl.ds(s * near, near)
+            pltpu.make_async_copy(
+                piece_ref.at[:, :, chip], piece_any.at[:, :, chip], out_sem.at[1 + s]
+            ).start()
+
+        back_out.wait()
+        for s in range(2):
+            chip = pl.ds(s * near, near)
+            pltpu.make_async_copy(
+                piece_ref.at[:, :, chip], piece_any.at[:, :, chip], out_sem.at[1 + s]
+            ).wait()
+
+    back = shaped((chips, 2, each, width), bf16)
+    pieces = shaped((wide, 2, chips, 2, half, part), bf16)
+    return pl.pallas_call(
+        kernel,
+        in_specs=[UNUSED] * 3,
+        out_specs=[UNUSED] * 2,
+        out_shape=[back, pieces],
+        scratch_shapes=[
+            pltpu.VMEM((slots, width), bf16),
+            pltpu.VMEM((slots, width), bf16),
             pltpu.VMEM((chips, 2, rows_up, width), bf16),
             pltpu.VMEM((chips, 2, rows_down, width), bf16),
             pltpu.VMEM((slots, ff), f32),
             pltpu.VMEM((slots, ff), f32),
+            pltpu.VMEM((slots, ff), bf16),
+            pltpu.VMEM((slots, 2 * ff), bf16),
+            pltpu.VMEM(back.shape, bf16),
+            pltpu.VMEM((near, 2, rows_up - half, width // 2), f32),
+            pltpu.VMEM(pieces.shape, bf16),
+            pltpu.SemaphoreType.DMA((2,)),
             pltpu.SemaphoreType.DMA((ways,)),
             pltpu.SemaphoreType.DMA((ways,)),
+            pltpu.SemaphoreType.DMA((3,)),
         ],
-    )
-
-
-def expert_weight_grads(picked, grad_pre, acted, grad_out, rows_up, rows_down, chips, wide, earlier):
-    slots, width = picked.shape
-    half, part = (rows_up + rows_down) // 2, width // wide
-    steps = 2
-    near = chips // steps
-
-    def kernel(picked_ref, pre_ref, acted_ref, grad_ref, *refs):
-        out_ref, keep_ref = refs[-2:]
-        columns = width // 2
-        for n in range(2):
-            at = slice(n * columns, (n + 1) * columns)
-            for m in range(near // 2):
-                block = slice(m * 4 * rows_up, (m + 1) * 4 * rows_up)
-                up = transposed_times(picked_ref[:, block], pre_ref[:, at])
-                for i in range(4):
-                    rows = up[i * rows_up : (i + 1) * rows_up]
-                    k, c = 2 * m + i // 2, i % 2
-                    keep_ref[k, c] = rows[half:]
-                    low = rows[:half].astype(bf16)
-                    for j in range(columns // part):
-                        z = n * (columns // part) + j
-                        out_ref[z, c, 0, k] = low[:, j * part : (j + 1) * part]
-            down = transposed_times(acted_ref[...], grad_ref[:, at])
-            for k in range(near):
-                for c in range(2):
-                    base = (2 * k + c) * rows_down
-                    rest = jnp.concatenate([keep_ref[k, c], down[base : base + rows_down]], axis=0)
-                    rest = rest.astype(bf16)
-                    for j in range(columns // part):
-                        z = n * (columns // part) + j
-                        out_ref[z, c, 1, k] = rest[:, j * part : (j + 1) * part]
-
-    return pl.pallas_call(
-        kernel,
-        grid=(steps,),
-        in_specs=[
-            pl.BlockSpec((slots, width // steps), lambda s: (0, s)),
-            pl.BlockSpec(grad_pre.shape, lambda s: (0, 0)),
-            pl.BlockSpec((slots, acted.shape[1] // steps), lambda s: (0, s)),
-            pl.BlockSpec(grad_out.shape, lambda s: (0, 0)),
-            *([UNUSED] * len(earlier)),
-        ],
-        out_specs=pl.BlockSpec((wide, 2, 2, near, half, part), lambda s: (0, 0, 0, s, 0, 0)),
-        out_shape=shaped((wide, 2, 2, chips, half, part), bf16),
-        scratch_shapes=[pltpu.VMEM((near, 2, rows_up - half, width // 2), f32)],
         compiler_params=pltpu.CompilerParams(vmem_limit_bytes=VMEM_LIMIT),
         cost_estimate=pl.CostEstimate(
-            flops=2 * slots * 3 * width * acted.shape[1],
-            bytes_accessed=4 * 4 * slots * width,
+            flops=2 * slots * 9 * width * ff,
+            bytes_accessed=12 * slots * width + 8 * width * 3 * ff,
             transcendentals=0,
         ),
-    )(picked, grad_pre, acted, grad_out, *earlier)
+    )(picked, grad_out, parts)
 
 
 def residual_grad(pick, returned, residual, gain, cotangent, earlier):
@@ -429,11 +428,11 @@
         grad = grad + cot_ref[...].astype(f32)
         grad_ref[...] = grad
         branch_ref[...] = grad.astype(bf16)
-        gain_grad_ref[...] = grad_gain
+        gain_grad_ref[...] = gain_tile(grad_gain, False)
 
     return call(
         kernel,
-        [shaped((rows, width), f32), shaped((rows, width), bf16), shaped((1, width), f32)],
+        [shaped((rows, width), f32), shaped((rows, width), bf16), shaped((width, 128), f32)],
         (pick, returned, residual, gain, cotangent),
         earlier,
         flops=2 * slots * width * rows,
@@ -463,7 +462,7 @@
     )[0]
 
 
-def attend_back(grad_branch, mine, other, queries, before, own, first, cosine, sine):
+def attend_back(grad_branch, mine, other, queries, before, own, first, cosine, sine, earlier):
     rows, width = grad_branch.shape
     kv_width = KEY_VALUE_HEADS * HEAD_SIZE
     wide = len(mine)
@@ -516,6 +515,7 @@
             shaped((rows, 2 * kv_width), f32),
         ],
         (grad_branch, queries, before, own, first, cosine, sine, device_place(), *mine, *other),
+        earlier,
         specs=[*([WHOLE] * 7), SCALAR, *([UNUSED] * (2 * wide))],
         flops=2 * rows * width * width + 20 * rows * rows * width,
         scratch=[
@@ -547,12 +547,12 @@
     )[0]
 
 
-def input_grad(blocks, weights, tokens, gain, grad_residual):
+def input_grad(blocks, weights, tokens, gain, grad_residual, gain_grad, earlier):
     rows, width = tokens.shape
     columns = blocks.shape[0] * HEAD_SIZE
 
     def kernel(
-        block_ref, all_ref, token_ref, gain_ref, residual_ref, out_ref, gain_grad_ref, w_ref, sem
+        block_ref, all_ref, token_ref, gain_ref, residual_ref, other_ref, out_ref, tile_ref, w_ref, sem
     ):
         copies = fetch(all_ref, w_ref, sem, 1)
         total = jnp.zeros((rows, width), f32)
@@ -563,13 +563,14 @@
             total = total + times_transposed(pair, w_ref[:, i * 256 : (i + 1) * 256])
         grad, grad_gain = norm_back(token_ref[...].astype(f32), gain_ref[...], total)
         out_ref[...] = (residual_ref[...] + grad).astype(bf16)
-        gain_grad_ref[...] = grad_gain
+        tile_ref[...] = (other_ref[...] + gain_tile(grad_gain, True)).astype(bf16)
 
     return call(
         kernel,
-        [shaped((rows, width), bf16), shaped((1, width), f32)],
-        (blocks, weights, tokens, gain, grad_residual),
-        specs=[WHOLE, UNUSED, WHOLE, WHOLE, WHOLE],
+        [shaped((rows, width), bf16), shaped((width, 128), bf16)],
+        (blocks, weights, tokens, gain, grad_residual, gain_grad),
+        earlier,
+        specs=[WHOLE, UNUSED, WHOLE, WHOLE, WHOLE, WHOLE],
         flops=2 * rows * width * columns,
         scratch=[pltpu.VMEM((width, columns), bf16), pltpu.SemaphoreType.DMA((columns // 512,))],
     )
@@ -582,53 +583,32 @@
     ]
 
 
-def gather_over_rep(piece):
-    wide = lax.axis_size("z")
-    ways = 2 * wide
-    moved = []
-    for k in range(wide):
-        for j in range(2):
-            step = j * wide + k
-            moved.append(
-                lax.ppermute(piece, REP, [(i, i ^ step) for i in range(ways)]) if step else piece
-            )
-    return moved
-
-
-def expert_outputs(moved, rows_up, rows_down):
-    wide = len(moved) // 2
-    experts, half, part = moved[0].shape
+def expert_outputs(pieces, rows_up, rows_down):
+    wide, experts, _, half, part = pieces.shape
     width = wide * part
     split = rows_up - half
-    place = jnp.stack([lax.axis_index("h"), lax.axis_index("z")]).astype(jnp.int32)
-
-    def kernel(place_ref, *refs):
-        up_ref, down_ref = refs[2 * wide :]
-        low = place_ref[0] == 0
-        for k in range(wide):
-            at = pl.ds(pl.multiple_of((place_ref[1] ^ k) * part, 128), part)
-            same, other = refs[2 * k][0].astype(f32), refs[2 * k + 1][0].astype(f32)
-            rest = jnp.where(low, other, same)
-            up_ref[0, :half, at] = jnp.where(low, same, other)
+
+    def kernel(piece_ref, up_ref, down_ref):
+        for z in range(wide):
+            at = slice(z * part, (z + 1) * part)
+            rest = piece_ref[z, 0, 1].astype(f32)
+            up_ref[0, :half, at] = piece_ref[z, 0, 0].astype(f32)
             up_ref[0, half:, at] = rest[:split]
             down_ref[0, :, at] = rest[split:]
 
     return pl.pallas_call(
         kernel,
-        grid_spec=pltpu.PrefetchScalarGridSpec(
-            num_scalar_prefetch=1,
-            grid=(experts,),
-            in_specs=[pl.BlockSpec((1, half, part), lambda e, p: (e, 0, 0))] * (2 * wide),
-            out_specs=[
-                pl.BlockSpec((1, rows_up, width), lambda e, p: (e, 0, 0)),
-                pl.BlockSpec((1, rows_down, width), lambda e, p: (e, 0, 0)),
-            ],
-        ),
+        grid=(experts,),
+        in_specs=[pl.BlockSpec((wide, 1, 2, half, part), lambda e: (0, e, 0, 0, 0))],
+        out_specs=[
+            pl.BlockSpec((1, rows_up, width), lambda e: (e, 0, 0)),
+            pl.BlockSpec((1, rows_down, width), lambda e: (e, 0, 0)),
+        ],
         out_shape=[
             shaped((experts, rows_up, width), f32),
             shaped((experts, rows_down, width), f32),
         ],
-    )(place, *moved)
+    )(pieces)
 
 
 def after(value, *earlier):
@@ -638,76 +618,198 @@
     return value
 
 
-def pack_attention_grads(blocks, out_rows, wide, earlier):
-    count, rows, column = blocks.shape
-    rows -= 8
-    half = rows // 2
-    total = count + out_rows.shape[1] // column
-    each = total // wide
-
-    def kernel(block_ref, out_ref, piece_ref):
-        piece_ref[...] = jnp.zeros_like(piece_ref)
-        gains = block_ref[0, rows:].astype(f32)
-        for b in range(1, count):
-            gains = gains + block_ref[b, rows:].astype(f32)
-        for h in range(2):
-            at = slice(h * half, (h + 1) * half)
-            for b in range(total):
-                if b < count:
-                    value = block_ref[b, at]
+def to_square(value):
+    return jnp.stack([value, lax.ppermute(value, "x", SWAP)])
+
+
+def part_to_square(value, across, axis):
+    size = value.shape[axis] // 2
+    mine = lax.dynamic_slice_in_dim(value, across * size, size, axis)
+    sent = lax.dynamic_slice_in_dim(value, (1 - across) * size, size, axis)
+    return jnp.stack([mine, lax.ppermute(sent, "x", SWAP)])
+
+
+def part_to_core(value, core, axis):
+    size = value.shape[axis] // 2
+    return lax.ppermute(lax.dynamic_slice_in_dim(value, (1 - core) * size, size, axis), "c", SWAP)
+
+
+def twice(value, earlier):
+    size = value.shape[0]
+
+    def kernel(in_ref, out_ref):
+        out_ref[:size] = in_ref[...]
+        out_ref[size:] = in_ref[...]
+
+    return call(kernel, [shaped((2 * size, *value.shape[1:]), value.dtype)], (value,), earlier)[0]
+
+
+def sum_of_halves(value, earlier):
+    size = value.shape[0] // 2
+
+    def kernel(in_ref, out_ref):
+        out_ref[...] = (in_ref[:size].astype(f32) + in_ref[size:].astype(f32)).astype(bf16)
+
+    return call(kernel, [shaped((size, *value.shape[1:]), value.dtype)], (value,), earlier)[0]
+
+
+def hold(values, earlier):
+    def kernel(*refs):
+        del refs
+
+    return pl.pallas_call(
+        kernel,
+        in_specs=[UNUSED] * (len(values) + len(earlier)),
+        out_specs=[UNUSED] * len(values),
+        out_shape=[shaped(one.shape, one.dtype) for one in values],
+        input_output_aliases={i: i for i in range(len(values))},
+    )(*values, *earlier)
+
+
+def out_weight_grads(near, far, grad_near, grad_far, ways, earlier):
+    _, width, rows = near.shape
+    columns = grad_far.shape[2]
+    core = lax.axis_index("c").astype(jnp.int32).reshape(1)
+
+    def kernel(core_ref, near_ref, far_ref, grad_near_ref, grad_far_ref, out_ref, left_ref):
+        at = pl.ds(pl.multiple_of(core_ref[0] * columns, 128), columns)
+        for i in range(2):
+            left_ref[:, i * rows : (i + 1) * rows] = near_ref[i]
+            left_ref[:, (2 + i) * rows : (3 + i) * rows] = far_ref[i]
+        right = jnp.concatenate(
+            [grad_near_ref[0, :, at], grad_near_ref[1, :, at], grad_far_ref[0], grad_far_ref[1]],
+            axis=0,
+        )
+        each = width // ways
+        for i in range(ways):
+            left = left_ref[i * each : (i + 1) * each, :]
+            out_ref[i] = matmul(left, right).astype(bf16)
+
+    return call(
+        kernel,
+        [shaped((ways, width // ways, columns), bf16)],
+        (core, near, far, grad_near, grad_far),
+        earlier,
+        specs=[SCALAR, *([WHOLE] * 4)],
+        flops=8 * width * rows * columns,
+        scratch=[pltpu.VMEM((width, 4 * rows), bf16)],
+    )[0]
+
+
+def qkv_weight_grads(near, far, grad_near, grad_far, ways):
+    _, rows, width = near.shape
+    heads = grad_far.shape[1]
+    columns = heads * HEAD_SIZE
+    core = lax.axis_index("c").astype(jnp.int32).reshape(1)
+
+    def kernel(core_ref, near_ref, far_ref, grad_near_ref, grad_far_ref, out_ref, left_ref, right_ref):
+        for i in range(2):
+            left_ref[i * rows : (i + 1) * rows, :] = near_ref[i]
+            left_ref[(2 + i) * rows : (3 + i) * rows, :] = far_ref[i]
+            for head in range(heads):
+                at = slice(head * HEAD_SIZE, (head + 1) * HEAD_SIZE)
+                mine = grad_near_ref[i, core_ref[0] * heads + head]
+                right_ref[i * rows : (i + 1) * rows, at] = mine
+                right_ref[(2 + i) * rows : (3 + i) * rows, at] = grad_far_ref[i, head]
+        each = width // ways
+        for i in range(ways):
+            block = slice(i * each, (i + 1) * each)
+            out_ref[i] = transposed_times(left_ref[:, block], right_ref[...]).astype(bf16)
+
+    return call(
+        kernel,
+        [shaped((ways, width // ways, columns), bf16)],
+        (core, near, far, grad_near, grad_far),
+        specs=[SCALAR, *([WHOLE] * 4)],
+        flops=8 * width * rows * columns,
+        scratch=[pltpu.VMEM((4 * rows, width), bf16), pltpu.VMEM((4 * rows, columns), bf16)],
+    )[0]
+
+
+def moved_over_y(blocks):
+    wide = lax.axis_size("y")
+    y = lax.axis_index("y")
+    moved = [lax.dynamic_index_in_dim(blocks, y, 0, keepdims=False)]
+    for k in range(1, wide):
+        sent = lax.dynamic_index_in_dim(blocks, y ^ k, 0, keepdims=False)
+        moved.append(lax.ppermute(sent, "y", [(i, i ^ k) for i in range(wide)]))
+    return moved
+
+
+def tiles_of(qkv, out, gains, tiles, squares):
+    terms = qkv.shape[0]
+    rows = qkv.shape[1] // squares
+    count = qkv.shape[2] // HEAD_SIZE
+
+    def kernel(qkv_ref, out_ref, *refs):
+        gain_refs, tile_ref = refs[:-1], refs[-1]
+        for t in range(tiles):
+            for p in range(squares):
+                block = slice(p * rows, (p + 1) * rows)
+                if t < count:
+                    at = slice(t * HEAD_SIZE, (t + 1) * HEAD_SIZE)
+                    values = [qkv_ref[i, block, at] for i in range(terms)]
+                elif t < tiles - 1:
+                    at = slice((t - count) * HEAD_SIZE, (t - count + 1) * HEAD_SIZE)
+                    values = [out_ref[block, at]]
                 else:
-                    value = out_ref[at, (b - count) * column : (b - count + 1) * column]
-                to = (b % each) * column
-                piece_ref[h * wide + b // each, :half, to : to + column] = value
-        for p in range(2 * wide):
-            piece_ref[p, half:, :column] = gains.astype(bf16)
+                    values = [ref[block] for ref in gain_refs]
+                total = values[0].astype(f32)
+                for value in values[1:]:
+                    total = total + value.astype(f32)
+                tile_ref[t * squares + p] = total.astype(bf16)
 
     return call(
-        kernel, [shaped((2 * wide, half + 8, each * column), bf16)], (blocks, out_rows), earlier
+        kernel, [shaped((tiles * squares, rows, HEAD_SIZE), bf16)], (qkv, out, *gains)
     )[0]
 
 
-def sum_and_copy(pieces):
-    count, rows, columns = pieces.shape
-
-    def kernel(piece_ref, copy_ref, gain_ref):
-        total = piece_ref[0].astype(f32)
-        for p in range(1, count):
-            total = total + piece_ref[p].astype(f32)
-        gain_ref[...] = total[rows - 8 :, :128]
-        low = total[: rows - 8].astype(bf16)
-        for p in range(count):
-            copy_ref[p] = low
-
-    return pl.pallas_call(
-        kernel,
-        out_shape=[
-            jax.ShapeDtypeStruct((count, rows - 8, columns), bf16),
-            jax.ShapeDtypeStruct((8, 128), f32),
+def sum_and_copy(parts, squares, copies, earlier):
+    count, rows, columns = parts.shape
+
+    def kernel(part_ref, copy_ref):
+        for p in range(squares):
+            total = part_ref[p].astype(f32)
+            for i in range(1, count // squares):
+                total = total + part_ref[i * squares + p].astype(f32)
+            low = total.astype(bf16)
+            for i in range(copies):
+                copy_ref[i, p] = low
+
+    return call(kernel, [shaped((copies, squares, rows, columns), bf16)], (parts,), earlier)[0]
+
+
+def attention_outputs(tiles, query_width, kv_width):
+    count, squares, rows, column = tiles.shape
+    heads = (query_width + kv_width) // column // squares
+    outs = count - 1 - heads
+
+    def kernel(tile_ref, query_ref, keyval_ref, out_ref, gain_ref):
+        gains = jnp.zeros((rows, column), f32)
+        for q in range(squares):
+            for t in range(heads):
+                at = (q * heads + t) * column
+                value = tile_ref[t, q].astype(f32)
+                if at < query_width:
+                    query_ref[:, at : at + column] = value
+                else:
+                    keyval_ref[:, at - query_width : at - query_width + column] = value
+            for t in range(outs):
+                at = (q * outs + t) * column
+                out_ref[:, at : at + column] = tile_ref[heads + t, q].astype(f32)
+            gains = gains + tile_ref[count - 1, q].astype(f32)
+        gain_ref[...] = gains
+
+    return call(
+        kernel,
+        [
+            shaped((rows, query_width), f32),
+            shaped((rows, kv_width), f32),
+            shaped((rows, squares * outs * column), f32),
+            shaped((rows, column), f32),
         ],
-    )(pieces)
-
-
-def attention_outputs(pieces, widths):
-    count, half, part = pieces.shape
-    wide = count // 2
-
-    def kernel(piece_ref, *out_refs):
-        for h in range(2):
-            for z in range(wide):
-                left, right, base = z * part, (z + 1) * part, 0
-                for ref, size in zip(out_refs, widths):
-                    low, high = max(left, base), min(right, base + size)
-                    if low < high:
-                        ref[h * half : (h + 1) * half, low - base : high - base] = piece_ref[
-                            h * wide + z, :, low - left : high - left
-                        ].astype(f32)
-                    base += size
-
-    return pl.pallas_call(
-        kernel,
-        out_shape=[jax.ShapeDtypeStruct((2 * half, size), f32) for size in widths],
-    )(pieces)
+        (tiles,),
+    )
 
 
 def per_device(
@@ -744,7 +846,6 @@
     out_part = jnp.concatenate(
         [lax.dynamic_slice_in_dim(w_out, column, part, 1), gains_own], axis=0
     )
-    out_part = spread(out_part, experts, CHIPS)
     expert_part = jnp.concatenate(
         [
             lax.dynamic_slice_in_dim(w_gateup, column, part, 2),
@@ -752,6 +853,8 @@
         ],
         axis=1,
     )
+    out_part = spread(out_part, experts, CHIPS)
+    expert_part = exchange(after(expert_part, out_part), CHIPS)
     gains_mine = out_part[:, rows_out : rows_out + 2, :owned]
     gains = in_core_order(core, gains_mine, lax.ppermute(gains_mine, "c", SWAP))
     gains = gains.transpose(2, 0, 1, 3).reshape(2, width).astype(f32)
@@ -767,10 +870,12 @@
     pick = picks.astype(bf16).reshape(experts * CAP, rows)
     slot_weight = jnp.sum(jnp.where(picks, weight.T[:, None, :], 0.0), axis=2)
     grad_out = matmul(pick, cotangent) * slot_weight.reshape(-1, 1)
-    grad_out = exchange(after(grad_out, out_part).astype(bf16), CHIPS)
-
-    expert_part = exchange(after(expert_part, grad_out, *out_mine[1:]), CHIPS)
-    expert_parts = lax.all_gather(expert_part, ("z", "c"), axis=0)
+    grad_out_sent = after(grad_out, expert_part).astype(bf16)
+    grad_out = exchange(grad_out_sent, CHIPS)
+
+    expert_parts = lax.all_gather(
+        after(expert_part, *out_mine[1:], grad_out_sent), ("z", "c"), axis=0
+    )
 
     lengths = seq_lengths[0]
     starts = jnp.cumsum(lengths) - lengths
@@ -784,85 +889,89 @@
     ring = [(i, (i + 1) % shards) for i in range(shards)]
     back_ring = [((i + 1) % shards, i) for i in range(shards)]
     before = lax.ppermute(keyval, SHARD, ring)
-    attended_turned, residual, normed_ffn = attend(
-        queries, before, keyval, first, out_mine, out_other, tokens, gain_ffn, (grad_out,)
-    )
-
-    picked = exchange(pick_rows(pick, normed_ffn, ()), CHIPS)
-    normed_all = lax.all_gather(after(normed, picked), SHARD, axis=0, tiled=True)
-    attended_cols = exchange(after(attended_turned, picked), SHARD)
-    attended_cols = attended_cols.reshape(shards, owned, rows)
-    acted, grad_pre, returned = run_experts(
-        picked, grad_out, expert_parts, rows_up, rows_down
-    )
-    pieces = expert_weight_grads(
-        picked,
-        grad_pre,
-        acted,
-        grad_out,
-        rows_up,
-        rows_down,
-        experts,
-        wide_z,
-        (returned, attended_cols),
-    )
+    attended_turned, residual, picked = attend(
+        queries, before, keyval, first, out_mine, out_other, tokens, gain_ffn, pick, ()
+    )
+
+    picked = exchange(hold((picked,), (grad_out,))[0], CHIPS)
+    normed_near = to_square(after(normed, picked))
+    attended_near = to_square(after(attended_turned, picked))
+    returned, pieces = run_experts(picked, grad_out, expert_parts, rows_up, rows_down)
+    returned, pieces = hold((returned, pieces), (normed_near, attended_near))
     returned = exchange(returned, CHIPS)
+    normed_far = lax.ppermute(normed_near, "c", SWAP)
+    attended_far = lax.ppermute(attended_near, "c", SWAP)
     pieces = pieces.reshape(2 * wide_z, *pieces.shape[2:])
     over_z = lax.psum_scatter(pieces, ("z", "c"), scatter_dimension=0, tiled=False)
 
-    grad_residual, grad_branch, grad_gain_ffn = residual_grad(
-        pick, returned, residual, gain_ffn, cotangent, (normed_all,)
-    )
-    grad_branch_all = lax.all_gather(grad_branch, SHARD, axis=0, tiled=True)
+    grad_residual, grad_branch, gain_grad = residual_grad(
+        pick, returned, residual, gain_ffn, cotangent, (normed_far, attended_far)
+    )
+    across = lax.axis_index("x")
+    branch_near = part_to_square(grad_branch, across, 1)
+    over_rep = twice(over_z, (branch_near,))
     grad_queries, grad_before, grad_own = attend_back(
-        grad_branch, out_mine, out_other, queries, before, keyval, first, cosine, sine
-    )
+        grad_branch,
+        out_mine,
+        out_other,
+        queries,
+        before,
+        keyval,
+        first,
+        cosine,
+        sine,
+        (over_rep,),
+    )
+    over_rep = exchange(over_rep, ("h", *CHIPS))
+    out_terms = out_weight_grads(
+        attended_near,
+        attended_far,
+        branch_near,
+        part_to_core(branch_near, core, 2),
+        lax.axis_size("y"),
+        (grad_before,),
+    )
+    out_grads = lax.psum_scatter(out_terms, "y", scatter_dimension=0, tiled=True)
     from_next = lax.ppermute(grad_before, SHARD, back_ring)
-    over_z = over_z.reshape(2 * experts, *over_z.shape[2:])
-    over_rep = exchange(over_z, ("h", *CHIPS)).reshape(2, experts, *over_z.shape[1:])
-    over_rep = (over_rep[0].astype(f32) + over_rep[1].astype(f32)).astype(bf16)
     grad_blocks = qkv_blocks_of(
-        grad_queries, grad_own, from_next, cosine, sine, (over_rep,)
-    )
-    grad_tokens, grad_gain_attn = input_grad(
-        grad_blocks, qkv_full, tokens, gain_attn, grad_residual
-    )
-
-    grad_cols = exchange(grad_blocks, SHARD)
-    moved = gather_over_rep(over_rep)
-    shard_gateup, shard_down = expert_outputs(moved, rows_up, rows_down)
-    qkv_block = transposed_times(normed_all, grad_cols.reshape(shards * rows, HEAD_SIZE))
-    grad_gains = jnp.concatenate([grad_gain_attn, grad_gain_ffn]).reshape(2, shards, owned)
-    gain_rows = jnp.pad(
-        grad_gains.transpose(1, 0, 2).astype(bf16), ((0, 0), (0, 6), (0, HEAD_SIZE - owned))
-    )
-    qkv_block = jnp.concatenate(
-        [qkv_block.astype(bf16).reshape(shards, owned, HEAD_SIZE), gain_rows], axis=1
-    )
-    out_rows = jnp.einsum(
-        "jat,jtn->an",
-        attended_cols,
-        grad_branch_all.reshape(shards, rows, width),
-        preferred_element_type=f32,
-    ).astype(bf16)
-    qkv_blocks = exchange(after(qkv_block, over_rep), SHARD)
-    attn_pieces = exchange(pack_attention_grads(qkv_blocks, out_rows, wide_z, moved[1:]), REP)
-    attn_copies, gain_sums = sum_and_copy(attn_pieces)
-    grad_query, grad_keyval, grad_out_w = attention_outputs(
-        exchange(attn_copies, REP), (width, 2 * kv_width, width)
+        grad_queries, grad_own, from_next, cosine, sine, (over_rep, out_terms)
+    )
+
+    blocks_near = part_to_square(grad_blocks, across, 0)
+    qkv_grads = qkv_weight_grads(
+        normed_near,
+        normed_far,
+        blocks_near,
+        part_to_core(blocks_near, core, 1),
+        lax.axis_size("y"),
+    )
+    over_rep = sum_of_halves(over_rep, (qkv_grads,))
+    grad_tokens, tile = input_grad(
+        grad_blocks, qkv_full, tokens, gain_attn, grad_residual, gain_grad, (qkv_grads,)
+    )
+    gain_terms = moved_over_y(tile.reshape(lax.axis_size("y"), -1, HEAD_SIZE))
+    qkv_grads = exchange(qkv_grads, "y")
+    shard_gateup, shard_down = expert_outputs(
+        lax.all_gather(over_rep, "z", axis=0), rows_up, rows_down
+    )
+    reps = 2 * wide_z
+    tiles = exchange(tiles_of(qkv_grads, out_grads.reshape(-1, part), gain_terms, reps, 4), REP + ("x", "c"))
+    tiles = exchange(sum_and_copy(tiles, 4, reps, (shard_down,)), REP)
+    grad_query, grad_keyval, grad_out_w, gain_sums = attention_outputs(
+        tiles, width, 2 * kv_width
     )
 
     output = add_expert_rows(
-        pick, slot_weight.reshape(-1, 1), returned, residual, (grad_blocks,)
+        pick, slot_weight.reshape(-1, 1), returned, residual, (qkv_grads,)
     )
     return (
         output,
         grad_tokens,
-        gain_sums[0, :owned],
+        gain_sums[:, 0],
         grad_query,
         grad_keyval,
         grad_out_w,
-        gain_sums[1, :owned],
+        gain_sums[:, 64],
         shard_gateup,
         shard_down,
     )

time: 402 us -> 383 us (0.953); the launches traced: 400 us -> 375 us
  blocking collectives: 115 us -> 28.4 us
  waiting for transfers between devices: 83.9 us -> 138 us
  matrix products: 11.4 us -> 0.67 us
  local copies, waits for them, and re-layouts: 15.8 us -> 25.7 us
  Pallas kernels: 83.2 us -> 88.5 us
    all_to_all x4 -> x1, blocking collectives: 115 us -> 28.4 us  [exchange(): return lax.all_to_all(parts, axes, 0, 0, tiled=True)]
    all_to_all x7 -> x8, waiting for transfers between devices: 27.8 us -> 68.1 us  [exchange(): return lax.all_to_all(parts, axes, 0, 0, tiled=True)]
    dot_general x2 -> x0, matrix products: 9.41 us -> none  [the longest x1 4.78 us: dot_general(): lax.dot_general(left, right, (dims, ((), ())), preferred_element_type=f32)]
    ppermute x1, waiting for transfers between devices: 0.01 us -> 8.53 us  [per_device(): from_next = lax.ppermute(grad_before, SHARD, back_ring)]
    pallas_call x4, Pallas kernels: 22.2 us -> 29.2 us  [the longest x1 22.4 us: run_experts(): pl.pallas_call(kernel, in_specs=[UNUSED] * 3, out_specs=[UNUSED] * 2, out...]
    unnamed x56 -> x60, local copies, waits for them, and re-layouts: 3.02 us -> 8.93 us
    all_to_all x7 -> x8, starting transfers between devices: 33.3 us -> 36.6 us  [exchange(): return lax.all_to_all(parts, axes, 0, 0, tiled=True)]
    ppermute x7 -> x11, starting transfers between devices: 13.8 us -> 10.8 us  [the longest x3 4.72 us: moved_over_y(): moved.append(lax.ppermute(sent, 'y', [(i, i ^ k) for i in range(wide)]))]
  transfers between devices with their start and end apart: 29 -> 34, of which waited for: 11 -> 19; matrix products, arithmetic and copies ran while one was open for 9% -> 8% of each run, Pallas kernels for 19% -> 22%
where the time goes in v6:
time: 383 us; the launch traced here: 375 us
  waiting for transfers between devices  138 us (36%)
  Pallas kernels  88.5 us (23%)
  starting transfers between devices  59.6 us (16%)
  blocking collectives  28.4 us (7%)
  local copies, waits for them, and re-layouts  25.7 us (7%)
  between operations  19 us (5%)
  other arithmetic  15.5 us (4%)
    all_to_all x8, waiting for transfers between devices, exchange(): return lax.all_to_all(parts, axes, 0, 0, tiled=True)  68.1 us
    pallas_call x14, Pallas kernels, call(): pl.pallas_call(body, in_specs=[*specs, *[UNUSED] * len(earlier)], out_spe...  59.3 us
    all_to_all x8, starting transfers between devices, exchange(): return lax.all_to_all(parts, axes, 0, 0, tiled=True)  36.6 us
    all_to_all x1, blocking collectives, exchange(): return lax.all_to_all(parts, axes, 0, 0, tiled=True)  28.4 us
    ppermute x3, waiting for transfers between devices, gather_over_z(): lax.ppermute(part, 'z', [(i, i ^ k) for i in range(wide)])  24.5 us
    pallas_call x1, Pallas kernels, run_experts(): pl.pallas_call(kernel, in_specs=[UNUSED] * 3, out_specs=[UNUSED] * 2, out...  22.4 us
    ppermute x3, waiting for transfers between devices, moved_over_y(): moved.append(lax.ppermute(sent, 'y', [(i, i ^ k) for i in range(wide)]))  11.9 us
    ppermute x2, waiting for transfers between devices, part_to_square(): return jnp.stack([mine, lax.ppermute(sent, 'x', SWAP)])  10.6 us
  transfers between devices with their start and end apart: 34, of which 19 were waited for; matrix products, arithmetic and copies ran while one was open for 8% of the time, Pallas kernels for 22%

profile of v6, /device:TPU:0, one launch (start us, length us, event | category | flops | bytes accessed | tf_op | source)
XLA Modules:
  0.0 375.5 jit_solution(16349684581664494887)
XLA Ops:
  11.7 5.5 %all-to-all-start = ((bf16[8,112,384]{2,1,0:T(8,128)(2,1)}), bf16[8,112,384]{2,1,0:T(8,128)(2,1)S(1)}, u32[]{:S(2)}, u32[]{:S(2)}) async-start(bf16[8,112,384]{2,1,0:T(8,128)(2,1)} %broadcast_in_dim.58), calls=%async_computation | async-start | bytes 1376256 | tf_op jit(solution)/shard_map/all_to_all | solution.py:33
  19.1 14.3 %all-to-all-done.refs_8_ = bf16[8,112,384]{2,1,0:T(8,128)(2,1)S(1)} async-done(((bf16[8,112,384]{2,1,0:T(8,128)(2,1)}), bf16[8,112,384]{2,1,0:T(8,128)(2,1)S(1)}, u32[]{:S(2)}, u32[]{:S(2)}) %all-to-all-start) | async-done | bytes 688160 | tf_op jit(solution)/shard_map/all_to_all | solution.py:33
  48.8 10.5 %collective-permute-done.2.refs_9_ = bf16[8,112,384]{2,1,0:T(8,128)(2,1)S(1)} collective-permute-done((bf16[8,112,384]{2,1,0:T(8,128)(2,1)S(1)}, bf16[8,112,384]{2,1,0:T(8,128)(2,1)S(1)}, u32[]{:S(2)}, u32[]{:S(2)}) %collective-permute-start.2) | collective-permute-done | bytes 688160 | tf_op jit(solution)/shard_map/ppermute | solution.py:582
  60.5 12.6 %collective-permute-done.3.refs_10_ = bf16[8,112,384]{2,1,0:T(8,128)(2,1)S(1)} collective-permute-done((bf16[8,112,384]{2,1,0:T(8,128)(2,1)S(1)}, bf16[8,112,384]{2,1,0:T(8,128)(2,1)S(1)}, u32[]{:S(2)}, u32[]{:S(2)}) %collective-permute-start.3) | collective-permute-done | bytes 688160 | tf_op jit(solution)/shard_map/ppermute | solution.py:582
  83.3 5.2 %all-to-all-start.2 = ((bf16[8,80,1536]{2,1,0:T(8,128)(2,1)}), bf16[8,80,1536]{2,1,0:T(8,128)(2,1)S(1)}, u32[]{:S(2)}, u32[]{:S(2)}) async-start(bf16[8,80,1536]{2,1,0:T(8,128)(2,1)} %bitcast.65), calls=%async_computation.2 | async-start | bytes 3932160 | tf_op jit(solution)/shard_map/all_to_all | solution.py:33
  93.0 5.1 %shard_map.187 = (bf16[128,1536]{1,0:T(8,128)(2,1)}, bf16[128,1536]{1,0:T(8,128)(2,1)}, bf16[128,512]{1,0:T(8,128)(2,1)}) custom-call(bf16[128,1536]{1,0:T(8,128)(2,1)} %refs_2_.1, f32[1,1536]{1,0:T(1,128)} %slice.45.refs_1_.refs_3_, bf16[1536,2048]{1,0:T(8,128)(2,1)} %all-gather.6.cloned.1.call-done.refs_2_.refs_1_, ...), custom_call_target="tpu_custom_call" | custom-call | flops 805306368 | bytes 7739392 | tf_op jit(solution)/shard_map/pallas_call | solution.py:68
  100.4 6.0 %collective-permute-done.1.refs_1_.refs_2_ = bf16[128,512]{1,0:T(8,128)(2,1)S(1)} collective-permute-done((bf16[128,512]{1,0:T(8,128)(2,1)}, bf16[128,512]{1,0:T(8,128)(2,1)S(1)}, u32[]{:S(2)}, u32[]{:S(2)}) %collective-permute-start.1) | collective-permute-done | bytes 131104 | tf_op jit(solution)/shard_map/ppermute | solution.py:891
  107.0 6.7 %shard_map.188 = (bf16[1536,128]{1,0:T(8,128)(2,1)}, f32[128,1536]{1,0:T(8,128)}, bf16[640,1536]{1,0:T(8,128)(2,1)}) custom-call(bf16[128,1536]{1,0:T(8,128)(2,1)} %get-tuple-element.33.refs_0_.refs_1_, bf16[128,512]{1,0:T(8,128)(2,1)} %copy-done.18, bf16[128,512]{1,0:T(8,128)(2,1)} %get-tuple-element.34.refs_2_.refs_3_, s32[128,1]{1,0:T(8,128)} %copy.53.refs_3_.refs_4_, ...), custom_call_target="tpu_custom_call" | custom-call | flops 805306368 | bytes 9869832 | tf_op jit(solution)/shard_map/pallas_call | solution.py:68
  115.1 28.4 %all_to_all.57 = bf16[8,80,1536]{2,1,0:T(8,128)(2,1)S(1)} all-to-all(bf16[8,80,1536]{2,1,0:T(8,128)(2,1)} %bitcast.63), channel_id=1, replica_groups=mesh['h'=2,'z'=4,'y'=4,'x'=2,'c'=2] {'y','x'}, dimensions={0} | all-to-all | bytes 3932160 | tf_op jit(solution)/shard_map/all_to_all | solution.py:33
  148.4 22.4 %shard_map.190 = (bf16[8,2,80,1536]{3,2,1,0:T(8,128)(2,1)}, bf16[4,2,8,2,72,384]{5,4,3,2,1,0:T(8,128)(2,1)}) custom-call(bf16[640,1536]{1,0:T(8,128)(2,1)} %bitcast.67, bf16[640,1536]{1,0:T(8,128)(2,1)} %bitcast.62, bf16[8,8,144,384]{3,2,1,0:T(8,128)(2,1)} %bitcast.80), custom_call_target="tpu_custom_call" | custom-call | flops 13589544960 | bytes 40108032 | tf_op jit(solution)/shard_map/pallas_call | solution.py:387
  173.8 4.7 %all-to-all-start.4 = ((bf16[8,2,80,1536]{3,2,1,0:T(8,128)(2,1)}), bf16[8,2,80,1536]{3,2,1,0:T(8,128)(2,1)}, u32[]{:S(2)}, u32[]{:S(2)}) async-start(bf16[8,2,80,1536]{3,2,1,0:T(8,128)(2,1)} %get-tuple-element.40), calls=%async_computation.4 | async-start | bytes 7864320 | tf_op jit(solution)/shard_map/all_to_all | solution.py:33
  182.2 40.4 %all-to-all-done.4.refs_1_.refs_2_ = bf16[8,2,80,1536]{3,2,1,0:T(8,128)(2,1)} async-done(((bf16[8,2,80,1536]{3,2,1,0:T(8,128)(2,1)}), bf16[8,2,80,1536]{3,2,1,0:T(8,128)(2,1)}, u32[]{:S(2)}, u32[]{:S(2)}) %all-to-all-start.4) | async-done | bytes 3932192 | tf_op jit(solution)/shard_map/all_to_all | solution.py:33
  222.6 4.6 %shard_map.192 = (f32[128,1536]{1,0:T(8,128)}, bf16[128,1536]{1,0:T(8,128)(2,1)}, f32[1536,128]{1,0:T(8,128)}) custom-call(bf16[640,128]{1,0:T(8,128)(2,1)} %get-tuple-element.72.refs_6_.refs_0_, bf16[8,2,80,1536]{3,2,1,0:T(8,128)(2,1)} %all-to-all-done.4.refs_1_.refs_2_, f32[128,1536]{1,0:T(8,128)} %get-tuple-element.41.refs_2_.refs_3_, ...), custom_call_target="tpu_custom_call" | custom-call | flops 251658240 | bytes 7247872 | tf_op jit(solution)/shard_map/pallas_call | solution.py:68
  229.1 4.9 %collective-permute-done.13 = bf16[128,768]{1,0:T(8,128)(2,1)S(1)} collective-permute-done((bf16[128,768]{1,0:T(8,128)(2,1)S(1)}, bf16[128,768]{1,0:T(8,128)(2,1)S(1)}, u32[]{:S(2)}, u32[]{:S(2)}) %collective-permute-start.13) | collective-permute-done | bytes 196640 | tf_op jit(solution)/shard_map/ppermute | solution.py:629
  237.4 5.1 %all-to-all-start.5 = ((bf16[16,2,72,384]{3,2,1,0:T(8,128)(2,1)}), bf16[16,2,72,384]{3,2,1,0:T(8,128)(2,1)S(1)}, u32[]{:S(2)}, u32[]{:S(2)}) async-start(bf16[16,2,72,384]{3,2,1,0:T(8,128)(2,1)} %shard_map.193.refs_16_), calls=%async_computation.6 | async-start | bytes 3538944 | tf_op jit(solution)/shard_map/all_to_all | solution.py:33
  242.8 10.0 %shard_map.194 = (bf16[12,128,128]{2,1,0:T(8,128)(2,1)}, bf16[128,512]{1,0:T(8,128)(2,1)}, f32[128,512]{1,0:T(8,128)}) custom-call(bf16[128,1536]{1,0:T(8,128)(2,1)} %get-tuple-element.42.refs_0_, bf16[128,1536]{1,0:T(8,128)(2,1)} %get-tuple-element.33.refs_0_.refs_1_, bf16[128,512]{1,0:T(8,128)(2,1)} %copy-done.18, ...), custom_call_target="tpu_custom_call" | custom-call | flops 1107296256 | bytes 7471624 | tf_op jit(solution)/shard_map/pallas_call | solution.py:68
  260.9 8.5 %collective-permute-done.14.refs_2_ = bf16[128,512]{1,0:T(8,128)(2,1)S(1)} collective-permute-done((bf16[128,512]{1,0:T(8,128)(2,1)S(1)}, bf16[128,512]{1,0:T(8,128)(2,1)S(1)}, u32[]{:S(2)}, u32[]{:S(2)}) %collective-permute-start.14) | collective-permute-done | bytes 131104 | tf_op jit(solution)/shard_map/ppermute | solution.py:935
  276.9 5.8 %collective-permute-done.16 = bf16[8,128,128]{2,1,0:T(8,128)(2,1)S(1)} collective-permute-done((bf16[8,128,128]{2,1,0:T(8,128)(2,1)S(1)}, bf16[8,128,128]{2,1,0:T(8,128)(2,1)S(1)}, u32[]{:S(2)}, u32[]{:S(2)}) %collective-permute-start.16) | collective-permute-done | bytes 262176 | tf_op jit(solution)/shard_map/ppermute | solution.py:629
  291.4 4.9 %all-to-all-start.6 = ((bf16[4,384,512]{2,1,0:T(8,128)(2,1)}), bf16[4,384,512]{2,1,0:T(8,128)(2,1)S(1)}, u32[]{:S(2)}, u32[]{:S(2)}) async-start(bf16[4,384,512]{2,1,0:T(8,128)(2,1)} %shard_map.197.refs_6_.refs_1_), calls=%async_computation.7 | async-start | bytes 3145728 | tf_op jit(solution)/shard_map/all_to_all | solution.py:33
  296.4 6.9 %shard_map.199 = (bf16[128,1536]{1,0:T(8,128)(2,1)}, bf16[1536,128]{1,0:T(8,128)(2,1)}) custom-call(bf16[16,128,128]{2,1,0:T(8,128)(2,1)} %shard_map.196.refs_0_, bf16[1536,2048]{1,0:T(8,128)(2,1)} %all-gather.6.cloned.1.call-done.refs_2_.refs_1_, bf16[128,1536]{1,0:T(8,128)(2,1)} %refs_2_.1, f32[1,1536]{1,0:T(1,128)} %slice.45.refs_1_.refs_3_, ...), custom_call_target="tpu_custom_call" | custom-call | flops 805306368 | bytes 9574400 | tf_op jit(solution)/shard_map/pallas_call | solution.py:68
  309.7 9.4 %collective-permute-done.18.refs_3_ = bf16[384,128]{1,0:T(8,128)(2,1)S(1)} collective-permute-done((bf16[384,128]{1,0:T(8,128)(2,1)S(1)}, bf16[384,128]{1,0:T(8,128)(2,1)S(1)}, u32[]{:S(2)}, u32[]{:S(2)}) %collective-permute-start.18) | collective-permute-done | bytes 98336 | tf_op jit(solution)/shard_map/ppermute | solution.py:735
  332.9 6.8 %shard_map.202 = (f32[8,96,1536]{2,1,0:T(8,128)}, f32[8,48,1536]{2,1,0:T(8,128)}) custom-call(bf16[4,8,2,72,384]{4,3,2,1,0:T(8,128)(2,1)} %bitcast.64), custom_call_target="tpu_custom_call" | custom-call | tf_op jit(solution)/shard_map/pallas_call | solution.py:599
  351.4 4.3 %shard_map.198 = bf16[128,1536]{1,0:T(8,128)(2,1)} custom-call(bf16[640,128]{1,0:T(8,128)(2,1)} %get-tuple-element.72.refs_6_.refs_0_, f32[640,1]{1,0:T(8,128)} %reshape.123.refs_1_, bf16[8,2,80,1536]{3,2,1,0:T(8,128)(2,1)} %all-to-all-done.4.refs_1_.refs_2_, f32[128,1536]{1,0:T(8,128)} %get-tuple-element.41.refs_2_.refs_3_, bf16[4,384,512]{2,1,0:T(8,128)(2,1)} %copy-done.3), custom_call_target="tpu_custom_call" | custom-call | flops 503316480 | bytes 5278208 | tf_op jit(solution)/shard_map/pallas_call | solution.py:68
  355.8 8.4 %all-to-all-done.8.refs_0_ = bf16[8,4,96,128]{3,2,1,0:T(8,128)(2,1)S(1)} async-done(((bf16[8,4,96,128]{3,2,1,0:T(8,128)(2,1)}), bf16[8,4,96,128]{3,2,1,0:T(8,128)(2,1)S(1)}, u32[]{:S(2)}, u32[]{:S(2)}) %all-to-all-start.8) | async-done | bytes 786464 | tf_op jit(solution)/shard_map/all_to_all | solution.py:33
  (190 shorter events, 115.2 us)
Async XLA Ops:
  7.2 85.8 %all-gather.6.cloned.1.call-start = ((), (), s32[]{:S(2)}) async-start(), calls=%async_computation.11 | async-start | bytes 6684672 | tf_op jit(solution)/shard_map/all_gather | solution.py:839
  11.7 21.7 %all-to-all-start = ((bf16[8,112,384]{2,1,0:T(8,128)(2,1)}), bf16[8,112,384]{2,1,0:T(8,128)(2,1)S(1)}, u32[]{:S(2)}, u32[]{:S(2)}) async-start(bf16[8,112,384]{2,1,0:T(8,128)(2,1)} %broadcast_in_dim.58), calls=%async_computation | async-start | bytes 1376256 | tf_op jit(solution)/shard_map/all_to_all | solution.py:33
  36.8 40.8 %all-to-all-start.1 = ((bf16[8,144,384]{2,1,0:T(8,128)(2,1)}), bf16[8,144,384]{2,1,0:T(8,128)(2,1)S(1)}, u32[]{:S(2)}, u32[]{:S(2)}) async-start(bf16[8,144,384]{2,1,0:T(8,128)(2,1)} %maximum_add_fusion), calls=%async_computation.1 | async-start | bytes 1769472 | tf_op jit(solution)/shard_map/all_to_all | solution.py:33
  40.5 107.9 %all-gather.8.cloned.1.call-start = ((), (), s32[]{:S(2)}) async-start(), calls=%async_computation.14 | async-start | bytes 7962624 | tf_op jit(solution)/shard_map/all_gather | solution.py:876
  40.5 18.8 %collective-permute-start.2 = (bf16[8,112,384]{2,1,0:T(8,128)(2,1)S(1)}, bf16[8,112,384]{2,1,0:T(8,128)(2,1)S(1)}, u32[]{:S(2)}, u32[]{:S(2)}) collective-permute-start(bf16[8,112,384]{2,1,0:T(8,128)(2,1)S(1)} %all-to-all-done.refs_8_), channel_id=1, source_target_pairs={{0,16},{16,0},{32,48},{48,32},{1,17},{17,1},{33,49},{49,33},{2,18}... | collective-permute-start | bytes 2064392 | tf_op jit(solution)/shard_map/ppermute | solution.py:582
  42.9 30.1 %collective-permute-start.3 = (bf16[8,112,384]{2,1,0:T(8,128)(2,1)S(1)}, bf16[8,112,384]{2,1,0:T(8,128)(2,1)S(1)}, u32[]{:S(2)}, u32[]{:S(2)}) collective-permute-start(bf16[8,112,384]{2,1,0:T(8,128)(2,1)S(1)} %all-to-all-done.refs_8_), channel_id=1, source_target_pairs={{0,32},{16,48},{32,0},{48,16},{1,33},{17,49},{33,1},{49,17},{2,34}... | collective-permute-start | bytes 2064392 | tf_op jit(solution)/shard_map/ppermute | solution.py:582
  47.2 28.5 %collective-permute-start.4 = (bf16[8,112,384]{2,1,0:T(8,128)(2,1)S(1)}, bf16[8,112,384]{2,1,0:T(8,128)(2,1)}, u32[]{:S(2)}, u32[]{:S(2)}) collective-permute-start(bf16[8,112,384]{2,1,0:T(8,128)(2,1)S(1)} %all-to-all-done.refs_8_), channel_id=1, source_target_pairs={{0,48},{16,32},{32,16},{48,0},{1,49},{17,33},{33,17},{49,1},{2,50}... | collective-permute-start | bytes 2064392 | tf_op jit(solution)/shard_map/ppermute | solution.py:582
  83.3 30.4 %all-to-all-start.2 = ((bf16[8,80,1536]{2,1,0:T(8,128)(2,1)}), bf16[8,80,1536]{2,1,0:T(8,128)(2,1)S(1)}, u32[]{:S(2)}, u32[]{:S(2)}) async-start(bf16[8,80,1536]{2,1,0:T(8,128)(2,1)} %bitcast.65), calls=%async_computation.2 | async-start | bytes 3932160 | tf_op jit(solution)/shard_map/all_to_all | solution.py:33
  88.6 146.3 %reduce-scatter.3.cloned.1.call-start = ((), (), s32[]{:S(2)}) async-start(), calls=%async_computation.12 | async-start | bytes 7962624 | tf_op jit(solution)/shard_map/reduce_scatter | solution.py:905
  89.0 11.3 %collective-permute-start.5 = (bf16[8,112,384]{2,1,0:T(8,128)(2,1)S(1)}, bf16[8,112,384]{2,1,0:T(8,128)(2,1)}, u32[]{:S(2)}, u32[]{:S(2)}) collective-permute-start(bf16[8,112,384]{2,1,0:T(8,128)(2,1)S(1)} %all-to-all-done.refs_8_), channel_id=1, source_target_pairs={{0,1},{1,0},{2,3},{3,2},{4,5},{5,4},{6,7},{7,6},{8,9},{9,8},{10,11... | collective-permute-start | bytes 2064392 | tf_op jit(solution)/shard_map/ppermute | solution.py:863
  145.5 25.3 %collective-permute-start.10 = (bf16[1536,128]{1,0:T(8,128)(2,1)}, bf16[1536,128]{1,0:T(8,128)(2,1)}, u32[]{:S(2)}, u32[]{:S(2)}) collective-permute-start(bf16[1536,128]{1,0:T(8,128)(2,1)} %broadcast_add_fusion), channel_id=1, source_target_pairs={{0,2},{2,0},{1,3},{3,1},{4,6},{6,4},{5,7},{7,5},{8,10},{10,8},{9,1... | collective-permute-start | bytes 1179656 | tf_op jit(solution)/shard_map/ppermute | solution.py:622
  147.0 25.8 %collective-permute-start.9 = (bf16[128,1536]{1,0:T(8,128)(2,1)}, bf16[128,1536]{1,0:T(8,128)(2,1)S(1)}, u32[]{:S(2)}, u32[]{:S(2)}) collective-permute-start(bf16[128,1536]{1,0:T(8,128)(2,1)} %broadcast_add_fusion.1), channel_id=1, source_target_pairs={{0,2},{2,0},{1,3},{3,1},{4,6},{6,4},{5,7},{7,5},{8,10},{10,8},{9,1... | collective-permute-start | bytes 1179656 | tf_op jit(solution)/shard_map/ppermute | solution.py:622
  173.8 48.8 %all-to-all-start.4 = ((bf16[8,2,80,1536]{3,2,1,0:T(8,128)(2,1)}), bf16[8,2,80,1536]{3,2,1,0:T(8,128)(2,1)}, u32[]{:S(2)}, u32[]{:S(2)}) async-start(bf16[8,2,80,1536]{3,2,1,0:T(8,128)(2,1)} %get-tuple-element.40), calls=%async_computation.4 | async-start | bytes 7864320 | tf_op jit(solution)/shard_map/all_to_all | solution.py:33
  234.0 18.8 %collective-permute-start.15 = (bf16[2,128,384]{2,1,0:T(8,128)(2,1)S(1)}, bf16[2,128,384]{2,1,0:T(8,128)(2,1)S(1)}, u32[]{:S(2)}, u32[]{:S(2)}) collective-permute-start(bf16[2,128,384]{2,1,0:T(8,128)(2,1)S(1)} %fusion.1), channel_id=1, source_target_pairs={{0,1},{1,0},{2,3},{3,2},{4,5},{5,4},{6,7},{7,6},{8,9},{9,8},{10,11... | collective-permute-start | bytes 589832 | tf_op jit(solution)/shard_map/ppermute | solution.py:634
  237.4 32.8 %all-to-all-start.5 = ((bf16[16,2,72,384]{3,2,1,0:T(8,128)(2,1)}), bf16[16,2,72,384]{3,2,1,0:T(8,128)(2,1)S(1)}, u32[]{:S(2)}, u32[]{:S(2)}) async-start(bf16[16,2,72,384]{3,2,1,0:T(8,128)(2,1)} %shard_map.193.refs_16_), calls=%async_computation.6 | async-start | bytes 3538944 | tf_op jit(solution)/shard_map/all_to_all | solution.py:33
  242.6 79.1 %reduce-scatter.5.cloned.1.call-start = ((), (), s32[]{:S(2)}) async-start(), calls=%async_computation.13 | async-start | bytes 1474560 | tf_op jit(solution)/shard_map/reduce_scatter | solution.py:934
  257.2 75.8 %all-gather.10.cloned.1.call-start = ((), (), s32[]{:S(2)}) async-start(), calls=%async_computation.15 | async-start | bytes 4423680 | tf_op jit(solution)/shard_map/all_gather | solution.py:955
  257.2 12.2 %collective-permute-start.14 = (bf16[128,512]{1,0:T(8,128)(2,1)S(1)}, bf16[128,512]{1,0:T(8,128)(2,1)S(1)}, u32[]{:S(2)}, u32[]{:S(2)}) collective-permute-start(bf16[128,512]{1,0:T(8,128)(2,1)S(1)} %copy-done.22), channel_id=1, source_target_pairs={{1,0},{2,1},{3,2},{4,3},{5,4},{6,5},{7,6},{8,7},{9,8},{10,9},{11,1... | collective-permute-start | bytes 393224 | tf_op jit(solution)/shard_map/ppermute | solution.py:935
  291.4 30.2 %all-to-all-start.6 = ((bf16[4,384,512]{2,1,0:T(8,128)(2,1)}), bf16[4,384,512]{2,1,0:T(8,128)(2,1)S(1)}, u32[]{:S(2)}, u32[]{:S(2)}) async-start(bf16[4,384,512]{2,1,0:T(8,128)(2,1)} %shard_map.197.refs_6_.refs_1_), calls=%async_computation.7 | async-start | bytes 3145728 | tf_op jit(solution)/shard_map/all_to_all | solution.py:33
  305.0 14.1 %collective-permute-start.18 = (bf16[384,128]{1,0:T(8,128)(2,1)S(1)}, bf16[384,128]{1,0:T(8,128)(2,1)S(1)}, u32[]{:S(2)}, u32[]{:S(2)}) collective-permute-start(bf16[384,128]{1,0:T(8,128)(2,1)S(1)} %get-tuple-element.65), channel_id=1, source_target_pairs={{0,4},{4,0},{8,12},{12,8},{1,5},{5,1},{9,13},{13,9},{2,6},{6,2},{1... | collective-permute-start | bytes 294920 | tf_op jit(solution)/shard_map/ppermute | solution.py:735
  307.1 14.6 %collective-permute-start.19 = (bf16[384,128]{1,0:T(8,128)(2,1)S(1)}, bf16[384,128]{1,0:T(8,128)(2,1)S(1)}, u32[]{:S(2)}, u32[]{:S(2)}) collective-permute-start(bf16[384,128]{1,0:T(8,128)(2,1)S(1)} %get-tuple-element.64), channel_id=1, source_target_pairs={{0,8},{4,12},{8,0},{12,4},{1,9},{5,13},{9,1},{13,5},{2,10},{6,14},... | collective-permute-start | bytes 294920 | tf_op jit(solution)/shard_map/ppermute | solution.py:735
  309.7 11.9 %collective-permute-start.20 = (bf16[384,128]{1,0:T(8,128)(2,1)S(1)}, bf16[384,128]{1,0:T(8,128)(2,1)S(1)}, u32[]{:S(2)}, u32[]{:S(2)}) collective-permute-start(bf16[384,128]{1,0:T(8,128)(2,1)S(1)} %get-tuple-element.63), channel_id=1, source_target_pairs={{0,12},{4,8},{8,4},{12,0},{1,13},{5,9},{9,5},{13,1},{2,14},{6,10},... | collective-permute-start | bytes 294920 | tf_op jit(solution)/shard_map/ppermute | solution.py:735
  325.6 18.3 %all-to-all-start.7 = ((bf16[32,96,128]{2,1,0:T(8,128)(2,1)}), bf16[32,96,128]{2,1,0:T(8,128)(2,1)S(1)}, u32[]{:S(2)}, u32[]{:S(2)}) async-start(bf16[32,96,128]{2,1,0:T(8,128)(2,1)} %shard_map.200), calls=%async_computation.9 | async-start | bytes 1572864 | tf_op jit(solution)/shard_map/all_to_all | solution.py:33
  347.0 17.2 %all-to-all-start.8 = ((bf16[8,4,96,128]{3,2,1,0:T(8,128)(2,1)}), bf16[8,4,96,128]{3,2,1,0:T(8,128)(2,1)S(1)}, u32[]{:S(2)}, u32[]{:S(2)}) async-start(bf16[8,4,96,128]{3,2,1,0:T(8,128)(2,1)} %shard_map.203), calls=%async_computation.10 | async-start | bytes 1572864 | tf_op jit(solution)/shard_map/all_to_all | solution.py:33
  (40 other events, 444.7 us)
Sparse Core Ops, SparseCore 0:
  10.3 57.3 all-gather.5
  83.2 42.9 all-gather.7
  173.9 43.1 reduce-scatter.2
  257.3 24.6 reduce-scatter.4
  291.6 41.3 all-gather.9

commit v7 on v6

--- a/solution.py
+++ b/solution.py
@@ -278,8 +278,8 @@
     near = chips // 2
 
     def kernel(
-        picked_any, grad_any, part_ref, back_any, piece_any,
-        picked_ref, grad_ref, up_w, down_w, gate_ref, upper_ref, acted_ref, pre_ref, back_ref,
+        picked_any, grad_any, part_ref, back_any, expert_any, piece_any,
+        picked_ref, grad_ref, up_w, down_w, gate_ref, upper_ref, acted_ref, pre_ref, back_ref, expert_ref,
         keep_ref, piece_ref, in_sem, up_sem, down_sem, out_sem,
     ):
         rows_in = pltpu.make_async_copy(picked_any, picked_ref, in_sem.at[0])
@@ -335,13 +335,15 @@
             to = pl.ds(pl.multiple_of(j * columns, 128), columns)
             weights = up_w[pl.ds(j * near, near)].reshape(columns, 2 * ff)
             back = times_transposed(pre_ref[...], weights).astype(bf16)
-            back_ref[:, 0, :, to] = back.reshape(chips, each, columns)
+            back_ref[:, :, to] = back.reshape(chips, each, columns)
             weights = down_w[:, :, :, to].reshape(ff, columns)
             forward = matmul(acted_ref[...], weights).astype(bf16)
-            back_ref[:, 1, :, to] = forward.reshape(chips, each, columns)
+            expert_ref[:, :, to] = forward.reshape(chips, each, columns)
 
         back_out = pltpu.make_async_copy(back_ref, back_any, out_sem.at[0])
+        expert_out = pltpu.make_async_copy(expert_ref, expert_any, out_sem.at[3])
         back_out.start()
+        expert_out.start()
 
         @pl.loop(0, 2)
         def _(s):
@@ -376,19 +378,20 @@
             ).start()
 
         back_out.wait()
+        expert_out.wait()
         for s in range(2):
             chip = pl.ds(s * near, near)
             pltpu.make_async_copy(
                 piece_ref.at[:, :, chip], piece_any.at[:, :, chip], out_sem.at[1 + s]
             ).wait()
 
-    back = shaped((chips, 2, each, width), bf16)
+    back = shaped((chips, each, width), bf16)
     pieces = shaped((wide, 2, chips, 2, half, part), bf16)
     return pl.pallas_call(
         kernel,
         in_specs=[UNUSED] * 3,
-        out_specs=[UNUSED] * 2,
-        out_shape=[back, pieces],
+        out_specs=[UNUSED] * 3,
+        out_shape=[back, back, pieces],
         scratch_shapes=[
             pltpu.VMEM((slots, width), bf16),
             pltpu.VMEM((slots, width), bf16),
@@ -399,12 +402,13 @@
             pltpu.VMEM((slots, ff), bf16),
             pltpu.VMEM((slots, 2 * ff), bf16),
             pltpu.VMEM(back.shape, bf16),
+            pltpu.VMEM(back.shape, bf16),
             pltpu.VMEM((near, 2, rows_up - half, width // 2), f32),
             pltpu.VMEM(pieces.shape, bf16),
             pltpu.SemaphoreType.DMA((2,)),
             pltpu.SemaphoreType.DMA((ways,)),
             pltpu.SemaphoreType.DMA((ways,)),
-            pltpu.SemaphoreType.DMA((3,)),
+            pltpu.SemaphoreType.DMA((4,)),
         ],
         compiler_params=pltpu.CompilerParams(vmem_limit_bytes=VMEM_LIMIT),
         cost_estimate=pl.CostEstimate(
@@ -422,7 +426,7 @@
     def kernel(pick_ref, back_ref, residual_ref, gain_ref, cot_ref, grad_ref, branch_ref, gain_grad_ref):
         for block in range(width // 512):
             at = slice(block * 512, (block + 1) * 512)
-            back = back_ref[:, 0, :, at].reshape(slots, 512)
+            back = back_ref[:, :, at].reshape(slots, 512)
             grad_ref[:, at] = transposed_times(pick_ref[...], back)
         grad, grad_gain = norm_back(residual_ref[...], gain_ref[...], grad_ref[...])
         grad = grad + cot_ref[...].astype(f32)
@@ -449,7 +453,7 @@
         low = (back - high.astype(f32)).astype(bf16)
         for block in range(width // 512):
             at = slice(block * 512, (block + 1) * 512)
-            expert = back_ref[:, 1, :, at].reshape(slots, 512)
+            expert = back_ref[:, :, at].reshape(slots, 512)
             mixture = transposed_times(high, expert) + transposed_times(low, expert)
             out_ref[:, at] = (residual_ref[:, at] + mixture).astype(bf16)
 
@@ -471,8 +475,13 @@
     def kernel(
         grad_ref, query_ref, before_ref, own_ref, first_ref, cos_ref, sin_ref, place_ref, *refs
     ):
-        out_ref, prev_ref, self_ref, attended_ref, w_ref, sem = refs[2 * wide :]
+        out_ref, prev_ref, self_ref, attended_ref, prob_ref, w_ref, sem = refs[2 * wide :]
         copies = fetch_parts(place_ref, refs[:wide], refs[wide : 2 * wide], w_ref, sem)
+        allowed = allowed_keys(first_ref, rows)
+        for head in range(QUERY_HEADS):
+            at = slice(head * HEAD_SIZE, (head + 1) * HEAD_SIZE)
+            keys, _ = keys_and_values(before_ref, own_ref, head // GROUP)
+            prob_ref[head] = probabilities(query_ref[:, at], keys, allowed)
         for copy in copies:
             copy.wait()
         for half in range(2):
@@ -480,7 +489,6 @@
             weights = w_ref[half * (chips // 2) : (half + 1) * (chips // 2)]
             weights = weights.reshape(width // 2, width)
             attended_ref[:, at] = times_transposed(grad_ref[...], weights).astype(bf16)
-        allowed = allowed_keys(first_ref, rows)
         cos, sin = cos_ref[...], sin_ref[...]
         for group in range(KEY_VALUE_HEADS):
             keys, values = keys_and_values(before_ref, own_ref, group)
@@ -488,7 +496,7 @@
             for head in range(group * GROUP, (group + 1) * GROUP):
                 at = slice(head * HEAD_SIZE, (head + 1) * HEAD_SIZE)
                 query, upper = query_ref[:, at], attended_ref[:, at]
-                probs = probabilities(query, keys, allowed)
+                probs = prob_ref[head]
                 grad_probs = times_transposed(upper, values)
                 inner = jnp.sum(probs * grad_probs, axis=-1, keepdims=True)
                 raw = (probs * (grad_probs - inner) * SCALE).astype(bf16)
@@ -520,6 +528,7 @@
         flops=2 * rows * width * width + 20 * rows * rows * width,
         scratch=[
             pltpu.VMEM((rows, width), bf16),
+            pltpu.VMEM((QUERY_HEADS, rows, 2 * rows), f32),
             pltpu.VMEM((chips, 2, width // (2 * chips), width), bf16),
             pltpu.SemaphoreType.DMA((2 * wide,)),
         ],
@@ -611,17 +620,6 @@
     )(pieces)
 
 
-def after(value, *earlier):
-    for one in earlier:
-        zero = jnp.minimum(jnp.abs(one[(0,) * one.ndim].astype(f32)), 0.0)
-        value = value + zero.astype(value.dtype)
-    return value
-
-
-def to_square(value):
-    return jnp.stack([value, lax.ppermute(value, "x", SWAP)])
-
-
 def part_to_square(value, across, axis):
     size = value.shape[axis] // 2
     mine = lax.dynamic_slice_in_dim(value, across * size, size, axis)
@@ -696,7 +694,7 @@
     )[0]
 
 
-def qkv_weight_grads(near, far, grad_near, grad_far, ways):
+def qkv_weight_grads(near, far, grad_near, grad_far, ways, earlier):
     _, rows, width = near.shape
     heads = grad_far.shape[1]
     columns = heads * HEAD_SIZE
@@ -720,6 +718,7 @@
         kernel,
         [shaped((ways, width // ways, columns), bf16)],
         (core, near, far, grad_near, grad_far),
+        earlier,
         specs=[SCALAR, *([WHOLE] * 4)],
         flops=8 * width * rows * columns,
         scratch=[pltpu.VMEM((4 * rows, width), bf16), pltpu.VMEM((4 * rows, columns), bf16)],
@@ -779,7 +778,7 @@
     return call(kernel, [shaped((copies, squares, rows, columns), bf16)], (parts,), earlier)[0]
 
 
-def attention_outputs(tiles, query_width, kv_width):
+def attention_outputs(tiles, query_width, kv_width, earlier):
     count, squares, rows, column = tiles.shape
     heads = (query_width + kv_width) // column // squares
     outs = count - 1 - heads
@@ -809,6 +808,7 @@
             shaped((rows, column), f32),
         ],
         (tiles,),
+        earlier,
     )
 
 
@@ -854,7 +854,7 @@
         axis=1,
     )
     out_part = spread(out_part, experts, CHIPS)
-    expert_part = exchange(after(expert_part, out_part), CHIPS)
+    expert_part = exchange(hold((expert_part,), (out_part,))[0], CHIPS)
     gains_mine = out_part[:, rows_out : rows_out + 2, :owned]
     gains = in_core_order(core, gains_mine, lax.ppermute(gains_mine, "c", SWAP))
     gains = gains.transpose(2, 0, 1, 3).reshape(2, width).astype(f32)
@@ -870,12 +870,9 @@
     pick = picks.astype(bf16).reshape(experts * CAP, rows)
     slot_weight = jnp.sum(jnp.where(picks, weight.T[:, None, :], 0.0), axis=2)
     grad_out = matmul(pick, cotangent) * slot_weight.reshape(-1, 1)
-    grad_out_sent = after(grad_out, expert_part).astype(bf16)
+    grad_out_sent = hold((grad_out.astype(bf16),), (expert_part,))[0]
     grad_out = exchange(grad_out_sent, CHIPS)
 
-    expert_parts = lax.all_gather(
-        after(expert_part, *out_mine[1:], grad_out_sent), ("z", "c"), axis=0
-    )
 
     lengths = seq_lengths[0]
     starts = jnp.cumsum(lengths) - lengths
@@ -884,8 +881,9 @@
     cosine, sine = rotary_tables(row_at - first_at)
     first = (first_at - shard * rows).astype(jnp.int32)[:, None]
     normed, queries, keyval = project_qkv(
-        tokens, gain_attn, qkv_full, cosine, sine, ()
-    )
+        tokens, gain_attn, qkv_full, cosine, sine, (*out_mine[1:], expert_part, grad_out_sent)
+    )
+    expert_parts = lax.all_gather(hold((expert_part,), (queries,))[0], ("z", "c"), axis=0)
     ring = [(i, (i + 1) % shards) for i in range(shards)]
     back_ring = [((i + 1) % shards, i) for i in range(shards)]
     before = lax.ppermute(keyval, SHARD, ring)
@@ -894,11 +892,19 @@
     )
 
     picked = exchange(hold((picked,), (grad_out,))[0], CHIPS)
-    normed_near = to_square(after(normed, picked))
-    attended_near = to_square(after(attended_turned, picked))
-    returned, pieces = run_experts(picked, grad_out, expert_parts, rows_up, rows_down)
-    returned, pieces = hold((returned, pieces), (normed_near, attended_near))
+    normed, attended_turned = hold((normed, attended_turned), (picked,))
+    normed_moved = lax.ppermute(normed, "x", SWAP)
+    attended_moved = lax.ppermute(attended_turned, "x", SWAP)
+    returned, expert_rows, pieces = run_experts(
+        picked, grad_out, expert_parts, rows_up, rows_down
+    )
+    returned, expert_rows, pieces = hold(
+        (returned, expert_rows, pieces), (normed_moved, attended_moved)
+    )
+    normed_near = jnp.stack([normed, normed_moved])
+    attended_near = jnp.stack([attended_turned, attended_moved])
     returned = exchange(returned, CHIPS)
+    expert_rows = exchange(expert_rows, CHIPS)
     normed_far = lax.ppermute(normed_near, "c", SWAP)
     attended_far = lax.ppermute(attended_near, "c", SWAP)
     pieces = pieces.reshape(2 * wide_z, *pieces.shape[2:])
@@ -909,7 +915,6 @@
     )
     across = lax.axis_index("x")
     branch_near = part_to_square(grad_branch, across, 1)
-    over_rep = twice(over_z, (branch_near,))
     grad_queries, grad_before, grad_own = attend_back(
         grad_branch,
         out_mine,
@@ -920,35 +925,37 @@
         first,
         cosine,
         sine,
-        (over_rep,),
-    )
-    over_rep = exchange(over_rep, ("h", *CHIPS))
+        (),
+    )
+    from_next = lax.ppermute(grad_before, SHARD, back_ring)
+    grad_blocks = qkv_blocks_of(
+        grad_queries, grad_own, from_next, cosine, sine, ()
+    )
+
+    blocks_near = part_to_square(grad_blocks, across, 0)
+    doubled = twice(over_z, (expert_rows, blocks_near))
+    qkv_grads = qkv_weight_grads(
+        normed_near,
+        normed_far,
+        blocks_near,
+        part_to_core(blocks_near, core, 1),
+        lax.axis_size("y"),
+        (doubled,),
+    )
+    over_rep = exchange(doubled, ("h", *CHIPS))
     out_terms = out_weight_grads(
         attended_near,
         attended_far,
         branch_near,
         part_to_core(branch_near, core, 2),
         lax.axis_size("y"),
-        (grad_before,),
+        (doubled,),
     )
     out_grads = lax.psum_scatter(out_terms, "y", scatter_dimension=0, tiled=True)
-    from_next = lax.ppermute(grad_before, SHARD, back_ring)
-    grad_blocks = qkv_blocks_of(
-        grad_queries, grad_own, from_next, cosine, sine, (over_rep, out_terms)
-    )
-
-    blocks_near = part_to_square(grad_blocks, across, 0)
-    qkv_grads = qkv_weight_grads(
-        normed_near,
-        normed_far,
-        blocks_near,
-        part_to_core(blocks_near, core, 1),
-        lax.axis_size("y"),
-    )
-    over_rep = sum_of_halves(over_rep, (qkv_grads,))
     grad_tokens, tile = input_grad(
         grad_blocks, qkv_full, tokens, gain_attn, grad_residual, gain_grad, (qkv_grads,)
     )
+    over_rep = sum_of_halves(over_rep, (tile,))
     gain_terms = moved_over_y(tile.reshape(lax.axis_size("y"), -1, HEAD_SIZE))
     qkv_grads = exchange(qkv_grads, "y")
     shard_gateup, shard_down = expert_outputs(
@@ -956,13 +963,13 @@
     )
     reps = 2 * wide_z
     tiles = exchange(tiles_of(qkv_grads, out_grads.reshape(-1, part), gain_terms, reps, 4), REP + ("x", "c"))
-    tiles = exchange(sum_and_copy(tiles, 4, reps, (shard_down,)), REP)
+    tiles = exchange(sum_and_copy(tiles, 4, reps, ()), REP)
     grad_query, grad_keyval, grad_out_w, gain_sums = attention_outputs(
-        tiles, width, 2 * kv_width
+        tiles, width, 2 * kv_width, (shard_down,)
     )
 
     output = add_expert_rows(
-        pick, slot_weight.reshape(-1, 1), returned, residual, (qkv_grads,)
+        pick, slot_weight.reshape(-1, 1), expert_rows, residual, (qkv_grads,)
     )
     return (
         output,

time: 383 us -> 362 us (0.945); the launches traced: 375 us -> 361 us
  blocking collectives: 28.4 us -> 53.7 us
  waiting for transfers between devices: 138 us -> 117 us
  local copies, waits for them, and re-layouts: 25.7 us -> 20.2 us
  other arithmetic: 15.5 us -> 10.5 us
  between operations: 19 us -> 14.3 us
    all_to_all x1 -> x2, blocking collectives: 28.4 us -> 53.7 us  [exchange(): return lax.all_to_all(parts, axes, 0, 0, tiled=True)]
    ppermute x3, waiting for transfers between devices: 24.5 us -> 13.2 us  [gather_over_z(): lax.ppermute(part, 'z', [(i, i ^ k) for i in range(wide)])]
    all_to_all x8, waiting for transfers between devices: 68.1 us -> 59.5 us  [exchange(): return lax.all_to_all(parts, axes, 0, 0, tiled=True)]
    ppermute x3, waiting for transfers between devices: 11.9 us -> 18.9 us  [moved_over_y(): moved.append(lax.ppermute(sent, 'y', [(i, i ^ k) for i in range(wide)]))]
    ppermute x1, waiting for transfers between devices: 8.53 us -> 2.71 us  [per_device(): from_next = lax.ppermute(grad_before, SHARD, back_ring)]
    add x4 -> x0, other arithmetic: 4.85 us -> none  [after(): value = value + zero.astype(value.dtype)]
    ppermute x2, waiting for transfers between devices: 10.6 us -> 5.99 us  [part_to_square(): return jnp.stack([mine, lax.ppermute(sent, 'x', SWAP)])]
    slice x7 -> x0, local copies, waits for them, and re-layouts: 4.37 us -> none  [after(): zero = jnp.minimum(jnp.abs(one[(0,) * one.ndim].astype(f32)), 0.0)]
  transfers between devices with their start and end apart: 34 -> 34, of which waited for: 19 -> 17; matrix products, arithmetic and copies ran while one was open for 8% -> 5% of each run, Pallas kernels for 22% -> 21%
where the time goes in v7:
time: 362 us; the launch traced here: 361 us
  waiting for transfers between devices  117 us (32%)
  Pallas kernels  85 us (23%)
  starting transfers between devices  58.3 us (16%)
  blocking collectives  53.7 us (15%)
  local copies, waits for them, and re-layouts  20.2 us (6%)
  between operations  14.3 us (4%)
  other arithmetic  10.5 us (3%)
    all_to_all x8, waiting for transfers between devices, exchange(): return lax.all_to_all(parts, axes, 0, 0, tiled=True)  59.5 us
    pallas_call x14, Pallas kernels, call(): pl.pallas_call(body, in_specs=[*specs, *[UNUSED] * len(earlier)], out_spe...  55.6 us
    all_to_all x2, blocking collectives, exchange(): return lax.all_to_all(parts, axes, 0, 0, tiled=True)  53.7 us
    all_to_all x8, starting transfers between devices, exchange(): return lax.all_to_all(parts, axes, 0, 0, tiled=True)  37 us
    pallas_call x1, Pallas kernels, run_experts(): pl.pallas_call(kernel, in_specs=[UNUSED] * 3, out_specs=[UNUSED] * 3, out...  22.4 us
    ppermute x3, waiting for transfers between devices, moved_over_y(): moved.append(lax.ppermute(sent, 'y', [(i, i ^ k) for i in range(wide)]))  18.9 us
    ppermute x3, waiting for transfers between devices, gather_over_z(): lax.ppermute(part, 'z', [(i, i ^ k) for i in range(wide)])  13.2 us
    unnamed x70, local copies, waits for them, and re-layouts  10.6 us
  transfers between devices with their start and end apart: 34, of which 17 were waited for; matrix products, arithmetic and copies ran while one was open for 5% of the time, Pallas kernels for 21%

profile of v7, /device:TPU:0, one launch (start us, length us, event | category | flops | bytes accessed | tf_op | source)
XLA Modules:
  0.0 360.8 jit_solution(716479002715639375)
XLA Ops:
  11.8 5.5 %all-to-all-start = ((bf16[8,112,384]{2,1,0:T(8,128)(2,1)}), bf16[8,112,384]{2,1,0:T(8,128)(2,1)S(1)}, u32[]{:S(2)}, u32[]{:S(2)}) async-start(bf16[8,112,384]{2,1,0:T(8,128)(2,1)} %broadcast_in_dim.58), calls=%async_computation | async-start | bytes 1376256 | tf_op jit(solution)/shard_map/all_to_all | solution.py:33
  23.2 10.3 %all-to-all-done.refs_1_.refs_8_ = bf16[8,112,384]{2,1,0:T(8,128)(2,1)S(1)} async-done(((bf16[8,112,384]{2,1,0:T(8,128)(2,1)}), bf16[8,112,384]{2,1,0:T(8,128)(2,1)S(1)}, u32[]{:S(2)}, u32[]{:S(2)}) %all-to-all-start) | async-done | bytes 688160 | tf_op jit(solution)/shard_map/all_to_all | solution.py:33
  40.4 4.3 %collective-permute-start.2 = (bf16[8,112,384]{2,1,0:T(8,128)(2,1)}, bf16[8,112,384]{2,1,0:T(8,128)(2,1)S(1)}, u32[]{:S(2)}, u32[]{:S(2)}) collective-permute-start(bf16[8,112,384]{2,1,0:T(8,128)(2,1)} %copy-done.5), channel_id=1, source_target_pairs={{0,32},{16,48},{32,0},{48,16},{1,33},{17,49},{33,1},{49,17},{2,34}... | collective-permute-start | bytes 2064392 | tf_op jit(solution)/shard_map/ppermute | solution.py:591
  47.1 12.3 %all-to-all-done.1.refs_1_.refs_8_.refs_0_ = bf16[8,144,384]{2,1,0:T(8,128)(2,1)S(1)} async-done(((bf16[8,144,384]{2,1,0:T(8,128)(2,1)}), bf16[8,144,384]{2,1,0:T(8,128)(2,1)S(1)}, u32[]{:S(2)}, u32[]{:S(2)}) %all-to-all-start.1) | async-done | bytes 884768 | tf_op jit(solution)/shard_map/all_to_all | solution.py:33
  60.3 10.5 %collective-permute-done.2.refs_6_.refs_10_ = bf16[8,112,384]{2,1,0:T(8,128)(2,1)S(1)} collective-permute-done((bf16[8,112,384]{2,1,0:T(8,128)(2,1)}, bf16[8,112,384]{2,1,0:T(8,128)(2,1)S(1)}, u32[]{:S(2)}, u32[]{:S(2)}) %collective-permute-start.2) | collective-permute-done | bytes 688160 | tf_op jit(solution)/shard_map/ppermute | solution.py:591
  73.5 5.0 %shard_map.189 = (bf16[128,1536]{1,0:T(8,128)(2,1)}, bf16[128,1536]{1,0:T(8,128)(2,1)}, bf16[128,512]{1,0:T(8,128)(2,1)}) custom-call(bf16[128,1536]{1,0:T(8,128)(2,1)} %refs_2_.1, f32[1,1536]{1,0:T(1,128)} %slice.23.refs_1_.refs_3_, bf16[1536,2048]{1,0:T(8,128)(2,1)} %all-gather.6.cloned.1.call-done.refs_2_.refs_1_, ...), custom_call_target="tpu_custom_call" | custom-call | flops 805306368 | bytes 7739392 | tf_op jit(solution)/shard_map/pallas_call | solution.py:68
  78.6 5.4 %all-to-all-start.2 = ((bf16[8,80,1536]{2,1,0:T(8,128)(2,1)}), bf16[8,80,1536]{2,1,0:T(8,128)(2,1)}, u32[]{:S(2)}, u32[]{:S(2)}) async-start(bf16[8,80,1536]{2,1,0:T(8,128)(2,1)} %bitcast.13), calls=%async_computation.2 | async-start | bytes 3932160 | tf_op jit(solution)/shard_map/all_to_all | solution.py:33
  89.4 9.8 %collective-permute-done.4.refs_1_.refs_2_ = bf16[128,512]{1,0:T(8,128)(2,1)S(1)} collective-permute-done((bf16[128,512]{1,0:T(8,128)(2,1)S(1)}, bf16[128,512]{1,0:T(8,128)(2,1)S(1)}, u32[]{:S(2)}, u32[]{:S(2)}) %collective-permute-start.4) | collective-permute-done | bytes 131104 | tf_op jit(solution)/shard_map/ppermute | solution.py:889
  99.9 6.7 %shard_map.190 = (bf16[1536,128]{1,0:T(8,128)(2,1)}, f32[128,1536]{1,0:T(8,128)}, bf16[640,1536]{1,0:T(8,128)(2,1)}) custom-call(bf16[128,1536]{1,0:T(8,128)(2,1)} %get-tuple-element.37.refs_0_.refs_1_, bf16[128,512]{1,0:T(8,128)(2,1)} %copy-done.26, bf16[128,512]{1,0:T(8,128)(2,1)} %get-tuple-element.38.refs_2_.refs_3_, s32[128,1]{1,0:T(8,128)} %copy.59.refs_3_.refs_4_, ...), custom_call_target="tpu_custom_call" | custom-call | flops 805306368 | bytes 9869832 | tf_op jit(solution)/shard_map/pallas_call | solution.py:68
  106.6 28.2 %all_to_all.62 = bf16[8,80,1536]{2,1,0:T(8,128)(2,1)} all-to-all(bf16[8,80,1536]{2,1,0:T(8,128)(2,1)} %bitcast.54), channel_id=1, replica_groups=mesh['h'=2,'z'=4,'y'=4,'x'=2,'c'=2] {'y','x'}, dimensions={0} | all-to-all | bytes 3932160 | tf_op jit(solution)/shard_map/all_to_all | solution.py:33
  136.8 22.4 %shard_map.193 = (bf16[8,80,1536]{2,1,0:T(8,128)(2,1)}, bf16[8,80,1536]{2,1,0:T(8,128)(2,1)}, bf16[4,2,8,2,72,384]{5,4,3,2,1,0:T(8,128)(2,1)}) custom-call(bf16[640,1536]{1,0:T(8,128)(2,1)} %bitcast.53, bf16[640,1536]{1,0:T(8,128)(2,1)} %bitcast.14.refs_1_.grad_any, bf16[8,8,144,384]{3,2,1,0:T(8,128)(2,1)} %bitcast.71), custom_call_target="tpu_custom_call" | custom-call | flops 13589544960 | bytes 40108032 | tf_op jit(solution)/shard_map/pallas_call | solution.py:390
  164.9 20.8 %all-to-all-done.5.refs_1_ = bf16[8,80,1536]{2,1,0:T(8,128)(2,1)S(1)} async-done(((bf16[8,80,1536]{2,1,0:T(8,128)(2,1)}), bf16[8,80,1536]{2,1,0:T(8,128)(2,1)S(1)}, u32[]{:S(2)}, u32[]{:S(2)}) %all-to-all-start.5) | async-done | bytes 1966112 | tf_op jit(solution)/shard_map/all_to_all | solution.py:33
  194.3 4.1 %shard_map.196 = (f32[128,1536]{1,0:T(8,128)}, bf16[128,1536]{1,0:T(8,128)(2,1)}, f32[1536,128]{1,0:T(8,128)}) custom-call(bf16[640,128]{1,0:T(8,128)(2,1)} %get-tuple-element.80.refs_6_.refs_0_, bf16[8,80,1536]{2,1,0:T(8,128)(2,1)} %copy-done.7, f32[128,1536]{1,0:T(8,128)} %get-tuple-element.48.refs_2_.refs_3_, f32[1,1536]{1,0:T(1,128)} %slice.25.refs_5_.refs_3_, ...), custom_call_target="tpu_custom_call" | custom-call | flops 251658240 | bytes 5281792 | tf_op jit(solution)/shard_map/pallas_call | solution.py:68
  198.4 7.7 %shard_map.197 = (bf16[12,128,128]{2,1,0:T(8,128)(2,1)}, bf16[128,512]{1,0:T(8,128)(2,1)}, f32[128,512]{1,0:T(8,128)}) custom-call(bf16[128,1536]{1,0:T(8,128)(2,1)} %get-tuple-element.50.refs_0_, bf16[128,1536]{1,0:T(8,128)(2,1)} %get-tuple-element.37.refs_0_.refs_1_, bf16[128,512]{1,0:T(8,128)(2,1)} %copy-done.26, ...), custom_call_target="tpu_custom_call" | custom-call | flops 1107296256 | bytes 7471624 | tf_op jit(solution)/shard_map/pallas_call | solution.py:68
  206.1 3.9 %collective-permute-start.13 = (bf16[128,512]{1,0:T(8,128)(2,1)}, bf16[128,512]{1,0:T(8,128)(2,1)S(1)}, u32[]{:S(2)}, u32[]{:S(2)}) collective-permute-start(bf16[128,512]{1,0:T(8,128)(2,1)} %get-tuple-element.53), channel_id=1, source_target_pairs={{1,0},{2,1},{3,2},{4,3},{5,4},{6,5},{7,6},{8,7},{9,8},{10,9},{11,1... | collective-permute-start | bytes 393224 | tf_op jit(solution)/shard_map/ppermute | solution.py:930
  219.8 6.0 %collective-permute-done.14 = bf16[8,128,128]{2,1,0:T(8,128)(2,1)S(1)} collective-permute-done((bf16[8,128,128]{2,1,0:T(8,128)(2,1)S(1)}, bf16[8,128,128]{2,1,0:T(8,128)(2,1)S(1)}, u32[]{:S(2)}, u32[]{:S(2)}) %collective-permute-start.14) | collective-permute-done | bytes 262176 | tf_op jit(solution)/shard_map/ppermute | solution.py:627
  234.0 5.8 %all-to-all-start.9 = ((bf16[16,2,72,384]{3,2,1,0:T(8,128)(2,1)}), bf16[16,2,72,384]{3,2,1,0:T(8,128)(2,1)S(1)}, u32[]{:S(2)}, u32[]{:S(2)}) async-start(bf16[16,2,72,384]{3,2,1,0:T(8,128)(2,1)} %shard_map.199.refs_5_), calls=%async_computation.11 | async-start | bytes 3538944 | tf_op jit(solution)/shard_map/all_to_all | solution.py:33
  242.2 3.8 %shard_map.200.refs_6_ = bf16[4,384,512]{2,1,0:T(8,128)(2,1)} custom-call(s32[1]{0:T(128)} %bitcast.11.refs_0_, bf16[2,128,1536]{2,1,0:T(8,128)(2,1)} %pad_maximum_fusion.1.refs_1_, bf16[2,128,1536]{2,1,0:T(8,128)(2,1)} %copy-done.14, bf16[2,8,128,128]{3,2,1,0:T(8,128)(2,1)} %pad_maximum_fusion.3.refs_2_.refs_3_, bf16[2,4,128,128]{3,2,1,0:T(8,128)(2,1)} %copy-done.27, ...), custom_call_target="tpu_custom_call" | custom-call | flops 805306368 | bytes 3932164 | tf_op jit(solution)/shard_map/pallas_call | solution.py:68
  246.1 6.7 %shard_map.202 = (bf16[128,1536]{1,0:T(8,128)(2,1)}, bf16[1536,128]{1,0:T(8,128)(2,1)}) custom-call(bf16[16,128,128]{2,1,0:T(8,128)(2,1)} %shard_map.198.refs_0_, bf16[1536,2048]{1,0:T(8,128)(2,1)} %all-gather.6.cloned.1.call-done.refs_2_.refs_1_, bf16[128,1536]{1,0:T(8,128)(2,1)} %refs_2_.1, f32[1,1536]{1,0:T(1,128)} %slice.23.refs_1_.refs_3_, ...), custom_call_target="tpu_custom_call" | custom-call | flops 805306368 | bytes 9574400 | tf_op jit(solution)/shard_map/pallas_call | solution.py:68
  252.8 14.4 %all-to-all-done.9.refs_0_ = bf16[16,2,72,384]{3,2,1,0:T(8,128)(2,1)S(1)} async-done(((bf16[16,2,72,384]{3,2,1,0:T(8,128)(2,1)}), bf16[16,2,72,384]{3,2,1,0:T(8,128)(2,1)S(1)}, u32[]{:S(2)}, u32[]{:S(2)}) %all-to-all-start.9) | async-done | bytes 1769504 | tf_op jit(solution)/shard_map/all_to_all | solution.py:33
  280.1 16.3 %collective-permute-done.18.refs_3_ = bf16[384,128]{1,0:T(8,128)(2,1)S(1)} collective-permute-done((bf16[384,128]{1,0:T(8,128)(2,1)S(1)}, bf16[384,128]{1,0:T(8,128)(2,1)S(1)}, u32[]{:S(2)}, u32[]{:S(2)}) %collective-permute-start.18) | collective-permute-done | bytes 98336 | tf_op jit(solution)/shard_map/ppermute | solution.py:734
  303.0 25.5 %all_to_all.63.refs_0_ = bf16[32,96,128]{2,1,0:T(8,128)(2,1)} all-to-all(bf16[32,96,128]{2,1,0:T(8,128)(2,1)} %shard_map.204), channel_id=1, replica_groups=mesh['h'=2,'z'=4,'y'=4,'x'=2,'c'=2] {'h','z','x','c'}, dimensions={0} | all-to-all | bytes 1572864 | tf_op jit(solution)/shard_map/all_to_all | solution.py:33
  330.6 5.5 %all-to-all-start.8 = ((bf16[8,4,96,128]{3,2,1,0:T(8,128)(2,1)}), bf16[8,4,96,128]{3,2,1,0:T(8,128)(2,1)S(1)}, u32[]{:S(2)}, u32[]{:S(2)}) async-start(bf16[8,4,96,128]{3,2,1,0:T(8,128)(2,1)} %shard_map.205), calls=%async_computation.10 | async-start | bytes 1572864 | tf_op jit(solution)/shard_map/all_to_all | solution.py:33
  340.6 7.0 %shard_map.207 = (f32[8,96,1536]{2,1,0:T(8,128)}, f32[8,48,1536]{2,1,0:T(8,128)}) custom-call(bf16[4,8,2,72,384]{4,3,2,1,0:T(8,128)(2,1)} %bitcast.55), custom_call_target="tpu_custom_call" | custom-call | tf_op jit(solution)/shard_map/pallas_call | solution.py:608
  (193 shorter events, 98.6 us)
Async XLA Ops:
  7.2 66.3 %all-gather.6.cloned.1.call-start = ((), (), s32[]{:S(2)}) async-start(), calls=%async_computation.12 | async-start | bytes 6684672 | tf_op jit(solution)/shard_map/all_gather | solution.py:839
  11.8 21.7 %all-to-all-start = ((bf16[8,112,384]{2,1,0:T(8,128)(2,1)}), bf16[8,112,384]{2,1,0:T(8,128)(2,1)S(1)}, u32[]{:S(2)}, u32[]{:S(2)}) async-start(bf16[8,112,384]{2,1,0:T(8,128)(2,1)} %broadcast_in_dim.58), calls=%async_computation | async-start | bytes 1376256 | tf_op jit(solution)/shard_map/all_to_all | solution.py:33
  34.3 25.0 %all-to-all-start.1 = ((bf16[8,144,384]{2,1,0:T(8,128)(2,1)}), bf16[8,144,384]{2,1,0:T(8,128)(2,1)S(1)}, u32[]{:S(2)}, u32[]{:S(2)}) async-start(bf16[8,144,384]{2,1,0:T(8,128)(2,1)} %shard_map.187), calls=%async_computation.1 | async-start | bytes 1769472 | tf_op jit(solution)/shard_map/all_to_all | solution.py:33
  38.0 98.8 %all-gather.8.cloned.1.call-start = ((), (), s32[]{:S(2)}) async-start(), calls=%async_computation.15 | async-start | bytes 7962624 | tf_op jit(solution)/shard_map/all_gather | solution.py:886
  38.1 22.2 %collective-permute-start.1 = (bf16[8,112,384]{2,1,0:T(8,128)(2,1)}, bf16[8,112,384]{2,1,0:T(8,128)(2,1)S(1)}, u32[]{:S(2)}, u32[]{:S(2)}) collective-permute-start(bf16[8,112,384]{2,1,0:T(8,128)(2,1)} %copy-done.5), channel_id=1, source_target_pairs={{0,16},{16,0},{32,48},{48,32},{1,17},{17,1},{33,49},{49,33},{2,18}... | collective-permute-start | bytes 2064392 | tf_op jit(solution)/shard_map/ppermute | solution.py:591
  40.4 30.4 %collective-permute-start.2 = (bf16[8,112,384]{2,1,0:T(8,128)(2,1)}, bf16[8,112,384]{2,1,0:T(8,128)(2,1)S(1)}, u32[]{:S(2)}, u32[]{:S(2)}) collective-permute-start(bf16[8,112,384]{2,1,0:T(8,128)(2,1)} %copy-done.5), channel_id=1, source_target_pairs={{0,32},{16,48},{32,0},{48,16},{1,33},{17,49},{33,1},{49,17},{2,34}... | collective-permute-start | bytes 2064392 | tf_op jit(solution)/shard_map/ppermute | solution.py:591
  44.8 28.8 %collective-permute-start.3 = (bf16[8,112,384]{2,1,0:T(8,128)(2,1)}, bf16[8,112,384]{2,1,0:T(8,128)(2,1)}, u32[]{:S(2)}, u32[]{:S(2)}) collective-permute-start(bf16[8,112,384]{2,1,0:T(8,128)(2,1)} %copy-done.5), channel_id=1, source_target_pairs={{0,48},{16,32},{32,16},{48,0},{1,49},{17,33},{33,17},{49,1},{2,50}... | collective-permute-start | bytes 2064392 | tf_op jit(solution)/shard_map/ppermute | solution.py:591
  78.6 28.0 %all-to-all-start.2 = ((bf16[8,80,1536]{2,1,0:T(8,128)(2,1)}), bf16[8,80,1536]{2,1,0:T(8,128)(2,1)}, u32[]{:S(2)}, u32[]{:S(2)}) async-start(bf16[8,80,1536]{2,1,0:T(8,128)(2,1)} %bitcast.13), calls=%async_computation.2 | async-start | bytes 3932160 | tf_op jit(solution)/shard_map/all_to_all | solution.py:33
  84.0 142.6 %reduce-scatter.3.cloned.1.call-start = ((), (), s32[]{:S(2)}) async-start(), calls=%async_computation.13 | async-start | bytes 7962624 | tf_op jit(solution)/shard_map/reduce_scatter | solution.py:911
  85.1 14.1 %collective-permute-start.4 = (bf16[128,512]{1,0:T(8,128)(2,1)S(1)}, bf16[128,512]{1,0:T(8,128)(2,1)S(1)}, u32[]{:S(2)}, u32[]{:S(2)}) collective-permute-start(bf16[128,512]{1,0:T(8,128)(2,1)S(1)} %copy-done.25), channel_id=1, source_target_pairs={{0,1},{1,2},{2,3},{3,4},{4,5},{5,6},{6,7},{7,8},{8,9},{9,10},{10,1... | collective-permute-start | bytes 393224 | tf_op jit(solution)/shard_map/ppermute | solution.py:889
  134.8 24.4 %collective-permute-start.9 = (bf16[128,1536]{1,0:T(8,128)(2,1)}, bf16[128,1536]{1,0:T(8,128)(2,1)S(1)}, u32[]{:S(2)}, u32[]{:S(2)}) collective-permute-start(bf16[128,1536]{1,0:T(8,128)(2,1)} %get-tuple-element.45), channel_id=1, source_target_pairs={{0,2},{2,0},{1,3},{3,1},{4,6},{6,4},{5,7},{7,5},{8,10},{10,8},{9,1... | collective-permute-start | bytes 1179656 | tf_op jit(solution)/shard_map/ppermute | solution.py:896
  135.5 23.7 %collective-permute-start.10 = (bf16[1536,128]{1,0:T(8,128)(2,1)}, bf16[1536,128]{1,0:T(8,128)(2,1)S(1)}, u32[]{:S(2)}, u32[]{:S(2)}) collective-permute-start(bf16[1536,128]{1,0:T(8,128)(2,1)} %get-tuple-element.46), channel_id=1, source_target_pairs={{0,2},{2,0},{1,3},{3,1},{4,6},{6,4},{5,7},{7,5},{8,10},{10,8},{9,1... | collective-permute-start | bytes 1179656 | tf_op jit(solution)/shard_map/ppermute | solution.py:897
  160.2 25.6 %all-to-all-start.5 = ((bf16[8,80,1536]{2,1,0:T(8,128)(2,1)}), bf16[8,80,1536]{2,1,0:T(8,128)(2,1)S(1)}, u32[]{:S(2)}, u32[]{:S(2)}) async-start(bf16[8,80,1536]{2,1,0:T(8,128)(2,1)} %get-tuple-element.49), calls=%async_computation.5 | async-start | bytes 3932160 | tf_op jit(solution)/shard_map/all_to_all | solution.py:33
  164.9 26.8 %collective-permute-start.11 = (bf16[2,128,1536]{2,1,0:T(8,128)(2,1)}, bf16[2,128,1536]{2,1,0:T(8,128)(2,1)S(1)}, u32[]{:S(2)}, u32[]{:S(2)}) collective-permute-start(bf16[2,128,1536]{2,1,0:T(8,128)(2,1)} %pad_maximum_fusion.1.refs_1_), channel_id=1, source_target_pairs={{0,1},{1,0},{2,3},{3,2},{4,5},{5,4},{6,7},{7,6},{8,9},{9,8},{10,11... | collective-permute-start | bytes 2359304 | tf_op jit(solution)/shard_map/ppermute | solution.py:908
  187.0 39.6 %all-to-all-start.4 = ((bf16[8,80,1536]{2,1,0:T(8,128)(2,1)}), bf16[8,80,1536]{2,1,0:T(8,128)(2,1)S(1)}, u32[]{:S(2)}, u32[]{:S(2)}) async-start(bf16[8,80,1536]{2,1,0:T(8,128)(2,1)} %get-tuple-element.47), calls=%async_computation.4 | async-start | bytes 3932160 | tf_op jit(solution)/shard_map/all_to_all | solution.py:33
  190.6 108.4 %reduce-scatter.5.cloned.1.call-start = ((), (), s32[]{:S(2)}) async-start(), calls=%async_computation.14 | async-start | bytes 1474560 | tf_op jit(solution)/shard_map/reduce_scatter | solution.py:954
  217.4 13.0 %collective-permute-start.17 = (bf16[2,128,384]{2,1,0:T(8,128)(2,1)S(1)}, bf16[2,128,384]{2,1,0:T(8,128)(2,1)}, u32[]{:S(2)}, u32[]{:S(2)}) collective-permute-start(bf16[2,128,384]{2,1,0:T(8,128)(2,1)S(1)} %fusion.1), channel_id=1, source_target_pairs={{0,1},{1,0},{2,3},{3,2},{4,5},{5,4},{6,7},{7,6},{8,9},{9,8},{10,11... | collective-permute-start | bytes 589832 | tf_op jit(solution)/shard_map/ppermute | solution.py:632
  234.0 33.1 %all-to-all-start.9 = ((bf16[16,2,72,384]{3,2,1,0:T(8,128)(2,1)}), bf16[16,2,72,384]{3,2,1,0:T(8,128)(2,1)S(1)}, u32[]{:S(2)}, u32[]{:S(2)}) async-start(bf16[16,2,72,384]{3,2,1,0:T(8,128)(2,1)} %shard_map.199.refs_5_), calls=%async_computation.11 | async-start | bytes 3538944 | tf_op jit(solution)/shard_map/all_to_all | solution.py:33
  239.8 100.8 %all-gather.10.cloned.1.call-start = ((), (), s32[]{:S(2)}) async-start(), calls=%async_computation.16 | async-start | bytes 4423680 | tf_op jit(solution)/shard_map/all_gather | solution.py:962
  271.0 28.0 %all-to-all-start.6 = ((bf16[4,384,512]{2,1,0:T(8,128)(2,1)}), bf16[4,384,512]{2,1,0:T(8,128)(2,1)S(1)}, u32[]{:S(2)}, u32[]{:S(2)}) async-start(bf16[4,384,512]{2,1,0:T(8,128)(2,1)} %shard_map.200.refs_6_), calls=%async_computation.7 | async-start | bytes 3145728 | tf_op jit(solution)/shard_map/all_to_all | solution.py:33
  275.4 21.0 %collective-permute-start.18 = (bf16[384,128]{1,0:T(8,128)(2,1)S(1)}, bf16[384,128]{1,0:T(8,128)(2,1)S(1)}, u32[]{:S(2)}, u32[]{:S(2)}) collective-permute-start(bf16[384,128]{1,0:T(8,128)(2,1)S(1)} %get-tuple-element.73), channel_id=1, source_target_pairs={{0,4},{4,0},{8,12},{12,8},{1,5},{5,1},{9,13},{13,9},{2,6},{6,2},{1... | collective-permute-start | bytes 294920 | tf_op jit(solution)/shard_map/ppermute | solution.py:734
  277.4 21.7 %collective-permute-start.19 = (bf16[384,128]{1,0:T(8,128)(2,1)S(1)}, bf16[384,128]{1,0:T(8,128)(2,1)S(1)}, u32[]{:S(2)}, u32[]{:S(2)}) collective-permute-start(bf16[384,128]{1,0:T(8,128)(2,1)S(1)} %get-tuple-element.72), channel_id=1, source_target_pairs={{0,8},{4,12},{8,0},{12,4},{1,9},{5,13},{9,1},{13,5},{2,10},{6,14},... | collective-permute-start | bytes 294920 | tf_op jit(solution)/shard_map/ppermute | solution.py:734
  280.1 19.0 %collective-permute-start.20 = (bf16[384,128]{1,0:T(8,128)(2,1)S(1)}, bf16[384,128]{1,0:T(8,128)(2,1)S(1)}, u32[]{:S(2)}, u32[]{:S(2)}) collective-permute-start(bf16[384,128]{1,0:T(8,128)(2,1)S(1)} %get-tuple-element.71), channel_id=1, source_target_pairs={{0,12},{4,8},{8,4},{12,0},{1,13},{5,9},{9,5},{13,1},{2,14},{6,10},... | collective-permute-start | bytes 294920 | tf_op jit(solution)/shard_map/ppermute | solution.py:734
  330.6 18.9 %all-to-all-start.8 = ((bf16[8,4,96,128]{3,2,1,0:T(8,128)(2,1)}), bf16[8,4,96,128]{3,2,1,0:T(8,128)(2,1)S(1)}, u32[]{:S(2)}, u32[]{:S(2)}) async-start(bf16[8,4,96,128]{3,2,1,0:T(8,128)(2,1)} %shard_map.205), calls=%async_computation.10 | async-start | bytes 1572864 | tf_op jit(solution)/shard_map/all_to_all | solution.py:33
  (45 other events, 213.4 us)
Sparse Core Ops, SparseCore 0:
  10.3 57.4 all-gather.5
  78.7 42.9 all-gather.7
  160.3 50.9 reduce-scatter.2
  234.1 40.1 reduce-scatter.4
  275.8 55.0 all-gather.9

commit v8 on v7

--- a/solution.py
+++ b/solution.py
@@ -23,7 +23,7 @@
 bf16 = jnp.bfloat16
 f32 = jnp.float32
 
-VMEM_LIMIT = 60 * 1024 * 1024
+VMEM_LIMIT = 63 * 1024 * 1024
 WHOLE = pl.BlockSpec(memory_space=pltpu.VMEM)
 UNUSED = pl.BlockSpec(memory_space=pl.ANY)
 SCALAR = pl.BlockSpec(memory_space=pltpu.SMEM)
@@ -268,37 +268,34 @@
     )
 
 
+def expert_copies(part_ref, to_ref, base, rows, semaphores):
+    ways, part = part_ref.shape[0], part_ref.shape[3]
+    return [
+        pltpu.make_async_copy(
+            part_ref.at[i, :, pl.ds(base, rows), :],
+            to_ref.at[:, i % 2, :, pl.ds(i // 2 * part, part)],
+            semaphores.at[i],
+        )
+        for i in range(ways)
+    ]
+
+
 def run_experts(picked, grad_out, parts, rows_up, rows_down):
     slots, width = picked.shape
     ways, chips, _, part = parts.shape
-    wide = ways // 2
     ff = chips * 2 * rows_down
     each = slots // chips
-    half = (rows_up + rows_down) // 2
     near = chips // 2
 
     def kernel(
-        picked_any, grad_any, part_ref, back_any, expert_any, piece_any,
-        picked_ref, grad_ref, up_w, down_w, gate_ref, upper_ref, acted_ref, pre_ref, back_ref, expert_ref,
-        keep_ref, piece_ref, in_sem, up_sem, down_sem, out_sem,
+        picked_any, grad_any, part_ref, back_any, acted_any, pre_any,
+        picked_ref, grad_ref, up_w, down_w, gate_ref, upper_ref, acted_ref, pre_ref, back_ref,
+        in_sem, up_sem, down_sem, out_sem,
     ):
         rows_in = pltpu.make_async_copy(picked_any, picked_ref, in_sem.at[0])
         grads_in = pltpu.make_async_copy(grad_any, grad_ref, in_sem.at[1])
-        ups, downs = [], []
-        for i in range(ways):
-            to = pl.ds(i // 2 * part, part)
-            ups.append(
-                pltpu.make_async_copy(
-                    part_ref.at[i, :, pl.ds(0, rows_up), :], up_w.at[:, i % 2, :, to], up_sem.at[i]
-                )
-            )
-            downs.append(
-                pltpu.make_async_copy(
-                    part_ref.at[i, :, pl.ds(rows_up, rows_down), :],
-                    down_w.at[:, i % 2, :, to],
-                    down_sem.at[i],
-                )
-            )
+        ups = expert_copies(part_ref, up_w, 0, rows_up, up_sem)
+        downs = expert_copies(part_ref, down_w, rows_up, rows_down, down_sem)
         for copy in [rows_in, *ups, grads_in, *downs]:
             copy.start()
         for copy in [rows_in, *ups]:
@@ -328,22 +325,88 @@
             upper = pl.ds(pl.multiple_of(ff + j * (ff // 2), 128), ff // 2)
             pre_ref[:, upper] = (grad_act * silu).astype(bf16)
 
+        outs = [
+            pltpu.make_async_copy(acted_ref, acted_any, out_sem.at[0]),
+            pltpu.make_async_copy(pre_ref, pre_any, out_sem.at[1]),
+        ]
+        for copy in outs:
+            copy.start()
         columns = width // 2
-
-        @pl.loop(0, 2)
-        def _(j):
-            to = pl.ds(pl.multiple_of(j * columns, 128), columns)
-            weights = up_w[pl.ds(j * near, near)].reshape(columns, 2 * ff)
+        for j in range(2):
+            to = slice(j * columns, (j + 1) * columns)
+            weights = up_w[j * near : (j + 1) * near].reshape(columns, 2 * ff)
             back = times_transposed(pre_ref[...], weights).astype(bf16)
             back_ref[:, :, to] = back.reshape(chips, each, columns)
-            weights = down_w[:, :, :, to].reshape(ff, columns)
-            forward = matmul(acted_ref[...], weights).astype(bf16)
-            expert_ref[:, :, to] = forward.reshape(chips, each, columns)
-
-        back_out = pltpu.make_async_copy(back_ref, back_any, out_sem.at[0])
-        expert_out = pltpu.make_async_copy(expert_ref, expert_any, out_sem.at[3])
-        back_out.start()
-        expert_out.start()
+            copy = pltpu.make_async_copy(
+                back_ref.at[:, :, to], back_any.at[:, :, to], out_sem.at[2 + j]
+            )
+            copy.start()
+            outs.append(copy)
+        for copy in outs:
+            copy.wait()
+
+    back = shaped((chips, each, width), bf16)
+    return pl.pallas_call(
+        kernel,
+        in_specs=[UNUSED] * 3,
+        out_specs=[UNUSED] * 3,
+        out_shape=[back, shaped((slots, ff), bf16), shaped((slots, 2 * ff), bf16)],
+        scratch_shapes=[
+            pltpu.VMEM((slots, width), bf16),
+            pltpu.VMEM((slots, width), bf16),
+            pltpu.VMEM((chips, 2, rows_up, width), bf16),
+            pltpu.VMEM((chips, 2, rows_down, width), bf16),
+            pltpu.VMEM((slots, ff), f32),
+            pltpu.VMEM((slots, ff), f32),
+            pltpu.VMEM((slots, ff), bf16),
+            pltpu.VMEM((slots, 2 * ff), bf16),
+            pltpu.VMEM(back.shape, bf16),
+            pltpu.SemaphoreType.DMA((2,)),
+            pltpu.SemaphoreType.DMA((ways,)),
+            pltpu.SemaphoreType.DMA((ways,)),
+            pltpu.SemaphoreType.DMA((4,)),
+        ],
+        compiler_params=pltpu.CompilerParams(vmem_limit_bytes=VMEM_LIMIT),
+        cost_estimate=pl.CostEstimate(
+            flops=2 * slots * 5 * width * ff,
+            bytes_accessed=12 * slots * width + 2 * width * 3 * ff,
+            transcendentals=0,
+        ),
+    )(picked, grad_out, parts)
+
+
+def expert_weight_grads(picked, grad_out, acted, grad_pre, parts, rows_up, rows_down, earlier):
+    slots, width = picked.shape
+    ways, chips, _, part = parts.shape
+    wide = ways // 2
+    ff = acted.shape[1]
+    each = slots // chips
+    half = (rows_up + rows_down) // 2
+    near = chips // 2
+    columns = width // 2
+
+    def kernel(picked_any, grad_any, acted_any, pre_any, part_ref, *refs):
+        expert_any, piece_any = refs[len(earlier) : len(earlier) + 2]
+        (
+            picked_ref, grad_ref, acted_ref, pre_ref, down_w, expert_ref, keep_ref, piece_ref,
+            in_sem, down_sem, out_sem,
+        ) = refs[len(earlier) + 2 :]
+        ins = [
+            pltpu.make_async_copy(source, to, in_sem.at[i])
+            for i, (source, to) in enumerate(
+                (
+                    (picked_any, picked_ref),
+                    (pre_any, pre_ref),
+                    (acted_any, acted_ref),
+                    (grad_any, grad_ref),
+                )
+            )
+        ]
+        downs = expert_copies(part_ref, down_w, rows_up, rows_down, down_sem)
+        for copy in ins + downs:
+            copy.start()
+        for copy in ins:
+            copy.wait()
 
         @pl.loop(0, 2)
         def _(s):
@@ -374,49 +437,52 @@
                             piece_ref[z, c, s * near + k, 1] = rest[:, j * part : (j + 1) * part]
             chip = pl.ds(s * near, near)
             pltpu.make_async_copy(
-                piece_ref.at[:, :, chip], piece_any.at[:, :, chip], out_sem.at[1 + s]
+                piece_ref.at[:, :, chip], piece_any.at[:, :, chip], out_sem.at[s]
             ).start()
 
-        back_out.wait()
-        expert_out.wait()
+        for copy in downs:
+            copy.wait()
+        for j in range(2):
+            to = slice(j * columns, (j + 1) * columns)
+            weights = down_w[:, :, :, to].reshape(ff, columns)
+            forward = matmul(acted_ref[...], weights).astype(bf16)
+            expert_ref[:, :, to] = forward.reshape(chips, each, columns)
+        expert_out = pltpu.make_async_copy(expert_ref, expert_any, out_sem.at[2])
+        expert_out.start()
         for s in range(2):
             chip = pl.ds(s * near, near)
             pltpu.make_async_copy(
-                piece_ref.at[:, :, chip], piece_any.at[:, :, chip], out_sem.at[1 + s]
+                piece_ref.at[:, :, chip], piece_any.at[:, :, chip], out_sem.at[s]
             ).wait()
-
-    back = shaped((chips, each, width), bf16)
+        expert_out.wait()
+
+    expert = shaped((chips, each, width), bf16)
     pieces = shaped((wide, 2, chips, 2, half, part), bf16)
     return pl.pallas_call(
         kernel,
-        in_specs=[UNUSED] * 3,
-        out_specs=[UNUSED] * 3,
-        out_shape=[back, back, pieces],
+        in_specs=[UNUSED] * (5 + len(earlier)),
+        out_specs=[UNUSED] * 2,
+        out_shape=[expert, pieces],
         scratch_shapes=[
             pltpu.VMEM((slots, width), bf16),
             pltpu.VMEM((slots, width), bf16),
-            pltpu.VMEM((chips, 2, rows_up, width), bf16),
-            pltpu.VMEM((chips, 2, rows_down, width), bf16),
-            pltpu.VMEM((slots, ff), f32),
-            pltpu.VMEM((slots, ff), f32),
             pltpu.VMEM((slots, ff), bf16),
             pltpu.VMEM((slots, 2 * ff), bf16),
-            pltpu.VMEM(back.shape, bf16),
-            pltpu.VMEM(back.shape, bf16),
-            pltpu.VMEM((near, 2, rows_up - half, width // 2), f32),
+            pltpu.VMEM((chips, 2, rows_down, width), bf16),
+            pltpu.VMEM(expert.shape, bf16),
+            pltpu.VMEM((near, 2, rows_up - half, columns), f32),
             pltpu.VMEM(pieces.shape, bf16),
-            pltpu.SemaphoreType.DMA((2,)),
+            pltpu.SemaphoreType.DMA((4,)),
             pltpu.SemaphoreType.DMA((ways,)),
-            pltpu.SemaphoreType.DMA((ways,)),
-            pltpu.SemaphoreType.DMA((4,)),
+            pltpu.SemaphoreType.DMA((3,)),
         ],
         compiler_params=pltpu.CompilerParams(vmem_limit_bytes=VMEM_LIMIT),
         cost_estimate=pl.CostEstimate(
-            flops=2 * slots * 9 * width * ff,
-            bytes_accessed=12 * slots * width + 8 * width * 3 * ff,
+            flops=2 * slots * 4 * width * ff,
+            bytes_accessed=10 * slots * width + 8 * width * 3 * ff,
             transcendentals=0,
         ),
-    )(picked, grad_out, parts)
+    )(picked, grad_out, acted, grad_pre, parts, *earlier)
 
 
 def residual_grad(pick, returned, residual, gain, cotangent, earlier):
@@ -895,16 +961,14 @@
     normed, attended_turned = hold((normed, attended_turned), (picked,))
     normed_moved = lax.ppermute(normed, "x", SWAP)
     attended_moved = lax.ppermute(attended_turned, "x", SWAP)
-    returned, expert_rows, pieces = run_experts(
-        picked, grad_out, expert_parts, rows_up, rows_down
-    )
-    returned, expert_rows, pieces = hold(
-        (returned, expert_rows, pieces), (normed_moved, attended_moved)
+    returned, acted, grad_pre = run_experts(picked, grad_out, expert_parts, rows_up, rows_down)
+    returned = hold((returned,), (normed_moved, attended_moved))[0]
+    expert_rows, pieces = expert_weight_grads(
+        picked, grad_out, acted, grad_pre, expert_parts, rows_up, rows_down, (returned,)
     )
     normed_near = jnp.stack([normed, normed_moved])
     attended_near = jnp.stack([attended_turned, attended_moved])
-    returned = exchange(returned, CHIPS)
-    expert_rows = exchange(expert_rows, CHIPS)
+    returned, expert_rows, pieces = hold((exchange(returned, CHIPS), expert_rows, pieces), ())
     normed_far = lax.ppermute(normed_near, "c", SWAP)
     attended_far = lax.ppermute(attended_near, "c", SWAP)
     pieces = pieces.reshape(2 * wide_z, *pieces.shape[2:])
@@ -913,6 +977,7 @@
     grad_residual, grad_branch, gain_grad = residual_grad(
         pick, returned, residual, gain_ffn, cotangent, (normed_far, attended_far)
     )
+    expert_rows = exchange(expert_rows, CHIPS)
     across = lax.axis_index("x")
     branch_near = part_to_square(grad_branch, across, 1)
     grad_queries, grad_before, grad_own = attend_back(

time: 362 us -> 359 us (level)
  waiting for transfers between devices: 117 us -> 106 us
  starting transfers between devices: 58.3 us -> 62.5 us
    all_to_all x8, waiting for transfers between devices: 59.5 us -> 42.5 us  [exchange(): return lax.all_to_all(parts, axes, 0, 0, tiled=True)]
    pallas_call x0 -> x1, Pallas kernels: none -> 12.1 us  [expert_weight_grads(): pl.pallas_call(kernel, in_specs=[UNUSED] * (5 + len(earlier)), out_specs=...]
    pallas_call x1, Pallas kernels: 22.4 us -> 13.9 us  [run_experts(): pl.pallas_call(kernel, in_specs=[UNUSED] * 3, out_specs=[UNUSED] * 3, out...]
    reduce_scatter x1, waiting for transfers between devices: 0.01 us -> 6 us  [per_device(): lax.psum_scatter(pieces, ('z', 'c'), scatter_dimension=0, tiled=False)]
    unnamed x70 -> x58, local copies, waits for them, and re-layouts: 10.6 us -> 11 us
  transfers between devices with their start and end apart: 34 -> 34, of which waited for: 17 -> 18; matrix products, arithmetic and copies ran while one was open for 5% -> 5% of each run, Pallas kernels for 21% -> 22%
where the time goes in v8:
time: 359 us; the launch traced here: 357 us
  waiting for transfers between devices  106 us (30%)
  Pallas kernels  88.2 us (25%)
  starting transfers between devices  62.5 us (17%)
  blocking collectives  52.7 us (15%)
  local copies, waits for them, and re-layouts  21.4 us (6%)
  between operations  14.3 us (4%)
  other arithmetic  10.3 us (3%)
    pallas_call x14, Pallas kernels, call(): pl.pallas_call(body, in_specs=[*specs, *[UNUSED] * len(earlier)], out_spe...  55.3 us
    all_to_all x2, blocking collectives, exchange(): return lax.all_to_all(parts, axes, 0, 0, tiled=True)  52.7 us
    all_to_all x8, waiting for transfers between devices, exchange(): return lax.all_to_all(parts, axes, 0, 0, tiled=True)  42.5 us
    all_to_all x8, starting transfers between devices, exchange(): return lax.all_to_all(parts, axes, 0, 0, tiled=True)  40.2 us
    ppermute x3, waiting for transfers between devices, moved_over_y(): moved.append(lax.ppermute(sent, 'y', [(i, i ^ k) for i in range(wide)]))  18.4 us
    pallas_call x1, Pallas kernels, run_experts(): pl.pallas_call(kernel, in_specs=[UNUSED] * 3, out_specs=[UNUSED] * 3, out...  13.9 us
    ppermute x3, waiting for transfers between devices, gather_over_z(): lax.ppermute(part, 'z', [(i, i ^ k) for i in range(wide)])  13.1 us
    pallas_call x1, Pallas kernels, expert_weight_grads(): pl.pallas_call(kernel, in_specs=[UNUSED] * (5 + len(earlier)), out_specs=...  12.1 us
  transfers between devices with their start and end apart: 34, of which 18 were waited for; matrix products, arithmetic and copies ran while one was open for 5% of the time, Pallas kernels for 22%

profile of v8, /device:TPU:0, one launch (start us, length us, event | category | flops | bytes accessed | tf_op | source)
XLA Modules:
  0.0 357.0 jit_solution(6427716968975062183)
XLA Ops:
  10.8 5.5 %all-to-all-start = ((bf16[8,112,384]{2,1,0:T(8,128)(2,1)}), bf16[8,112,384]{2,1,0:T(8,128)(2,1)S(1)}, u32[]{:S(2)}, u32[]{:S(2)}) async-start(bf16[8,112,384]{2,1,0:T(8,128)(2,1)} %broadcast_in_dim.58), calls=%async_computation | async-start | bytes 1376256 | tf_op jit(solution)/shard_map/all_to_all | solution.py:33
  23.8 7.7 %all-to-all-done.refs_1_.refs_8_ = bf16[8,112,384]{2,1,0:T(8,128)(2,1)S(1)} async-done(((bf16[8,112,384]{2,1,0:T(8,128)(2,1)}), bf16[8,112,384]{2,1,0:T(8,128)(2,1)S(1)}, u32[]{:S(2)}, u32[]{:S(2)}) %all-to-all-start) | async-done | bytes 688160 | tf_op jit(solution)/shard_map/all_to_all | solution.py:33
  45.2 12.3 %all-to-all-done.1.refs_1_.refs_8_.refs_0_ = bf16[8,144,384]{2,1,0:T(8,128)(2,1)S(1)} async-done(((bf16[8,144,384]{2,1,0:T(8,128)(2,1)}), bf16[8,144,384]{2,1,0:T(8,128)(2,1)S(1)}, u32[]{:S(2)}, u32[]{:S(2)}) %all-to-all-start.1) | async-done | bytes 884768 | tf_op jit(solution)/shard_map/all_to_all | solution.py:33
  58.4 10.5 %collective-permute-done.2.refs_6_.refs_10_ = bf16[8,112,384]{2,1,0:T(8,128)(2,1)} collective-permute-done((bf16[8,112,384]{2,1,0:T(8,128)(2,1)}, bf16[8,112,384]{2,1,0:T(8,128)(2,1)}, u32[]{:S(2)}, u32[]{:S(2)}) %collective-permute-start.2) | collective-permute-done | bytes 688160 | tf_op jit(solution)/shard_map/ppermute | solution.py:657
  71.4 5.0 %shard_map.189 = (bf16[128,1536]{1,0:T(8,128)(2,1)}, bf16[128,1536]{1,0:T(8,128)(2,1)}, bf16[128,512]{1,0:T(8,128)(2,1)}) custom-call(bf16[128,1536]{1,0:T(8,128)(2,1)} %refs_2_.1, f32[1,1536]{1,0:T(1,128)} %slice.23.refs_1_.refs_3_, bf16[1536,2048]{1,0:T(8,128)(2,1)} %all-gather.6.cloned.1.call-done.refs_2_.refs_1_, ...), custom_call_target="tpu_custom_call" | custom-call | flops 805306368 | bytes 7739392 | tf_op jit(solution)/shard_map/pallas_call | solution.py:68
  76.5 5.5 %all-to-all-start.2 = ((bf16[8,80,1536]{2,1,0:T(8,128)(2,1)}), bf16[8,80,1536]{2,1,0:T(8,128)(2,1)}, u32[]{:S(2)}, u32[]{:S(2)}) async-start(bf16[8,80,1536]{2,1,0:T(8,128)(2,1)} %bitcast.13), calls=%async_computation.2 | async-start | bytes 3932160 | tf_op jit(solution)/shard_map/all_to_all | solution.py:33
  88.1 11.1 %collective-permute-done.4.refs_1_.refs_2_ = bf16[128,512]{1,0:T(8,128)(2,1)S(1)} collective-permute-done((bf16[128,512]{1,0:T(8,128)(2,1)S(1)}, bf16[128,512]{1,0:T(8,128)(2,1)S(1)}, u32[]{:S(2)}, u32[]{:S(2)}) %collective-permute-start.4) | collective-permute-done | bytes 131104 | tf_op jit(solution)/shard_map/ppermute | solution.py:955
  99.9 6.7 %shard_map.190 = (bf16[1536,128]{1,0:T(8,128)(2,1)}, f32[128,1536]{1,0:T(8,128)}, bf16[640,1536]{1,0:T(8,128)(2,1)}) custom-call(bf16[128,1536]{1,0:T(8,128)(2,1)} %get-tuple-element.39.refs_0_.refs_1_, bf16[128,512]{1,0:T(8,128)(2,1)} %copy-done.18, bf16[128,512]{1,0:T(8,128)(2,1)} %get-tuple-element.40.refs_2_.refs_3_, s32[128,1]{1,0:T(8,128)} %copy.60.refs_3_.refs_4_, ...), custom_call_target="tpu_custom_call" | custom-call | flops 805306368 | bytes 9869832 | tf_op jit(solution)/shard_map/pallas_call | solution.py:68
  106.6 28.2 %all_to_all.62 = bf16[8,80,1536]{2,1,0:T(8,128)(2,1)} all-to-all(bf16[8,80,1536]{2,1,0:T(8,128)(2,1)} %bitcast.55), channel_id=1, replica_groups=mesh['h'=2,'z'=4,'y'=4,'x'=2,'c'=2] {'y','x'}, dimensions={0} | all-to-all | bytes 3932160 | tf_op jit(solution)/shard_map/all_to_all | solution.py:33
  136.9 13.9 %shard_map.193 = (bf16[8,80,1536]{2,1,0:T(8,128)(2,1)}, bf16[640,768]{1,0:T(8,128)(2,1)}, bf16[640,1536]{1,0:T(8,128)(2,1)}) custom-call(bf16[640,1536]{1,0:T(8,128)(2,1)} %bitcast.53, bf16[640,1536]{1,0:T(8,128)(2,1)} %bitcast.14.refs_1_.grad_any, bf16[8,8,144,384]{3,2,1,0:T(8,128)(2,1)} %bitcast.71), custom_call_target="tpu_custom_call" | custom-call | flops 7549747200 | bytes 18874368 | tf_op jit(solution)/shard_map/pallas_call | solution.py:349
  151.6 4.3 %all-to-all-start.4 = ((bf16[8,80,1536]{2,1,0:T(8,128)(2,1)}), bf16[8,80,1536]{2,1,0:T(8,128)(2,1)}, u32[]{:S(2)}, u32[]{:S(2)}) async-start(bf16[8,80,1536]{2,1,0:T(8,128)(2,1)} %shard_map.195.refs_0_), calls=%async_computation.4 | async-start | bytes 3932160 | tf_op jit(solution)/shard_map/all_to_all | solution.py:33
  156.0 12.1 %shard_map.196 = (bf16[8,80,1536]{2,1,0:T(8,128)(2,1)}, bf16[4,2,8,2,72,384]{5,4,3,2,1,0:T(8,128)(2,1)}) custom-call(bf16[640,1536]{1,0:T(8,128)(2,1)} %bitcast.54, bf16[640,1536]{1,0:T(8,128)(2,1)} %bitcast.14.refs_1_.grad_any, bf16[640,768]{1,0:T(8,128)(2,1)} %get-tuple-element.47.acted_any, bf16[640,1536]{1,0:T(8,128)(2,1)} %get-tuple-element.48.pre_any, ...), custom_call_target="tpu_custom_call" | custom-call | flops 6039797760 | bytes 38141952 | tf_op jit(solution)/shard_map/pallas_call | solution.py:461
  168.1 8.2 %all-to-all-done.4.refs_0_ = bf16[8,80,1536]{2,1,0:T(8,128)(2,1)} async-done(((bf16[8,80,1536]{2,1,0:T(8,128)(2,1)}), bf16[8,80,1536]{2,1,0:T(8,128)(2,1)}, u32[]{:S(2)}, u32[]{:S(2)}) %all-to-all-start.4) | async-done | bytes 1966112 | tf_op jit(solution)/shard_map/all_to_all | solution.py:33
  191.1 7.6 %shard_map.199 = (bf16[12,128,128]{2,1,0:T(8,128)(2,1)}, bf16[128,512]{1,0:T(8,128)(2,1)}, f32[128,512]{1,0:T(8,128)}) custom-call(bf16[128,1536]{1,0:T(8,128)(2,1)} %get-tuple-element.54.refs_0_, bf16[128,1536]{1,0:T(8,128)(2,1)} %get-tuple-element.39.refs_0_.refs_1_, bf16[128,512]{1,0:T(8,128)(2,1)} %copy-done.18, ...), custom_call_target="tpu_custom_call" | custom-call | flops 1107296256 | bytes 7471624 | tf_op jit(solution)/shard_map/pallas_call | solution.py:68
  203.4 5.5 %collective-permute-done.13.refs_2_ = bf16[128,512]{1,0:T(8,128)(2,1)S(1)} collective-permute-done((bf16[128,512]{1,0:T(8,128)(2,1)}, bf16[128,512]{1,0:T(8,128)(2,1)S(1)}, u32[]{:S(2)}, u32[]{:S(2)}) %collective-permute-start.13) | collective-permute-done | bytes 131104 | tf_op jit(solution)/shard_map/ppermute | solution.py:995
  222.5 6.0 %reduce-scatter.3.cloned.1.call-done = bf16[1,8,2,72,384]{4,3,2,1,0:T(8,128)(2,1)} async-done(((bf16[8,8,2,72,384]{4,3,2,1,0:T(8,128)(2,1)}), bf16[1,8,2,72,384]{4,3,2,1,0:T(8,128)(2,1)}) %reduce-scatter.3.cloned.1.call-update) | async-done | bytes 884752 | tf_op jit(solution)/shard_map/reduce_scatter | solution.py:975
  234.7 6.8 %all-to-all-start.9 = ((bf16[16,2,72,384]{3,2,1,0:T(8,128)(2,1)}), bf16[16,2,72,384]{3,2,1,0:T(8,128)(2,1)}, u32[]{:S(2)}, u32[]{:S(2)}) async-start(bf16[16,2,72,384]{3,2,1,0:T(8,128)(2,1)} %shard_map.201.refs_5_), calls=%async_computation.11 | async-start | bytes 3538944 | tf_op jit(solution)/shard_map/all_to_all | solution.py:33
  247.8 6.6 %shard_map.204 = (bf16[128,1536]{1,0:T(8,128)(2,1)}, bf16[1536,128]{1,0:T(8,128)(2,1)}) custom-call(bf16[16,128,128]{2,1,0:T(8,128)(2,1)} %shard_map.200.refs_0_, bf16[1536,2048]{1,0:T(8,128)(2,1)} %all-gather.6.cloned.1.call-done.refs_2_.refs_1_, bf16[128,1536]{1,0:T(8,128)(2,1)} %refs_2_.1, f32[1,1536]{1,0:T(1,128)} %slice.23.refs_1_.refs_3_, ...), custom_call_target="tpu_custom_call" | custom-call | flops 805306368 | bytes 9574400 | tf_op jit(solution)/shard_map/pallas_call | solution.py:68
  254.4 12.3 %all-to-all-done.9.refs_0_ = bf16[16,2,72,384]{3,2,1,0:T(8,128)(2,1)} async-done(((bf16[16,2,72,384]{3,2,1,0:T(8,128)(2,1)}), bf16[16,2,72,384]{3,2,1,0:T(8,128)(2,1)}, u32[]{:S(2)}, u32[]{:S(2)}) %all-to-all-start.9) | async-done | bytes 1769504 | tf_op jit(solution)/shard_map/all_to_all | solution.py:33
  269.3 4.5 %all-to-all-start.6 = ((bf16[4,384,512]{2,1,0:T(8,128)(2,1)}), bf16[4,384,512]{2,1,0:T(8,128)(2,1)}, u32[]{:S(2)}, u32[]{:S(2)}) async-start(bf16[4,384,512]{2,1,0:T(8,128)(2,1)} %shard_map.202.refs_6_), calls=%async_computation.7 | async-start | bytes 3145728 | tf_op jit(solution)/shard_map/all_to_all | solution.py:33
  279.2 15.8 %collective-permute-done.18.refs_3_ = bf16[384,128]{1,0:T(8,128)(2,1)S(1)} collective-permute-done((bf16[384,128]{1,0:T(8,128)(2,1)S(1)}, bf16[384,128]{1,0:T(8,128)(2,1)S(1)}, u32[]{:S(2)}, u32[]{:S(2)}) %collective-permute-start.18) | collective-permute-done | bytes 98336 | tf_op jit(solution)/shard_map/ppermute | solution.py:800
  301.0 24.5 %all_to_all.63.refs_0_ = bf16[32,96,128]{2,1,0:T(8,128)(2,1)} all-to-all(bf16[32,96,128]{2,1,0:T(8,128)(2,1)} %shard_map.206), channel_id=1, replica_groups=mesh['h'=2,'z'=4,'y'=4,'x'=2,'c'=2] {'h','z','x','c'}, dimensions={0} | all-to-all | bytes 1572864 | tf_op jit(solution)/shard_map/all_to_all | solution.py:33
  327.6 5.6 %all-to-all-start.8 = ((bf16[8,4,96,128]{3,2,1,0:T(8,128)(2,1)}), bf16[8,4,96,128]{3,2,1,0:T(8,128)(2,1)}, u32[]{:S(2)}, u32[]{:S(2)}) async-start(bf16[8,4,96,128]{3,2,1,0:T(8,128)(2,1)} %shard_map.207), calls=%async_computation.10 | async-start | bytes 1572864 | tf_op jit(solution)/shard_map/all_to_all | solution.py:33
  337.7 6.9 %shard_map.209 = (f32[8,96,1536]{2,1,0:T(8,128)}, f32[8,48,1536]{2,1,0:T(8,128)}) custom-call(bf16[4,8,2,72,384]{4,3,2,1,0:T(8,128)(2,1)} %bitcast.56), custom_call_target="tpu_custom_call" | custom-call | tf_op jit(solution)/shard_map/pallas_call | solution.py:674
  (183 shorter events, 109.6 us)
Async XLA Ops:
  7.2 64.2 %all-gather.6.cloned.1.call-start = ((), (), s32[]{:S(2)}) async-start(), calls=%async_computation.12 | async-start | bytes 6684672 | tf_op jit(solution)/shard_map/all_gather | solution.py:905
  10.8 20.7 %all-to-all-start = ((bf16[8,112,384]{2,1,0:T(8,128)(2,1)}), bf16[8,112,384]{2,1,0:T(8,128)(2,1)S(1)}, u32[]{:S(2)}, u32[]{:S(2)}) async-start(bf16[8,112,384]{2,1,0:T(8,128)(2,1)} %broadcast_in_dim.58), calls=%async_computation | async-start | bytes 1376256 | tf_op jit(solution)/shard_map/all_to_all | solution.py:33
  32.4 25.0 %all-to-all-start.1 = ((bf16[8,144,384]{2,1,0:T(8,128)(2,1)}), bf16[8,144,384]{2,1,0:T(8,128)(2,1)S(1)}, u32[]{:S(2)}, u32[]{:S(2)}) async-start(bf16[8,144,384]{2,1,0:T(8,128)(2,1)} %shard_map.187), calls=%async_computation.1 | async-start | bytes 1769472 | tf_op jit(solution)/shard_map/all_to_all | solution.py:33
  36.1 100.7 %all-gather.8.cloned.1.call-start = ((), (), s32[]{:S(2)}) async-start(), calls=%async_computation.15 | async-start | bytes 7962624 | tf_op jit(solution)/shard_map/all_gather | solution.py:952
  36.2 22.2 %collective-permute-start.1 = (bf16[8,112,384]{2,1,0:T(8,128)(2,1)}, bf16[8,112,384]{2,1,0:T(8,128)(2,1)}, u32[]{:S(2)}, u32[]{:S(2)}) collective-permute-start(bf16[8,112,384]{2,1,0:T(8,128)(2,1)} %copy-done.3), channel_id=1, source_target_pairs={{0,16},{16,0},{32,48},{48,32},{1,17},{17,1},{33,49},{49,33},{2,18}... | collective-permute-start | bytes 2064392 | tf_op jit(solution)/shard_map/ppermute | solution.py:657
  38.5 30.3 %collective-permute-start.2 = (bf16[8,112,384]{2,1,0:T(8,128)(2,1)}, bf16[8,112,384]{2,1,0:T(8,128)(2,1)}, u32[]{:S(2)}, u32[]{:S(2)}) collective-permute-start(bf16[8,112,384]{2,1,0:T(8,128)(2,1)} %copy-done.3), channel_id=1, source_target_pairs={{0,32},{16,48},{32,0},{48,16},{1,33},{17,49},{33,1},{49,17},{2,34}... | collective-permute-start | bytes 2064392 | tf_op jit(solution)/shard_map/ppermute | solution.py:657
  42.8 28.6 %collective-permute-start.3 = (bf16[8,112,384]{2,1,0:T(8,128)(2,1)}, bf16[8,112,384]{2,1,0:T(8,128)(2,1)}, u32[]{:S(2)}, u32[]{:S(2)}) collective-permute-start(bf16[8,112,384]{2,1,0:T(8,128)(2,1)} %copy-done.3), channel_id=1, source_target_pairs={{0,48},{16,32},{32,16},{48,0},{1,49},{17,33},{33,17},{49,1},{2,50}... | collective-permute-start | bytes 2064392 | tf_op jit(solution)/shard_map/ppermute | solution.py:657
  76.5 30.0 %all-to-all-start.2 = ((bf16[8,80,1536]{2,1,0:T(8,128)(2,1)}), bf16[8,80,1536]{2,1,0:T(8,128)(2,1)}, u32[]{:S(2)}, u32[]{:S(2)}) async-start(bf16[8,80,1536]{2,1,0:T(8,128)(2,1)} %bitcast.13), calls=%async_computation.2 | async-start | bytes 3932160 | tf_op jit(solution)/shard_map/all_to_all | solution.py:33
  83.0 16.2 %collective-permute-start.4 = (bf16[128,512]{1,0:T(8,128)(2,1)S(1)}, bf16[128,512]{1,0:T(8,128)(2,1)S(1)}, u32[]{:S(2)}, u32[]{:S(2)}) collective-permute-start(bf16[128,512]{1,0:T(8,128)(2,1)S(1)} %copy-done.17), channel_id=1, source_target_pairs={{0,1},{1,2},{2,3},{3,4},{4,5},{5,6},{6,7},{7,8},{8,9},{9,10},{10,1... | collective-permute-start | bytes 393224 | tf_op jit(solution)/shard_map/ppermute | solution.py:955
  134.8 16.0 %collective-permute-start.10 = (bf16[1536,128]{1,0:T(8,128)(2,1)}, bf16[1536,128]{1,0:T(8,128)(2,1)}, u32[]{:S(2)}, u32[]{:S(2)}) collective-permute-start(bf16[1536,128]{1,0:T(8,128)(2,1)} %get-tuple-element.46), channel_id=1, source_target_pairs={{0,2},{2,0},{1,3},{3,1},{4,6},{6,4},{5,7},{7,5},{8,10},{10,8},{9,1... | collective-permute-start | bytes 1179656 | tf_op jit(solution)/shard_map/ppermute | solution.py:963
  135.4 15.4 %collective-permute-start.9 = (bf16[128,1536]{1,0:T(8,128)(2,1)}, bf16[128,1536]{1,0:T(8,128)(2,1)S(1)}, u32[]{:S(2)}, u32[]{:S(2)}) collective-permute-start(bf16[128,1536]{1,0:T(8,128)(2,1)} %get-tuple-element.45), channel_id=1, source_target_pairs={{0,2},{2,0},{1,3},{3,1},{4,6},{6,4},{5,7},{7,5},{8,10},{10,8},{9,1... | collective-permute-start | bytes 1179656 | tf_op jit(solution)/shard_map/ppermute | solution.py:962
  151.6 24.7 %all-to-all-start.4 = ((bf16[8,80,1536]{2,1,0:T(8,128)(2,1)}), bf16[8,80,1536]{2,1,0:T(8,128)(2,1)}, u32[]{:S(2)}, u32[]{:S(2)}) async-start(bf16[8,80,1536]{2,1,0:T(8,128)(2,1)} %shard_map.195.refs_0_), calls=%async_computation.4 | async-start | bytes 3932160 | tf_op jit(solution)/shard_map/all_to_all | solution.py:33
  155.9 72.6 %reduce-scatter.3.cloned.1.call-start = ((), (), s32[]{:S(2)}) async-start(), calls=%async_computation.13 | async-start | bytes 7962624 | tf_op jit(solution)/shard_map/reduce_scatter | solution.py:975
  179.2 43.3 %all-to-all-start.5 = ((bf16[8,80,1536]{2,1,0:T(8,128)(2,1)}), bf16[8,80,1536]{2,1,0:T(8,128)(2,1)}, u32[]{:S(2)}, u32[]{:S(2)}) async-start(bf16[8,80,1536]{2,1,0:T(8,128)(2,1)} %get-tuple-element.51), calls=%async_computation.5 | async-start | bytes 3932160 | tf_op jit(solution)/shard_map/all_to_all | solution.py:33
  183.6 114.0 %reduce-scatter.5.cloned.1.call-start = ((), (), s32[]{:S(2)}) async-start(), calls=%async_computation.14 | async-start | bytes 1474560 | tf_op jit(solution)/shard_map/reduce_scatter | solution.py:1019
  203.4 11.7 %collective-permute-start.16 = (bf16[128,768]{1,0:T(8,128)(2,1)}, bf16[128,768]{1,0:T(8,128)(2,1)S(1)}, u32[]{:S(2)}, u32[]{:S(2)}) collective-permute-start(bf16[128,768]{1,0:T(8,128)(2,1)} %get-tuple-element.80), channel_id=1, source_target_pairs={{0,2},{2,0},{1,3},{3,1},{4,6},{6,4},{5,7},{7,5},{8,10},{10,8},{9,1... | collective-permute-start | bytes 589832 | tf_op jit(solution)/shard_map/ppermute | solution.py:693
  215.9 15.2 %collective-permute-start.17 = (bf16[2,128,384]{2,1,0:T(8,128)(2,1)}, bf16[2,128,384]{2,1,0:T(8,128)(2,1)}, u32[]{:S(2)}, u32[]{:S(2)}) collective-permute-start(bf16[2,128,384]{2,1,0:T(8,128)(2,1)} %fusion.1), channel_id=1, source_target_pairs={{0,1},{1,0},{2,3},{3,2},{4,5},{5,4},{6,7},{7,6},{8,9},{9,8},{10,11... | collective-permute-start | bytes 589832 | tf_op jit(solution)/shard_map/ppermute | solution.py:698
  234.7 31.9 %all-to-all-start.9 = ((bf16[16,2,72,384]{3,2,1,0:T(8,128)(2,1)}), bf16[16,2,72,384]{3,2,1,0:T(8,128)(2,1)}, u32[]{:S(2)}, u32[]{:S(2)}) async-start(bf16[16,2,72,384]{3,2,1,0:T(8,128)(2,1)} %shard_map.201.refs_5_), calls=%async_computation.11 | async-start | bytes 3538944 | tf_op jit(solution)/shard_map/all_to_all | solution.py:33
  241.6 96.1 %all-gather.10.cloned.1.call-start = ((), (), s32[]{:S(2)}) async-start(), calls=%async_computation.16 | async-start | bytes 4423680 | tf_op jit(solution)/shard_map/all_gather | solution.py:1027
  269.3 28.3 %all-to-all-start.6 = ((bf16[4,384,512]{2,1,0:T(8,128)(2,1)}), bf16[4,384,512]{2,1,0:T(8,128)(2,1)}, u32[]{:S(2)}, u32[]{:S(2)}) async-start(bf16[4,384,512]{2,1,0:T(8,128)(2,1)} %shard_map.202.refs_6_), calls=%async_computation.7 | async-start | bytes 3145728 | tf_op jit(solution)/shard_map/all_to_all | solution.py:33
  274.5 20.5 %collective-permute-start.18 = (bf16[384,128]{1,0:T(8,128)(2,1)S(1)}, bf16[384,128]{1,0:T(8,128)(2,1)S(1)}, u32[]{:S(2)}, u32[]{:S(2)}) collective-permute-start(bf16[384,128]{1,0:T(8,128)(2,1)S(1)} %get-tuple-element.77), channel_id=1, source_target_pairs={{0,4},{4,0},{8,12},{12,8},{1,5},{5,1},{9,13},{13,9},{2,6},{6,2},{1... | collective-permute-start | bytes 294920 | tf_op jit(solution)/shard_map/ppermute | solution.py:800
  276.4 21.1 %collective-permute-start.19 = (bf16[384,128]{1,0:T(8,128)(2,1)S(1)}, bf16[384,128]{1,0:T(8,128)(2,1)S(1)}, u32[]{:S(2)}, u32[]{:S(2)}) collective-permute-start(bf16[384,128]{1,0:T(8,128)(2,1)S(1)} %get-tuple-element.76), channel_id=1, source_target_pairs={{0,8},{4,12},{8,0},{12,4},{1,9},{5,13},{9,1},{13,5},{2,10},{6,14},... | collective-permute-start | bytes 294920 | tf_op jit(solution)/shard_map/ppermute | solution.py:800
  279.1 18.5 %collective-permute-start.20 = (bf16[384,128]{1,0:T(8,128)(2,1)S(1)}, bf16[384,128]{1,0:T(8,128)(2,1)S(1)}, u32[]{:S(2)}, u32[]{:S(2)}) collective-permute-start(bf16[384,128]{1,0:T(8,128)(2,1)S(1)} %get-tuple-element.75), channel_id=1, source_target_pairs={{0,12},{4,8},{8,4},{12,0},{1,13},{5,9},{9,5},{13,1},{2,14},{6,10},... | collective-permute-start | bytes 294920 | tf_op jit(solution)/shard_map/ppermute | solution.py:800
  327.6 19.0 %all-to-all-start.8 = ((bf16[8,4,96,128]{3,2,1,0:T(8,128)(2,1)}), bf16[8,4,96,128]{3,2,1,0:T(8,128)(2,1)}, u32[]{:S(2)}, u32[]{:S(2)}) async-start(bf16[8,4,96,128]{3,2,1,0:T(8,128)(2,1)} %shard_map.207), calls=%async_computation.10 | async-start | bytes 1572864 | tf_op jit(solution)/shard_map/all_to_all | solution.py:33
  (39 other events, 162.1 us)
Sparse Core Ops, SparseCore 0:
  10.3 56.4 all-gather.5
  76.6 43.0 all-gather.7
  176.4 52.0 reduce-scatter.2
  234.8 40.2 reduce-scatter.4
  277.2 52.9 all-gather.9

commit v9 on v8

--- a/solution.py
+++ b/solution.py
@@ -489,23 +489,38 @@
     rows, width = residual.shape
     slots = pick.shape[0]
 
-    def kernel(pick_ref, back_ref, residual_ref, gain_ref, cot_ref, grad_ref, branch_ref, gain_grad_ref):
-        for block in range(width // 512):
-            at = slice(block * 512, (block + 1) * 512)
+    def kernel(
+        pick_ref, back_any, residual_ref, gain_ref, cot_ref, grad_ref, branch_ref, product_ref,
+        back_ref, sem,
+    ):
+        blocks = [slice(i * 512, (i + 1) * 512) for i in range(width // 512)]
+        copies = [
+            pltpu.make_async_copy(back_any.at[:, :, at], back_ref.at[:, :, at], sem.at[i])
+            for i, at in enumerate(blocks)
+        ]
+        for copy in copies:
+            copy.start()
+        for copy, at in zip(copies, blocks):
+            copy.wait()
             back = back_ref[:, :, at].reshape(slots, 512)
             grad_ref[:, at] = transposed_times(pick_ref[...], back)
-        grad, grad_gain = norm_back(residual_ref[...], gain_ref[...], grad_ref[...])
+        grad, products = norm_back(residual_ref[...], gain_ref[...], grad_ref[...])
         grad = grad + cot_ref[...].astype(f32)
         grad_ref[...] = grad
         branch_ref[...] = grad.astype(bf16)
-        gain_grad_ref[...] = gain_tile(grad_gain, False)
+        product_ref[...] = products.astype(bf16)
 
     return call(
         kernel,
-        [shaped((rows, width), f32), shaped((rows, width), bf16), shaped((width, 128), f32)],
+        [shaped((rows, width), f32), shaped((rows, width), bf16), shaped((rows, width), bf16)],
         (pick, returned, residual, gain, cotangent),
         earlier,
+        specs=[WHOLE, UNUSED, WHOLE, WHOLE, WHOLE],
         flops=2 * slots * width * rows,
+        scratch=[
+            pltpu.VMEM(returned.shape, bf16),
+            pltpu.SemaphoreType.DMA((width // 512,)),
+        ],
     )
 
 
@@ -638,7 +653,8 @@
             total = total + times_transposed(pair, w_ref[:, i * 256 : (i + 1) * 256])
         grad, grad_gain = norm_back(token_ref[...].astype(f32), gain_ref[...], total)
         out_ref[...] = (residual_ref[...] + grad).astype(bf16)
-        tile_ref[...] = (other_ref[...] + gain_tile(grad_gain, True)).astype(bf16)
+        other = gain_tile(other_ref[...].astype(f32), False)
+        tile_ref[...] = (other + gain_tile(grad_gain, True)).astype(bf16)
 
     return call(
         kernel,
@@ -700,21 +716,84 @@
 
 def twice(value, earlier):
     size = value.shape[0]
-
-    def kernel(in_ref, out_ref):
-        out_ref[:size] = in_ref[...]
-        out_ref[size:] = in_ref[...]
-
-    return call(kernel, [shaped((2 * size, *value.shape[1:]), value.dtype)], (value,), earlier)[0]
+    near = size // 2
+
+    def kernel(in_any, *refs):
+        out_any, value_ref, in_sem, out_sem = refs[len(earlier) :]
+        blocks = [pl.ds(i * near, near) for i in range(2)]
+        ins = [
+            pltpu.make_async_copy(in_any.at[at], value_ref.at[at], in_sem.at[i])
+            for i, at in enumerate(blocks)
+        ]
+        for copy in ins:
+            copy.start()
+        outs = []
+        for i, at in enumerate(blocks):
+            ins[i].wait()
+            for j in range(2):
+                to = pl.ds(j * size + i * near, near)
+                copy = pltpu.make_async_copy(value_ref.at[at], out_any.at[to], out_sem.at[2 * i + j])
+                copy.start()
+                outs.append(copy)
+        for copy in outs:
+            copy.wait()
+
+    return pl.pallas_call(
+        kernel,
+        in_specs=[UNUSED] * (1 + len(earlier)),
+        out_specs=UNUSED,
+        out_shape=shaped((2 * size, *value.shape[1:]), value.dtype),
+        scratch_shapes=[
+            pltpu.VMEM(value.shape, value.dtype),
+            pltpu.SemaphoreType.DMA((2,)),
+            pltpu.SemaphoreType.DMA((4,)),
+        ],
+        compiler_params=pltpu.CompilerParams(vmem_limit_bytes=VMEM_LIMIT),
+    )(value, *earlier)
 
 
 def sum_of_halves(value, earlier):
     size = value.shape[0] // 2
-
-    def kernel(in_ref, out_ref):
-        out_ref[...] = (in_ref[:size].astype(f32) + in_ref[size:].astype(f32)).astype(bf16)
-
-    return call(kernel, [shaped((size, *value.shape[1:]), value.dtype)], (value,), earlier)[0]
+    out = shaped((size, *value.shape[1:]), value.dtype)
+
+    def kernel(in_any, *refs):
+        out_any, in_ref, out_ref, in_sem, out_sem = refs[len(earlier) :]
+        near = size // 2
+        copies = [
+            pltpu.make_async_copy(
+                in_any.at[pl.ds(i * near, near)], in_ref.at[pl.ds(i * near, near)], in_sem.at[i]
+            )
+            for i in range(4)
+        ]
+        for i in (0, 2, 1, 3):
+            copies[i].start()
+        outs = []
+        for i in range(2):
+            copies[i].wait()
+            copies[2 + i].wait()
+            at = slice(i * near, (i + 1) * near)
+            low = in_ref[at].astype(f32)
+            out_ref[at] = (low + in_ref[size + i * near : size + (i + 1) * near].astype(f32)).astype(bf16)
+            block = pl.ds(i * near, near)
+            copy = pltpu.make_async_copy(out_ref.at[block], out_any.at[block], out_sem.at[i])
+            copy.start()
+            outs.append(copy)
+        for copy in outs:
+            copy.wait()
+
+    return pl.pallas_call(
+        kernel,
+        in_specs=[UNUSED] * (1 + len(earlier)),
+        out_specs=UNUSED,
+        out_shape=out,
+        scratch_shapes=[
+            pltpu.VMEM(value.shape, value.dtype),
+            pltpu.VMEM(out.shape, value.dtype),
+            pltpu.SemaphoreType.DMA((4,)),
+            pltpu.SemaphoreType.DMA((2,)),
+        ],
+        compiler_params=pltpu.CompilerParams(vmem_limit_bytes=VMEM_LIMIT),
+    )(value, *earlier)
 
 
 def hold(values, earlier):

time: 359 us -> 358 us (level)
    pallas_call x0 -> x2, Pallas kernels: none -> 4.59 us  [the longest x1 2.33 us: sum_of_halves(): pl.pallas_call(kernel, in_specs=[UNUSED] * (1 + len(earlier)), out_specs=...]
    pallas_call x14 -> x12, Pallas kernels: 55.3 us -> 50.7 us  [call(): pl.pallas_call(body, in_specs=[*specs, *[UNUSED] * len(earlier)], out_spe...]
where the time goes in v9:
time: 358 us; the launch traced here: 356 us
  waiting for transfers between devices  105 us (29%)
  Pallas kernels  88.3 us (25%)
  starting transfers between devices  62.6 us (17%)
  blocking collectives  52.7 us (15%)
  local copies, waits for them, and re-layouts  21.4 us (6%)
  between operations  14.4 us (4%)
  other arithmetic  10.3 us (3%)
    all_to_all x2, blocking collectives, exchange(): return lax.all_to_all(parts, axes, 0, 0, tiled=True)  52.7 us
    pallas_call x12, Pallas kernels, call(): pl.pallas_call(body, in_specs=[*specs, *[UNUSED] * len(earlier)], out_spe...  50.7 us
    all_to_all x8, waiting for transfers between devices, exchange(): return lax.all_to_all(parts, axes, 0, 0, tiled=True)  42.7 us
    all_to_all x8, starting transfers between devices, exchange(): return lax.all_to_all(parts, axes, 0, 0, tiled=True)  40.2 us
    ppermute x3, waiting for transfers between devices, moved_over_y(): moved.append(lax.ppermute(sent, 'y', [(i, i ^ k) for i in range(wide)]))  18.2 us
    pallas_call x1, Pallas kernels, run_experts(): pl.pallas_call(kernel, in_specs=[UNUSED] * 3, out_specs=[UNUSED] * 3, out...  13.9 us
    ppermute x3, waiting for transfers between devices, gather_over_z(): lax.ppermute(part, 'z', [(i, i ^ k) for i in range(wide)])  13.1 us
    pallas_call x1, Pallas kernels, expert_weight_grads(): pl.pallas_call(kernel, in_specs=[UNUSED] * (5 + len(earlier)), out_specs=...  12.1 us
  transfers between devices with their start and end apart: 34, of which 18 were waited for; matrix products, arithmetic and copies ran while one was open for 5% of the time, Pallas kernels for 22%

profile of v9, /device:TPU:0, one launch (start us, length us, event | category | flops | bytes accessed | tf_op | source)
XLA Modules:
  0.0 356.5 jit_solution(8457543950502842248)
XLA Ops:
  10.8 5.5 %all-to-all-start = ((bf16[8,112,384]{2,1,0:T(8,128)(2,1)}), bf16[8,112,384]{2,1,0:T(8,128)(2,1)S(1)}, u32[]{:S(2)}, u32[]{:S(2)}) async-start(bf16[8,112,384]{2,1,0:T(8,128)(2,1)} %broadcast_in_dim.58), calls=%async_computation | async-start | bytes 1376256 | tf_op jit(solution)/shard_map/all_to_all | solution.py:33
  23.8 7.7 %all-to-all-done.refs_1_.refs_8_ = bf16[8,112,384]{2,1,0:T(8,128)(2,1)S(1)} async-done(((bf16[8,112,384]{2,1,0:T(8,128)(2,1)}), bf16[8,112,384]{2,1,0:T(8,128)(2,1)S(1)}, u32[]{:S(2)}, u32[]{:S(2)}) %all-to-all-start) | async-done | bytes 688160 | tf_op jit(solution)/shard_map/all_to_all | solution.py:33
  45.2 12.3 %all-to-all-done.1.refs_1_.refs_8_.refs_0_ = bf16[8,144,384]{2,1,0:T(8,128)(2,1)S(1)} async-done(((bf16[8,144,384]{2,1,0:T(8,128)(2,1)}), bf16[8,144,384]{2,1,0:T(8,128)(2,1)S(1)}, u32[]{:S(2)}, u32[]{:S(2)}) %all-to-all-start.1) | async-done | bytes 884768 | tf_op jit(solution)/shard_map/all_to_all | solution.py:33
  58.4 10.5 %collective-permute-done.2.refs_6_.refs_10_ = bf16[8,112,384]{2,1,0:T(8,128)(2,1)} collective-permute-done((bf16[8,112,384]{2,1,0:T(8,128)(2,1)}, bf16[8,112,384]{2,1,0:T(8,128)(2,1)}, u32[]{:S(2)}, u32[]{:S(2)}) %collective-permute-start.2) | collective-permute-done | bytes 688160 | tf_op jit(solution)/shard_map/ppermute | solution.py:673
  71.4 5.0 %shard_map.189 = (bf16[128,1536]{1,0:T(8,128)(2,1)}, bf16[128,1536]{1,0:T(8,128)(2,1)}, bf16[128,512]{1,0:T(8,128)(2,1)}) custom-call(bf16[128,1536]{1,0:T(8,128)(2,1)} %refs_2_.1, f32[1,1536]{1,0:T(1,128)} %slice.23.refs_1_.refs_3_, bf16[1536,2048]{1,0:T(8,128)(2,1)} %all-gather.6.cloned.1.call-done.refs_2_.refs_1_, ...), custom_call_target="tpu_custom_call" | custom-call | flops 805306368 | bytes 7739392 | tf_op jit(solution)/shard_map/pallas_call | solution.py:68
  76.5 5.5 %all-to-all-start.2 = ((bf16[8,80,1536]{2,1,0:T(8,128)(2,1)}), bf16[8,80,1536]{2,1,0:T(8,128)(2,1)}, u32[]{:S(2)}, u32[]{:S(2)}) async-start(bf16[8,80,1536]{2,1,0:T(8,128)(2,1)} %bitcast.13), calls=%async_computation.2 | async-start | bytes 3932160 | tf_op jit(solution)/shard_map/all_to_all | solution.py:33
  88.1 11.1 %collective-permute-done.4.refs_1_.refs_2_ = bf16[128,512]{1,0:T(8,128)(2,1)S(1)} collective-permute-done((bf16[128,512]{1,0:T(8,128)(2,1)S(1)}, bf16[128,512]{1,0:T(8,128)(2,1)S(1)}, u32[]{:S(2)}, u32[]{:S(2)}) %collective-permute-start.4) | collective-permute-done | bytes 131104 | tf_op jit(solution)/shard_map/ppermute | solution.py:1034
  99.9 6.7 %shard_map.190 = (bf16[1536,128]{1,0:T(8,128)(2,1)}, f32[128,1536]{1,0:T(8,128)}, bf16[640,1536]{1,0:T(8,128)(2,1)}) custom-call(bf16[128,1536]{1,0:T(8,128)(2,1)} %get-tuple-element.39.refs_0_.refs_1_, bf16[128,512]{1,0:T(8,128)(2,1)} %copy-done.18, bf16[128,512]{1,0:T(8,128)(2,1)} %get-tuple-element.40.refs_2_.refs_3_, s32[128,1]{1,0:T(8,128)} %copy.60.refs_3_.refs_4_, ...), custom_call_target="tpu_custom_call" | custom-call | flops 805306368 | bytes 9869832 | tf_op jit(solution)/shard_map/pallas_call | solution.py:68
  106.6 28.2 %all_to_all.62 = bf16[8,80,1536]{2,1,0:T(8,128)(2,1)} all-to-all(bf16[8,80,1536]{2,1,0:T(8,128)(2,1)} %bitcast.55), channel_id=1, replica_groups=mesh['h'=2,'z'=4,'y'=4,'x'=2,'c'=2] {'y','x'}, dimensions={0} | all-to-all | bytes 3932160 | tf_op jit(solution)/shard_map/all_to_all | solution.py:33
  136.9 13.9 %shard_map.193 = (bf16[8,80,1536]{2,1,0:T(8,128)(2,1)}, bf16[640,768]{1,0:T(8,128)(2,1)}, bf16[640,1536]{1,0:T(8,128)(2,1)}) custom-call(bf16[640,1536]{1,0:T(8,128)(2,1)} %bitcast.53, bf16[640,1536]{1,0:T(8,128)(2,1)} %bitcast.14.refs_1_.grad_any, bf16[8,8,144,384]{3,2,1,0:T(8,128)(2,1)} %bitcast.71), custom_call_target="tpu_custom_call" | custom-call | flops 7549747200 | bytes 18874368 | tf_op jit(solution)/shard_map/pallas_call | solution.py:349
  156.0 12.1 %shard_map.196 = (bf16[8,80,1536]{2,1,0:T(8,128)(2,1)}, bf16[4,2,8,2,72,384]{5,4,3,2,1,0:T(8,128)(2,1)}) custom-call(bf16[640,1536]{1,0:T(8,128)(2,1)} %bitcast.54, bf16[640,1536]{1,0:T(8,128)(2,1)} %bitcast.14.refs_1_.grad_any, bf16[640,768]{1,0:T(8,128)(2,1)} %get-tuple-element.47.acted_any, bf16[640,1536]{1,0:T(8,128)(2,1)} %get-tuple-element.48.pre_any, ...), custom_call_target="tpu_custom_call" | custom-call | flops 6039797760 | bytes 38141952 | tf_op jit(solution)/shard_map/pallas_call | solution.py:461
  168.1 8.2 %all-to-all-done.4.refs_0_ = bf16[8,80,1536]{2,1,0:T(8,128)(2,1)} async-done(((bf16[8,80,1536]{2,1,0:T(8,128)(2,1)}), bf16[8,80,1536]{2,1,0:T(8,128)(2,1)}, u32[]{:S(2)}, u32[]{:S(2)}) %all-to-all-start.4) | async-done | bytes 1966112 | tf_op jit(solution)/shard_map/all_to_all | solution.py:33
  187.0 4.7 %shard_map.198 = (f32[128,1536]{1,0:T(8,128)}, bf16[128,1536]{1,0:T(8,128)(2,1)}, bf16[128,1536]{1,0:T(8,128)(2,1)}) custom-call(bf16[640,128]{1,0:T(8,128)(2,1)} %get-tuple-element.84.refs_6_.refs_0_, bf16[8,80,1536]{2,1,0:T(8,128)(2,1)} %get-tuple-element.53.refs_1_, f32[128,1536]{1,0:T(8,128)} %get-tuple-element.52.refs_2_.refs_3_, ...), custom_call_target="tpu_custom_call" | custom-call | flops 251658240 | bytes 4888576 | tf_op jit(solution)/shard_map/pallas_call | solution.py:68
  191.7 7.6 %shard_map.199 = (bf16[12,128,128]{2,1,0:T(8,128)(2,1)}, bf16[128,512]{1,0:T(8,128)(2,1)}, f32[128,512]{1,0:T(8,128)}) custom-call(bf16[128,1536]{1,0:T(8,128)(2,1)} %get-tuple-element.54.refs_0_, bf16[128,1536]{1,0:T(8,128)(2,1)} %get-tuple-element.39.refs_0_.refs_1_, bf16[128,512]{1,0:T(8,128)(2,1)} %copy-done.18, ...), custom_call_target="tpu_custom_call" | custom-call | flops 1107296256 | bytes 7471624 | tf_op jit(solution)/shard_map/pallas_call | solution.py:68
  204.1 4.9 %collective-permute-done.13.refs_2_ = bf16[128,512]{1,0:T(8,128)(2,1)S(1)} collective-permute-done((bf16[128,512]{1,0:T(8,128)(2,1)}, bf16[128,512]{1,0:T(8,128)(2,1)S(1)}, u32[]{:S(2)}, u32[]{:S(2)}) %collective-permute-start.13) | collective-permute-done | bytes 131104 | tf_op jit(solution)/shard_map/ppermute | solution.py:1074
  222.5 6.0 %reduce-scatter.3.cloned.1.call-done = bf16[1,8,2,72,384]{4,3,2,1,0:T(8,128)(2,1)} async-done(((bf16[8,8,2,72,384]{4,3,2,1,0:T(8,128)(2,1)}), bf16[1,8,2,72,384]{4,3,2,1,0:T(8,128)(2,1)}) %reduce-scatter.3.cloned.1.call-update) | async-done | bytes 884752 | tf_op jit(solution)/shard_map/reduce_scatter | solution.py:1054
  234.5 6.8 %all-to-all-start.9 = ((bf16[16,2,72,384]{3,2,1,0:T(8,128)(2,1)}), bf16[16,2,72,384]{3,2,1,0:T(8,128)(2,1)}, u32[]{:S(2)}, u32[]{:S(2)}) async-start(bf16[16,2,72,384]{3,2,1,0:T(8,128)(2,1)} %shard_map.201.refs_5_), calls=%async_computation.11 | async-start | bytes 3538944 | tf_op jit(solution)/shard_map/all_to_all | solution.py:33
  247.5 6.5 %shard_map.204 = (bf16[128,1536]{1,0:T(8,128)(2,1)}, bf16[1536,128]{1,0:T(8,128)(2,1)}) custom-call(bf16[16,128,128]{2,1,0:T(8,128)(2,1)} %shard_map.200.refs_0_, bf16[1536,2048]{1,0:T(8,128)(2,1)} %all-gather.6.cloned.1.call-done.refs_2_.refs_1_, bf16[128,1536]{1,0:T(8,128)(2,1)} %refs_2_.1, f32[1,1536]{1,0:T(1,128)} %slice.23.refs_1_.refs_3_, ...), custom_call_target="tpu_custom_call" | custom-call | flops 805306368 | bytes 9181184 | tf_op jit(solution)/shard_map/pallas_call | solution.py:68
  254.1 12.5 %all-to-all-done.9.in_any = bf16[16,2,72,384]{3,2,1,0:T(8,128)(2,1)} async-done(((bf16[16,2,72,384]{3,2,1,0:T(8,128)(2,1)}), bf16[16,2,72,384]{3,2,1,0:T(8,128)(2,1)}, u32[]{:S(2)}, u32[]{:S(2)}) %all-to-all-start.9) | async-done | bytes 1769504 | tf_op jit(solution)/shard_map/all_to_all | solution.py:33
  269.0 4.5 %all-to-all-start.6 = ((bf16[4,384,512]{2,1,0:T(8,128)(2,1)}), bf16[4,384,512]{2,1,0:T(8,128)(2,1)}, u32[]{:S(2)}, u32[]{:S(2)}) async-start(bf16[4,384,512]{2,1,0:T(8,128)(2,1)} %shard_map.202.refs_6_), calls=%async_computation.7 | async-start | bytes 3145728 | tf_op jit(solution)/shard_map/all_to_all | solution.py:33
  278.9 15.6 %collective-permute-done.18.refs_3_ = bf16[384,128]{1,0:T(8,128)(2,1)S(1)} collective-permute-done((bf16[384,128]{1,0:T(8,128)(2,1)S(1)}, bf16[384,128]{1,0:T(8,128)(2,1)S(1)}, u32[]{:S(2)}, u32[]{:S(2)}) %collective-permute-start.18) | collective-permute-done | bytes 98336 | tf_op jit(solution)/shard_map/ppermute | solution.py:879
  300.5 24.5 %all_to_all.63.refs_0_ = bf16[32,96,128]{2,1,0:T(8,128)(2,1)} all-to-all(bf16[32,96,128]{2,1,0:T(8,128)(2,1)} %shard_map.206), channel_id=1, replica_groups=mesh['h'=2,'z'=4,'y'=4,'x'=2,'c'=2] {'h','z','x','c'}, dimensions={0} | all-to-all | bytes 1572864 | tf_op jit(solution)/shard_map/all_to_all | solution.py:33
  327.2 5.6 %all-to-all-start.8 = ((bf16[8,4,96,128]{3,2,1,0:T(8,128)(2,1)}), bf16[8,4,96,128]{3,2,1,0:T(8,128)(2,1)}, u32[]{:S(2)}, u32[]{:S(2)}) async-start(bf16[8,4,96,128]{3,2,1,0:T(8,128)(2,1)} %shard_map.207), calls=%async_computation.10 | async-start | bytes 1572864 | tf_op jit(solution)/shard_map/all_to_all | solution.py:33
  337.2 6.9 %shard_map.209 = (f32[8,96,1536]{2,1,0:T(8,128)}, f32[8,48,1536]{2,1,0:T(8,128)}) custom-call(bf16[4,8,2,72,384]{4,3,2,1,0:T(8,128)(2,1)} %bitcast.56), custom_call_target="tpu_custom_call" | custom-call | tf_op jit(solution)/shard_map/pallas_call | solution.py:690
  (183 shorter events, 109.4 us)
Async XLA Ops:
  7.2 64.2 %all-gather.6.cloned.1.call-start = ((), (), s32[]{:S(2)}) async-start(), calls=%async_computation.12 | async-start | bytes 6684672 | tf_op jit(solution)/shard_map/all_gather | solution.py:984
  10.8 20.7 %all-to-all-start = ((bf16[8,112,384]{2,1,0:T(8,128)(2,1)}), bf16[8,112,384]{2,1,0:T(8,128)(2,1)S(1)}, u32[]{:S(2)}, u32[]{:S(2)}) async-start(bf16[8,112,384]{2,1,0:T(8,128)(2,1)} %broadcast_in_dim.58), calls=%async_computation | async-start | bytes 1376256 | tf_op jit(solution)/shard_map/all_to_all | solution.py:33
  32.4 25.0 %all-to-all-start.1 = ((bf16[8,144,384]{2,1,0:T(8,128)(2,1)}), bf16[8,144,384]{2,1,0:T(8,128)(2,1)S(1)}, u32[]{:S(2)}, u32[]{:S(2)}) async-start(bf16[8,144,384]{2,1,0:T(8,128)(2,1)} %shard_map.187), calls=%async_computation.1 | async-start | bytes 1769472 | tf_op jit(solution)/shard_map/all_to_all | solution.py:33
  36.1 100.7 %all-gather.8.cloned.1.call-start = ((), (), s32[]{:S(2)}) async-start(), calls=%async_computation.15 | async-start | bytes 7962624 | tf_op jit(solution)/shard_map/all_gather | solution.py:1031
  36.2 22.2 %collective-permute-start.1 = (bf16[8,112,384]{2,1,0:T(8,128)(2,1)}, bf16[8,112,384]{2,1,0:T(8,128)(2,1)}, u32[]{:S(2)}, u32[]{:S(2)}) collective-permute-start(bf16[8,112,384]{2,1,0:T(8,128)(2,1)} %copy-done.3), channel_id=1, source_target_pairs={{0,16},{16,0},{32,48},{48,32},{1,17},{17,1},{33,49},{49,33},{2,18}... | collective-permute-start | bytes 2064392 | tf_op jit(solution)/shard_map/ppermute | solution.py:673
  38.5 30.3 %collective-permute-start.2 = (bf16[8,112,384]{2,1,0:T(8,128)(2,1)}, bf16[8,112,384]{2,1,0:T(8,128)(2,1)}, u32[]{:S(2)}, u32[]{:S(2)}) collective-permute-start(bf16[8,112,384]{2,1,0:T(8,128)(2,1)} %copy-done.3), channel_id=1, source_target_pairs={{0,32},{16,48},{32,0},{48,16},{1,33},{17,49},{33,1},{49,17},{2,34}... | collective-permute-start | bytes 2064392 | tf_op jit(solution)/shard_map/ppermute | solution.py:673
  42.8 28.6 %collective-permute-start.3 = (bf16[8,112,384]{2,1,0:T(8,128)(2,1)}, bf16[8,112,384]{2,1,0:T(8,128)(2,1)}, u32[]{:S(2)}, u32[]{:S(2)}) collective-permute-start(bf16[8,112,384]{2,1,0:T(8,128)(2,1)} %copy-done.3), channel_id=1, source_target_pairs={{0,48},{16,32},{32,16},{48,0},{1,49},{17,33},{33,17},{49,1},{2,50}... | collective-permute-start | bytes 2064392 | tf_op jit(solution)/shard_map/ppermute | solution.py:673
  76.5 30.0 %all-to-all-start.2 = ((bf16[8,80,1536]{2,1,0:T(8,128)(2,1)}), bf16[8,80,1536]{2,1,0:T(8,128)(2,1)}, u32[]{:S(2)}, u32[]{:S(2)}) async-start(bf16[8,80,1536]{2,1,0:T(8,128)(2,1)} %bitcast.13), calls=%async_computation.2 | async-start | bytes 3932160 | tf_op jit(solution)/shard_map/all_to_all | solution.py:33
  83.0 16.2 %collective-permute-start.4 = (bf16[128,512]{1,0:T(8,128)(2,1)S(1)}, bf16[128,512]{1,0:T(8,128)(2,1)S(1)}, u32[]{:S(2)}, u32[]{:S(2)}) collective-permute-start(bf16[128,512]{1,0:T(8,128)(2,1)S(1)} %copy-done.17), channel_id=1, source_target_pairs={{0,1},{1,2},{2,3},{3,4},{4,5},{5,6},{6,7},{7,8},{8,9},{9,10},{10,1... | collective-permute-start | bytes 393224 | tf_op jit(solution)/shard_map/ppermute | solution.py:1034
  134.8 16.0 %collective-permute-start.10 = (bf16[1536,128]{1,0:T(8,128)(2,1)}, bf16[1536,128]{1,0:T(8,128)(2,1)}, u32[]{:S(2)}, u32[]{:S(2)}) collective-permute-start(bf16[1536,128]{1,0:T(8,128)(2,1)} %get-tuple-element.46), channel_id=1, source_target_pairs={{0,2},{2,0},{1,3},{3,1},{4,6},{6,4},{5,7},{7,5},{8,10},{10,8},{9,1... | collective-permute-start | bytes 1179656 | tf_op jit(solution)/shard_map/ppermute | solution.py:1042
  135.4 15.4 %collective-permute-start.9 = (bf16[128,1536]{1,0:T(8,128)(2,1)}, bf16[128,1536]{1,0:T(8,128)(2,1)S(1)}, u32[]{:S(2)}, u32[]{:S(2)}) collective-permute-start(bf16[128,1536]{1,0:T(8,128)(2,1)} %get-tuple-element.45), channel_id=1, source_target_pairs={{0,2},{2,0},{1,3},{3,1},{4,6},{6,4},{5,7},{7,5},{8,10},{10,8},{9,1... | collective-permute-start | bytes 1179656 | tf_op jit(solution)/shard_map/ppermute | solution.py:1041
  151.6 24.7 %all-to-all-start.4 = ((bf16[8,80,1536]{2,1,0:T(8,128)(2,1)}), bf16[8,80,1536]{2,1,0:T(8,128)(2,1)}, u32[]{:S(2)}, u32[]{:S(2)}) async-start(bf16[8,80,1536]{2,1,0:T(8,128)(2,1)} %shard_map.195.refs_0_), calls=%async_computation.4 | async-start | bytes 3932160 | tf_op jit(solution)/shard_map/all_to_all | solution.py:33
  155.9 72.6 %reduce-scatter.3.cloned.1.call-start = ((), (), s32[]{:S(2)}) async-start(), calls=%async_computation.13 | async-start | bytes 7962624 | tf_op jit(solution)/shard_map/reduce_scatter | solution.py:1054
  179.2 43.3 %all-to-all-start.5 = ((bf16[8,80,1536]{2,1,0:T(8,128)(2,1)}), bf16[8,80,1536]{2,1,0:T(8,128)(2,1)}, u32[]{:S(2)}, u32[]{:S(2)}) async-start(bf16[8,80,1536]{2,1,0:T(8,128)(2,1)} %get-tuple-element.51), calls=%async_computation.5 | async-start | bytes 3932160 | tf_op jit(solution)/shard_map/all_to_all | solution.py:33
  183.6 113.6 %reduce-scatter.5.cloned.1.call-start = ((), (), s32[]{:S(2)}) async-start(), calls=%async_computation.14 | async-start | bytes 1474560 | tf_op jit(solution)/shard_map/reduce_scatter | solution.py:1098
  204.1 11.1 %collective-permute-start.16 = (bf16[128,768]{1,0:T(8,128)(2,1)}, bf16[128,768]{1,0:T(8,128)(2,1)S(1)}, u32[]{:S(2)}, u32[]{:S(2)}) collective-permute-start(bf16[128,768]{1,0:T(8,128)(2,1)} %get-tuple-element.80), channel_id=1, source_target_pairs={{0,2},{2,0},{1,3},{3,1},{4,6},{6,4},{5,7},{7,5},{8,10},{10,8},{9,1... | collective-permute-start | bytes 589832 | tf_op jit(solution)/shard_map/ppermute | solution.py:709
  215.9 14.9 %collective-permute-start.17 = (bf16[2,128,384]{2,1,0:T(8,128)(2,1)}, bf16[2,128,384]{2,1,0:T(8,128)(2,1)}, u32[]{:S(2)}, u32[]{:S(2)}) collective-permute-start(bf16[2,128,384]{2,1,0:T(8,128)(2,1)} %fusion.1), channel_id=1, source_target_pairs={{0,1},{1,0},{2,3},{3,2},{4,5},{5,4},{6,7},{7,6},{8,9},{9,8},{10,11... | collective-permute-start | bytes 589832 | tf_op jit(solution)/shard_map/ppermute | solution.py:714
  234.5 32.1 %all-to-all-start.9 = ((bf16[16,2,72,384]{3,2,1,0:T(8,128)(2,1)}), bf16[16,2,72,384]{3,2,1,0:T(8,128)(2,1)}, u32[]{:S(2)}, u32[]{:S(2)}) async-start(bf16[16,2,72,384]{3,2,1,0:T(8,128)(2,1)} %shard_map.201.refs_5_), calls=%async_computation.11 | async-start | bytes 3538944 | tf_op jit(solution)/shard_map/all_to_all | solution.py:33
  241.3 95.9 %all-gather.10.cloned.1.call-start = ((), (), s32[]{:S(2)}) async-start(), calls=%async_computation.16 | async-start | bytes 4423680 | tf_op jit(solution)/shard_map/all_gather | solution.py:1106
  269.0 28.2 %all-to-all-start.6 = ((bf16[4,384,512]{2,1,0:T(8,128)(2,1)}), bf16[4,384,512]{2,1,0:T(8,128)(2,1)}, u32[]{:S(2)}, u32[]{:S(2)}) async-start(bf16[4,384,512]{2,1,0:T(8,128)(2,1)} %shard_map.202.refs_6_), calls=%async_computation.7 | async-start | bytes 3145728 | tf_op jit(solution)/shard_map/all_to_all | solution.py:33
  274.2 20.3 %collective-permute-start.18 = (bf16[384,128]{1,0:T(8,128)(2,1)S(1)}, bf16[384,128]{1,0:T(8,128)(2,1)S(1)}, u32[]{:S(2)}, u32[]{:S(2)}) collective-permute-start(bf16[384,128]{1,0:T(8,128)(2,1)S(1)} %get-tuple-element.77), channel_id=1, source_target_pairs={{0,4},{4,0},{8,12},{12,8},{1,5},{5,1},{9,13},{13,9},{2,6},{6,2},{1... | collective-permute-start | bytes 294920 | tf_op jit(solution)/shard_map/ppermute | solution.py:879
  276.1 21.0 %collective-permute-start.19 = (bf16[384,128]{1,0:T(8,128)(2,1)S(1)}, bf16[384,128]{1,0:T(8,128)(2,1)S(1)}, u32[]{:S(2)}, u32[]{:S(2)}) collective-permute-start(bf16[384,128]{1,0:T(8,128)(2,1)S(1)} %get-tuple-element.76), channel_id=1, source_target_pairs={{0,8},{4,12},{8,0},{12,4},{1,9},{5,13},{9,1},{13,5},{2,10},{6,14},... | collective-permute-start | bytes 294920 | tf_op jit(solution)/shard_map/ppermute | solution.py:879
  278.8 18.3 %collective-permute-start.20 = (bf16[384,128]{1,0:T(8,128)(2,1)S(1)}, bf16[384,128]{1,0:T(8,128)(2,1)S(1)}, u32[]{:S(2)}, u32[]{:S(2)}) collective-permute-start(bf16[384,128]{1,0:T(8,128)(2,1)S(1)} %get-tuple-element.75), channel_id=1, source_target_pairs={{0,12},{4,8},{8,4},{12,0},{1,13},{5,9},{9,5},{13,1},{2,14},{6,10},... | collective-permute-start | bytes 294920 | tf_op jit(solution)/shard_map/ppermute | solution.py:879
  327.2 19.0 %all-to-all-start.8 = ((bf16[8,4,96,128]{3,2,1,0:T(8,128)(2,1)}), bf16[8,4,96,128]{3,2,1,0:T(8,128)(2,1)}, u32[]{:S(2)}, u32[]{:S(2)}) async-start(bf16[8,4,96,128]{3,2,1,0:T(8,128)(2,1)} %shard_map.207), calls=%async_computation.10 | async-start | bytes 1572864 | tf_op jit(solution)/shard_map/all_to_all | solution.py:33
  (39 other events, 161.4 us)
Sparse Core Ops, SparseCore 0:
  10.3 56.4 all-gather.5
  76.6 43.0 all-gather.7
  176.4 52.0 reduce-scatter.2
  234.6 40.3 reduce-scatter.4
  277.1 52.8 all-gather.9

commit v10 on v9

--- a/solution.py
+++ b/solution.py
@@ -1004,7 +1004,7 @@
     gains = in_core_order(core, gains_mine, lax.ppermute(gains_mine, "c", SWAP))
     gains = gains.transpose(2, 0, 1, 3).reshape(2, width).astype(f32)
     gain_attn, gain_ffn = gains[:1], gains[1:]
-    out_mine = gather_over_z(out_part)
+    out_mine = gather_over_z(out_part[:, :rows_out])
     out_other = [lax.ppermute(one, "c", SWAP) for one in out_mine]
     chosen = routes[:, :, None] == jnp.arange(experts, dtype=jnp.int32)
     member = jnp.any(chosen, axis=1)

time: 358 us -> 359 us (level)
    ppermute x1, waiting for transfers between devices: 11.1 us -> 18.6 us  [per_device(): before = lax.ppermute(keyval, SHARD, ring)]
    ppermute x3, waiting for transfers between devices: 13.1 us -> 9.01 us  [gather_over_z(): lax.ppermute(part, 'z', [(i, i ^ k) for i in range(wide)])]
    unnamed x58 -> x62, local copies, waits for them, and re-layouts: 10.9 us -> 9.47 us
where the time goes in v10:
time: 359 us; the launch traced here: 357 us
  waiting for transfers between devices  106 us (30%)
  Pallas kernels  88.6 us (25%)
  starting transfers between devices  62.7 us (17%)
  blocking collectives  52.8 us (15%)
  local copies, waits for them, and re-layouts  20 us (6%)
  between operations  14.4 us (4%)
  other arithmetic  10.3 us (3%)
    all_to_all x2, blocking collectives, exchange(): return lax.all_to_all(parts, axes, 0, 0, tiled=True)  52.8 us
    pallas_call x12, Pallas kernels, call(): pl.pallas_call(body, in_specs=[*specs, *[UNUSED] * len(earlier)], out_spe...  51.1 us
    all_to_all x8, waiting for transfers between devices, exchange(): return lax.all_to_all(parts, axes, 0, 0, tiled=True)  42.9 us
    all_to_all x8, starting transfers between devices, exchange(): return lax.all_to_all(parts, axes, 0, 0, tiled=True)  40.3 us
    ppermute x1, waiting for transfers between devices, per_device(): before = lax.ppermute(keyval, SHARD, ring)  18.6 us
    ppermute x3, waiting for transfers between devices, moved_over_y(): moved.append(lax.ppermute(sent, 'y', [(i, i ^ k) for i in range(wide)]))  18.4 us
    pallas_call x1, Pallas kernels, run_experts(): pl.pallas_call(kernel, in_specs=[UNUSED] * 3, out_specs=[UNUSED] * 3, out...  13.9 us
    pallas_call x1, Pallas kernels, expert_weight_grads(): pl.pallas_call(kernel, in_specs=[UNUSED] * (5 + len(earlier)), out_specs=...  12.1 us
  transfers between devices with their start and end apart: 34, of which 18 were waited for; matrix products, arithmetic and copies ran while one was open for 5% of the time, Pallas kernels for 22%

profile of v10, /device:TPU:0, one launch (start us, length us, event | category | flops | bytes accessed | tf_op | source)
XLA Modules:
  0.0 357.1 jit_solution(11676127464501880266)
XLA Ops:
  10.8 5.5 %all-to-all-start = ((bf16[8,112,384]{2,1,0:T(8,128)(2,1)}), bf16[8,112,384]{2,1,0:T(8,128)(2,1)S(1)}, u32[]{:S(2)}, u32[]{:S(2)}) async-start(bf16[8,112,384]{2,1,0:T(8,128)(2,1)} %broadcast_in_dim.58), calls=%async_computation | async-start | bytes 1376256 | tf_op jit(solution)/shard_map/all_to_all | solution.py:33
  23.3 8.2 %all-to-all-done.refs_1_ = bf16[8,112,384]{2,1,0:T(8,128)(2,1)S(1)} async-done(((bf16[8,112,384]{2,1,0:T(8,128)(2,1)}), bf16[8,112,384]{2,1,0:T(8,128)(2,1)S(1)}, u32[]{:S(2)}, u32[]{:S(2)}) %all-to-all-start) | async-done | bytes 688160 | tf_op jit(solution)/shard_map/all_to_all | solution.py:33
  45.3 12.2 %all-to-all-done.1.refs_1_.refs_8_.refs_0_ = bf16[8,144,384]{2,1,0:T(8,128)(2,1)S(1)} async-done(((bf16[8,144,384]{2,1,0:T(8,128)(2,1)}), bf16[8,144,384]{2,1,0:T(8,128)(2,1)S(1)}, u32[]{:S(2)}, u32[]{:S(2)}) %all-to-all-start.1) | async-done | bytes 884768 | tf_op jit(solution)/shard_map/all_to_all | solution.py:33
  58.5 6.4 %collective-permute-done.2.refs_6_.refs_10_ = bf16[8,96,384]{2,1,0:T(8,128)(2,1)} collective-permute-done((bf16[8,96,384]{2,1,0:T(8,128)(2,1)S(1)}, bf16[8,96,384]{2,1,0:T(8,128)(2,1)}, u32[]{:S(2)}, u32[]{:S(2)}) %collective-permute-start.2) | collective-permute-done | bytes 589856 | tf_op jit(solution)/shard_map/ppermute | solution.py:673
  67.5 5.0 %shard_map.189 = (bf16[128,1536]{1,0:T(8,128)(2,1)}, bf16[128,1536]{1,0:T(8,128)(2,1)}, bf16[128,512]{1,0:T(8,128)(2,1)}) custom-call(bf16[128,1536]{1,0:T(8,128)(2,1)} %refs_2_.1, f32[1,1536]{1,0:T(1,128)} %slice.26.refs_1_.refs_3_, bf16[1536,2048]{1,0:T(8,128)(2,1)} %all-gather.6.cloned.1.call-done.refs_2_.refs_1_, ...), custom_call_target="tpu_custom_call" | custom-call | flops 805306368 | bytes 7739392 | tf_op jit(solution)/shard_map/pallas_call | solution.py:68
  72.6 5.5 %all-to-all-start.2 = ((bf16[8,80,1536]{2,1,0:T(8,128)(2,1)}), bf16[8,80,1536]{2,1,0:T(8,128)(2,1)}, u32[]{:S(2)}, u32[]{:S(2)}) async-start(bf16[8,80,1536]{2,1,0:T(8,128)(2,1)} %bitcast.13), calls=%async_computation.2 | async-start | bytes 3932160 | tf_op jit(solution)/shard_map/all_to_all | solution.py:33
  84.4 18.6 %collective-permute-done.4.refs_1_.refs_2_ = bf16[128,512]{1,0:T(8,128)(2,1)S(1)} collective-permute-done((bf16[128,512]{1,0:T(8,128)(2,1)S(1)}, bf16[128,512]{1,0:T(8,128)(2,1)S(1)}, u32[]{:S(2)}, u32[]{:S(2)}) %collective-permute-start.4) | collective-permute-done | bytes 131104 | tf_op jit(solution)/shard_map/ppermute | solution.py:1034
  103.7 6.7 %shard_map.190 = (bf16[1536,128]{1,0:T(8,128)(2,1)}, f32[128,1536]{1,0:T(8,128)}, bf16[640,1536]{1,0:T(8,128)(2,1)}) custom-call(bf16[128,1536]{1,0:T(8,128)(2,1)} %get-tuple-element.39.refs_0_.refs_1_, bf16[128,512]{1,0:T(8,128)(2,1)} %copy-done.22, bf16[128,512]{1,0:T(8,128)(2,1)} %get-tuple-element.40.refs_2_.refs_3_, s32[128,1]{1,0:T(8,128)} %copy.60.refs_3_.refs_4_, ...), custom_call_target="tpu_custom_call" | custom-call | flops 805306368 | bytes 9083400 | tf_op jit(solution)/shard_map/pallas_call | solution.py:68
  110.4 28.3 %all_to_all.62 = bf16[8,80,1536]{2,1,0:T(8,128)(2,1)} all-to-all(bf16[8,80,1536]{2,1,0:T(8,128)(2,1)} %bitcast.55), channel_id=1, replica_groups=mesh['h'=2,'z'=4,'y'=4,'x'=2,'c'=2] {'y','x'}, dimensions={0} | all-to-all | bytes 3932160 | tf_op jit(solution)/shard_map/all_to_all | solution.py:33
  140.7 13.9 %shard_map.193 = (bf16[8,80,1536]{2,1,0:T(8,128)(2,1)}, bf16[640,768]{1,0:T(8,128)(2,1)}, bf16[640,1536]{1,0:T(8,128)(2,1)}) custom-call(bf16[640,1536]{1,0:T(8,128)(2,1)} %bitcast.53, bf16[640,1536]{1,0:T(8,128)(2,1)} %bitcast.14.refs_1_.grad_any, bf16[8,8,144,384]{3,2,1,0:T(8,128)(2,1)} %bitcast.71), custom_call_target="tpu_custom_call" | custom-call | flops 7549747200 | bytes 18874368 | tf_op jit(solution)/shard_map/pallas_call | solution.py:349
  155.4 4.3 %all-to-all-start.4 = ((bf16[8,80,1536]{2,1,0:T(8,128)(2,1)}), bf16[8,80,1536]{2,1,0:T(8,128)(2,1)}, u32[]{:S(2)}, u32[]{:S(2)}) async-start(bf16[8,80,1536]{2,1,0:T(8,128)(2,1)} %shard_map.195.refs_0_), calls=%async_computation.4 | async-start | bytes 3932160 | tf_op jit(solution)/shard_map/all_to_all | solution.py:33
  159.8 12.1 %shard_map.196 = (bf16[8,80,1536]{2,1,0:T(8,128)(2,1)}, bf16[4,2,8,2,72,384]{5,4,3,2,1,0:T(8,128)(2,1)}) custom-call(bf16[640,1536]{1,0:T(8,128)(2,1)} %bitcast.54, bf16[640,1536]{1,0:T(8,128)(2,1)} %bitcast.14.refs_1_.grad_any, bf16[640,768]{1,0:T(8,128)(2,1)} %get-tuple-element.47.acted_any, bf16[640,1536]{1,0:T(8,128)(2,1)} %get-tuple-element.48.pre_any, ...), custom_call_target="tpu_custom_call" | custom-call | flops 6039797760 | bytes 38141952 | tf_op jit(solution)/shard_map/pallas_call | solution.py:461
  171.9 8.2 %all-to-all-done.4.refs_0_ = bf16[8,80,1536]{2,1,0:T(8,128)(2,1)} async-done(((bf16[8,80,1536]{2,1,0:T(8,128)(2,1)}), bf16[8,80,1536]{2,1,0:T(8,128)(2,1)}, u32[]{:S(2)}, u32[]{:S(2)}) %all-to-all-start.4) | async-done | bytes 1966112 | tf_op jit(solution)/shard_map/all_to_all | solution.py:33
  190.8 4.9 %shard_map.198 = (f32[128,1536]{1,0:T(8,128)}, bf16[128,1536]{1,0:T(8,128)(2,1)}, bf16[128,1536]{1,0:T(8,128)(2,1)}) custom-call(bf16[640,128]{1,0:T(8,128)(2,1)} %get-tuple-element.84.refs_6_.refs_0_, bf16[8,80,1536]{2,1,0:T(8,128)(2,1)} %get-tuple-element.53.refs_1_, f32[128,1536]{1,0:T(8,128)} %get-tuple-element.52.refs_2_.refs_3_, ...), custom_call_target="tpu_custom_call" | custom-call | flops 251658240 | bytes 4888576 | tf_op jit(solution)/shard_map/pallas_call | solution.py:68
  195.7 7.7 %shard_map.199 = (bf16[12,128,128]{2,1,0:T(8,128)(2,1)}, bf16[128,512]{1,0:T(8,128)(2,1)}, f32[128,512]{1,0:T(8,128)}) custom-call(bf16[128,1536]{1,0:T(8,128)(2,1)} %get-tuple-element.54.refs_0_, bf16[128,1536]{1,0:T(8,128)(2,1)} %get-tuple-element.39.refs_0_.refs_1_, bf16[128,512]{1,0:T(8,128)(2,1)} %copy-done.22, ...), custom_call_target="tpu_custom_call" | custom-call | flops 1107296256 | bytes 6685192 | tf_op jit(solution)/shard_map/pallas_call | solution.py:68
  208.2 4.6 %collective-permute-done.13.refs_2_ = bf16[128,512]{1,0:T(8,128)(2,1)S(1)} collective-permute-done((bf16[128,512]{1,0:T(8,128)(2,1)}, bf16[128,512]{1,0:T(8,128)(2,1)S(1)}, u32[]{:S(2)}, u32[]{:S(2)}) %collective-permute-start.13) | collective-permute-done | bytes 131104 | tf_op jit(solution)/shard_map/ppermute | solution.py:1074
  235.0 6.9 %all-to-all-start.9 = ((bf16[16,2,72,384]{3,2,1,0:T(8,128)(2,1)}), bf16[16,2,72,384]{3,2,1,0:T(8,128)(2,1)}, u32[]{:S(2)}, u32[]{:S(2)}) async-start(bf16[16,2,72,384]{3,2,1,0:T(8,128)(2,1)} %shard_map.201.refs_5_), calls=%async_computation.11 | async-start | bytes 3538944 | tf_op jit(solution)/shard_map/all_to_all | solution.py:33
  248.1 6.5 %shard_map.204 = (bf16[128,1536]{1,0:T(8,128)(2,1)}, bf16[1536,128]{1,0:T(8,128)(2,1)}) custom-call(bf16[16,128,128]{2,1,0:T(8,128)(2,1)} %shard_map.200.refs_0_, bf16[1536,2048]{1,0:T(8,128)(2,1)} %all-gather.6.cloned.1.call-done.refs_2_.refs_1_, bf16[128,1536]{1,0:T(8,128)(2,1)} %refs_2_.1, f32[1,1536]{1,0:T(1,128)} %slice.26.refs_1_.refs_3_, ...), custom_call_target="tpu_custom_call" | custom-call | flops 805306368 | bytes 9181184 | tf_op jit(solution)/shard_map/pallas_call | solution.py:68
  254.7 12.3 %all-to-all-done.9.in_any = bf16[16,2,72,384]{3,2,1,0:T(8,128)(2,1)} async-done(((bf16[16,2,72,384]{3,2,1,0:T(8,128)(2,1)}), bf16[16,2,72,384]{3,2,1,0:T(8,128)(2,1)}, u32[]{:S(2)}, u32[]{:S(2)}) %all-to-all-start.9) | async-done | bytes 1769504 | tf_op jit(solution)/shard_map/all_to_all | solution.py:33
  269.3 4.5 %all-to-all-start.6 = ((bf16[4,384,512]{2,1,0:T(8,128)(2,1)}), bf16[4,384,512]{2,1,0:T(8,128)(2,1)}, u32[]{:S(2)}, u32[]{:S(2)}) async-start(bf16[4,384,512]{2,1,0:T(8,128)(2,1)} %shard_map.202.refs_6_), calls=%async_computation.7 | async-start | bytes 3145728 | tf_op jit(solution)/shard_map/all_to_all | solution.py:33
  279.2 15.8 %collective-permute-done.18.refs_3_ = bf16[384,128]{1,0:T(8,128)(2,1)S(1)} collective-permute-done((bf16[384,128]{1,0:T(8,128)(2,1)S(1)}, bf16[384,128]{1,0:T(8,128)(2,1)S(1)}, u32[]{:S(2)}, u32[]{:S(2)}) %collective-permute-start.18) | collective-permute-done | bytes 98336 | tf_op jit(solution)/shard_map/ppermute | solution.py:879
  301.0 24.5 %all_to_all.63.refs_0_ = bf16[32,96,128]{2,1,0:T(8,128)(2,1)} all-to-all(bf16[32,96,128]{2,1,0:T(8,128)(2,1)} %shard_map.206), channel_id=1, replica_groups=mesh['h'=2,'z'=4,'y'=4,'x'=2,'c'=2] {'h','z','x','c'}, dimensions={0} | all-to-all | bytes 1572864 | tf_op jit(solution)/shard_map/all_to_all | solution.py:33
  327.8 5.6 %all-to-all-start.8 = ((bf16[8,4,96,128]{3,2,1,0:T(8,128)(2,1)}), bf16[8,4,96,128]{3,2,1,0:T(8,128)(2,1)}, u32[]{:S(2)}, u32[]{:S(2)}) async-start(bf16[8,4,96,128]{3,2,1,0:T(8,128)(2,1)} %shard_map.207), calls=%async_computation.10 | async-start | bytes 1572864 | tf_op jit(solution)/shard_map/all_to_all | solution.py:33
  337.8 6.9 %shard_map.209 = (f32[8,96,1536]{2,1,0:T(8,128)}, f32[8,48,1536]{2,1,0:T(8,128)}) custom-call(bf16[4,8,2,72,384]{4,3,2,1,0:T(8,128)(2,1)} %bitcast.56), custom_call_target="tpu_custom_call" | custom-call | tf_op jit(solution)/shard_map/pallas_call | solution.py:690
  (188 shorter events, 107.6 us)
Async XLA Ops:
  7.2 60.3 %all-gather.6.cloned.1.call-start = ((), (), s32[]{:S(2)}) async-start(), calls=%async_computation.12 | async-start | bytes 6684672 | tf_op jit(solution)/shard_map/all_gather | solution.py:984
  10.8 20.8 %all-to-all-start = ((bf16[8,112,384]{2,1,0:T(8,128)(2,1)}), bf16[8,112,384]{2,1,0:T(8,128)(2,1)S(1)}, u32[]{:S(2)}, u32[]{:S(2)}) async-start(bf16[8,112,384]{2,1,0:T(8,128)(2,1)} %broadcast_in_dim.58), calls=%async_computation | async-start | bytes 1376256 | tf_op jit(solution)/shard_map/all_to_all | solution.py:33
  32.5 25.0 %all-to-all-start.1 = ((bf16[8,144,384]{2,1,0:T(8,128)(2,1)}), bf16[8,144,384]{2,1,0:T(8,128)(2,1)S(1)}, u32[]{:S(2)}, u32[]{:S(2)}) async-start(bf16[8,144,384]{2,1,0:T(8,128)(2,1)} %shard_map.187), calls=%async_computation.1 | async-start | bytes 1769472 | tf_op jit(solution)/shard_map/all_to_all | solution.py:33
  36.2 104.5 %all-gather.8.cloned.1.call-start = ((), (), s32[]{:S(2)}) async-start(), calls=%async_computation.15 | async-start | bytes 7962624 | tf_op jit(solution)/shard_map/all_gather | solution.py:1031
  36.6 21.8 %collective-permute-start.1 = (bf16[8,96,384]{2,1,0:T(8,128)(2,1)S(1)}, bf16[8,96,384]{2,1,0:T(8,128)(2,1)S(1)}, u32[]{:S(2)}, u32[]{:S(2)}) collective-permute-start(bf16[8,96,384]{2,1,0:T(8,128)(2,1)S(1)} %slice.34.refs_8_), channel_id=1, source_target_pairs={{0,16},{16,0},{32,48},{48,32},{1,17},{17,1},{33,49},{49,33},{2,18}... | collective-permute-start | bytes 1769480 | tf_op jit(solution)/shard_map/ppermute | solution.py:673
  39.0 25.9 %collective-permute-start.2 = (bf16[8,96,384]{2,1,0:T(8,128)(2,1)S(1)}, bf16[8,96,384]{2,1,0:T(8,128)(2,1)}, u32[]{:S(2)}, u32[]{:S(2)}) collective-permute-start(bf16[8,96,384]{2,1,0:T(8,128)(2,1)S(1)} %slice.34.refs_8_), channel_id=1, source_target_pairs={{0,32},{16,48},{32,0},{48,16},{1,33},{17,49},{33,1},{49,17},{2,34}... | collective-permute-start | bytes 1769480 | tf_op jit(solution)/shard_map/ppermute | solution.py:673
  43.3 24.2 %collective-permute-start.3 = (bf16[8,96,384]{2,1,0:T(8,128)(2,1)S(1)}, bf16[8,96,384]{2,1,0:T(8,128)(2,1)}, u32[]{:S(2)}, u32[]{:S(2)}) collective-permute-start(bf16[8,96,384]{2,1,0:T(8,128)(2,1)S(1)} %slice.34.refs_8_), channel_id=1, source_target_pairs={{0,48},{16,32},{32,16},{48,0},{1,49},{17,33},{33,17},{49,1},{2,50}... | collective-permute-start | bytes 1769480 | tf_op jit(solution)/shard_map/ppermute | solution.py:673
  72.6 37.8 %all-to-all-start.2 = ((bf16[8,80,1536]{2,1,0:T(8,128)(2,1)}), bf16[8,80,1536]{2,1,0:T(8,128)(2,1)}, u32[]{:S(2)}, u32[]{:S(2)}) async-start(bf16[8,80,1536]{2,1,0:T(8,128)(2,1)} %bitcast.13), calls=%async_computation.2 | async-start | bytes 3932160 | tf_op jit(solution)/shard_map/all_to_all | solution.py:33
  79.2 23.8 %collective-permute-start.4 = (bf16[128,512]{1,0:T(8,128)(2,1)S(1)}, bf16[128,512]{1,0:T(8,128)(2,1)S(1)}, u32[]{:S(2)}, u32[]{:S(2)}) collective-permute-start(bf16[128,512]{1,0:T(8,128)(2,1)S(1)} %copy-done.21), channel_id=1, source_target_pairs={{0,1},{1,2},{2,3},{3,4},{4,5},{5,6},{6,7},{7,8},{8,9},{9,10},{10,1... | collective-permute-start | bytes 393224 | tf_op jit(solution)/shard_map/ppermute | solution.py:1034
  138.6 16.0 %collective-permute-start.10 = (bf16[1536,128]{1,0:T(8,128)(2,1)}, bf16[1536,128]{1,0:T(8,128)(2,1)}, u32[]{:S(2)}, u32[]{:S(2)}) collective-permute-start(bf16[1536,128]{1,0:T(8,128)(2,1)} %get-tuple-element.46), channel_id=1, source_target_pairs={{0,2},{2,0},{1,3},{3,1},{4,6},{6,4},{5,7},{7,5},{8,10},{10,8},{9,1... | collective-permute-start | bytes 1179656 | tf_op jit(solution)/shard_map/ppermute | solution.py:1042
  139.2 15.4 %collective-permute-start.9 = (bf16[128,1536]{1,0:T(8,128)(2,1)}, bf16[128,1536]{1,0:T(8,128)(2,1)S(1)}, u32[]{:S(2)}, u32[]{:S(2)}) collective-permute-start(bf16[128,1536]{1,0:T(8,128)(2,1)} %get-tuple-element.45), channel_id=1, source_target_pairs={{0,2},{2,0},{1,3},{3,1},{4,6},{6,4},{5,7},{7,5},{8,10},{10,8},{9,1... | collective-permute-start | bytes 1179656 | tf_op jit(solution)/shard_map/ppermute | solution.py:1041
  155.4 24.7 %all-to-all-start.4 = ((bf16[8,80,1536]{2,1,0:T(8,128)(2,1)}), bf16[8,80,1536]{2,1,0:T(8,128)(2,1)}, u32[]{:S(2)}, u32[]{:S(2)}) async-start(bf16[8,80,1536]{2,1,0:T(8,128)(2,1)} %shard_map.195.refs_0_), calls=%async_computation.4 | async-start | bytes 3932160 | tf_op jit(solution)/shard_map/all_to_all | solution.py:33
  159.8 69.3 %reduce-scatter.3.cloned.1.call-start = ((), (), s32[]{:S(2)}) async-start(), calls=%async_computation.13 | async-start | bytes 7962624 | tf_op jit(solution)/shard_map/reduce_scatter | solution.py:1054
  183.0 43.3 %all-to-all-start.5 = ((bf16[8,80,1536]{2,1,0:T(8,128)(2,1)}), bf16[8,80,1536]{2,1,0:T(8,128)(2,1)}, u32[]{:S(2)}, u32[]{:S(2)}) async-start(bf16[8,80,1536]{2,1,0:T(8,128)(2,1)} %get-tuple-element.51), calls=%async_computation.5 | async-start | bytes 3932160 | tf_op jit(solution)/shard_map/all_to_all | solution.py:33
  187.4 110.3 %reduce-scatter.5.cloned.1.call-start = ((), (), s32[]{:S(2)}) async-start(), calls=%async_computation.14 | async-start | bytes 1474560 | tf_op jit(solution)/shard_map/reduce_scatter | solution.py:1098
  208.2 10.8 %collective-permute-start.16 = (bf16[128,768]{1,0:T(8,128)(2,1)}, bf16[128,768]{1,0:T(8,128)(2,1)S(1)}, u32[]{:S(2)}, u32[]{:S(2)}) collective-permute-start(bf16[128,768]{1,0:T(8,128)(2,1)} %get-tuple-element.80), channel_id=1, source_target_pairs={{0,2},{2,0},{1,3},{3,1},{4,6},{6,4},{5,7},{7,5},{8,10},{10,8},{9,1... | collective-permute-start | bytes 589832 | tf_op jit(solution)/shard_map/ppermute | solution.py:709
  219.7 11.7 %collective-permute-start.17 = (bf16[2,128,384]{2,1,0:T(8,128)(2,1)}, bf16[2,128,384]{2,1,0:T(8,128)(2,1)}, u32[]{:S(2)}, u32[]{:S(2)}) collective-permute-start(bf16[2,128,384]{2,1,0:T(8,128)(2,1)} %fusion.1), channel_id=1, source_target_pairs={{0,1},{1,0},{2,3},{3,2},{4,5},{5,4},{6,7},{7,6},{8,9},{9,8},{10,11... | collective-permute-start | bytes 589832 | tf_op jit(solution)/shard_map/ppermute | solution.py:714
  235.0 31.9 %all-to-all-start.9 = ((bf16[16,2,72,384]{3,2,1,0:T(8,128)(2,1)}), bf16[16,2,72,384]{3,2,1,0:T(8,128)(2,1)}, u32[]{:S(2)}, u32[]{:S(2)}) async-start(bf16[16,2,72,384]{3,2,1,0:T(8,128)(2,1)} %shard_map.201.refs_5_), calls=%async_computation.11 | async-start | bytes 3538944 | tf_op jit(solution)/shard_map/all_to_all | solution.py:33
  241.9 95.9 %all-gather.10.cloned.1.call-start = ((), (), s32[]{:S(2)}) async-start(), calls=%async_computation.16 | async-start | bytes 4423680 | tf_op jit(solution)/shard_map/all_gather | solution.py:1106
  269.3 28.3 %all-to-all-start.6 = ((bf16[4,384,512]{2,1,0:T(8,128)(2,1)}), bf16[4,384,512]{2,1,0:T(8,128)(2,1)}, u32[]{:S(2)}, u32[]{:S(2)}) async-start(bf16[4,384,512]{2,1,0:T(8,128)(2,1)} %shard_map.202.refs_6_), calls=%async_computation.7 | async-start | bytes 3145728 | tf_op jit(solution)/shard_map/all_to_all | solution.py:33
  274.5 20.5 %collective-permute-start.18 = (bf16[384,128]{1,0:T(8,128)(2,1)S(1)}, bf16[384,128]{1,0:T(8,128)(2,1)S(1)}, u32[]{:S(2)}, u32[]{:S(2)}) collective-permute-start(bf16[384,128]{1,0:T(8,128)(2,1)S(1)} %get-tuple-element.77), channel_id=1, source_target_pairs={{0,4},{4,0},{8,12},{12,8},{1,5},{5,1},{9,13},{13,9},{2,6},{6,2},{1... | collective-permute-start | bytes 294920 | tf_op jit(solution)/shard_map/ppermute | solution.py:879
  276.5 21.1 %collective-permute-start.19 = (bf16[384,128]{1,0:T(8,128)(2,1)S(1)}, bf16[384,128]{1,0:T(8,128)(2,1)S(1)}, u32[]{:S(2)}, u32[]{:S(2)}) collective-permute-start(bf16[384,128]{1,0:T(8,128)(2,1)S(1)} %get-tuple-element.76), channel_id=1, source_target_pairs={{0,8},{4,12},{8,0},{12,4},{1,9},{5,13},{9,1},{13,5},{2,10},{6,14},... | collective-permute-start | bytes 294920 | tf_op jit(solution)/shard_map/ppermute | solution.py:879
  279.2 18.5 %collective-permute-start.20 = (bf16[384,128]{1,0:T(8,128)(2,1)S(1)}, bf16[384,128]{1,0:T(8,128)(2,1)S(1)}, u32[]{:S(2)}, u32[]{:S(2)}) collective-permute-start(bf16[384,128]{1,0:T(8,128)(2,1)S(1)} %get-tuple-element.75), channel_id=1, source_target_pairs={{0,12},{4,8},{8,4},{12,0},{1,13},{5,9},{9,5},{13,1},{2,14},{6,10},... | collective-permute-start | bytes 294920 | tf_op jit(solution)/shard_map/ppermute | solution.py:879
  327.8 19.0 %all-to-all-start.8 = ((bf16[8,4,96,128]{3,2,1,0:T(8,128)(2,1)}), bf16[8,4,96,128]{3,2,1,0:T(8,128)(2,1)}, u32[]{:S(2)}, u32[]{:S(2)}) async-start(bf16[8,4,96,128]{3,2,1,0:T(8,128)(2,1)} %shard_map.207), calls=%async_computation.10 | async-start | bytes 1572864 | tf_op jit(solution)/shard_map/all_to_all | solution.py:33
  (41 other events, 187.5 us)
Sparse Core Ops, SparseCore 0:
  10.3 56.4 all-gather.5
  72.7 45.2 all-gather.7
  180.2 48.8 reduce-scatter.2
  235.1 40.2 reduce-scatter.4
  277.5 52.9 all-gather.9
